TPU v7x, 32 devices: a whole 2x2x4 slice. The times are simulated.
32 devices in a mesh: clip: 8 (over z, y), head: 4 (over x, core).
Axes of the slice: x: 2, y: 2, z: 4, core: 2. Of those that a mesh axis runs over, the one named last changes fastest.
Arguments:
- tokens: bfloat16 [32768, 768], P(('clip', 'head')), may hold values from -6 to 6
- frame_counts: int32 [8], P('clip'), may hold values from 8 to 16, as said below
- token_mask: int32 [32768], P(('clip', 'head')), may hold values 0 or 1
- targets: int32 [32768], P(('clip', 'head')), may hold values from 0 to 1023
- norm_gain: float32 [2, 2, 768], replicated, may hold values from 0.5 to 1.5
- norm_bias: float32 [2, 2, 768], replicated, may hold values from -1.2 to 1.2
- w_qkv: bfloat16 [2, 3, 768, 768], P(None, None, None, 'head'), may hold values from -0.21875 to 0.21875
- qv_bias: float32 [2, 2, 768], P(None, None, 'head'), may hold values from -1.2 to 1.2
- w_out: bfloat16 [2, 768, 768], P(None, 'head'), may hold values from -1.25 to 1.25
- vec_bias: float32 [2, 2, 768], replicated, may hold values from -1.2 to 1.2
- w_up: bfloat16 [2, 768, 3072], P(None, None, 'head'), may hold values from -0.21875 to 0.21875
- up_bias: float32 [2, 3072], P(None, 'head'), may hold values from -1.2 to 1.2
- w_down: bfloat16 [2, 3072, 768], P(None, 'head'), may hold values from -0.109375 to 0.109375
- code_head: bfloat16 [768, 1024], replicated, may hold values from -0.3125 to 0.3125
Outputs:
- loss_mean: float32 [], replicated
- grad_input: float32 [32768, 768], P(('clip', 'head'))
- grad_norm_gain: float32 [2, 2, 768], replicated
- grad_norm_bias: float32 [2, 2, 768], replicated
- grad_qkv: float32 [2, 3, 768, 768], P(None, None, None, 'head')
- grad_qv_bias: float32 [2, 2, 768], P(None, None, 'head')
- grad_out: float32 [2, 768, 768], P(None, 'head')
- grad_vec_bias: float32 [2, 2, 768], replicated
- grad_up: float32 [2, 768, 3072], P(None, None, 'head')
- grad_up_bias: float32 [2, 3072], P(None, 'head')
- grad_down: float32 [2, 3072, 768], P(None, 'head')
Inputs may be any that keep to these rules, and one draw needn't show every extreme that they name: `frame_counts`: every clip has 8 or 16 real frames, and both counts occur; frames from the count on are padding.
All inputs are finite; a program needn't handle non-finite values. No bound on the sum of `token_mask` on one device may be relied on, other than what follows from the above.
Results may differ from a plain program's by a relative error of at most 0.013.
Values may be sent and summed in bfloat16 or wider, within the bound.
No kernel may reach another device: no remote copies, remote signals or barrier semaphores. Data moves between devices by JAX's collectives and lax.ppermute only.
A program may use at most 320 MiB of HBM per device.

v0:
```python
from functools import partial

import jax
import jax.numpy as jnp
from jax import lax
from jax.sharding import PartitionSpec as P

HD = 64
FRAMES = 16
SIDE = 16
TUBE = 4


epsilon = 1e-06
masked_score = -1e30


def layer_norm(stream, gain, shift):
    centre = jnp.mean(stream, axis=-1, keepdims=True)
    centred = stream - centre
    spread = jnp.mean(centred * centred, axis=-1, keepdims=True)
    return centred * lax.rsqrt(spread + epsilon) * gain + shift


def norm_back(stream_in, gain, shift, grad_normed):
    _, pullback = jax.vjp(layer_norm, stream_in, gain, shift)
    return pullback(grad_normed)


def gelu_back(hidden, grad_active):
    _, pullback = jax.vjp(partial(jax.nn.gelu, approximate=True), hidden)
    return pullback(grad_active)[0]


def windows_of(values, window_kind):
    trailing = values.shape[1:]
    if window_kind == 0:
        return values.reshape((values.shape[0] // (SIDE * SIDE), SIDE * SIDE) + trailing)
    clip_count = values.shape[0] // (FRAMES * SIDE * SIDE)
    tile_count = SIDE // TUBE
    lattice = values.reshape((clip_count, FRAMES, tile_count, TUBE, tile_count, TUBE) + trailing)
    axis_order = (0, 2, 4, 1, 3, 5) + tuple(range(6, 6 + len(trailing)))
    return lattice.transpose(axis_order).reshape(
        (clip_count * tile_count * tile_count, FRAMES * TUBE * TUBE) + trailing
    )


def rows_of(values, window_kind):
    trailing = values.shape[2:]
    if window_kind == 0:
        return values.reshape((-1,) + trailing)
    tile_count = SIDE // TUBE
    clip_count = values.shape[0] // (tile_count * tile_count)
    lattice = values.reshape((clip_count, tile_count, tile_count, FRAMES, TUBE, TUBE) + trailing)
    axis_order = (0, 3, 1, 4, 2, 5) + tuple(range(6, 6 + len(trailing)))
    return lattice.transpose(axis_order).reshape((-1,) + trailing)


def mask_of(valid_rows, window_kind):
    inside = windows_of(valid_rows, window_kind)
    return jnp.logical_or(inside[:, None, :], jnp.logical_not(inside[:, :, None]))


def spread_rows(values):
    return lax.all_gather(values, "head", axis=0, tiled=True)


def collect_rows(values, weight):
    return lax.psum_scatter(
        jnp.dot(values, weight, preferred_element_type=jnp.float32),
        "head",
        scatter_dimension=0,
        tiled=True,
    )


def spread_grads(values):
    return lax.all_gather(values, "head", axis=0, tiled=True)


def collect_grads(values):
    return lax.psum_scatter(
        values.astype(jnp.bfloat16), "head", scatter_dimension=0, tiled=True
    ).astype(jnp.float32)


def split_windows(qkv, window_kind):
    head_local = qkv.shape[2] // HD
    windowed = windows_of(qkv.reshape(qkv.shape[0], 3, head_local, HD), window_kind)
    return (windowed[:, :, 0], windowed[:, :, 1], windowed[:, :, 2])


def window_scores(queries, keys_win, allowed):
    scores = jnp.einsum(
        "wqhd,wkhd->whqk", queries, keys_win, preferred_element_type=jnp.float32
    ) * HD ** (-0.5)
    return jnp.where(allowed[:, None], scores, masked_score)


def attend(qkv, allowed, window_kind):
    queries, keys_win, values_win = split_windows(qkv, window_kind)
    scores = window_scores(queries, keys_win, allowed)
    score_top = jnp.max(scores, axis=-1, keepdims=True)
    exp_terms = jnp.exp(scores - score_top)
    exp_total = jnp.sum(exp_terms, axis=-1, keepdims=True)
    soft_probs = (exp_terms / exp_total).astype(jnp.bfloat16)
    attended = jnp.einsum(
        "whqk,wkhd->wqhd", soft_probs, values_win, preferred_element_type=jnp.float32
    )
    rows_back = (
        rows_of(attended, window_kind).reshape(qkv.shape[0], qkv.shape[2]).astype(jnp.bfloat16)
    )
    return (rows_back, score_top + jnp.log(exp_total))


def attend_back(qkv, log_total, grad_attended, allowed, window_kind):
    row_count = qkv.shape[0]
    head_local = qkv.shape[2] // HD
    queries, keys_win, values_win = split_windows(qkv, window_kind)
    grad_win = windows_of(grad_attended.reshape(row_count, head_local, HD), window_kind)
    scores = window_scores(queries, keys_win, allowed)
    soft_probs = jnp.exp(scores - log_total)
    grad_probs = jnp.einsum(
        "wqhd,wkhd->whqk", grad_win, values_win, preferred_element_type=jnp.float32
    )
    row_delta = jnp.sum(soft_probs * grad_probs, axis=-1, keepdims=True)
    grad_scores = (soft_probs * (grad_probs - row_delta)).astype(jnp.bfloat16)
    grad_queries = jnp.einsum(
        "whqk,wkhd->wqhd", grad_scores, keys_win, preferred_element_type=jnp.float32
    ) * HD ** (-0.5)
    grad_keys = jnp.einsum(
        "whqk,wqhd->wkhd", grad_scores, queries, preferred_element_type=jnp.float32
    ) * HD ** (-0.5)
    grad_values = jnp.einsum(
        "whqk,wqhd->wkhd",
        soft_probs.astype(jnp.bfloat16),
        grad_win,
        preferred_element_type=jnp.float32,
    )
    stacked = jnp.stack([grad_queries, grad_keys, grad_values], axis=2)
    return rows_of(stacked, window_kind).reshape(row_count, 3, head_local * HD).astype(jnp.bfloat16)


def project_qkv(normed, weight, bias_pair):
    projected = jnp.einsum("rd,jdc->rjc", normed, weight, preferred_element_type=jnp.float32)
    bias_rows = jnp.stack([bias_pair[0], jnp.zeros_like(bias_pair[0]), bias_pair[1]])
    return (projected + bias_rows).astype(jnp.bfloat16)


def code_loss(stream, code_head, targets, token_weight):
    logits = jnp.dot(stream.astype(jnp.bfloat16), code_head, preferred_element_type=jnp.float32)
    score_top = jnp.max(logits, axis=1, keepdims=True)
    log_total = score_top + jnp.log(jnp.sum(jnp.exp(logits - score_top), axis=1, keepdims=True))
    onehot = targets[:, None] == jnp.arange(logits.shape[1], dtype=jnp.int32)[None, :]
    picked = jnp.sum(jnp.where(onehot, logits, 0.0), axis=1)
    loss_local = jnp.sum(token_weight * (log_total[:, 0] - picked))
    soft_codes = jnp.exp(logits - log_total)
    grad_logits = (token_weight[:, None] * (soft_codes - onehot.astype(jnp.float32))).astype(
        jnp.bfloat16
    )
    grad_stream = jnp.einsum(
        "rc,dc->rd", grad_logits, code_head, preferred_element_type=jnp.float32
    )
    return (loss_local, grad_stream)


def on_device(
    tokens,
    frame_counts,
    token_mask,
    targets,
    norm_gain,
    norm_bias,
    w_qkv,
    qv_bias,
    w_out,
    vec_bias,
    w_up,
    up_bias,
    w_down,
    code_head,
):
    head_count = lax.axis_size("head")
    head_index = lax.axis_index("head")
    local_rows = tokens.shape[0]
    group_rows = local_rows * head_count
    clip_rows = FRAMES * SIDE * SIDE
    position = jnp.arange(group_rows, dtype=jnp.int32)
    clip_number = position // clip_rows
    frame_number = position // (SIDE * SIDE) % FRAMES
    clip_table = jnp.arange(frame_counts.shape[0], dtype=jnp.int32)
    count_row = jnp.sum(
        jnp.where(clip_number[:, None] == clip_table[None, :], frame_counts[None, :], 0), axis=1
    )
    valid_group = frame_number < count_row
    valid_local = lax.dynamic_slice_in_dim(valid_group, head_index * local_rows, local_rows, 0)
    token_weight = token_mask.astype(jnp.float32) * valid_local.astype(jnp.float32)
    block_terms = [None, None]
    gain_grads = [[None, None], [None, None]]
    shift_grads = [[None, None], [None, None]]
    vec_grads = [[None, None], [None, None]]
    stream = tokens.astype(jnp.float32)
    masks = [mask_of(valid_group, 0), mask_of(valid_group, 1)]
    kept_attention = []
    kept_mlp = []
    for layer_index in range(2):
        normed = layer_norm(stream, norm_gain[layer_index, 0], norm_bias[layer_index, 0]).astype(
            jnp.bfloat16
        )
        gathered = spread_rows(normed)
        qkv = project_qkv(gathered, w_qkv[layer_index], qv_bias[layer_index])
        attended, log_total = attend(qkv, masks[layer_index], layer_index)
        kept_attention.append((stream, gathered, qkv, attended, log_total))
        stream = stream + collect_rows(attended, w_out[layer_index]) + vec_bias[layer_index, 0]
        normed = layer_norm(stream, norm_gain[layer_index, 1], norm_bias[layer_index, 1]).astype(
            jnp.bfloat16
        )
        gathered = spread_rows(normed)
        hidden = (
            jnp.dot(gathered, w_up[layer_index], preferred_element_type=jnp.float32)
            + up_bias[layer_index]
        )
        active = jax.nn.gelu(hidden, approximate=True).astype(jnp.bfloat16)
        kept_mlp.append((stream, gathered, hidden, active))
        stream = stream + collect_rows(active, w_down[layer_index]) + vec_bias[layer_index, 1]
    loss_local, grad_stream = code_loss(stream, code_head, targets, token_weight)
    for layer_index in (1, 0):
        stream_in, gathered, hidden, active = kept_mlp[layer_index]
        grad_local = grad_stream.astype(jnp.bfloat16)
        vec_grads[layer_index][1] = jnp.sum(grad_local, axis=0, dtype=jnp.float32)
        grad_rows = spread_grads(grad_local)
        down_grad = jnp.einsum("rf,rd->fd", active, grad_rows, preferred_element_type=jnp.float32)
        grad_active = jnp.einsum(
            "rd,fd->rf", grad_rows, w_down[layer_index], preferred_element_type=jnp.float32
        )
        grad_hidden = gelu_back(hidden, grad_active).astype(jnp.bfloat16)
        up_shift = jnp.sum(grad_hidden, axis=0, dtype=jnp.float32)
        up_grad = jnp.einsum("rd,rf->df", gathered, grad_hidden, preferred_element_type=jnp.float32)
        grad_normed = collect_grads(
            jnp.einsum(
                "rf,df->rd", grad_hidden, w_up[layer_index], preferred_element_type=jnp.float32
            )
        )
        grad_inner, gain_grads[layer_index][1], shift_grads[layer_index][1] = norm_back(
            stream_in, norm_gain[layer_index, 1], norm_bias[layer_index, 1], grad_normed
        )
        grad_stream = grad_stream + grad_inner
        stream_in, gathered, qkv, attended, log_total = kept_attention[layer_index]
        grad_local = grad_stream.astype(jnp.bfloat16)
        vec_grads[layer_index][0] = jnp.sum(grad_local, axis=0, dtype=jnp.float32)
        grad_rows = spread_grads(grad_local)
        out_grad = jnp.einsum("rc,rd->cd", attended, grad_rows, preferred_element_type=jnp.float32)
        grad_attended = jnp.einsum(
            "rd,cd->rc", grad_rows, w_out[layer_index], preferred_element_type=jnp.float32
        ).astype(jnp.bfloat16)
        grad_qkv = attend_back(qkv, log_total, grad_attended, masks[layer_index], layer_index)
        qkv_grad = jnp.einsum("rd,rjc->jdc", gathered, grad_qkv, preferred_element_type=jnp.float32)
        qkv_shift = jnp.sum(grad_qkv, axis=0, dtype=jnp.float32)
        qv_shift = jnp.stack([qkv_shift[0], qkv_shift[2]])
        grad_normed = collect_grads(
            jnp.einsum(
                "rjc,jdc->rd", grad_qkv, w_qkv[layer_index], preferred_element_type=jnp.float32
            )
        )
        grad_inner, gain_grads[layer_index][0], shift_grads[layer_index][0] = norm_back(
            stream_in, norm_gain[layer_index, 0], norm_bias[layer_index, 0], grad_normed
        )
        grad_stream = grad_stream + grad_inner
        layer_terms = (qkv_grad, qv_shift, out_grad, up_grad, up_shift, down_grad)
        block_terms[layer_index] = tuple(layer_terms)
    summed = lax.psum(block_terms[0] + block_terms[1], "clip")
    block_terms = [tuple(summed[:6]), tuple(summed[6:])]
    gains = jnp.stack([jnp.stack(gain_grads[0]), jnp.stack(gain_grads[1])])
    shifts = jnp.stack([jnp.stack(shift_grads[0]), jnp.stack(shift_grads[1])])
    vecs = jnp.stack([jnp.stack(vec_grads[0]), jnp.stack(vec_grads[1])])
    gain_sum, shift_sum, vec_sum, loss_total = lax.psum(
        (gains, shifts, vecs, loss_local), ("clip", "head")
    )

    def stack_member(member_index):
        return jnp.stack([block_terms[0][member_index], block_terms[1][member_index]])

    slot_total = frame_counts.shape[0] * lax.axis_size("clip") * clip_rows
    loss_mean = loss_total / slot_total
    return (
        loss_mean,
        grad_stream,
        gain_sum,
        shift_sum,
        stack_member(0),
        stack_member(1),
        stack_member(2),
        vec_sum,
        stack_member(3),
        stack_member(4),
        stack_member(5),
    )


def solution(mesh):
    placed = (
        P(("clip", "head"), None),
        P("clip"),
        P(("clip", "head")),
        P(("clip", "head")),
        P(),
        P(),
        P(None, None, None, "head"),
        P(None, None, "head"),
        P(None, "head", None),
        P(),
        P(None, None, "head"),
        P(None, "head"),
        P(None, "head", None),
        P(),
    )
    return jax.shard_map(
        on_device,
        mesh=mesh,
        in_specs=placed,
        out_specs=(
            P(),
            P(("clip", "head"), None),
            P(),
            P(),
            P(None, None, None, "head"),
            P(None, None, "head"),
            P(None, "head", None),
            P(),
            P(None, None, "head"),
            P(None, "head"),
            P(None, "head", None),
        ),
        check_vma=False,
    )
```

profile of v0, /device:TPU:0, one launch (start us, length us, event | category | flops | bytes accessed | tf_op | source)
XLA Modules:
  0.0 1971.6 jit_solution(13583452142574630614)
XLA Ops:
  20.5 43.6 %all-gather.9.cloned.1.call-done = bf16[4096,768]{1,0:T(8,128)(2,1)} async-done(((bf16[1024,768]{1,0:T(8,128)(2,1)}), bf16[4096,768]{1,0:T(8,128)(2,1)}) %all-gather.9.cloned.1.call-update) | async-done | bytes 6291472 | tf_op jit(solution)/shard_map/all_gather | solution.py:65
  96.9 98.5 %reduce-scatter.9.cloned.1.call-done = f32[1024,768]{1,0:T(8,128)} async-done(((f32[4096,768]{1,0:T(8,128)}), f32[1024,768]{1,0:T(8,128)}) %reduce-scatter.9.cloned.1.call-update) | async-done | bytes 3145744 | tf_op jit(solution)/shard_map/reduce_scatter | solution.py:69
  201.3 46.4 %all-gather.11.cloned.1.call-done = bf16[4096,768]{1,0:T(8,128)(2,1)} async-done(((bf16[1024,768]{1,0:T(8,128)(2,1)}), bf16[4096,768]{1,0:T(8,128)(2,1)}) %all-gather.11.cloned.1.call-update) | async-done | bytes 6291472 | tf_op jit(solution)/shard_map/all_gather | solution.py:65
  247.7 7.6 fusion.100
  259.9 10.8 fusion.97
  271.2 98.8 %reduce-scatter.11.cloned.1.call-done = f32[1024,768]{1,0:T(8,128)} async-done(((f32[4096,768]{1,0:T(8,128)}), f32[1024,768]{1,0:T(8,128)}) %reduce-scatter.11.cloned.1.call-update) | async-done | bytes 3145744 | tf_op jit(solution)/shard_map/reduce_scatter | solution.py:69
  379.4 43.7 %all-gather.13.cloned.1.call-done = bf16[4096,768]{1,0:T(8,128)(2,1)} async-done(((bf16[1024,768]{1,0:T(8,128)(2,1)}), bf16[4096,768]{1,0:T(8,128)(2,1)}) %all-gather.13.cloned.1.call-update) | async-done | bytes 6291472 | tf_op jit(solution)/shard_map/all_gather | solution.py:65
  432.8 8.0 copy.46
  440.8 23.3 %reshape_reshape.9 = bf16[1,16,4,4,4,4,3,3,64]{8,7,5,4,3,2,1,6,0:T(4,128)(2,1)} reshape(bf16[4096,3,192]{2,0,1:T(8,128)(2,1)} %copy.46) | data formatting | bytes 9437184 | tf_op jit(solution)/shard_map/reshape;reshape | solution.py:41
  464.0 10.9 copy.47
  491.7 8.2 copy.53
  500.0 8.5 convert_element_type.191
  508.5 8.0 fusion.121
  516.5 99.1 %reduce-scatter.13.cloned.1.call-done = f32[1024,768]{1,0:T(8,128)} async-done(((f32[4096,768]{1,0:T(8,128)}), f32[1024,768]{1,0:T(8,128)}) %reduce-scatter.13.cloned.1.call-update) | async-done | bytes 3145744 | tf_op jit(solution)/shard_map/reduce_scatter | solution.py:69
  622.4 46.5 %all-gather.15.cloned.1.call-done = bf16[4096,768]{1,0:T(8,128)(2,1)} async-done(((bf16[1024,768]{1,0:T(8,128)(2,1)}), bf16[4096,768]{1,0:T(8,128)(2,1)}) %all-gather.15.cloned.1.call-update) | async-done | bytes 6291472 | tf_op jit(solution)/shard_map/all_gather | solution.py:65
  668.9 8.1 fusion.93
  681.6 10.7 fusion.90
  692.4 99.1 %reduce-scatter.15.cloned.1.call-done = f32[1024,768]{1,0:T(8,128)} async-done(((f32[4096,768]{1,0:T(8,128)}), f32[1024,768]{1,0:T(8,128)}) %reduce-scatter.15.cloned.1.call-update) | async-done | bytes 3145744 | tf_op jit(solution)/shard_map/reduce_scatter | solution.py:69
  803.9 46.3 %all-gather.17.cloned.1.call-done = bf16[4096,768]{1,0:T(8,128)(2,1)} async-done(((bf16[1024,768]{1,0:T(8,128)(2,1)}), bf16[4096,768]{1,0:T(8,128)(2,1)}) %all-gather.17.cloned.1.call-update) | async-done | bytes 6291472 | tf_op jit(solution)/shard_map/all_gather | solution.py:78
  850.2 17.1 convert_reduce_fusion.1
  870.0 8.3 convolution_convert_fusion.1
  878.4 58.5 %reduce-scatter.17.cloned.1.call-done = bf16[1024,768]{1,0:T(8,128)(2,1)} async-done(((bf16[4096,768]{1,0:T(8,128)(2,1)}), bf16[1024,768]{1,0:T(8,128)(2,1)}) %reduce-scatter.17.cloned.1.call-update) | async-done | bytes 1572880 | tf_op jit(solution)/shard_map/reduce_scatter | solution.py:82
  946.7 46.5 %all-gather.19.cloned.1.call-done = bf16[4096,768]{1,0:T(8,128)(2,1)} async-done(((bf16[1024,768]{1,0:T(8,128)(2,1)}), bf16[4096,768]{1,0:T(8,128)(2,1)}) %all-gather.19.cloned.1.call-update) | async-done | bytes 6291472 | tf_op jit(solution)/shard_map/all_gather | solution.py:78
  1000.9 8.5 reshape_reshape.20
  1015.1 6.8 fusion.62
  1021.9 13.4 multiply_reduce_fusion.1
  1035.3 9.7 multiply_convert_fusion.1
  1058.9 11.0 convert_reduce_fusion
  1069.9 17.0 copy.64
  1086.9 23.3 %convert_element_type.207 = bf16[4096,3,192]{2,0,1:T(8,128)(2,1)} reshape(bf16[1,16,4,4,4,4,3,3,64]{8,7,5,4,3,2,1,6,0:T(4,128)(2,1)} %copy.64) | data formatting | bytes 9437184 | tf_op jit(solution)/shard_map/convert_element_type | solution.py:141
  1110.2 9.8 bitcast_convert_fusion.1
  1120.1 58.5 %reduce-scatter.19.cloned.1.call-done = bf16[1024,768]{1,0:T(8,128)(2,1)} async-done(((bf16[4096,768]{1,0:T(8,128)(2,1)}), bf16[1024,768]{1,0:T(8,128)(2,1)}) %reduce-scatter.19.cloned.1.call-update) | async-done | bytes 1572880 | tf_op jit(solution)/shard_map/reduce_scatter | solution.py:82
  1191.7 46.5 %all-gather.21.cloned.1.call-done = bf16[4096,768]{1,0:T(8,128)(2,1)} async-done(((bf16[1024,768]{1,0:T(8,128)(2,1)}), bf16[4096,768]{1,0:T(8,128)(2,1)}) %all-gather.21.cloned.1.call-update) | async-done | bytes 6291472 | tf_op jit(solution)/shard_map/all_gather | solution.py:78
  1238.2 18.2 convert_reduce_fusion.2
  1259.0 8.3 convolution_convert_fusion
  1267.4 58.5 %reduce-scatter.21.cloned.1.call-done = bf16[1024,768]{1,0:T(8,128)(2,1)} async-done(((bf16[4096,768]{1,0:T(8,128)(2,1)}), bf16[1024,768]{1,0:T(8,128)(2,1)}) %reduce-scatter.21.cloned.1.call-update) | async-done | bytes 1572880 | tf_op jit(solution)/shard_map/reduce_scatter | solution.py:82
  1335.1 46.2 %all-gather.23.cloned.1.call-done = bf16[4096,768]{1,0:T(8,128)(2,1)} async-done(((bf16[1024,768]{1,0:T(8,128)(2,1)}), bf16[4096,768]{1,0:T(8,128)(2,1)}) %all-gather.23.cloned.1.call-update) | async-done | bytes 6291472 | tf_op jit(solution)/shard_map/all_gather | solution.py:78
  1386.9 7.1 fusion.82
  1394.1 7.5 multiply_reduce_fusion
  1401.6 6.9 multiply_convert_fusion
  1433.2 7.5 bitcast_convert_fusion
  1440.9 10.2 convolution_bitcast_fusion.2
  1451.1 12.6 convolution_bitcast_fusion
  1471.4 6.6 convolution_bitcast_fusion.3
  1478.0 12.1 convolution_bitcast_fusion.1
  1501.8 38.5 %all-reduce.1 = (f32[1,2,192]{2,1,0:T(2,128)S(1)}, f32[1,2,192]{2,1,0:T(2,128)S(1)}, f32[1,768]{1,0:T(1,128)S(1)}, f32[1,768]{1,0:T(1,128)S(1)}) all-reduce(f32[1,2,192]{2,1,0:T(2,128)S(1)} %maximum_bitcast_fusion.7, f32[1,2,192]{2,1,0:T(2,128)S(1)} %maximum_bitcast_fusion.6, ...), channel_id=1, replica_groups=mesh['clip'=8,'head'=4] {'clip'}, use_global_device_ids=true, to_apply=%region_50.51 | all-reduce | flops 2304 | bytes 18432 | tf_op jit(solution)/shard_map/psum | solution.py:271
  1546.3 41.7 %all-reduce = (f32[]{:T(128)}, f32[2,2,768]{2,1,0:T(2,128)}, f32[2,2,768]{2,1,0:T(2,128)}, f32[2,2,768]{2,1,0:T(2,128)}) all-reduce(f32[]{:T(128)} %get-tuple-element.76, f32[2,2,768]{2,1,0:T(2,128)S(1)} %pad_maximum_fusion.4, f32[2,2,768]{2,1,0:T(2,128)S(1)} %pad_maximum_fusion.5, ...), channel_id=1, replica_groups=mesh['clip'=8,'head'=4] {'clip','head'}, use_global_device_ids=true, to_apply=%region_20.21 | all-reduce | flops 9217 | bytes 73736 | tf_op jit(solution)/shard_map/psum | solution.py:276
  1593.4 358.1 %all-reduce.5.cloned.1.call-done = (f32[1,3,768,192]{2,3,1,0:T(8,128)}, f32[1,3,768,192]{2,3,1,0:T(8,128)}, f32[1,192,768]{2,1,0:T(8,128)}, f32[1,192,768]{2,1,0...) async-done(((f32[1,3,768,192]{2,3,1,0:T(8,128)}, f32[1,3,768,192]{2,3,1,0:T(8,128)}, ...) | async-done | bytes 14155792 | tf_op jit(solution)/shard_map/psum | solution.py:271
  (437 shorter events, 252.2 us)
Async XLA Ops:
  7.2 784.3 %copy-start = (bf16[768,1024]{1,0:T(8,128)(2,1)S(1)}, bf16[768,1024]{1,0:T(8,128)(2,1)}, u32[]{:S(2)}) copy-start(bf16[768,1024]{1,0:T(8,128)(2,1)} %param.27) | copy-start | bytes 4718596
  7.2 56.8 %all-gather.9.cloned.1.call-start = ((), (), s32[]{:S(2)}) async-start(), calls=%async_computation.8 | async-start | bytes 7864320 | tf_op jit(solution)/shard_map/all_gather | solution.py:65
  12.4 185.9 %copy-start.62 = (f32[768]{0:T(1024)}, f32[768]{0:T(1024)S(1)}, u32[]{:S(2)}) copy-start(f32[768]{0:T(1024)S(1)} %get-tuple-element.113) | copy-start | bytes 9220
  12.4 362.3 %copy-start.60 = (f32[768]{0:T(1024)}, f32[768]{0:T(1024)S(1)}, u32[]{:S(2)}) copy-start(f32[768]{0:T(1024)S(1)} %get-tuple-element.111) | copy-start | bytes 9220
  14.8 180.6 %reduce-scatter.9.cloned.1.call-start = ((), (), s32[]{:S(2)}) async-start(), calls=%async_computation.9 | async-start | bytes 15728640 | tf_op jit(solution)/shard_map/reduce_scatter | solution.py:69
  96.2 151.5 %all-gather.11.cloned.1.call-start = ((), (), s32[]{:S(2)}) async-start(), calls=%async_computation.10 | async-start | bytes 7864320 | tf_op jit(solution)/shard_map/all_gather | solution.py:65
  201.2 168.7 %reduce-scatter.11.cloned.1.call-start = ((), (), s32[]{:S(2)}) async-start(), calls=%async_computation.11 | async-start | bytes 15728640 | tf_op jit(solution)/shard_map/reduce_scatter | solution.py:69
  201.3 54.1 %copy-start.90 = (f32[768]{0:T(1024)}, f32[768]{0:T(1024)S(1)}, u32[]{:S(2)}) copy-start(f32[768]{0:T(1024)S(1)} %get-tuple-element.40) | copy-start | bytes 9220
  201.3 648.9 %copy-start.92 = (f32[768]{0:T(1024)}, f32[768]{0:T(1024)S(1)}, u32[]{:S(2)}) copy-start(f32[768]{0:T(1024)S(1)} %get-tuple-element.39) | copy-start | bytes 9220
  270.7 152.4 %all-gather.13.cloned.1.call-start = ((), (), s32[]{:S(2)}) async-start(), calls=%async_computation.12 | async-start | bytes 7864320 | tf_op jit(solution)/shard_map/all_gather | solution.py:65
  374.9 48.3 %copy-start.42 = (bf16[1,3,768,192]{2,3,1,0:T(8,128)(2,1)S(1)}, bf16[1,3,768,192]{2,3,1,0:T(8,128)(2,1)}, u32[]{:S(2)}) copy-start(bf16[1,3,768,192]{2,3,1,0:T(8,128)(2,1)} %get-tuple-element.88) | copy-start | bytes 2654212
  376.6 239.1 %reduce-scatter.13.cloned.1.call-start = ((), (), s32[]{:S(2)}) async-start(), calls=%async_computation.13 | async-start | bytes 15728640 | tf_op jit(solution)/shard_map/reduce_scatter | solution.py:69
  516.5 152.4 %all-gather.15.cloned.1.call-start = ((), (), s32[]{:S(2)}) async-start(), calls=%async_computation.14 | async-start | bytes 7864320 | tf_op jit(solution)/shard_map/all_gather | solution.py:65
  622.3 169.1 %reduce-scatter.15.cloned.1.call-start = ((), (), s32[]{:S(2)}) async-start(), calls=%async_computation.15 | async-start | bytes 15728640 | tf_op jit(solution)/shard_map/reduce_scatter | solution.py:69
  692.3 157.9 %all-gather.17.cloned.1.call-start = ((), (), s32[]{:S(2)}) async-start(), calls=%async_computation.16 | async-start | bytes 7864320 | tf_op jit(solution)/shard_map/all_gather | solution.py:78
  803.6 133.3 %reduce-scatter.17.cloned.1.call-start = ((), (), s32[]{:S(2)}) async-start(), calls=%async_computation.17 | async-start | bytes 7864320 | tf_op jit(solution)/shard_map/reduce_scatter | solution.py:82
  878.3 114.8 %all-gather.19.cloned.1.call-start = ((), (), s32[]{:S(2)}) async-start(), calls=%async_computation.18 | async-start | bytes 7864320 | tf_op jit(solution)/shard_map/all_gather | solution.py:78
  946.6 231.9 %reduce-scatter.19.cloned.1.call-start = ((), (), s32[]{:S(2)}) async-start(), calls=%async_computation.19 | async-start | bytes 7864320 | tf_op jit(solution)/shard_map/reduce_scatter | solution.py:82
  1021.9 23.1 %slice-start.3 = ((s8[9437184]{0:T(1024)(128)(4,1)}), s8[1048576]{0:T(1024)(128)(4,1)S(1)}, s32[]{:S(2)}) async-start(s8[9437184]{0:T(1024)(128)(4,1)} %bitcast.267), calls=%async_computation.28 | async-start | bytes 2097152
  1021.9 23.1 %slice-start.4 = ((s8[9437184]{0:T(1024)(128)(4,1)}), s8[4194304]{0:T(1024)(128)(4,1)S(1)}, s32[]{:S(2)}) async-start(s8[9437184]{0:T(1024)(128)(4,1)} %bitcast.267), calls=%async_computation.29 | async-start | bytes 8388608
  1086.9 23.3 %copy-start.39 = (bf16[2,3,768,192]{2,3,1,0:T(8,128)(2,1)S(1)}, bf16[2,3,768,192]{2,3,1,0:T(8,128)(2,1)}, u32[]{:S(2)}) copy-start(bf16[2,3,768,192]{2,3,1,0:T(8,128)(2,1)} %param.20) | copy-start | bytes 5308420
  1120.0 58.6 %copy-start.55 = (f32[1024]{0:T(1024)S(1)}, f32[1024]{0:T(1024)}, u32[]{:S(2)}) copy-start(f32[1024]{0:T(1024)} %copy-done.54) | copy-start | bytes 12292
  1120.0 58.6 %copy-start.61 = (f32[768]{0:T(1024)S(1)}, f32[768]{0:T(1024)}, u32[]{:S(2)}) copy-start(f32[768]{0:T(1024)} %copy-done.60) | copy-start | bytes 9220
  1120.0 62.6 %copy-start.76 = (f32[1024]{0:T(1024)S(1)}, f32[1024]{0:T(1024)}, u32[]{:S(2)}) copy-start(f32[1024]{0:T(1024)} %copy-done.75) | copy-start | bytes 12292
  1120.0 62.6 %copy-start.70 = (f32[1024]{0:T(1024)S(1)}, f32[1024]{0:T(1024)}, u32[]{:S(2)}) copy-start(f32[1024]{0:T(1024)} %copy-done.69) | copy-start | bytes 12292
  1120.0 118.1 %all-gather.21.cloned.1.call-start = ((), (), s32[]{:S(2)}) async-start(), calls=%async_computation.20 | async-start | bytes 7864320 | tf_op jit(solution)/shard_map/all_gather | solution.py:78
  1186.7 51.5 %copy-start.91 = (f32[768]{0:T(1024)S(1)}, f32[768]{0:T(1024)}, u32[]{:S(2)}) copy-start(f32[768]{0:T(1024)} %copy-done.90) | copy-start | bytes 9220
  1191.6 134.2 %reduce-scatter.21.cloned.1.call-start = ((), (), s32[]{:S(2)}) async-start(), calls=%async_computation.21 | async-start | bytes 7864320 | tf_op jit(solution)/shard_map/reduce_scatter | solution.py:82
  1267.3 58.5 %copy-start.57 = (f32[1024]{0:T(1024)S(1)}, f32[1024]{0:T(1024)}, u32[]{:S(2)}) copy-start(f32[1024]{0:T(1024)} %copy-done.56) | copy-start | bytes 12292
  1267.3 58.5 %copy-start.63 = (f32[768]{0:T(1024)S(1)}, f32[768]{0:T(1024)}, u32[]{:S(2)}) copy-start(f32[768]{0:T(1024)} %copy-done.62) | copy-start | bytes 9220
  1267.3 58.5 %copy-start.66 = (f32[1024]{0:T(1024)S(1)}, f32[1024]{0:T(1024)}, u32[]{:S(2)}) copy-start(f32[1024]{0:T(1024)} %copy-done.65) | copy-start | bytes 12292
  1267.3 62.2 %copy-start.74 = (f32[1024]{0:T(1024)S(1)}, f32[1024]{0:T(1024)}, u32[]{:S(2)}) copy-start(f32[1024]{0:T(1024)} %copy-done.73) | copy-start | bytes 12292
  1267.4 113.9 %all-gather.23.cloned.1.call-start = ((), (), s32[]{:S(2)}) async-start(), calls=%async_computation.22 | async-start | bytes 7864320 | tf_op jit(solution)/shard_map/all_gather | solution.py:78
  1332.6 48.7 %copy-start.47 = (bf16[2,192,768]{2,1,0:T(8,128)(2,1)S(1)}, bf16[2,192,768]{2,1,0:T(8,128)(2,1)}, u32[]{:S(2)}) copy-start(bf16[2,192,768]{2,1,0:T(8,128)(2,1)} %param.22) | copy-start | bytes 1769476
  1334.8 206.8 %reduce-scatter.23.cloned.1.call-start = ((), (), s32[]{:S(2)}) async-start(), calls=%async_computation.23 | async-start | bytes 7864320 | tf_op jit(solution)/shard_map/reduce_scatter | solution.py:82
  1440.8 510.7 %all-reduce.5.cloned.1.call-start = ((), (), s32[]{:S(2)}) async-start(), calls=%async_computation.24 | async-start | bytes 28311552 | tf_op jit(solution)/shard_map/psum | solution.py:271
  1440.8 22.9 %slice-start.8 = ((s8[6291456]{0:T(1024)(128)(4,1)}), s8[4194304]{0:T(1024)(128)(4,1)S(1)}, s32[]{:S(2)}) async-start(s8[6291456]{0:T(1024)(128)(4,1)} %bitcast.275), calls=%async_computation.33 | async-start | bytes 8388608
  1440.8 25.2 %slice-start.6 = ((s8[6291456]{0:T(1024)(128)(4,1)}), s8[4194304]{0:T(1024)(128)(4,1)S(1)}, s32[]{:S(2)}) async-start(s8[6291456]{0:T(1024)(128)(4,1)} %bitcast.271), calls=%async_computation.31 | async-start | bytes 8388608
  1440.8 25.2 %slice-start.12 = ((s8[6291456]{0:T(1024)(128)(4,1)}), s8[4194304]{0:T(1024)(128)(4,1)S(1)}, s32[]{:S(2)}) async-start(s8[6291456]{0:T(1024)(128)(4,1)} %bitcast.290), calls=%async_computation.37 | async-start | bytes 8388608
  1451.1 15.0 slice-start.7
  1471.4 18.7 slice-start.18
  1471.4 21.0 %slice-start.10 = ((s8[4718592]{0:T(1024)(128)(4,1)}), s8[4194304]{0:T(1024)(128)(4,1)S(1)}, s32[]{:S(2)}) async-start(s8[4718592]{0:T(1024)(128)(4,1)} %bitcast.288), calls=%async_computation.35 | async-start | bytes 8388608
  1471.4 21.0 %slice-start.14 = ((s8[6291456]{0:T(1024)(128)(4,1)}), s8[4194304]{0:T(1024)(128)(4,1)S(1)}, s32[]{:S(2)}) async-start(s8[6291456]{0:T(1024)(128)(4,1)} %bitcast.298), calls=%async_computation.39 | async-start | bytes 8388608
  1497.6 44.0 %copy-start.9 = (bf16[1024,768]{1,0:T(8,128)(2,1)S(1)}, bf16[1024,768]{1,0:T(8,128)(2,1)}, u32[]{:S(2)}) copy-start(bf16[1024,768]{1,0:T(8,128)(2,1)} %param.14) | copy-start | bytes 4718596
  1497.6 43.9 %copy-start.53 = (f32[1024]{0:T(1024)S(1)}, f32[1024]{0:T(1024)}, u32[]{:S(2)}) copy-start(f32[1024]{0:T(1024)} %copy-done.52) | copy-start | bytes 12292
  1497.6 43.9 %copy-start.59 = (f32[768]{0:T(1024)S(1)}, f32[768]{0:T(1024)}, u32[]{:S(2)}) copy-start(f32[768]{0:T(1024)} %copy-done.58) | copy-start | bytes 9220
  1498.6 45.6 %copy-start.72 = (f32[1024]{0:T(1024)S(1)}, f32[1024]{0:T(1024)}, u32[]{:S(2)}) copy-start(f32[1024]{0:T(1024)} %copy-done.71) | copy-start | bytes 12292
  1498.7 45.6 %copy-start.68 = (f32[1024]{0:T(1024)S(1)}, f32[1024]{0:T(1024)}, u32[]{:S(2)}) copy-start(f32[1024]{0:T(1024)} %copy-done.67) | copy-start | bytes 12292
  (96 other events, 433.1 us)
Sparse Core Ops, SparseCore 0:
  14.9 49.0 all-gather.8
  96.3 99.0 reduce-scatter.8
  201.3 46.3 all-gather.10
  270.8 99.0 reduce-scatter.10
  376.7 46.3 all-gather.12
  516.6 99.0 reduce-scatter.12
  622.5 46.3 all-gather.14
  692.4 99.0 reduce-scatter.14
  803.8 46.3 all-gather.16
  878.5 58.3 reduce-scatter.16
  946.7 46.3 all-gather.18
  1120.1 58.3 reduce-scatter.18
  1191.7 46.3 all-gather.20
  1267.5 58.3 reduce-scatter.20
  1334.9 46.3 all-gather.22
  1440.9 58.3 reduce-scatter.22
  1505.9 445.5 all-reduce.4
where the time goes:
time: 1980 us; the launch traced here: 1970 us
  waiting for transfers between devices  1290 us (65%)
  matrix products  271 us (14%)
  local copies, waits for them, and re-layouts  183 us (9%)
  other arithmetic  122 us (6%)
  blocking collectives  80.2 us (4%)
    reduce_scatter x4, waiting for transfers between devices, collect_rows(): lax.psum_scatter(jnp.dot(values, weight, preferred_element_type=jnp.float...  396 us
    psum x1, waiting for transfers between devices, on_device(): summed = lax.psum(block_terms[0] + block_terms[1], 'clip')  358 us
    all_gather x4, waiting for transfers between devices, spread_grads(): return lax.all_gather(values, 'head', axis=0, tiled=True)  186 us
    all_gather x4, waiting for transfers between devices, spread_rows(): return lax.all_gather(values, 'head', axis=0, tiled=True)  180 us
    reduce_scatter x4, waiting for transfers between devices, collect_grads(): lax.psum_scatter(values.astype(jnp.bfloat16), 'head', scatter_dimension=0...  175 us
    psum x1, blocking collectives, on_device(): lax.psum((gains, shifts, vecs, loss_local), ('clip', 'head'))  41.7 us
    convert_element_type x2, local copies, waits for them, and re-layouts, attend_back(): rows_of(stacked, window_kind).reshape(row_count, 3, head_local * HD)  40.3 us
  transfers between devices with their start and end apart: 17, of which 16 were waited for; matrix products, arithmetic and copies ran while one was open for 4% of the time, Pallas kernels for 0%

commit v1 on v0

v1 whole, which is shorter than its diff:
```python
from functools import partial

import jax
import jax.numpy as jnp
from jax import lax
from jax.experimental import pallas as pl
from jax.experimental.pallas import tpu as pltpu
from jax.sharding import PartitionSpec as P

HD = 64
FRAMES = 16
SIDE = 16
TUBE = 4
WINDOW = 256
PAIR = 128

epsilon = 1e-06
masked_score = -1e30
f32 = jnp.float32
bf16 = jnp.bfloat16
VMEM_LIMIT = 48 * 1024 * 1024


def dot(a, b):
    return lax.dot_general(a, b, (((1,), (0,)), ((), ())), preferred_element_type=f32)


def dot_nt(a, b):
    return lax.dot_general(a, b, (((1,), (1,)), ((), ())), preferred_element_type=f32)


def dot_tn(a, b):
    return lax.dot_general(a, b, (((0,), (0,)), ((), ())), preferred_element_type=f32)


def allowed_of(place_ref):
    head_index = place_ref[0]
    frame_count = place_ref[1]

    def valid(axis):
        position = lax.broadcasted_iota(jnp.int32, (WINDOW, WINDOW), axis)
        frame = 4 * ((position >> 6) ^ head_index) + ((position >> 4) & 3)
        return frame < frame_count

    return jnp.logical_or(valid(1), jnp.logical_not(valid(0)))


def pair_parts(first_ref, second_ref, part):
    width = first_ref.shape[1] // 3
    cut = slice(part * width, (part + 1) * width)
    return jnp.concatenate([first_ref[:, cut], second_ref[:, cut]], axis=1)


def attend_kernel(masked, place_ref, first_ref, second_ref, out_first, out_second, lse_ref):
    query = pair_parts(first_ref, second_ref, 0) * jnp.asarray(HD ** (-0.5), bf16)
    key = pair_parts(first_ref, second_ref, 1)
    value = pair_parts(first_ref, second_ref, 2)
    lane = lax.broadcasted_iota(jnp.int32, (WINDOW, PAIR), 1)
    low = lane < HD
    if masked:
        allowed = allowed_of(place_ref)
    lse = jnp.zeros((WINDOW, PAIR), f32)
    outs = []
    for pair in range(query.shape[1] // PAIR):
        cut = slice(pair * PAIR, (pair + 1) * PAIR)
        found = []
        for half in range(2):
            mine = low if half == 0 else jnp.logical_not(low)
            query_half = jnp.where(mine, query[:, cut], jnp.zeros((), bf16))
            scores = dot_nt(query_half, key[:, cut])
            if masked:
                scores = jnp.where(allowed, scores, masked_score)
            top = jnp.max(scores, axis=1, keepdims=True)
            terms = jnp.exp(scores - top)
            total = jnp.sum(terms, axis=1, keepdims=True)
            probs = (terms * (1.0 / total)).astype(bf16)
            found.append(dot(probs, value[:, cut]))
            lse = jnp.where(lane == 2 * pair + half, top + jnp.log(total), lse)
        outs.append(jnp.where(low, found[0], found[1]).astype(bf16))
    joined = jnp.concatenate(outs, axis=1)
    width = out_first.shape[1]
    out_first[...] = joined[:, :width]
    out_second[...] = joined[:, width:]
    lse_ref[...] = lse


def attend(place, first, second, masked):
    rows = first.shape[0]
    width = first.shape[1] // 3
    block = lambda columns: pl.BlockSpec((WINDOW, columns), lambda i, s: (i, 0))
    return pl.pallas_call(
        partial(attend_kernel, masked),
        grid_spec=pltpu.PrefetchScalarGridSpec(
            num_scalar_prefetch=1,
            grid=(rows // WINDOW,),
            in_specs=[block(3 * width), block(3 * width)],
            out_specs=[block(width), block(width), block(PAIR)],
        ),
        out_shape=[
            jax.ShapeDtypeStruct((rows, width), bf16),
            jax.ShapeDtypeStruct((rows, width), bf16),
            jax.ShapeDtypeStruct((rows, PAIR), f32),
        ],
        compiler_params=pltpu.CompilerParams(vmem_limit_bytes=VMEM_LIMIT),
        cost_estimate=pl.CostEstimate(
            flops=16 * rows * WINDOW * width, bytes_accessed=16 * rows * width, transcendentals=0
        ),
        name="attend",
    )(place, first, second)


def attend_back_kernel(
    masked, place_ref, first_ref, second_ref, grad_first, grad_second, lse_ref, out_first, out_second
):
    query = pair_parts(first_ref, second_ref, 0) * jnp.asarray(HD ** (-0.5), bf16)
    key = pair_parts(first_ref, second_ref, 1)
    value = pair_parts(first_ref, second_ref, 2)
    grad = jnp.concatenate([grad_first[...], grad_second[...]], axis=1)
    lane = lax.broadcasted_iota(jnp.int32, (WINDOW, PAIR), 1)
    low = lane < HD
    if masked:
        allowed = allowed_of(place_ref)
    lse = lse_ref[...]
    zero = jnp.zeros((), bf16)
    results = [[], [], []]
    for pair in range(query.shape[1] // PAIR):
        cut = slice(pair * PAIR, (pair + 1) * PAIR)
        found = []
        for half in range(2):
            mine = low if half == 0 else jnp.logical_not(low)
            query_half = jnp.where(mine, query[:, cut], zero)
            grad_half = jnp.where(mine, grad[:, cut], zero)
            scores = dot_nt(query_half, key[:, cut])
            if masked:
                scores = jnp.where(allowed, scores, masked_score)
            head = 2 * pair + half
            probs = jnp.exp(scores - lse[:, head : head + 1])
            grad_probs = dot_nt(grad_half, value[:, cut])
            delta = jnp.sum(probs * grad_probs, axis=1, keepdims=True)
            grad_scores = (probs * (grad_probs - delta)).astype(bf16)
            grad_query = dot(grad_scores, key[:, cut]) * HD ** (-0.5)
            grad_key = dot_tn(grad_scores, query[:, cut])
            grad_value = dot_tn(probs.astype(bf16), grad[:, cut])
            found.append((grad_query, grad_key, grad_value))
        for part in range(3):
            results[part].append(jnp.where(low, found[0][part], found[1][part]).astype(bf16))
    joined = [jnp.concatenate(part, axis=1) for part in results]
    width = grad_first.shape[1]
    for part in range(3):
        out_first[:, part * width : (part + 1) * width] = joined[part][:, :width]
        out_second[:, part * width : (part + 1) * width] = joined[part][:, width:]


def attend_back(place, first, second, grad_first, grad_second, lse, masked):
    rows = first.shape[0]
    width = first.shape[1] // 3
    block = lambda columns: pl.BlockSpec((WINDOW, columns), lambda i, s: (i, 0))
    return pl.pallas_call(
        partial(attend_back_kernel, masked),
        grid_spec=pltpu.PrefetchScalarGridSpec(
            num_scalar_prefetch=1,
            grid=(rows // WINDOW,),
            in_specs=[block(3 * width), block(3 * width), block(width), block(width), block(PAIR)],
            out_specs=[block(3 * width), block(3 * width)],
        ),
        out_shape=[jax.ShapeDtypeStruct((rows, 3 * width), bf16)] * 2,
        compiler_params=pltpu.CompilerParams(vmem_limit_bytes=VMEM_LIMIT),
        cost_estimate=pl.CostEstimate(
            flops=40 * rows * WINDOW * width, bytes_accessed=32 * rows * width, transcendentals=0
        ),
        name="attend_back",
    )(place, first, second, grad_first, grad_second, lse)


def statistics(stream):
    centre = jnp.mean(stream, axis=-1, keepdims=True)
    centred = stream - centre
    spread = jnp.mean(centred * centred, axis=-1, keepdims=True)
    scale = lax.rsqrt(spread + epsilon)
    return centred * scale, scale


def layer_norm(stream, gain, shift):
    normal, _ = statistics(stream)
    return (normal * gain + shift).astype(bf16)


def norm_back(stream, gain, grad):
    normal, scale = statistics(stream)
    scaled = grad * gain
    mean_plain = jnp.mean(scaled, axis=-1, keepdims=True)
    mean_normal = jnp.mean(scaled * normal, axis=-1, keepdims=True)
    inner = scale * (scaled - mean_plain - normal * mean_normal)
    return inner, jnp.sum(grad * normal, axis=0), jnp.sum(grad, axis=0)


def gelu_both(hidden):
    root = 0.7978845608028654
    cubic = 0.044715
    square = hidden * hidden
    bend = jnp.tanh(root * hidden * (1.0 + cubic * square))
    active = 0.5 * hidden * (1.0 + bend)
    slope = 0.5 * (1.0 + bend) + 0.5 * hidden * (1.0 - bend * bend) * root * (
        1.0 + 3.0 * cubic * square
    )
    return active.astype(bf16), slope.astype(bf16)


def code_loss(stream, code_head, targets, token_weight):
    logits = jnp.dot(stream.astype(bf16), code_head, preferred_element_type=f32)
    score_top = jnp.max(logits, axis=1, keepdims=True)
    log_total = score_top + jnp.log(jnp.sum(jnp.exp(logits - score_top), axis=1, keepdims=True))
    onehot = targets[:, None] == jnp.arange(logits.shape[1], dtype=jnp.int32)[None, :]
    picked = jnp.sum(jnp.where(onehot, logits, 0.0), axis=1)
    loss_local = jnp.sum(token_weight * (log_total[:, 0] - picked))
    soft_codes = jnp.exp(logits - log_total)
    grad_logits = (token_weight[:, None] * (soft_codes - onehot.astype(f32))).astype(bf16)
    return loss_local, dot_nt(grad_logits, code_head)


def head_swap(values, distance):
    count = lax.axis_size("head")
    return lax.ppermute(values, "head", [(i, i ^ distance) for i in range(count)])


def clip_swap(values, distance):
    count = lax.axis_size("clip")
    return lax.ppermute(values, "clip", [(i, i ^ distance) for i in range(count)])


def gather_parts(own):
    across = head_swap(own, 2)
    return [own, head_swap(own, 1), across, head_swap(across, 1)]


def reduce_parts(part_of):
    beside = head_swap(part_of(1).astype(bf16), 1)
    beyond = head_swap(part_of(3).astype(bf16), 1)
    across = head_swap((part_of(2) + beyond.astype(f32)).astype(bf16), 2)
    return part_of(0) + beside.astype(f32) + across.astype(f32)


def reduce_clips(own):
    count = lax.axis_size("clip")
    half = own.shape[0] // 2
    upper = (lax.axis_index("clip") & 1) == 1
    own = own.astype(bf16)
    keep = jnp.where(upper, own[half:], own[:half])
    send = jnp.where(upper, own[:half], own[half:])
    total = keep.astype(f32) + clip_swap(send, 1).astype(f32)
    distance = 2
    while distance < count:
        sent = total.astype(bf16)
        total = sent.astype(f32) + clip_swap(sent, distance).astype(f32)
        distance *= 2
    mine = total.astype(bf16)
    other = clip_swap(mine, 1)
    return jnp.concatenate(
        [jnp.where(upper, other, mine), jnp.where(upper, mine, other)], axis=0
    ).astype(f32)


def reduce_small(values):
    for distance in (1, 2):
        values = values + head_swap(values, distance)
    distance = 1
    while distance < lax.axis_size("clip"):
        values = values + clip_swap(values, distance)
        distance *= 2
    return values


def by_distance(values, head_index, axis):
    def picked(order):
        return jnp.concatenate(
            [lax.slice_in_dim(values, i, i + 1, axis=axis) for i in order], axis=axis
        )

    values = jnp.where((head_index & 1) == 1, picked((1, 0, 3, 2)), values)
    return jnp.where((head_index & 2) == 2, picked((2, 3, 0, 1)), values)


def rows_to_tubes(rows, head_index):
    trailing = rows.shape[1:]
    tiles = SIDE // TUBE
    lattice = rows.reshape((FRAMES // 4, tiles, TUBE, tiles, TUBE) + trailing)
    lattice = lattice.transpose((0, 1, 3, 2, 4) + tuple(range(5, 5 + len(trailing))))
    return by_distance(
        lattice.reshape((FRAMES // 4, tiles, tiles * TUBE * TUBE) + trailing), head_index, 1
    )


def tubes_to_rows(values, head_index):
    trailing = values.shape[3:]
    tiles = SIDE // TUBE
    lattice = by_distance(values, head_index, 1).reshape(
        (FRAMES // 4, tiles, tiles, TUBE, TUBE) + trailing
    )
    lattice = lattice.transpose((0, 1, 3, 2, 4) + tuple(range(5, 5 + len(trailing))))
    return lattice.reshape((-1,) + trailing)


def frames_to_bands(values):
    pieces = [values[:, 0]] + [head_swap(values[:, k], k) for k in (1, 2, 3)]
    trailing = values.shape[3:]
    tiles = SIDE // TUBE
    stacked = jnp.stack(pieces).reshape((4, FRAMES // 4, tiles, TUBE * TUBE) + trailing)
    return stacked.transpose((2, 0, 1, 3) + tuple(range(4, 4 + len(trailing))))


def bands_to_frames(values):
    trailing = values.shape[4:]
    lattice = values.transpose((1, 2, 0, 3) + tuple(range(4, 4 + len(trailing))))
    lattice = lattice.reshape((4, FRAMES // 4, 4 * TUBE * TUBE) + trailing)
    pieces = [lattice[0]] + [head_swap(lattice[k], k) for k in (1, 2, 3)]
    return jnp.stack(pieces, axis=1)


def on_device(
    tokens,
    frame_counts,
    token_mask,
    targets,
    norm_gain,
    norm_bias,
    w_qkv,
    qv_bias,
    w_out,
    vec_bias,
    w_up,
    up_bias,
    w_down,
    code_head,
):
    head_index = lax.axis_index("head")
    local_rows, width = tokens.shape
    share = w_out.shape[1]
    units = w_up.shape[2]
    place = jnp.stack([head_index.astype(jnp.int32), frame_counts[0]])

    small_own = jnp.concatenate([up_bias.reshape(-1), qv_bias.reshape(-1)])
    small_parts = gather_parts(small_own)
    up_shift = [p[: 2 * units].reshape(2, units) for p in small_parts]
    qv_shift = [p[2 * units :].reshape(2, 2, share) for p in small_parts]
    parts_qkv, parts_out, parts_up, parts_down = [], [], [], []
    for layer in range(2):
        parts_qkv.append(gather_parts(jnp.concatenate(list(w_qkv[layer]), axis=1)))
        parts_out.append(gather_parts(w_out[layer]))
        parts_up.append(gather_parts(w_up[layer]))
        parts_down.append(gather_parts(w_down[layer]))

    arranged = rows_to_tubes(tokens, head_index)
    stream = arranged.reshape(local_rows, width).astype(f32)
    marks = rows_to_tubes(2 * targets + token_mask, head_index)
    marks = frames_to_bands(marks).reshape(local_rows)
    position = jnp.arange(local_rows, dtype=jnp.int32) % WINDOW
    frame = 4 * ((position >> 6) ^ head_index) + ((position >> 4) & 3)
    token_weight = (marks & 1).astype(f32) * (frame < frame_counts[0]).astype(f32)
    own_targets = marks >> 1

    kept = []
    for layer in range(2):
        masked = layer == 1
        if layer == 1:
            stream = frames_to_bands(
                stream.astype(bf16).reshape(arranged.shape)
            ).reshape(local_rows, width).astype(f32)
        stream_a = stream
        normed = layer_norm(stream, norm_gain[layer, 0], norm_bias[layer, 0])
        qkv = []
        for k in range(4):
            shift = jnp.concatenate(
                [qv_shift[k][layer, 0], jnp.zeros((share,), f32), qv_shift[k][layer, 1]]
            )
            qkv.append((dot(normed, parts_qkv[layer][k]) + shift).astype(bf16))
        attended, lse = [], []
        for half in range(2):
            a, b, c = attend(place, qkv[2 * half], qkv[2 * half + 1], masked)
            attended += [a, b]
            lse.append(c)
        branch = vec_bias[layer, 0]
        for k in range(4):
            branch = branch + dot(attended[k], parts_out[layer][k])
        stream = stream + branch
        stream_b = stream
        normed2 = layer_norm(stream, norm_gain[layer, 1], norm_bias[layer, 1])
        active, slope = [], []
        branch = vec_bias[layer, 1]
        for k in range(4):
            a, s = gelu_both(dot(normed2, parts_up[layer][k]) + up_shift[k][layer])
            active.append(a)
            slope.append(s)
            branch = branch + dot(a, parts_down[layer][k])
        stream = stream + branch
        kept.append((stream_a, normed, qkv, attended, lse, stream_b, normed2, active, slope))

    loss_local, grad_stream = code_loss(stream, code_head, own_targets, token_weight)

    big = [None, None]
    small = [None, None]
    for layer in (1, 0):
        masked = layer == 1
        stream_a, normed, qkv, attended, lse, stream_b, normed2, active, slope = kept[layer]
        g2 = grad_stream.astype(bf16)
        vec_1 = jnp.sum(g2, axis=0, dtype=f32)
        grad_hidden = [
            (dot_nt(g2, parts_down[layer][k]) * slope[k].astype(f32)).astype(bf16)
            for k in range(4)
        ]
        down_grad = reduce_clips(reduce_parts(lambda k: dot_tn(active[k], g2)))
        up_grad = reduce_clips(reduce_parts(lambda k: dot_tn(normed2, grad_hidden[k])))
        up_bias_grad = [jnp.sum(g, axis=0, dtype=f32) for g in grad_hidden]
        grad_normed = sum(dot_nt(grad_hidden[k], parts_up[layer][k]) for k in range(4))
        inner, gain_1, shift_1 = norm_back(stream_b, norm_gain[layer, 1], grad_normed)
        grad_stream = grad_stream + inner
        g1 = grad_stream.astype(bf16)
        vec_0 = jnp.sum(g1, axis=0, dtype=f32)
        out_grad = reduce_clips(reduce_parts(lambda k: dot_tn(attended[k], g1)))
        grad_attended = [dot_nt(g1, parts_out[layer][k]).astype(bf16) for k in range(4)]
        grad_qkv = []
        for half in range(2):
            i, j = 2 * half, 2 * half + 1
            grad_qkv += attend_back(
                place, qkv[i], qkv[j], grad_attended[i], grad_attended[j], lse[half], masked
            )
        qkv_grad = reduce_clips(reduce_parts(lambda k: dot_tn(normed, grad_qkv[k])))
        qkv_bias_grad = [jnp.sum(g, axis=0, dtype=f32) for g in grad_qkv]
        grad_normed = sum(dot_nt(grad_qkv[k], parts_qkv[layer][k]) for k in range(4))
        inner, gain_0, shift_0 = norm_back(stream_a, norm_gain[layer, 0], grad_normed)
        grad_stream = grad_stream + inner
        if layer == 1:
            tiles = SIDE // TUBE
            sent = grad_stream.astype(bf16).reshape(tiles, 4, FRAMES // 4, TUBE * TUBE, width)
            grad_stream = bands_to_frames(sent).reshape(local_rows, width).astype(f32)
        qkv_grad = jnp.stack([qkv_grad[:, j * share : (j + 1) * share] for j in range(3)])
        big[layer] = (qkv_grad, out_grad, up_grad, down_grad)
        qv_grad = [
            jnp.concatenate([g[:share], g[2 * share :]]) for g in qkv_bias_grad
        ]
        split = jnp.stack([jnp.concatenate([u, q]) for u, q in zip(up_bias_grad, qv_grad)])
        plain = jnp.concatenate([gain_0, gain_1, shift_0, shift_1, vec_0, vec_1])
        small[layer] = (split, plain)

    grad_input = tubes_to_rows(
        grad_stream.reshape(FRAMES // 4, 4, 64, width), head_index
    )

    splits = jnp.stack([small[0][0], small[1][0]])
    splits = by_distance(splits, head_index, 1)
    plains = jnp.concatenate([small[0][1], small[1][1], loss_local[None]])
    packed = jnp.concatenate([splits.reshape(-1), plains])
    packed = reduce_small(packed)
    splits_sum = packed[: splits.size].reshape(splits.shape)
    splits_own = by_distance(splits_sum, head_index, 1)[:, 0]
    plains_sum = packed[splits.size :]
    loss_total = plains_sum[-1]
    vectors = plains_sum[:-1].reshape(2, 3, 2, width)
    qv_bias_out = splits_own[:, units:].reshape(2, 2, share)
    up_bias_out = splits_own[:, :units]

    slot_total = lax.axis_size("clip") * frame_counts.shape[0] * FRAMES * SIDE * SIDE

    def stacked(member):
        return jnp.stack([big[0][member], big[1][member]])

    return (
        loss_total / slot_total,
        grad_input,
        vectors[:, 0],
        vectors[:, 1],
        stacked(0),
        qv_bias_out,
        stacked(1),
        vectors[:, 2],
        stacked(2),
        up_bias_out,
        stacked(3),
    )


def solution(mesh):
    placed = (
        P(("clip", "head"), None),
        P("clip"),
        P(("clip", "head")),
        P(("clip", "head")),
        P(),
        P(),
        P(None, None, None, "head"),
        P(None, None, "head"),
        P(None, "head", None),
        P(),
        P(None, None, "head"),
        P(None, "head"),
        P(None, "head", None),
        P(),
    )
    return jax.shard_map(
        on_device,
        mesh=mesh,
        in_specs=placed,
        out_specs=(
            P(),
            P(("clip", "head"), None),
            P(),
            P(),
            P(None, None, None, "head"),
            P(None, None, "head"),
            P(None, "head", None),
            P(),
            P(None, None, "head"),
            P(None, "head"),
            P(None, "head", None),
        ),
        check_vma=False,
    )
```

time: 1980 us -> 1000 us (0.51)
  waiting for transfers between devices: 1290 us -> 369 us
  starting transfers between devices: 1.5 us -> 86.6 us
  blocking collectives: 80.2 us -> 0 us
  Pallas kernels: 0 us -> 78.1 us
  local copies, waits for them, and re-layouts: 183 us -> 124 us
  other arithmetic: 122 us -> 75.3 us
    reduce_scatter x8 -> x0, waiting for transfers between devices: 571 us -> none  [the longest x4 396 us: collect_rows(): lax.psum_scatter(jnp.dot(values, weight, preferred_element_type=jnp.float...]
    ppermute x0 -> x97, waiting for transfers between devices: none -> 369 us  [the longest x35 188 us: clip_swap(): lax.ppermute(values, 'clip', [(i, i ^ distance) for i in range(count)])]
    all_gather x8 -> x0, waiting for transfers between devices: 366 us -> none  [the longest x4 186 us: spread_grads(): return lax.all_gather(values, 'head', axis=0, tiled=True)]
    psum x1 -> x0, waiting for transfers between devices: 358 us -> none  [on_device(): summed = lax.psum(block_terms[0] + block_terms[1], 'clip')]
    ppermute x0 -> x97, starting transfers between devices: none -> 86.6 us  [the longest x35 51.5 us: clip_swap(): lax.ppermute(values, 'clip', [(i, i ^ distance) for i in range(count)])]
    psum x2 -> x0, blocking collectives: 80.2 us -> none  [the longest x1 41.7 us: on_device(): lax.psum((gains, shifts, vecs, loss_local), ('clip', 'head'))]
    pallas_call x0 -> x8, Pallas kernels: none -> 78.1 us  [the longest x4 52.3 us: attend_back(): pl.pallas_call(partial(attend_back_kernel, masked), grid_spec=pltpu.Prefe...]
    convert_element_type x8 -> x10, local copies, waits for them, and re-layouts: 71.5 us -> 7.09 us  [the longest x8 5.03 us: on_device(): dot_nt(g1, parts_out[layer][k]).astype(bf16)]
  transfers between devices with their start and end apart: 17 -> 97, of which waited for: 16 -> 39; matrix products, arithmetic and copies ran while one was open for 4% -> 34% of each run, Pallas kernels for 0% -> 5%
where the time goes in v1:
time: 1000 us; the launch traced here: 992 us
  waiting for transfers between devices  369 us (37%)
  matrix products  252 us (25%)
  local copies, waits for them, and re-layouts  124 us (12%)
  starting transfers between devices  86.6 us (9%)
  Pallas kernels  78.1 us (8%)
  other arithmetic  75.3 us (8%)
    ppermute x35, waiting for transfers between devices, clip_swap(): lax.ppermute(values, 'clip', [(i, i ^ distance) for i in range(count)])  188 us
    ppermute x62, waiting for transfers between devices, head_swap(): lax.ppermute(values, 'head', [(i, i ^ distance) for i in range(count)])  181 us
    dot_general x33, matrix products, dot_nt(): lax.dot_general(a, b, (((1,), (1,)), ((), ())), preferred_element_type=f32)  89.3 us
    dot_general x32, matrix products, dot_tn(): lax.dot_general(a, b, (((0,), (0,)), ((), ())), preferred_element_type=f32)  75.8 us
    dot_general x31, matrix products, dot(): lax.dot_general(a, b, (((1,), (0,)), ((), ())), preferred_element_type=f32)  75.4 us
    pallas_call x4, Pallas kernels, attend_back(): pl.pallas_call(partial(attend_back_kernel, masked), grid_spec=pltpu.Prefe...  52.3 us
    ppermute x35, starting transfers between devices, clip_swap(): lax.ppermute(values, 'clip', [(i, i ^ distance) for i in range(count)])  51.5 us
    ppermute x62, starting transfers between devices, head_swap(): lax.ppermute(values, 'head', [(i, i ^ distance) for i in range(count)])  35.1 us
  transfers between devices with their start and end apart: 97, of which 39 were waited for; matrix products, arithmetic and copies ran while one was open for 34% of the time, Pallas kernels for 5%

profile of v1, /device:TPU:0, one launch (start us, length us, event | category | flops | bytes accessed | tf_op | source)
XLA Modules:
  0.0 992.0 jit_solution(3389770017294141452)
XLA Ops:
  54.9 4.9 convert_reduce_fusion
  96.8 6.3 attend.4
  114.6 6.4 attend.5
  134.1 20.9 %collective-permute-done.15 = bf16[768,768]{1,0:T(8,128)(2,1)} collective-permute-done((bf16[768,768]{1,0:T(8,128)(2,1)}, bf16[768,768]{1,0:T(8,128)(2,1)}, u32[]{:S(2)}, u32[]{:S(2)}) %collective-permute-start.15) | collective-permute-done | bytes 1179680 | tf_op jit(solution)/shard_map/ppermute | solution.py:223
  188.4 8.6 collective-permute-done.19
  210.5 6.3 attend.6
  220.7 6.8 attend.7
  230.4 23.0 %collective-permute-done.30 = bf16[768,768]{1,0:T(8,128)(2,1)} collective-permute-done((bf16[768,768]{1,0:T(8,128)(2,1)}, bf16[768,768]{1,0:T(8,128)(2,1)}, u32[]{:S(2)}, u32[]{:S(2)}) %collective-permute-start.30) | collective-permute-done | bytes 1179680 | tf_op jit(solution)/shard_map/ppermute | solution.py:223
  266.9 5.0 fusion.74
  282.2 11.9 %fusion.107 = (f32[1024]{0:T(1024)S(1)}, f32[1024,1024]{0,1:T(8,128)}) fusion(bf16[768,1024]{1,0:T(8,128)(2,1)S(1)} %copy-done, f32[1024,768]{1,0:T(8,128)} %copy-done.45, f32[1024,768]{1,0:T(8,128)} %fusion.74, f32[1024,768]{1,0:T(8,128)} %fusion.68, f32[1024,768]{1,0:T(8,128)} %fusion.64, bf16[768,768]{1,0:T(8,128)(2,1)} %copy-done.212, ...), kind=kOutput, calls=%fused_computation.423 | convolution fusion | flops 2832202752 | bytes 22685696 | tf_op jit(solution)/shard_map/dot_general | solution.py:210
  334.1 4.3 convert_reduce_fusion.6
  358.4 13.1 %attend_back.4 = (bf16[1024,576]{1,0:T(8,128)(2,1)S(1)}, bf16[1024,576]{1,0:T(8,128)(2,1)S(1)}) custom-call(s32[2]{0:T(128)S(1)} %pad_add_fusion.place_ref, bf16[1024,576]{1,0:T(8,128)(2,1)S(1)} %copy-done.32, bf16[1024,576]{1,0:T(8,128)(2,1)} %copy-done.34, bf16[1024,192]{1,0:T(8,128)(2,1)S(1)} %copy.123.grad_first, ...), custom_call_target="tpu_custom_call" | custom-call | flops 2013265920 | bytes 6291456 | tf_op jit(solution)/shard_map/attend_back/pallas_call | solution.py:158
  382.7 13.2 %attend_back.5 = (bf16[1024,576]{1,0:T(8,128)(2,1)S(1)}, bf16[1024,576]{1,0:T(8,128)(2,1)S(1)}) custom-call(s32[2]{0:T(128)S(1)} %pad_add_fusion.place_ref, bf16[1024,576]{1,0:T(8,128)(2,1)S(1)} %copy-done.30, bf16[1024,576]{1,0:T(8,128)(2,1)} %copy-done.33, bf16[1024,192]{1,0:T(8,128)(2,1)S(1)} %copy-done.20, bf16[1024,192]{1,0:T(8,128)(2,1)S(1)} %copy-done.22, ...), custom_call_target="tpu_custom_call" | custom-call | flops 2013265920 | bytes 6291456 | tf_op jit(solution)/shard_map/attend_back/pallas_call | solution.py:158
  423.4 6.1 collective-permute-done.34
  431.0 5.9 collective-permute-done.35
  458.6 4.8 convert_reduce_fusion.11
  472.5 5.0 convert_reduce_fusion.10
  495.8 12.9 %attend_back.6 = (bf16[1024,576]{1,0:T(8,128)(2,1)S(1)}, bf16[1024,576]{1,0:T(8,128)(2,1)S(1)}) custom-call(s32[2]{0:T(128)S(1)} %pad_add_fusion.place_ref, bf16[1024,576]{1,0:T(8,128)(2,1)S(1)} %copy-done.24, bf16[1024,576]{1,0:T(8,128)(2,1)} %copy-done.27, bf16[1024,192]{1,0:T(8,128)(2,1)S(1)} %copy.131.grad_first, ...), custom_call_target="tpu_custom_call" | custom-call | flops 2013265920 | bytes 6291456 | tf_op jit(solution)/shard_map/attend_back/pallas_call | solution.py:158
  519.5 13.1 %attend_back.7 = (bf16[1024,576]{1,0:T(8,128)(2,1)S(1)}, bf16[1024,576]{1,0:T(8,128)(2,1)S(1)}) custom-call(s32[2]{0:T(128)S(1)} %pad_add_fusion.place_ref, bf16[1024,576]{1,0:T(8,128)(2,1)S(1)} %copy-done.26, bf16[1024,576]{1,0:T(8,128)(2,1)} %copy-done.28, bf16[1024,192]{1,0:T(8,128)(2,1)S(1)} %copy.133.grad_first, bf16[1024,192]{1,0:T(8,128)(2,1)S(1)} %copy-done.21, ...), custom_call_target="tpu_custom_call" | custom-call | flops 2013265920 | bytes 6291456 | tf_op jit(solution)/shard_map/attend_back/pallas_call | solution.py:158
  549.9 5.2 reshape.577
  565.5 4.6 maximum_select_fusion
  582.8 4.6 fusion.14
  594.7 5.1 reshape.578
  613.7 4.7 collective-permute-done.40
  627.9 5.7 collective-permute-done.57
  636.4 6.8 collective-permute-done.67
  643.7 4.6 collective-permute-done.58
  648.9 4.6 collective-permute-done.68
  664.6 6.0 collective-permute-done.60
  672.5 4.5 collective-permute-done.61
  682.5 17.1 %collective-permute-done.50 = bf16[768,576]{0,1:T(8,128)(2,1)S(1)} collective-permute-done((bf16[768,576]{0,1:T(8,128)(2,1)S(1)}, bf16[768,576]{0,1:T(8,128)(2,1)S(1)}, u32[]{:S(2)}, u32[]{:S(2)}) %collective-permute-start.50) | collective-permute-done | bytes 884768 | tf_op jit(solution)/shard_map/ppermute | solution.py:223
  702.1 16.5 %collective-permute-done.43 = bf16[768,576]{0,1:T(8,128)(2,1)S(1)} collective-permute-done((bf16[768,576]{0,1:T(8,128)(2,1)S(1)}, bf16[768,576]{0,1:T(8,128)(2,1)S(1)}, u32[]{:S(2)}, u32[]{:S(2)}) %collective-permute-start.43) | collective-permute-done | bytes 884768 | tf_op jit(solution)/shard_map/ppermute | solution.py:223
  719.5 8.7 collective-permute-done.51
  729.2 14.7 %collective-permute-done.92 = bf16[768,768]{1,0:T(8,128)(2,1)S(1)} collective-permute-done((bf16[768,768]{1,0:T(8,128)(2,1)S(1)}, bf16[768,768]{1,0:T(8,128)(2,1)S(1)}, u32[]{:S(2)}, u32[]{:S(2)}) %collective-permute-start.92) | collective-permute-done | bytes 1179680 | tf_op jit(solution)/shard_map/ppermute | solution.py:223
  744.9 24.2 %collective-permute-done.78 = bf16[768,768]{1,0:T(8,128)(2,1)S(1)} collective-permute-done((bf16[768,768]{1,0:T(8,128)(2,1)S(1)}, bf16[768,768]{1,0:T(8,128)(2,1)S(1)}, u32[]{:S(2)}, u32[]{:S(2)}) %collective-permute-start.78) | collective-permute-done | bytes 1179680 | tf_op jit(solution)/shard_map/ppermute | solution.py:223
  772.6 8.4 collective-permute-done.52
  783.4 11.0 %collective-permute-done.85 = bf16[768,768]{1,0:T(8,128)(2,1)S(1)} collective-permute-done((bf16[768,768]{1,0:T(8,128)(2,1)S(1)}, bf16[768,768]{1,0:T(8,128)(2,1)S(1)}, u32[]{:S(2)}, u32[]{:S(2)}) %collective-permute-start.85) | collective-permute-done | bytes 1179680 | tf_op jit(solution)/shard_map/ppermute | solution.py:223
  799.1 19.3 %collective-permute-done.71 = bf16[768,768]{1,0:T(8,128)(2,1)S(1)} collective-permute-done((bf16[768,768]{1,0:T(8,128)(2,1)S(1)}, bf16[768,768]{1,0:T(8,128)(2,1)S(1)}, u32[]{:S(2)}, u32[]{:S(2)}) %collective-permute-start.71) | collective-permute-done | bytes 1179680 | tf_op jit(solution)/shard_map/ppermute | solution.py:223
  825.9 8.8 collective-permute-done.86
  835.4 11.9 %collective-permute-done.72 = bf16[384,768]{1,0:T(8,128)(2,1)S(1)} collective-permute-done((bf16[384,768]{1,0:T(8,128)(2,1)S(1)}, bf16[384,768]{1,0:T(8,128)(2,1)S(1)}, u32[]{:S(2)}, u32[]{:S(2)}) %collective-permute-start.72) | collective-permute-done | bytes 589856 | tf_op jit(solution)/shard_map/ppermute | solution.py:228
  848.2 9.6 collective-permute-done.46
  862.5 11.3 %collective-permute-start.95 = (bf16[384,768]{1,0:T(8,128)(2,1)S(1)}, bf16[384,768]{1,0:T(8,128)(2,1)S(1)}, u32[]{:S(2)}, u32[]{:S(2)}) collective-permute-start(bf16[384,768]{1,0:T(8,128)(2,1)S(1)} %add_convert_fusion.33), channel_id=1, source_target_pairs={{0,16},{4,20},{8,24},{12,28},{16,0},{20,4},{24,8},{28,12},{1,17},{... | collective-permute-start | bytes 1769480 | tf_op jit(solution)/shard_map/ppermute | solution.py:228
  874.6 18.9 %collective-permute-done.87 = bf16[384,768]{1,0:T(8,128)(2,1)S(1)} collective-permute-done((bf16[384,768]{1,0:T(8,128)(2,1)S(1)}, bf16[384,768]{1,0:T(8,128)(2,1)S(1)}, u32[]{:S(2)}, u32[]{:S(2)}) %collective-permute-start.87) | collective-permute-done | bytes 589856 | tf_op jit(solution)/shard_map/ppermute | solution.py:228
  893.7 9.7 collective-permute-done.73
  906.8 36.0 %collective-permute-done.81 = bf16[384,768]{1,0:T(8,128)(2,1)S(1)} collective-permute-done((bf16[384,768]{1,0:T(8,128)(2,1)S(1)}, bf16[384,768]{1,0:T(8,128)(2,1)S(1)}, u32[]{:S(2)}, u32[]{:S(2)}) %collective-permute-start.81) | collective-permute-done | bytes 589856 | tf_op jit(solution)/shard_map/ppermute | solution.py:228
  943.4 20.5 %collective-permute-done.74 = bf16[384,768]{1,0:T(8,128)(2,1)S(1)} collective-permute-done((bf16[384,768]{1,0:T(8,128)(2,1)S(1)}, bf16[384,768]{1,0:T(8,128)(2,1)S(1)}, u32[]{:S(2)}, u32[]{:S(2)}) %collective-permute-start.74) | collective-permute-done | bytes 589856 | tf_op jit(solution)/shard_map/ppermute | solution.py:228
  966.6 13.8 %collective-permute-done.75 = bf16[384,768]{1,0:T(8,128)(2,1)S(1)} collective-permute-done((bf16[384,768]{1,0:T(8,128)(2,1)S(1)}, bf16[384,768]{1,0:T(8,128)(2,1)S(1)}, u32[]{:S(2)}, u32[]{:S(2)}) %collective-permute-start.75) | collective-permute-done | bytes 589856 | tf_op jit(solution)/shard_map/ppermute | solution.py:228
  983.0 5.0 collective-permute-done.89
  (989 shorter events, 484.7 us)
Async XLA Ops:
  4.9 76.7 %collective-permute-start.7 = (f32[2304]{0:T(1024)}, f32[2304]{0:T(1024)}, u32[]{:S(2)}, u32[]{:S(2)}) collective-permute-start(f32[2304]{0:T(1024)} %constant_dynamic-update-slice_fusion.6), channel_id=1, source_target_pairs={{0,2},{1,3},{2,0},{3,1},{4,6},{5,7},{6,4},{7,5},{8,10},{9,11},{10,... | collective-permute-start | bytes 27656 | tf_op jit(solution)/shard_map/ppermute | solution.py:223
  7.8 77.0 %collective-permute-start.4 = (f32[2304]{0:T(1024)}, f32[2304]{0:T(1024)}, u32[]{:S(2)}, u32[]{:S(2)}) collective-permute-start(f32[2304]{0:T(1024)} %constant_dynamic-update-slice_fusion.6), channel_id=1, source_target_pairs={{0,1},{1,0},{2,3},{3,2},{4,5},{5,4},{6,7},{7,6},{8,9},{9,8},{10,11... | collective-permute-start | bytes 27656 | tf_op jit(solution)/shard_map/ppermute | solution.py:223
  9.7 98.0 %collective-permute-start.5 = (bf16[192,768]{1,0:T(8,128)(2,1)}, bf16[192,768]{1,0:T(8,128)(2,1)}, u32[]{:S(2)}, u32[]{:S(2)}) collective-permute-start(bf16[192,768]{1,0:T(8,128)(2,1)} %get-tuple-element.150), channel_id=1, source_target_pairs={{0,1},{1,0},{2,3},{3,2},{4,5},{5,4},{6,7},{7,6},{8,9},{9,8},{10,11... | collective-permute-start | bytes 884744 | tf_op jit(solution)/shard_map/ppermute | solution.py:223
  10.2 101.3 %collective-permute-start.10 = (bf16[192,768]{1,0:T(8,128)(2,1)}, bf16[192,768]{1,0:T(8,128)(2,1)}, u32[]{:S(2)}, u32[]{:S(2)}) collective-permute-start(bf16[192,768]{1,0:T(8,128)(2,1)} %get-tuple-element.150), channel_id=1, source_target_pairs={{0,2},{1,3},{2,0},{3,1},{4,6},{5,7},{6,4},{7,5},{8,10},{9,11},{10,... | collective-permute-start | bytes 884744 | tf_op jit(solution)/shard_map/ppermute | solution.py:223
  12.5 61.9 %collective-permute-start = (s32[4,64]{1,0:T(4,128)}, s32[4,64]{1,0:T(4,128)}, u32[]{:S(2)}, u32[]{:S(2)}) collective-permute-start(s32[4,64]{1,0:T(4,128)} %bitcast.2), channel_id=1, source_target_pairs={{0,1},{1,0},{2,3},{3,2},{4,5},{5,4},{6,7},{7,6},{8,9},{9,8},{10,11... | collective-permute-start | bytes 3080 | tf_op jit(solution)/shard_map/ppermute | solution.py:223
  87.6 46.4 %collective-permute-start.12 = (bf16[768,768]{1,0:T(8,128)(2,1)}, bf16[768,768]{1,0:T(8,128)(2,1)}, u32[]{:S(2)}, u32[]{:S(2)}) collective-permute-start(bf16[768,768]{1,0:T(8,128)(2,1)} %get-tuple-element.106), channel_id=1, source_target_pairs={{0,1},{1,0},{2,3},{3,2},{4,5},{5,4},{6,7},{7,6},{8,9},{9,8},{10,11... | collective-permute-start | bytes 3538952 | tf_op jit(solution)/shard_map/ppermute | solution.py:223
  93.7 36.0 %collective-permute-start.14 = (bf16[768,768]{1,0:T(8,128)(2,1)}, bf16[768,768]{1,0:T(8,128)(2,1)}, u32[]{:S(2)}, u32[]{:S(2)}) collective-permute-start(bf16[768,768]{1,0:T(8,128)(2,1)} %get-tuple-element.106), channel_id=1, source_target_pairs={{0,2},{1,3},{2,0},{3,1},{4,6},{5,7},{6,4},{7,5},{8,10},{9,11},{10,... | collective-permute-start | bytes 3538952 | tf_op jit(solution)/shard_map/ppermute | solution.py:223
  107.7 54.2 %collective-permute-start.13 = (bf16[768,768]{1,0:T(8,128)(2,1)}, bf16[768,768]{1,0:T(8,128)(2,1)}, u32[]{:S(2)}, u32[]{:S(2)}) collective-permute-start(bf16[768,768]{1,0:T(8,128)(2,1)} %get-tuple-element.108), channel_id=1, source_target_pairs={{0,1},{1,0},{2,3},{3,2},{4,5},{5,4},{6,7},{7,6},{8,9},{9,8},{10,11... | collective-permute-start | bytes 3538952 | tf_op jit(solution)/shard_map/ppermute | solution.py:223
  111.5 43.5 %collective-permute-start.15 = (bf16[768,768]{1,0:T(8,128)(2,1)}, bf16[768,768]{1,0:T(8,128)(2,1)}, u32[]{:S(2)}, u32[]{:S(2)}) collective-permute-start(bf16[768,768]{1,0:T(8,128)(2,1)} %get-tuple-element.108), channel_id=1, source_target_pairs={{0,2},{1,3},{2,0},{3,1},{4,6},{5,7},{6,4},{7,5},{8,10},{9,11},{10,... | collective-permute-start | bytes 3538952 | tf_op jit(solution)/shard_map/ppermute | solution.py:223
  123.0 106.7 %collective-permute-start.22 = (bf16[192,768]{1,0:T(8,128)(2,1)}, bf16[192,768]{1,0:T(8,128)(2,1)}, u32[]{:S(2)}, u32[]{:S(2)}) collective-permute-start(bf16[192,768]{1,0:T(8,128)(2,1)} %get-tuple-element.149), channel_id=1, source_target_pairs={{0,1},{1,0},{2,3},{3,2},{4,5},{5,4},{6,7},{7,6},{8,9},{9,8},{10,11... | collective-permute-start | bytes 884744 | tf_op jit(solution)/shard_map/ppermute | solution.py:223
  129.7 55.5 %collective-permute-start.23 = (bf16[768,576]{0,1:T(8,128)(2,1)}, bf16[768,576]{0,1:T(8,128)(2,1)}, u32[]{:S(2)}, u32[]{:S(2)}) collective-permute-start(bf16[768,576]{0,1:T(8,128)(2,1)} %pad_maximum_fusion.6), channel_id=1, source_target_pairs={{0,2},{1,3},{2,0},{3,1},{4,6},{5,7},{6,4},{7,5},{8,10},{9,11},{10,... | collective-permute-start | bytes 2654216 | tf_op jit(solution)/shard_map/ppermute | solution.py:223
  134.0 35.3 %collective-permute-start.16 = (bf16[768,768]{1,0:T(8,128)(2,1)}, bf16[768,768]{1,0:T(8,128)(2,1)S(1)}, u32[]{:S(2)}, u32[]{:S(2)}) collective-permute-start(bf16[768,768]{1,0:T(8,128)(2,1)} %collective-permute-done.14), channel_id=1, source_target_pairs={{0,1},{1,0},{2,3},{3,2},{4,5},{5,4},{6,7},{7,6},{8,9},{9,8},{10,11... | collective-permute-start | bytes 3538952 | tf_op jit(solution)/shard_map/ppermute | solution.py:223
  185.3 42.8 %collective-permute-start.25 = (bf16[192,768]{1,0:T(8,128)(2,1)}, bf16[192,768]{1,0:T(8,128)(2,1)}, u32[]{:S(2)}, u32[]{:S(2)}) collective-permute-start(bf16[192,768]{1,0:T(8,128)(2,1)} %get-tuple-element.149), channel_id=1, source_target_pairs={{0,2},{1,3},{2,0},{3,1},{4,6},{5,7},{6,4},{7,5},{8,10},{9,11},{10,... | collective-permute-start | bytes 884744 | tf_op jit(solution)/shard_map/ppermute | solution.py:223
  197.0 33.3 %collective-permute-start.29 = (bf16[768,768]{1,0:T(8,128)(2,1)}, bf16[768,768]{1,0:T(8,128)(2,1)}, u32[]{:S(2)}, u32[]{:S(2)}) collective-permute-start(bf16[768,768]{1,0:T(8,128)(2,1)} %get-tuple-element.105), channel_id=1, source_target_pairs={{0,2},{1,3},{2,0},{3,1},{4,6},{5,7},{6,4},{7,5},{8,10},{9,11},{10,... | collective-permute-start | bytes 3538952 | tf_op jit(solution)/shard_map/ppermute | solution.py:223
  205.5 47.9 %collective-permute-start.30 = (bf16[768,768]{1,0:T(8,128)(2,1)}, bf16[768,768]{1,0:T(8,128)(2,1)}, u32[]{:S(2)}, u32[]{:S(2)}) collective-permute-start(bf16[768,768]{1,0:T(8,128)(2,1)} %get-tuple-element.107), channel_id=1, source_target_pairs={{0,2},{1,3},{2,0},{3,1},{4,6},{5,7},{6,4},{7,5},{8,10},{9,11},{10,... | collective-permute-start | bytes 3538952 | tf_op jit(solution)/shard_map/ppermute | solution.py:223
  217.6 54.3 %collective-permute-start.27 = (bf16[768,768]{1,0:T(8,128)(2,1)}, bf16[768,768]{1,0:T(8,128)(2,1)S(1)}, u32[]{:S(2)}, u32[]{:S(2)}) collective-permute-start(bf16[768,768]{1,0:T(8,128)(2,1)} %get-tuple-element.105), channel_id=1, source_target_pairs={{0,1},{1,0},{2,3},{3,2},{4,5},{5,4},{6,7},{7,6},{8,9},{9,8},{10,11... | collective-permute-start | bytes 3538952 | tf_op jit(solution)/shard_map/ppermute | solution.py:223
  228.1 45.3 %collective-permute-start.28 = (bf16[768,768]{1,0:T(8,128)(2,1)}, bf16[768,768]{1,0:T(8,128)(2,1)S(1)}, u32[]{:S(2)}, u32[]{:S(2)}) collective-permute-start(bf16[768,768]{1,0:T(8,128)(2,1)} %get-tuple-element.107), channel_id=1, source_target_pairs={{0,1},{1,0},{2,3},{3,2},{4,5},{5,4},{6,7},{7,6},{8,9},{9,8},{10,11... | collective-permute-start | bytes 3538952 | tf_op jit(solution)/shard_map/ppermute | solution.py:223
  230.3 33.5 %collective-permute-start.31 = (bf16[768,768]{1,0:T(8,128)(2,1)}, bf16[768,768]{1,0:T(8,128)(2,1)S(1)}, u32[]{:S(2)}, u32[]{:S(2)}) collective-permute-start(bf16[768,768]{1,0:T(8,128)(2,1)} %collective-permute-done.29), channel_id=1, source_target_pairs={{0,1},{1,0},{2,3},{3,2},{4,5},{5,4},{6,7},{7,6},{8,9},{9,8},{10,11... | collective-permute-start | bytes 3538952 | tf_op jit(solution)/shard_map/ppermute | solution.py:223
  404.2 249.3 %collective-permute-start.77 = (bf16[768,768]{1,0:T(8,128)(2,1)}, bf16[768,768]{1,0:T(8,128)(2,1)}, u32[]{:S(2)}, u32[]{:S(2)}) collective-permute-start(bf16[768,768]{1,0:T(8,128)(2,1)} %convolution_convert_fusion.4), channel_id=1, source_target_pairs={{0,1},{1,0},{2,3},{3,2},{4,5},{5,4},{6,7},{7,6},{8,9},{9,8},{10,11... | collective-permute-start | bytes 3538952 | tf_op jit(solution)/shard_map/ppermute | solution.py:223
  420.4 324.5 %collective-permute-start.76 = (bf16[768,768]{1,0:T(8,128)(2,1)}, bf16[768,768]{1,0:T(8,128)(2,1)}, u32[]{:S(2)}, u32[]{:S(2)}) collective-permute-start(bf16[768,768]{1,0:T(8,128)(2,1)} %convolution_convert_fusion.5), channel_id=1, source_target_pairs={{0,1},{1,0},{2,3},{3,2},{4,5},{5,4},{6,7},{7,6},{8,9},{9,8},{10,11... | collective-permute-start | bytes 3538952 | tf_op jit(solution)/shard_map/ppermute | solution.py:223
  423.4 176.6 %collective-permute-start.62 = (bf16[192,768]{1,0:T(8,128)(2,1)}, bf16[192,768]{1,0:T(8,128)(2,1)}, u32[]{:S(2)}, u32[]{:S(2)}) collective-permute-start(bf16[192,768]{1,0:T(8,128)(2,1)} %convolution_convert_fusion.21), channel_id=1, source_target_pairs={{0,1},{1,0},{2,3},{3,2},{4,5},{5,4},{6,7},{7,6},{8,9},{9,8},{10,11... | collective-permute-start | bytes 884744 | tf_op jit(solution)/shard_map/ppermute | solution.py:223
  429.4 171.1 %collective-permute-start.64 = (bf16[192,768]{1,0:T(8,128)(2,1)}, bf16[192,768]{1,0:T(8,128)(2,1)}, u32[]{:S(2)}, u32[]{:S(2)}) collective-permute-start(bf16[192,768]{1,0:T(8,128)(2,1)} %add_convert_fusion.51), channel_id=1, source_target_pairs={{0,2},{1,3},{2,0},{3,1},{4,6},{5,7},{6,4},{7,5},{8,10},{9,11},{10,... | collective-permute-start | bytes 884744 | tf_op jit(solution)/shard_map/ppermute | solution.py:223
  599.9 60.0 %collective-permute-start.91 = (bf16[768,768]{1,0:T(8,128)(2,1)}, bf16[768,768]{1,0:T(8,128)(2,1)}, u32[]{:S(2)}, u32[]{:S(2)}) collective-permute-start(bf16[768,768]{1,0:T(8,128)(2,1)} %convolution_convert_fusion), channel_id=1, source_target_pairs={{0,1},{1,0},{2,3},{3,2},{4,5},{5,4},{6,7},{7,6},{8,9},{9,8},{10,11... | collective-permute-start | bytes 3538952 | tf_op jit(solution)/shard_map/ppermute | solution.py:223
  627.6 54.6 %collective-permute-start.48 = (bf16[768,576]{0,1:T(8,128)(2,1)S(1)}, bf16[768,576]{0,1:T(8,128)(2,1)S(1)}, u32[]{:S(2)}, u32[]{:S(2)}) collective-permute-start(bf16[768,576]{0,1:T(8,128)(2,1)S(1)} %copy-done.214), channel_id=1, source_target_pairs={{0,1},{1,0},{2,3},{3,2},{4,5},{5,4},{6,7},{7,6},{8,9},{9,8},{10,11... | collective-permute-start | bytes 2654216 | tf_op jit(solution)/shard_map/ppermute | solution.py:223
  680.5 38.1 %collective-permute-start.43 = (bf16[768,576]{0,1:T(8,128)(2,1)S(1)}, bf16[768,576]{0,1:T(8,128)(2,1)S(1)}, u32[]{:S(2)}, u32[]{:S(2)}) collective-permute-start(bf16[768,576]{0,1:T(8,128)(2,1)S(1)} %add_convert_fusion.31), channel_id=1, source_target_pairs={{0,2},{1,3},{2,0},{3,1},{4,6},{5,7},{6,4},{7,5},{8,10},{9,11},{10,... | collective-permute-start | bytes 2654216 | tf_op jit(solution)/shard_map/ppermute | solution.py:223
  682.3 46.2 %collective-permute-start.90 = (bf16[768,768]{1,0:T(8,128)(2,1)S(1)}, bf16[768,768]{1,0:T(8,128)(2,1)S(1)}, u32[]{:S(2)}, u32[]{:S(2)}) collective-permute-start(bf16[768,768]{1,0:T(8,128)(2,1)S(1)} %copy-done.201), channel_id=1, source_target_pairs={{0,1},{1,0},{2,3},{3,2},{4,5},{5,4},{6,7},{7,6},{8,9},{9,8},{10,11... | collective-permute-start | bytes 3538952 | tf_op jit(solution)/shard_map/ppermute | solution.py:223
  699.6 44.2 %collective-permute-start.92 = (bf16[768,768]{1,0:T(8,128)(2,1)S(1)}, bf16[768,768]{1,0:T(8,128)(2,1)S(1)}, u32[]{:S(2)}, u32[]{:S(2)}) collective-permute-start(bf16[768,768]{1,0:T(8,128)(2,1)S(1)} %add_convert_fusion.21), channel_id=1, source_target_pairs={{0,2},{1,3},{2,0},{3,1},{4,6},{5,7},{6,4},{7,5},{8,10},{9,11},{10,... | collective-permute-start | bytes 3538952 | tf_op jit(solution)/shard_map/ppermute | solution.py:223
  700.7 68.4 %collective-permute-start.78 = (bf16[768,768]{1,0:T(8,128)(2,1)S(1)}, bf16[768,768]{1,0:T(8,128)(2,1)S(1)}, u32[]{:S(2)}, u32[]{:S(2)}) collective-permute-start(bf16[768,768]{1,0:T(8,128)(2,1)S(1)} %add_convert_fusion.25), channel_id=1, source_target_pairs={{0,2},{1,3},{2,0},{3,1},{4,6},{5,7},{6,4},{7,5},{8,10},{9,11},{10,... | collective-permute-start | bytes 3538952 | tf_op jit(solution)/shard_map/ppermute | solution.py:223
  728.2 53.6 %collective-permute-start.83 = (bf16[768,768]{1,0:T(8,128)(2,1)S(1)}, bf16[768,768]{1,0:T(8,128)(2,1)S(1)}, u32[]{:S(2)}, u32[]{:S(2)}) collective-permute-start(bf16[768,768]{1,0:T(8,128)(2,1)S(1)} %copy-done.203), channel_id=1, source_target_pairs={{0,1},{1,0},{2,3},{3,2},{4,5},{5,4},{6,7},{7,6},{8,9},{9,8},{10,11... | collective-permute-start | bytes 3538952 | tf_op jit(solution)/shard_map/ppermute | solution.py:223
  728.4 66.0 %collective-permute-start.85 = (bf16[768,768]{1,0:T(8,128)(2,1)S(1)}, bf16[768,768]{1,0:T(8,128)(2,1)S(1)}, u32[]{:S(2)}, u32[]{:S(2)}) collective-permute-start(bf16[768,768]{1,0:T(8,128)(2,1)S(1)} %add_convert_fusion.23), channel_id=1, source_target_pairs={{0,2},{1,3},{2,0},{3,1},{4,6},{5,7},{6,4},{7,5},{8,10},{9,11},{10,... | collective-permute-start | bytes 3538952 | tf_op jit(solution)/shard_map/ppermute | solution.py:223
  744.9 50.8 %collective-permute-start.69 = (bf16[768,768]{1,0:T(8,128)(2,1)S(1)}, bf16[768,768]{1,0:T(8,128)(2,1)S(1)}, u32[]{:S(2)}, u32[]{:S(2)}) collective-permute-start(bf16[768,768]{1,0:T(8,128)(2,1)S(1)} %copy-done.202), channel_id=1, source_target_pairs={{0,1},{1,0},{2,3},{3,2},{4,5},{5,4},{6,7},{7,6},{8,9},{9,8},{10,11... | collective-permute-start | bytes 3538952 | tf_op jit(solution)/shard_map/ppermute | solution.py:223
  769.1 49.3 %collective-permute-start.71 = (bf16[768,768]{1,0:T(8,128)(2,1)S(1)}, bf16[768,768]{1,0:T(8,128)(2,1)S(1)}, u32[]{:S(2)}, u32[]{:S(2)}) collective-permute-start(bf16[768,768]{1,0:T(8,128)(2,1)S(1)} %add_convert_fusion.27), channel_id=1, source_target_pairs={{0,2},{1,3},{2,0},{3,1},{4,6},{5,7},{6,4},{7,5},{8,10},{9,11},{10,... | collective-permute-start | bytes 3538952 | tf_op jit(solution)/shard_map/ppermute | solution.py:223
  781.0 38.4 %collective-permute-start.93 = (bf16[384,768]{1,0:T(8,128)(2,1)S(1)}, bf16[384,768]{1,0:T(8,128)(2,1)S(1)}, u32[]{:S(2)}, u32[]{:S(2)}) collective-permute-start(bf16[384,768]{1,0:T(8,128)(2,1)S(1)} %broadcast_select_fusion.1), channel_id=1, source_target_pairs={{0,4},{4,0},{8,12},{12,8},{16,20},{20,16},{24,28},{28,24},{1,5},{5... | collective-permute-start | bytes 1769480 | tf_op jit(solution)/shard_map/ppermute | solution.py:228
  781.8 39.4 %collective-permute-start.79 = (bf16[384,768]{1,0:T(8,128)(2,1)S(1)}, bf16[384,768]{1,0:T(8,128)(2,1)S(1)}, u32[]{:S(2)}, u32[]{:S(2)}) collective-permute-start(bf16[384,768]{1,0:T(8,128)(2,1)S(1)} %broadcast_select_fusion.3), channel_id=1, source_target_pairs={{0,4},{4,0},{8,12},{12,8},{16,20},{20,16},{24,28},{28,24},{1,5},{5... | collective-permute-start | bytes 1769480 | tf_op jit(solution)/shard_map/ppermute | solution.py:228
  795.7 28.1 %collective-permute-start.53 = (bf16[384,576]{0,1:T(8,128)(2,1)S(1)}, bf16[384,576]{0,1:T(8,128)(2,1)S(1)}, u32[]{:S(2)}, u32[]{:S(2)}) collective-permute-start(bf16[384,576]{0,1:T(8,128)(2,1)S(1)} %add_convert_fusion.45), channel_id=1, source_target_pairs={{0,16},{4,20},{8,24},{12,28},{16,0},{20,4},{24,8},{28,12},{1,17},{... | collective-permute-start | bytes 1327112 | tf_op jit(solution)/shard_map/ppermute | solution.py:228
  819.4 27.9 %collective-permute-start.72 = (bf16[384,768]{1,0:T(8,128)(2,1)S(1)}, bf16[384,768]{1,0:T(8,128)(2,1)S(1)}, u32[]{:S(2)}, u32[]{:S(2)}) collective-permute-start(bf16[384,768]{1,0:T(8,128)(2,1)S(1)} %broadcast_select_fusion.4), channel_id=1, source_target_pairs={{0,4},{4,0},{8,12},{12,8},{16,20},{20,16},{24,28},{28,24},{1,5},{5... | collective-permute-start | bytes 1769480 | tf_op jit(solution)/shard_map/ppermute | solution.py:228
  821.2 40.6 %collective-permute-start.94 = (bf16[384,768]{1,0:T(8,128)(2,1)S(1)}, bf16[384,768]{1,0:T(8,128)(2,1)S(1)}, u32[]{:S(2)}, u32[]{:S(2)}) collective-permute-start(bf16[384,768]{1,0:T(8,128)(2,1)S(1)} %add_convert_fusion.34), channel_id=1, source_target_pairs={{0,8},{4,12},{8,0},{12,4},{16,24},{20,28},{24,16},{28,20},{1,9},{5... | collective-permute-start | bytes 1769480 | tf_op jit(solution)/shard_map/ppermute | solution.py:228
  822.2 40.3 %collective-permute-start.80 = (bf16[384,768]{1,0:T(8,128)(2,1)S(1)}, bf16[384,768]{1,0:T(8,128)(2,1)S(1)}, u32[]{:S(2)}, u32[]{:S(2)}) collective-permute-start(bf16[384,768]{1,0:T(8,128)(2,1)S(1)} %add_convert_fusion.40), channel_id=1, source_target_pairs={{0,8},{4,12},{8,0},{12,4},{16,24},{20,28},{24,16},{28,20},{1,9},{5... | collective-permute-start | bytes 1769480 | tf_op jit(solution)/shard_map/ppermute | solution.py:228
  823.7 34.2 %collective-permute-start.46 = (bf16[384,576]{0,1:T(8,128)(2,1)S(1)}, bf16[384,576]{0,1:T(8,128)(2,1)S(1)}, u32[]{:S(2)}, u32[]{:S(2)}) collective-permute-start(bf16[384,576]{0,1:T(8,128)(2,1)S(1)} %add_convert_fusion.48), channel_id=1, source_target_pairs={{0,16},{4,20},{8,24},{12,28},{16,0},{20,4},{24,8},{28,12},{1,17},{... | collective-permute-start | bytes 1327112 | tf_op jit(solution)/shard_map/ppermute | solution.py:228
  834.7 39.3 %collective-permute-start.54 = (bf16[384,576]{0,1:T(8,128)(2,1)S(1)}, bf16[384,576]{0,1:T(8,128)(2,1)S(1)}, u32[]{:S(2)}, u32[]{:S(2)}) collective-permute-start(bf16[384,576]{0,1:T(8,128)(2,1)S(1)} %add_convert_fusion.44), channel_id=1, source_target_pairs={{0,4},{4,0},{8,12},{12,8},{16,20},{20,16},{24,28},{28,24},{1,5},{5... | collective-permute-start | bytes 1327112 | tf_op jit(solution)/shard_map/ppermute | solution.py:228
  847.3 46.1 %collective-permute-start.87 = (bf16[384,768]{1,0:T(8,128)(2,1)S(1)}, bf16[384,768]{1,0:T(8,128)(2,1)S(1)}, u32[]{:S(2)}, u32[]{:S(2)}) collective-permute-start(bf16[384,768]{1,0:T(8,128)(2,1)S(1)} %add_convert_fusion.37), channel_id=1, source_target_pairs={{0,8},{4,12},{8,0},{12,4},{16,24},{20,28},{24,16},{28,20},{1,9},{5... | collective-permute-start | bytes 1769480 | tf_op jit(solution)/shard_map/ppermute | solution.py:228
  857.9 45.4 %collective-permute-start.73 = (bf16[384,768]{1,0:T(8,128)(2,1)S(1)}, bf16[384,768]{1,0:T(8,128)(2,1)S(1)}, u32[]{:S(2)}, u32[]{:S(2)}) collective-permute-start(bf16[384,768]{1,0:T(8,128)(2,1)S(1)} %add_convert_fusion.43), channel_id=1, source_target_pairs={{0,8},{4,12},{8,0},{12,4},{16,24},{20,28},{24,16},{28,20},{1,9},{5... | collective-permute-start | bytes 1769480 | tf_op jit(solution)/shard_map/ppermute | solution.py:228
  861.8 41.7 %collective-permute-start.47 = (bf16[384,576]{0,1:T(8,128)(2,1)S(1)}, bf16[384,576]{0,1:T(8,128)(2,1)S(1)}, u32[]{:S(2)}, u32[]{:S(2)}) collective-permute-start(bf16[384,576]{0,1:T(8,128)(2,1)S(1)} %add_convert_fusion.47), channel_id=1, source_target_pairs={{0,4},{4,0},{8,12},{12,8},{16,20},{20,16},{24,28},{28,24},{1,5},{5... | collective-permute-start | bytes 1327112 | tf_op jit(solution)/shard_map/ppermute | solution.py:228
  862.5 43.5 %collective-permute-start.95 = (bf16[384,768]{1,0:T(8,128)(2,1)S(1)}, bf16[384,768]{1,0:T(8,128)(2,1)S(1)}, u32[]{:S(2)}, u32[]{:S(2)}) collective-permute-start(bf16[384,768]{1,0:T(8,128)(2,1)S(1)} %add_convert_fusion.33), channel_id=1, source_target_pairs={{0,16},{4,20},{8,24},{12,28},{16,0},{20,4},{24,8},{28,12},{1,17},{... | collective-permute-start | bytes 1769480 | tf_op jit(solution)/shard_map/ppermute | solution.py:228
  874.0 68.7 %collective-permute-start.81 = (bf16[384,768]{1,0:T(8,128)(2,1)S(1)}, bf16[384,768]{1,0:T(8,128)(2,1)S(1)}, u32[]{:S(2)}, u32[]{:S(2)}) collective-permute-start(bf16[384,768]{1,0:T(8,128)(2,1)S(1)} %add_convert_fusion.39), channel_id=1, source_target_pairs={{0,16},{4,20},{8,24},{12,28},{16,0},{20,4},{24,8},{28,12},{1,17},{... | collective-permute-start | bytes 1769480 | tf_op jit(solution)/shard_map/ppermute | solution.py:228
  893.6 71.1 %collective-permute-start.88 = (bf16[384,768]{1,0:T(8,128)(2,1)S(1)}, bf16[384,768]{1,0:T(8,128)(2,1)S(1)}, u32[]{:S(2)}, u32[]{:S(2)}) collective-permute-start(bf16[384,768]{1,0:T(8,128)(2,1)S(1)} %add_convert_fusion.36), channel_id=1, source_target_pairs={{0,16},{4,20},{8,24},{12,28},{16,0},{20,4},{24,8},{28,12},{1,17},{... | collective-permute-start | bytes 1769480 | tf_op jit(solution)/shard_map/ppermute | solution.py:228
  903.5 60.5 %collective-permute-start.74 = (bf16[384,768]{1,0:T(8,128)(2,1)S(1)}, bf16[384,768]{1,0:T(8,128)(2,1)S(1)}, u32[]{:S(2)}, u32[]{:S(2)}) collective-permute-start(bf16[384,768]{1,0:T(8,128)(2,1)S(1)} %add_convert_fusion.42), channel_id=1, source_target_pairs={{0,16},{4,20},{8,24},{12,28},{16,0},{20,4},{24,8},{28,12},{1,17},{... | collective-permute-start | bytes 1769480 | tf_op jit(solution)/shard_map/ppermute | solution.py:228
  906.2 60.2 %collective-permute-start.96 = (bf16[384,768]{1,0:T(8,128)(2,1)S(1)}, bf16[384,768]{1,0:T(8,128)(2,1)S(1)}, u32[]{:S(2)}, u32[]{:S(2)}) collective-permute-start(bf16[384,768]{1,0:T(8,128)(2,1)S(1)} %add_convert_fusion.32), channel_id=1, source_target_pairs={{0,4},{4,0},{8,12},{12,8},{16,20},{20,16},{24,28},{28,24},{1,5},{5... | collective-permute-start | bytes 1769480 | tf_op jit(solution)/shard_map/ppermute | solution.py:228
  (286 other events, 3005.7 us)

commit v2 on v0

v2 whole, which is shorter than its diff:
```python
from functools import partial

import jax
import jax.numpy as jnp
from jax import lax
from jax.experimental import pallas as pl
from jax.experimental.pallas import tpu as pltpu
from jax.sharding import PartitionSpec as P

HD = 64
FRAMES = 16
SIDE = 16
TUBE = 4
WINDOW = 256
PAIR = 128
BAND = 64
CELL = 16
LSE_ROWS = 16

epsilon = 1e-06
masked_score = -1e30
f32 = jnp.float32
bf16 = jnp.bfloat16
VMEM_LIMIT = 56 * 1024 * 1024
TIMES = {
    "attend": 17, "feed": 23, "code_loss": 10, "feed_back": 21, "attend_back": 25,
    "grads_down": 8, "grads_up": 8, "grads_attn": 8, "emit": 3,
}
SCALE = 0.0001


def cost_of(name):
    time = TIMES[name] * SCALE
    return pl.CostEstimate(flops=int(time * 1.15e9), bytes_accessed=int(time * 3.6e6), transcendentals=0)


def dot(a, b):
    return lax.dot_general(a, b, (((1,), (0,)), ((), ())), preferred_element_type=f32)


def dot_nt(a, b):
    return lax.dot_general(a, b, (((1,), (1,)), ((), ())), preferred_element_type=f32)


def dot_tn(a, b):
    return lax.dot_general(a, b, (((0,), (0,)), ((), ())), preferred_element_type=f32)


def statistics(stream):
    centre = jnp.mean(stream, axis=-1, keepdims=True)
    centred = stream - centre
    spread = jnp.mean(centred * centred, axis=-1, keepdims=True)
    scale = lax.rsqrt(spread + epsilon)
    return centred * scale, scale


def by_eight(values):
    rows, columns = values.shape
    return jnp.sum(values.reshape(rows // 8, 8, columns), axis=0)


def gather_sums(acc_ref, values):
    first = pl.program_id(0) == 0
    parts = jnp.concatenate([by_eight(v) for v in values], axis=1)

    @pl.when(first)
    def _():
        acc_ref[...] = parts

    @pl.when(jnp.logical_not(first))
    def _():
        acc_ref[...] += parts


def last_step():
    return pl.program_id(0) == pl.num_programs(0) - 1


def norm_back(stream, gain, grad):
    normal, scale = statistics(stream)
    scaled = grad * gain
    mean_plain = jnp.mean(scaled, axis=-1, keepdims=True)
    mean_normal = jnp.mean(scaled * normal, axis=-1, keepdims=True)
    inner = scale * (scaled - mean_plain - normal * mean_normal)
    return inner, grad * normal


def gelu_both(hidden):
    root = 0.7978845608028654
    cubic = 0.044715
    square = hidden * hidden
    bend = jnp.tanh(hidden * (root + root * cubic * square))
    rise = 0.5 + 0.5 * bend
    active = hidden * rise
    slope = rise + (active - active * rise) * (2.0 * root + 6.0 * root * cubic * square)
    return active.astype(bf16), slope.astype(bf16)


def allowed_of(place_ref):
    head_index = place_ref[0]
    frame_count = place_ref[1]

    def valid(axis):
        position = lax.broadcasted_iota(jnp.int32, (WINDOW, WINDOW), axis)
        frame = 4 * ((position >> 6) ^ head_index) + ((position >> 4) & 3)
        return frame < frame_count

    return jnp.logical_or(valid(0), jnp.logical_not(valid(1)))


def shuffle_of(place_ref, axis):
    arranged = lax.broadcasted_iota(jnp.int32, (WINDOW, WINDOW), axis)
    plain = lax.broadcasted_iota(jnp.int32, (WINDOW, WINDOW), 1 - axis)
    band = (arranged >> 6) ^ place_ref[0]
    source = band * BAND + ((arranged >> 2) & 3) * 16 + ((arranged >> 4) & 3) * 4 + (arranged & 3)
    return (source == plain).astype(f32).astype(bf16)


def assemble_qkv(packs, scratch):
    width = scratch.shape[1]
    share = width // 4
    for k in range(4):
        for j in range(3):
            start = j * width + k * share
            scratch[start : start + share, :] = packs[k][j * share : (j + 1) * share, :]


def assemble_out(packs, scratch):
    share = scratch.shape[0] // 4
    for k in range(4):
        scratch[k * share : (k + 1) * share, :] = packs[k][3 * share :, :]


def stack_heads(pair):
    low = lax.broadcasted_iota(jnp.int32, pair.shape, 1) < HD
    zero = jnp.zeros((), bf16)
    return jnp.concatenate([jnp.where(low, pair, zero), jnp.where(low, zero, pair)], axis=0)


def attend_core(qkv, allowed, att_ref, lse_ref):
    width = att_ref.shape[1]
    pairs = width // PAIR

    def part(j, pair):
        return qkv[:, j * width + pair * PAIR : j * width + (pair + 1) * PAIR]

    def scores_of(pair):
        query = part(0, pair) * jnp.asarray(HD ** (-0.5), bf16)
        return dot_nt(stack_heads(part(1, pair)), query)

    ahead = scores_of(0)
    for pair in range(pairs):
        scores = ahead
        if pair + 1 < pairs:
            ahead = scores_of(pair + 1)
        probs = []
        for half in range(2):
            mine = scores[half * WINDOW : (half + 1) * WINDOW]
            if allowed is not None:
                mine = jnp.where(allowed, mine, masked_score)
            top = jnp.max(mine, axis=0, keepdims=True)
            terms = jnp.exp(mine - top)
            total = jnp.sum(terms, axis=0, keepdims=True)
            probs.append((terms * (1.0 / total)).astype(bf16))
            head = 2 * pair + half
            lse_ref[head : head + 1, :] = top + jnp.log(total)
        out = dot_tn(jnp.concatenate(probs, axis=0), stack_heads(part(2, pair)))
        att_ref[:, pair * PAIR : (pair + 1) * PAIR] = out.astype(bf16)


def attend_kernel(layer, place_ref, *refs):
    if layer == 0:
        tokens_ref, marks_ref, *refs = refs
        shuffle = shuffle_of(place_ref, 0)
        stream = dot(shuffle, tokens_ref[...])
    else:
        pieces, refs = refs[:4], refs[4:]
        stream = jnp.concatenate(
            [p[...].reshape(BAND, p.shape[-1]) for p in pieces], axis=0
        ).astype(f32)
    gain_ref, shift_ref, s0, s1, s2, s3, p0, p1, p2, p3, x_ref, normed_ref, qkv_ref, att_ref, lse_ref, *refs = refs
    *mark_refs, scratch = refs
    share = scratch.shape[1] // 4

    @pl.when(pl.program_id(0) == 0)
    def _():
        assemble_qkv((p0, p1, p2, p3), scratch)

    if layer == 0:
        chosen = shuffle_of(place_ref, 1).astype(f32)
        marks = jnp.sum(chosen * marks_ref[...], axis=0, keepdims=True)
        for k in range(4):
            mark_refs[k][pl.ds(pl.program_id(0), 1), :] = marks[:, k * BAND : (k + 1) * BAND]
    x_ref[...] = stream.astype(bf16)
    normal, _ = statistics(stream)
    normed = (normal * gain_ref[layer, 0:1] + shift_ref[layer, 0:1]).astype(bf16)
    normed_ref[...] = normed
    start = 2 * layer * share
    smalls = (s0, s1, s2, s3)
    bias = jnp.concatenate(
        [r[2:3, start : start + share] for r in smalls]
        + [jnp.zeros((1, 4 * share), f32)]
        + [r[2:3, start + share : start + 2 * share] for r in smalls],
        axis=1,
    )
    qkv = (dot_nt(normed, scratch[...]) + bias).astype(bf16)
    qkv_ref[...] = qkv
    allowed = allowed_of(place_ref) if layer == 1 else None
    attend_core(qkv, allowed, att_ref, lse_ref)


def whole(array):
    zeros = (0,) * array.ndim
    return pl.BlockSpec(array.shape, lambda i, s: zeros)


def rows_of(columns, rows=WINDOW):
    return pl.BlockSpec((rows, columns), lambda i, s: (i, 0))


def tube_of(columns):
    return pl.BlockSpec((4, 1, CELL, columns), lambda i, s: (0, i, 0, 0))


def sums_of(columns):
    return pl.BlockSpec((8, columns), lambda i, s: (0, 0))


def call(kernel, name, place, steps, operands, outs, scratch=(), aliases={}):
    return pl.pallas_call(
        kernel,
        grid_spec=pltpu.PrefetchScalarGridSpec(
            num_scalar_prefetch=1,
            grid=(steps,),
            in_specs=[spec for _, spec in operands],
            out_specs=[spec for _, _, spec in outs],
            scratch_shapes=list(scratch),
        ),
        out_shape=[jax.ShapeDtypeStruct(shape, dtype) for shape, dtype, _ in outs],
        compiler_params=pltpu.CompilerParams(vmem_limit_bytes=VMEM_LIMIT),
        cost_estimate=cost_of(name),
        input_output_aliases=aliases,
        name=name,
    )(place, *[array for array, _ in operands])


def attend(layer, place, inputs, gain, shift, smalls, packs):
    width = gain.shape[-1]
    rows = 4 * WINDOW
    if layer == 0:
        tokens, marks = inputs
        first = [(tokens, rows_of(width)), (marks, rows_of(1))]
    else:
        first = [(p, tube_of(width)) for p in inputs]
    operands = first + [(a, whole(a)) for a in (gain, shift, *smalls, *packs)]
    outs = [
        ((rows, width), bf16, rows_of(width)),
        ((rows, width), bf16, rows_of(width)),
        ((rows, 3 * width), bf16, rows_of(3 * width)),
        ((rows, width), bf16, rows_of(width)),
        ((4 * LSE_ROWS, WINDOW), f32, rows_of(WINDOW, LSE_ROWS)),
    ]
    if layer == 0:
        outs += [((4, BAND), f32, pl.BlockSpec((4, BAND), lambda i, s: (0, 0)))] * 4
    return call(
        partial(attend_kernel, layer), "attend", place, 4, operands, outs,
        [pltpu.VMEM((3 * width, width), bf16)],
    )


def attend_back_core(qkv, grad, lse_ref, allowed):
    width = grad.shape[1]
    pairs = width // PAIR

    def part(j, pair):
        return qkv[:, j * width + pair * PAIR : j * width + (pair + 1) * PAIR]

    def first_of(pair):
        query = part(0, pair) * jnp.asarray(HD ** (-0.5), bf16)
        grad_part = grad[:, pair * PAIR : (pair + 1) * PAIR]
        keys = stack_heads(part(1, pair))
        scores = dot_nt(keys, query)
        grad_probs = dot_nt(stack_heads(part(2, pair)), grad_part)
        return query, grad_part, keys, scores, grad_probs

    low = lax.broadcasted_iota(jnp.int32, (WINDOW, PAIR), 1) < HD
    results = [[], [], []]
    ahead = first_of(0)
    for pair in range(pairs):
        query, grad_part, keys, scores, grad_probs = ahead
        if pair + 1 < pairs:
            ahead = first_of(pair + 1)
        all_probs, all_scores = [], []
        for half in range(2):
            rows = slice(half * WINDOW, (half + 1) * WINDOW)
            mine = scores[rows]
            if allowed is not None:
                mine = jnp.where(allowed, mine, masked_score)
            head = 2 * pair + half
            probs = jnp.exp(mine - lse_ref[head : head + 1, :])
            grad_mine = grad_probs[rows]
            delta = jnp.sum(probs * grad_mine, axis=0, keepdims=True)
            all_probs.append(probs.astype(bf16))
            all_scores.append((probs * (grad_mine - delta)).astype(bf16))
        probs = jnp.concatenate(all_probs, axis=0)
        grad_scores = jnp.concatenate(all_scores, axis=0)
        grad_query = dot_tn(grad_scores, keys) * HD ** (-0.5)
        grad_key = dot(grad_scores, query)
        grad_value = dot(probs, grad_part)
        results[0].append(grad_query.astype(bf16))
        results[1].append(jnp.where(low, grad_key[:WINDOW], grad_key[WINDOW:]).astype(bf16))
        results[2].append(jnp.where(low, grad_value[:WINDOW], grad_value[WINDOW:]).astype(bf16))
    return [jnp.concatenate(part, axis=1) for part in results]


def attend_back_kernel(layer, place_ref, *refs):
    (stream_ref, g1_ref, x_ref, qkv_ref, lse_ref, gain_ref, p0, p1, p2, p3, *outs) = refs
    d0, d1, d2, d3, *outs = outs
    if layer == 1:
        pieces, outs = outs[:4], outs[4:]
    else:
        (final_ref, *outs) = outs
    sums_ref, scratch, out_scratch, acc = outs
    width = stream_ref.shape[1]
    share = width // 4

    @pl.when(pl.program_id(0) == 0)
    def _():
        assemble_qkv((p0, p1, p2, p3), scratch)
        assemble_out((p0, p1, p2, p3), out_scratch)

    grad_att = dot_nt(g1_ref[...], out_scratch[...]).astype(bf16)
    allowed = allowed_of(place_ref) if layer == 1 else None
    parts = attend_back_core(qkv_ref[...], grad_att, lse_ref, allowed)
    for k, ref in enumerate((d0, d1, d2, d3)):
        for j in range(3):
            ref[:, j * share : (j + 1) * share] = parts[j][:, k * share : (k + 1) * share]
    joined = jnp.concatenate(parts, axis=1)
    grad_normed = dot(joined, scratch[...])
    inner, scaled = norm_back(x_ref[...].astype(f32), gain_ref[layer, 0:1], grad_normed)
    gather_sums(acc, [parts[0].astype(f32), parts[2].astype(f32), scaled, grad_normed])
    stream = stream_ref[...] + inner
    if layer == 1:
        for k in range(4):
            pieces[k][...] = (
                stream[k * BAND : (k + 1) * BAND].astype(bf16).reshape(4, 1, CELL, width)
            )
    else:
        shuffle = shuffle_of(place_ref, 1)
        high = stream.astype(bf16)
        low = (stream - high.astype(f32)).astype(bf16)
        final_ref[...] = dot(shuffle, high) + dot(shuffle, low)

    @pl.when(last_step())
    def _():
        total = jnp.sum(acc[...], axis=0, keepdims=True)
        sums_ref[...] = jnp.zeros(sums_ref.shape, f32)
        for k in range(4):
            query = total[:, k * share : (k + 1) * share]
            value = total[:, width + k * share : width + (k + 1) * share]
            sums_ref[pl.ds(place_ref[0] ^ k, 1), : 2 * share] = jnp.concatenate([query, value], axis=1)
        sums_ref[4:5, :] = total[:, 2 * width : 3 * width]
        sums_ref[5:6, :] = total[:, 3 * width :]


def attend_back(layer, place, stream, g1, x, qkv, lse, gain, packs):
    rows, width = stream.shape
    share = width // 4
    operands = [
        (stream, rows_of(width)),
        (g1, rows_of(width)),
        (x, rows_of(width)),
        (qkv, rows_of(3 * width)),
        (lse, rows_of(WINDOW, LSE_ROWS)),
    ] + [(a, whole(a)) for a in (gain, *packs)]
    outs = [((rows, 3 * share), bf16, rows_of(3 * share))] * 4
    if layer == 1:
        outs = outs + [((4, 4, CELL, width), bf16, tube_of(width))] * 4
    else:
        outs = outs + [((rows, width), f32, rows_of(width))]
    outs = outs + [((8, width), f32, sums_of(width))]
    return call(
        partial(attend_back_kernel, layer), "attend_back", place, 4, operands, outs,
        [pltpu.VMEM((3 * width, width), bf16), pltpu.VMEM((width, width), bf16), pltpu.VMEM((8, 4 * width), f32)],
    )


def feed_kernel(layer, place_ref, *refs):
    (
        x_ref, att_ref, a0, a1, a2, a3, vec_ref, gain_ref, shift_ref, s0, s1, s2, s3,
        u0, u1, u2, u3, d0, d1, d2, d3, stream_ref, normed_ref, active_ref, slope_ref, *outs
    ) = refs
    ups, downs = (u0, u1, u2, u3), (d0, d1, d2, d3)
    *pieces, scratch = outs
    width = x_ref.shape[1]

    @pl.when(pl.program_id(0) == 0)
    def _():
        share = width // 4
        for k, part in enumerate((a0, a1, a2, a3)):
            scratch[k * share : (k + 1) * share, :] = part[...]

    stream = x_ref[...].astype(f32) + dot(att_ref[...], scratch[...]) + vec_ref[layer, 0:1]
    stream_ref[...] = stream
    normal, _ = statistics(stream)
    normed = (normal * gain_ref[layer, 1:2] + shift_ref[layer, 1:2]).astype(bf16)
    normed_ref[...] = normed
    total = stream + vec_ref[layer, 1:2]
    units = u0.shape[1]
    ahead = dot(normed, ups[0][...])
    for k in range(4):
        hidden = ahead
        if k < 3:
            ahead = dot(normed, ups[k + 1][...])
        cut = slice(k * units, (k + 1) * units)
        active, slope = gelu_both(hidden + (s0, s1, s2, s3)[k][layer : layer + 1, :])
        active_ref[:, cut] = active
        slope_ref[:, cut] = slope
        total = total + dot(active, downs[k][...])
    total = total.astype(bf16)
    if layer == 0:
        for k in range(4):
            pieces[k][...] = total[k * BAND : (k + 1) * BAND].reshape(1, BAND, width)
    else:
        pieces[0][...] = total


def feed_specs(layer, packs):
    ups, downs, across = packs
    width = across[0].shape[1]
    block = (width, width)

    def of_layer(a):
        return (a, pl.BlockSpec((None, *block), lambda i, s: (layer, 0, 0)))

    def of_half(a, half):
        return (a, pl.BlockSpec(block, lambda i, s: (half, 0)))

    return [
        *[of_layer(a) for a in ups],
        *[of_half(a, 0) for a in across],
        *[of_layer(a) for a in downs],
        *[of_half(a, 1) for a in across],
    ]


def feed(layer, place, x, att, attn_packs, vecs, gain, shift, smalls, packs):
    rows, width = x.shape
    units = packs[0][0].shape[2]
    last = pl.BlockSpec((width // 4, width), lambda i, s: (3, 0))
    operands = (
        [(x, rows_of(width)), (att, rows_of(width))]
        + [(a, last) for a in attn_packs]
        + [(a, whole(a)) for a in (vecs, gain, shift, *smalls)]
        + feed_specs(layer, packs)
    )
    outs = [
        ((rows, width), f32, rows_of(width)),
        ((rows, width), bf16, rows_of(width)),
        ((rows, 4 * units), bf16, rows_of(4 * units)),
        ((rows, 4 * units), bf16, rows_of(4 * units)),
    ]
    if layer == 0:
        piece = pl.BlockSpec((1, BAND, width), lambda i, s: (i, 0, 0))
        outs = outs + [((4, BAND, width), bf16, piece)] * 4
    else:
        outs = outs + [((rows, width), bf16, rows_of(width))]
    return call(
        partial(feed_kernel, layer), "feed", place, 4, operands, outs,
        [pltpu.VMEM((width, width), bf16)],
    )


def loss_kernel(place_ref, final_ref, head_ref, m0, m1, m2, m3, grad_ref, g2_ref, loss_ref, acc):
    logits = dot(final_ref[...], head_ref[...])
    spread = jnp.concatenate(
        [jnp.broadcast_to(m[f : f + 1, :], (CELL, BAND)) for m in (m0, m1, m2, m3) for f in range(4)],
        axis=0,
    )
    position = lax.broadcasted_iota(jnp.int32, (WINDOW, BAND), 0)
    lane = lax.broadcasted_iota(jnp.int32, (WINDOW, BAND), 1)
    mine = lane == pl.program_id(0) * CELL + (position & (CELL - 1))
    mark = jnp.sum(jnp.where(mine, spread, 0.0), axis=1, keepdims=True).astype(jnp.int32)
    place_of = lax.broadcasted_iota(jnp.int32, (WINDOW, 1), 0)
    frame = 4 * ((place_of >> 6) ^ place_ref[0]) + ((place_of >> 4) & 3)
    weight = jnp.where(frame < place_ref[1], (mark & 1).astype(f32), 0.0)
    top = jnp.max(logits, axis=1, keepdims=True)
    terms = jnp.exp(logits - top)
    total = jnp.sum(terms, axis=1, keepdims=True)
    code = lax.broadcasted_iota(jnp.int32, logits.shape, 1)
    chosen = code == (mark >> 1)
    picked = jnp.sum(jnp.where(chosen, logits, 0.0), axis=1, keepdims=True)
    entry = weight * (top + jnp.log(total) - picked)
    soft = terms * (1.0 / total)
    grad_logits = (weight * (soft - jnp.where(chosen, 1.0, 0.0))).astype(bf16)
    grad = dot_nt(grad_logits, head_ref[...])
    grad_ref[...] = grad
    g2_ref[...] = grad.astype(bf16)
    gather_sums(acc, [jnp.broadcast_to(entry, (WINDOW, PAIR))])

    @pl.when(last_step())
    def _():
        total = jnp.sum(acc[...], axis=0, keepdims=True)
        loss_ref[...] = jnp.broadcast_to(total[:, :1], loss_ref.shape)


def code_loss(place, final, code_head, marks):
    rows, width = final.shape
    operands = [(final, rows_of(width))] + [(a, whole(a)) for a in (code_head, *marks)]
    outs = [
        ((rows, width), f32, rows_of(width)),
        ((rows, width), bf16, rows_of(width)),
        ((8, width), f32, sums_of(width)),
    ]
    return call(
        loss_kernel, "code_loss", place, 4, operands, outs, [pltpu.VMEM((8, PAIR), f32)]
    )


def feed_back_kernel(layer, place_ref, *refs):
    if layer == 1:
        grad_ref, *refs = refs
        grad = grad_ref[...]
    else:
        pieces, refs = refs[:4], refs[4:]
        grad = jnp.concatenate(
            [p[...].reshape(BAND, p.shape[-1]) for p in pieces], axis=0
        ).astype(f32)
    (
        slope_ref, stream_ref, gain_ref, u0, u1, u2, u3, d0, d1, d2, d3, hidden_ref, next_ref, g1_ref, *outs
    ) = refs
    if layer == 0:
        (g2_ref, *outs) = outs
    sums_ref, acc = outs
    g2 = grad.astype(bf16)
    if layer == 0:
        g2_ref[...] = g2
    units = u0.shape[1]
    grad_normed = jnp.zeros(grad.shape, f32)
    sums = []
    ups, downs = (u0, u1, u2, u3), (d0, d1, d2, d3)
    ahead = dot_nt(g2, downs[0][...])
    for k in range(4):
        grad_active = ahead
        if k < 3:
            ahead = dot_nt(g2, downs[k + 1][...])
        cut = slice(k * units, (k + 1) * units)
        grad_hidden = (grad_active * slope_ref[:, cut].astype(f32)).astype(bf16)
        hidden_ref[:, cut] = grad_hidden
        sums.append(grad_hidden.astype(f32))
        grad_normed = grad_normed + dot_nt(grad_hidden, ups[k][...])
    inner, scaled = norm_back(stream_ref[...], gain_ref[layer, 1:2], grad_normed)
    grad = grad + inner
    next_ref[...] = grad
    g1 = grad.astype(bf16)
    g1_ref[...] = g1
    gather_sums(acc, sums + [scaled, grad_normed, g2.astype(f32), g1.astype(f32)])

    @pl.when(last_step())
    def _():
        total = jnp.sum(acc[...], axis=0, keepdims=True)
        for k in range(4):
            sums_ref[pl.ds(place_ref[0] ^ k, 1), :] = total[:, k * units : (k + 1) * units]
            start = 4 * units + k * grad.shape[1]
            sums_ref[4 + k : 5 + k, :] = total[:, start : start + grad.shape[1]]


def feed_back(layer, place, grad, slope, stream, gain, packs):
    rows, width = stream.shape
    units = packs[0][0].shape[2]
    if layer == 1:
        first = [(grad, rows_of(width))]
    else:
        piece = pl.BlockSpec((1, BAND, width), lambda i, s: (i, 0, 0))
        first = [(p, piece) for p in grad]
    operands = (
        first
        + [(slope, rows_of(4 * units)), (stream, rows_of(width))]
        + [(gain, whole(gain))]
        + feed_specs(layer, packs)
    )
    outs = [
        ((rows, 4 * units), bf16, rows_of(4 * units)),
        ((rows, width), f32, rows_of(width)),
        ((rows, width), bf16, rows_of(width)),
    ]
    if layer == 0:
        outs = outs + [((rows, width), bf16, rows_of(width))]
    outs = outs + [((8, width), f32, sums_of(width))]
    return call(
        partial(feed_back_kernel, layer), "feed_back", place, 4, operands, outs,
        [pltpu.VMEM((8, 4 * units + 4 * width), f32)],
    )


ORDER = (1, 3, 2, 0)


def grad_kernel(kind, place_ref, *refs):
    refs = list(refs)

    def take(count):
        taken = refs[:count]
        del refs[:count]
        return taken

    sources = {"attn": 7, "up": 2, "down": 2}[kind]
    arrays = take(sources)
    outs = take(4)
    bufs = take(7 if kind == "attn" else 5)
    out_bufs = take(4)
    in_sem, out_sem = refs
    width = out_bufs[0].shape[-1]
    copies = []

    def fetch(source, buf):
        copy = pltpu.make_async_copy(source, buf, in_sem.at[len(copies)])
        copy.start()
        copies.append(copy)
        return [copy, buf]

    def ready(item):
        if item[0] is not None:
            item[0].wait()
            item[0] = None
        return item[1]

    def columns(ref, k):
        return ref.at[:, pl.ds(k * width, width)]

    if kind == "attn":
        normed = fetch(arrays[0], bufs[0])
        sides = [fetch(arrays[3], bufs[3])]
        g1 = fetch(arrays[1], bufs[1])
        att = fetch(arrays[2], bufs[2])
        sides += [fetch(arrays[3 + n], bufs[3 + n]) for n in range(1, 4)]
        plan = [(normed, side) for side in sides]
    else:
        fixed, split = (arrays[1], arrays[0]) if kind == "down" else (arrays[0], arrays[1])
        fixed = fetch(fixed, bufs[4])
        split = [fetch(columns(split, k), bufs[n]) for n, k in enumerate(ORDER)]
        plan = [(s, fixed) if kind == "down" else (fixed, s) for s in split]
    sent = []
    for n, (left, right) in enumerate(plan):
        value = dot_tn(ready(left)[...], ready(right)[...])
        if kind == "attn":
            share = width // 4
            k = ORDER[n]
            beside = dot_tn(ready(g1)[...], ready(att)[:, k * share : (k + 1) * share])
            value = jnp.concatenate([value, beside], axis=1)
        out_bufs[n][...] = value.astype(bf16)
        copy = pltpu.make_async_copy(out_bufs[n], outs[n], out_sem.at[n])
        copy.start()
        sent.append(copy)
    for copy in sent:
        copy.wait()


def grads(kind, place, arrays, width):
    rows = arrays[1].shape[0]
    if kind == "attn":
        arrays = list(arrays[:3]) + [arrays[3][k] for k in ORDER]
        loads = [a.shape for a in arrays]
    else:
        loads = [(rows, width)] * 5
    anywhere = pl.BlockSpec(memory_space=pl.ANY)
    scratch = (
        [pltpu.VMEM(shape, bf16) for shape in loads]
        + [pltpu.VMEM((width, width), bf16)] * 4
        + [pltpu.SemaphoreType.DMA((len(loads),)), pltpu.SemaphoreType.DMA((4,))]
    )
    operands = [(a, anywhere) for a in arrays]
    outs = [((width, width), bf16, anywhere)] * 4
    return call(partial(grad_kernel, kind), "grads_" + kind, place, 1, operands, outs, scratch)


def emit_kernel(attention, split, aliased, place_ref, *refs):
    if split:
        mine_ref, other_ref, *refs = refs
        mine = pl.program_id(0) == place_ref[2]
        value = jnp.where(mine, mine_ref[...].astype(f32), other_ref[...].astype(f32))
    else:
        whole_ref, *refs = refs
        value = whole_ref[...].astype(f32)
    outs = refs[aliased:]
    if attention:
        qkv_ref, out_ref = outs
        share = qkv_ref.shape[-1]
        for j in range(3):
            qkv_ref[0, j] = value[:, j * share : (j + 1) * share]
        out_ref[0] = value[:, 3 * share :].T
    else:
        outs[0][0] = value


def emit(place, layer, attention, summed, earlier):
    split = len(summed) == 2
    width = summed[0].shape[1]
    half = width // 2
    share = width // 4
    if attention:
        outs = [
            ((2, 3, width, share), f32, pl.BlockSpec((1, 3, half, share), lambda i, s: (layer, 0, i, 0))),
            ((2, share, width), f32, pl.BlockSpec((1, share, half), lambda i, s: (layer, 0, i))),
        ]
    else:
        outs = [((2, width, width), f32, pl.BlockSpec((1, half, width), lambda i, s: (layer, i, 0)))]
    if split:
        operands = [(a, whole(a)) for a in summed]
    else:
        operands = [(summed[0], pl.BlockSpec((half, width), lambda i, s: (i, 0)))]
    aliases = {}
    if earlier is not None:
        aliases = {1 + len(operands) + n: n for n in range(len(earlier))}
        operands += [(e, pl.BlockSpec(memory_space=pl.ANY)) for e in earlier]
    return call(
        partial(emit_kernel, attention, split, len(aliases)), "emit", place, 2, operands, outs,
        aliases=aliases,
    )


def head_swap(values, distance):
    count = lax.axis_size("head")
    return lax.ppermute(values, "head", [(i, i ^ distance) for i in range(count)])


def clip_swap(values, distance):
    count = lax.axis_size("clip")
    return lax.ppermute(values, "clip", [(i, i ^ distance) for i in range(count)])


class Order:
    def __init__(self):
        self.last = ()
        self.pending = []

    def run(self, step, *values):
        values, _ = lax.optimization_barrier((values, self.last))
        out = step(*values)
        self.last = (jax.tree.leaves(out)[0],)
        return out

    def send(self, swap, values, distance):
        values, _ = lax.optimization_barrier((values, self.last))
        out = swap(values, distance)
        self.pending.append(out)
        return out

    def close(self):
        self.last = self.last + tuple(self.pending)
        self.pending = []


class Pack:
    def __init__(self, order, place, kind, arrays, width):
        self.order = order
        self.upper = place[2] == 1
        self.parts = order.run(lambda *a: grads(kind, place, a, width), *arrays)
        count = lax.axis_size("clip")
        self.distances = [1 << n for n in range(count.bit_length() - 1)] + [1]
        self.stage = 0

    def prepare(self):
        run = self.order.run
        if self.stage == 1:

            def add(part, beyond):
                return (part.astype(f32) + beyond.astype(f32)).astype(bf16)

            self.leaving = run(add, self.parts[2], self.beyond)
        elif self.stage == 2:

            def add(part, beside, across):
                total = part.astype(f32) + beside.astype(f32) + across.astype(f32)
                half = total.shape[0] // 2
                low, high = total[:half], total[half:]
                return (
                    jnp.where(self.upper, low, high).astype(bf16),
                    jnp.where(self.upper, high, low).astype(bf16),
                )

            self.leaving, self.sum = run(add, self.parts[3], self.beside, self.moved)
        elif self.stage > 2:

            def add(total, moved):
                return (total.astype(f32) + moved.astype(f32)).astype(bf16)

            self.leaving = self.sum = run(add, self.sum, self.moved)

    def launch(self):
        send = self.order.send
        if self.stage == 0:
            self.beside = send(head_swap, self.parts[0], 1)
            self.beyond = send(head_swap, self.parts[1], 1)
        elif self.stage == 1:
            self.moved = send(head_swap, self.leaving, 2)
        else:
            self.moved = send(clip_swap, self.leaving, self.distances[self.stage - 2])
        self.stage += 1

    def done(self):
        return self.stage == 2 + len(self.distances)

    def whole(self):
        assert self.done()
        return self.sum, self.moved


def on_device(
    tokens,
    frame_counts,
    token_mask,
    targets,
    norm_gain,
    norm_bias,
    w_qkv,
    qv_bias,
    w_out,
    vec_bias,
    w_up,
    up_bias,
    w_down,
    code_head,
):
    head_index = lax.axis_index("head")
    width = tokens.shape[1]
    share = w_out.shape[1]
    upper = lax.axis_index("clip") & 1
    place = jnp.stack(
        [head_index.astype(jnp.int32), frame_counts[0], upper.astype(jnp.int32)]
    )
    order = Order()

    def tied(values, *after):
        return lax.optimization_barrier((values, after))[0]

    clip_count = lax.axis_size("clip")
    own_small = jnp.concatenate([up_bias, qv_bias.reshape(1, width)], axis=0)
    piece = (w_up.shape[1] + w_down.shape[1]) // clip_count
    first_row = lax.axis_index("clip") * piece

    def chunk(layer):
        halves = [w_up[layer], w_down[layer]]
        rows = halves[0].shape[0]
        start = first_row % rows
        parts = [lax.dynamic_slice_in_dim(h, start, piece, 0) for h in halves]
        return jnp.where(first_row < rows, parts[0], parts[1])

    def gather_feed(chunk_across):
        return lax.all_gather(chunk_across, "clip", axis=0, tiled=True)

    def attn_pack(layer):
        transposed = w_qkv[layer].swapaxes(1, 2).reshape(-1, width)
        return jnp.concatenate([transposed, w_out[layer]], axis=0)

    def spread(own, across):
        return [own, head_swap(own, 1), across, head_swap(across, 1)]

    chunk_0 = head_swap(chunk(0), 2)
    smalls = spread(own_small, head_swap(own_small, 2))
    own = tied(attn_pack(0), chunk_0, smalls[2])
    attn = [spread(own, head_swap(own, 2)), None]
    feed_across = [gather_feed(chunk_0), None]
    ups = [w_up, head_swap(tied(w_up, attn[0][2]), 1)]
    downs = [w_down, head_swap(tied(w_down, attn[0][2]), 1)]
    packs = [None, None]

    marks = (2 * targets + token_mask).astype(f32).reshape(-1, 1)
    kept = []
    inputs = (tokens, marks)
    for layer in range(2):
        x, normed, qkv, att, lse, *mark_pieces = order.run(
            lambda *a: attend(layer, place, a, norm_gain, norm_bias, smalls, attn[layer]), *inputs
        )
        if layer == 0:
            marks = [mark_pieces[0]] + [head_swap(mark_pieces[k], k) for k in (1, 2, 3)]
            chunk_1 = head_swap(tied(chunk(1), x), 2)
            own = tied(attn_pack(1), chunk_1)
            attn[1] = spread(own, head_swap(own, 2))
            feed_across[1] = gather_feed(chunk_1)
        across = tied(feed_across[layer], x)
        packs[layer] = (ups, downs, [across, head_swap(across, 1)])
        stream, normed2, active, slope, *outs = order.run(
            lambda a, b: feed(
                layer, place, a, b, attn[layer], vec_bias, norm_gain, norm_bias, smalls, packs[layer]
            ),
            x, att,
        )
        kept.append((x, normed, qkv, att, lse, stream, normed2, active, slope))
        if layer == 0:
            inputs = [outs[0]] + [order.send(head_swap, outs[k], k) for k in (1, 2, 3)]
            inputs = [p.reshape(4, 4, CELL, width) for p in inputs]
            order.close()
    grad, g2, loss_sum = order.run(lambda a: code_loss(place, a, code_head, marks), outs[0])

    def run_feed_back(layer, grad):
        x, normed, qkv, att, lse, stream, normed2, active, slope = kept[layer]
        return order.run(
            lambda a: feed_back(layer, place, a, slope, stream, norm_gain, packs[layer]), grad
        )

    def run_attend_back(layer, grad_next, g1):
        x, normed, qkv, att, lse, *_ = kept[layer]
        return order.run(
            lambda a, b: attend_back(
                layer, place, a, b, x, qkv, lse, norm_gain, attn[layer]
            ),
            grad_next, g1,
        )

    def pack(kind, *arrays):
        return Pack(order, place, kind, arrays, width)

    def move(*ones):
        for one in ones:
            one.prepare()
        for one in ones:
            one.launch()

    normed, att, normed2, active = kept[1][1], kept[1][3], kept[1][6], kept[1][7]
    down_1 = pack("down", active, g2)
    move(down_1)
    grad_hidden, grad_next, g1, feed_sum_1 = run_feed_back(1, grad)
    order.close()

    up_1 = pack("up", normed2, grad_hidden)
    move(down_1, up_1)
    *rest, attn_sum_1 = run_attend_back(1, grad_next, g1)
    order.close()

    sides, outs = rest[:4], rest[4:]
    grad = [outs[0]] + [order.send(head_swap, outs[k], k) for k in (1, 2, 3)]
    grad = [p.reshape(4, BAND, width) for p in grad]
    move(down_1)
    attn_1 = pack("attn", normed, g1, att, sides)
    order.close()

    normed, att, normed2, active = kept[0][1], kept[0][3], kept[0][6], kept[0][7]
    move(up_1, attn_1, down_1)
    grad_hidden, grad_next, g1, g2, feed_sum_0 = run_feed_back(0, grad)
    down_0 = pack("down", active, g2)
    order.close()

    move(attn_1, up_1, down_1, down_0)
    up_0 = pack("up", normed2, grad_hidden)
    *rest, attn_sum_0 = run_attend_back(0, grad_next, g1)
    sides, (grad_input,) = rest[:4], rest[4:]
    order.close()

    move(down_0, up_0, attn_1, up_1, down_1)
    attn_0 = pack("attn", normed, g1, att, sides)
    packed = jnp.concatenate([feed_sum_0, feed_sum_1, attn_sum_0, attn_sum_1, loss_sum], axis=0)
    order.close()

    swaps = [(head_swap, 1), (head_swap, 2)]
    swaps += [(clip_swap, 1 << n) for n in range(clip_count.bit_length() - 1)]
    moving = [attn_0, up_0, down_0, attn_1, up_1, down_1]
    while not attn_0.done() or swaps:
        move(*[one for one in moving if not one.done()])
        if swaps:
            swap, distance = swaps.pop(0)
            packed = packed + order.send(swap, packed, distance)
        order.close()

    attn_out = emit(place, 0, True, attn_0.whole(), emit(place, 1, True, attn_1.whole(), None))
    up_out = emit(place, 0, False, up_0.whole(), emit(place, 1, False, up_1.whole(), None))
    down_out = emit(place, 0, False, down_0.whole(), emit(place, 1, False, down_1.whole(), None))

    feed_sums = packed[:16].reshape(2, 8, width)
    attn_sums = packed[16:32].reshape(2, 8, width)
    loss_total = packed[32, 0]
    own_feed = lax.dynamic_index_in_dim(feed_sums, head_index, 1, keepdims=False)
    own_attn = lax.dynamic_index_in_dim(attn_sums, head_index, 1, keepdims=False)
    slot_total = clip_count * frame_counts.shape[0] * FRAMES * SIDE * SIDE

    return (
        loss_total / slot_total,
        grad_input,
        jnp.stack([attn_sums[:, 4], feed_sums[:, 4]], axis=1),
        jnp.stack([attn_sums[:, 5], feed_sums[:, 5]], axis=1),
        attn_out[0],
        own_attn[:, : 2 * share].reshape(2, 2, share),
        attn_out[1],
        jnp.stack([feed_sums[:, 7], feed_sums[:, 6]], axis=1),
        up_out[0],
        own_feed,
        down_out[0],
    )


def solution(mesh):
    placed = (
        P(("clip", "head"), None),
        P("clip"),
        P(("clip", "head")),
        P(("clip", "head")),
        P(),
        P(),
        P(None, None, None, "head"),
        P(None, None, "head"),
        P(None, "head", None),
        P(),
        P(None, None, "head"),
        P(None, "head"),
        P(None, "head", None),
        P(),
    )
    return jax.shard_map(
        on_device,
        mesh=mesh,
        in_specs=placed,
        out_specs=(
            P(),
            P(("clip", "head"), None),
            P(),
            P(),
            P(None, None, None, "head"),
            P(None, None, "head"),
            P(None, "head", None),
            P(),
            P(None, None, "head"),
            P(None, "head"),
            P(None, "head", None),
        ),
        check_vma=False,
    )
```

time: 1980 us -> 667 us (0.34)
  waiting for transfers between devices: 1290 us -> 245 us
  Pallas kernels: 0 us -> 283 us
  matrix products: 271 us -> 0 us
  local copies, waits for them, and re-layouts: 183 us -> 32.2 us
  other arithmetic: 122 us -> 17.6 us
  blocking collectives: 80.2 us -> 0 us
  starting transfers between devices: 1.5 us -> 61.1 us
    reduce_scatter x8 -> x0, waiting for transfers between devices: 571 us -> none  [the longest x4 396 us: collect_rows(): lax.psum_scatter(jnp.dot(values, weight, preferred_element_type=jnp.float...]
    all_gather x8 -> x2, waiting for transfers between devices: 366 us -> 0.02 us  [gather_feed(): return lax.all_gather(chunk_across, 'clip', axis=0, tiled=True)]
    psum x1 -> x0, waiting for transfers between devices: 358 us -> none  [on_device(): summed = lax.psum(block_terms[0] + block_terms[1], 'clip')]
    pallas_call x0 -> x21, Pallas kernels: none -> 283 us  [call(): pl.pallas_call(kernel, grid_spec=pltpu.PrefetchScalarGridSpec(num_scalar_...]
    dot_general x36 -> x0, matrix products: 259 us -> none  [the longest x4 35.8 us: collect_rows(): jnp.dot(values, weight, preferred_element_type=jnp.float32)]
    ppermute x0 -> x71, waiting for transfers between devices: none -> 245 us  [the longest x44 123 us: head_swap(): lax.ppermute(values, 'head', [(i, i ^ distance) for i in range(count)])]
    psum x2 -> x0, blocking collectives: 80.2 us -> none  [the longest x1 41.7 us: on_device(): lax.psum((gains, shifts, vecs, loss_local), ('clip', 'head'))]
    reduce_sum x25 -> x0, other arithmetic: 72 us -> none  [the longest x6 20.6 us: layer_norm(): return centred * lax.rsqrt(spread + epsilon) * gain + shift]
  transfers between devices with their start and end apart: 17 -> 73, of which waited for: 16 -> 21; matrix products, arithmetic and copies ran while one was open for 4% -> 2% of each run, Pallas kernels for 0% -> 37%
where the time goes in v2:
time: 667 us; the launch traced here: 656 us
  Pallas kernels  283 us (42%)
  waiting for transfers between devices  245 us (37%)
  starting transfers between devices  61.1 us (9%)
  local copies, waits for them, and re-layouts  32.2 us (5%)
  between operations  18.2 us (3%)
  other arithmetic  17.6 us (3%)
    pallas_call x21, Pallas kernels, call(): pl.pallas_call(kernel, grid_spec=pltpu.PrefetchScalarGridSpec(num_scalar_...  283 us
    ppermute x44, waiting for transfers between devices, head_swap(): lax.ppermute(values, 'head', [(i, i ^ distance) for i in range(count)])  123 us
    ppermute x27, waiting for transfers between devices, clip_swap(): lax.ppermute(values, 'clip', [(i, i ^ distance) for i in range(count)])  121 us
    ppermute x27, starting transfers between devices, clip_swap(): lax.ppermute(values, 'clip', [(i, i ^ distance) for i in range(count)])  36.3 us
    ppermute x44, starting transfers between devices, head_swap(): lax.ppermute(values, 'head', [(i, i ^ distance) for i in range(count)])  24.7 us
    unnamed x151, local copies, waits for them, and re-layouts  24 us
  transfers between devices with their start and end apart: 73, of which 21 were waited for; matrix products, arithmetic and copies ran while one was open for 2% of the time, Pallas kernels for 37%

profile of v2, /device:TPU:0, one launch (start us, length us, event | category | flops | bytes accessed | tf_op | source)
XLA Modules:
  0.0 656.3 jit_solution(9909832799037656145)
XLA Ops:
  7.2 2.6 fusion
  10.1 3.0 collective-permute-start.3
  13.1 7.0 %collective-permute-done.3 = bf16[192,768]{1,0:T(8,128)(2,1)S(1)} collective-permute-done((bf16[192,768]{1,0:T(8,128)(2,1)S(1)}, bf16[192,768]{1,0:T(8,128)(2,1)S(1)}, u32[]{:S(2)}, u32[]{:S(2)}) %collective-permute-start.3) | collective-permute-done | bytes 294944 | tf_op jit(solution)/shard_map/ppermute | solution.py:724
  23.6 2.5 fusion.2
  26.5 26.4 %collective-permute-done.5.refs_10_.refs_4_.refs_8_ = bf16[768,768]{1,0:T(8,128)(2,1)} collective-permute-done((bf16[768,768]{1,0:T(8,128)(2,1)S(1)}, bf16[768,768]{1,0:T(8,128)(2,1)}, u32[]{:S(2)}, u32[]{:S(2)}) %collective-permute-start.5) | collective-permute-done | bytes 1179680 | tf_op jit(solution)/shard_map/ppermute | solution.py:724
  57.5 16.6 %attend.2 = (bf16[1024,768]{1,0:T(8,128)(2,1)}, bf16[1024,768]{1,0:T(8,128)(2,1)}, bf16[1024,2304]{1,0:T(8,128)(2,1)}, bf16[1024,768]{1,0:T(8,128)(2,1)}, f32[64...) custom-call(s32[3]{0:T(128)} %pad_add_fusion.place_ref, ...), custom_call_target="tpu_custom_call" | custom-call | flops 1955000 | bytes 6120 | tf_op jit(solution)/shard_map/attend/pallas_call | solution.py:230
  74.7 8.8 %collective-permute-done.13 = bf16[192,768]{1,0:T(8,128)(2,1)S(1)} collective-permute-done((bf16[192,768]{1,0:T(8,128)(2,1)S(1)}, bf16[192,768]{1,0:T(8,128)(2,1)S(1)}, u32[]{:S(2)}, u32[]{:S(2)}) %collective-permute-start.13) | collective-permute-done | bytes 294944 | tf_op jit(solution)/shard_map/ppermute | solution.py:724
  87.1 27.5 %collective-permute-done.15.refs_12_.refs_4_.refs_8_ = bf16[768,768]{1,0:T(8,128)(2,1)S(1)} collective-permute-done((bf16[768,768]{1,0:T(8,128)(2,1)S(1)}, bf16[768,768]{1,0:T(8,128)(2,1)S(1)}, u32[]{:S(2)}, u32[]{:S(2)}) %collective-permute-start.15) | collective-permute-done | bytes 1179680 | tf_op jit(solution)/shard_map/ppermute | solution.py:724
  116.1 23.3 %feed.2 = (f32[1024,768]{1,0:T(8,128)}, bf16[1024,768]{1,0:T(8,128)(2,1)}, bf16[1024,3072]{1,0:T(8,128)(2,1)}, bf16[1024,3072]{1,0:T(8,128)(2,1)}, bf16[4,64,768...) custom-call(s32[3]{0:T(128)} %pad_add_fusion.place_ref, ...), custom_call_target="tpu_custom_call" | custom-call | flops 2645000 | bytes 8280 | tf_op jit(solution)/shard_map/feed/pallas_call | solution.py:230
  141.6 9.0 %collective-permute-done.12 = bf16[4,64,768]{2,1,0:T(8,128)(2,1)S(1)} collective-permute-done((bf16[4,64,768]{2,1,0:T(8,128)(2,1)}, bf16[4,64,768]{2,1,0:T(8,128)(2,1)S(1)}, u32[]{:S(2)}, u32[]{:S(2)}) %collective-permute-start.12) | collective-permute-done | bytes 393248 | tf_op jit(solution)/shard_map/ppermute | solution.py:724
  150.6 9.0 %collective-permute-done.11 = bf16[4,64,768]{2,1,0:T(8,128)(2,1)S(1)} collective-permute-done((bf16[4,64,768]{2,1,0:T(8,128)(2,1)}, bf16[4,64,768]{2,1,0:T(8,128)(2,1)S(1)}, u32[]{:S(2)}, u32[]{:S(2)}) %collective-permute-start.11) | collective-permute-done | bytes 393248 | tf_op jit(solution)/shard_map/ppermute | solution.py:724
  160.9 16.0 %attend.3 = (bf16[1024,768]{1,0:T(8,128)(2,1)}, bf16[1024,768]{1,0:T(8,128)(2,1)}, bf16[1024,2304]{1,0:T(8,128)(2,1)}, bf16[1024,768]{1,0:T(8,128)(2,1)}, f32[64,256]{1,0:T(8,128)}) custom-call(s32[3]{0:T(128)} %pad_add_fusion.place_ref, bf16[4,4,16,768]{3,2,1,0:T(8,128)(2,1)} %bitcast.46, bf16[4,4,16,768]{3,2,1,0:T(8,128)(2,1)} %bitcast.49, ...), custom_call_target="tpu_custom_call" | custom-call | flops 1955000 | bytes 6120 | tf_op jit(solution)/shard_map/attend/pallas_call | solution.py:230
  178.9 2.8 collective-permute-done.17.refs_16_.refs_20_.refs_7_.refs_11_
  183.2 23.5 %feed.3 = (f32[1024,768]{1,0:T(8,128)}, bf16[1024,768]{1,0:T(8,128)(2,1)}, bf16[1024,3072]{1,0:T(8,128)(2,1)}, bf16[1024,3072]{1,0:T(8,128)(2,1)}, bf16[1024,768]{1,0:T(8,128)(2,1)}) custom-call(s32[3]{0:T(128)} %pad_add_fusion.place_ref, bf16[1024,768]{1,0:T(8,128)(2,1)} %get-tuple-element.287.refs_0_.refs_2_, ...), custom_call_target="tpu_custom_call" | custom-call | flops 2645000 | bytes 8280 | tf_op jit(solution)/shard_map/feed/pallas_call | solution.py:230
  207.3 10.8 %code_loss.1 = (f32[1024,768]{1,0:T(8,128)}, bf16[1024,768]{1,0:T(8,128)(2,1)}, f32[8,768]{1,0:T(8,128)}) custom-call(s32[3]{0:T(128)} %pad_add_fusion.place_ref, bf16[1024,768]{1,0:T(8,128)(2,1)} %get-tuple-element.292.final_ref, bf16[768,1024]{1,0:T(8,128)(2,1)} %head_ref.1, f32[4,64]{1,0:T(4,128)} %get-tuple-element.293.m0, f32[4,64]{1,0:T(4,128)} %copy-done.61, ...), custom_call_target="tpu_custom_call" | custom-call | flops 1150000 | bytes 3600 | tf_op jit(solution)/shard_map/code_loss/pallas_call | solution.py:230
  218.1 11.0 %grads_down.2 = (bf16[768,768]{1,0:T(8,128)(2,1)}, bf16[768,768]{1,0:T(8,128)(2,1)}, bf16[768,768]{1,0:T(8,128)(2,1)}, bf16[768,768]{1,0:T(8,128)(2,1)}) custom-call(s32[3]{0:T(128)} %pad_add_fusion.place_ref, bf16[1024,3072]{1,0:T(8,128)(2,1)} %get-tuple-element.300.refs_0_, bf16[1024,768]{1,0:T(8,128)(2,1)} %get-tuple-element.301.refs_1_), custom_call_target="tpu_custom_call" | custom-call | flops 920000 | bytes 2880 | tf_op jit(solution)/shard_map/grads_down/pallas_call | solution.py:230
  229.7 29.9 %feed_back.2 = (bf16[1024,3072]{1,0:T(8,128)(2,1)}, f32[1024,768]{1,0:T(8,128)}, bf16[1024,768]{1,0:T(8,128)(2,1)}, f32[8,768]{1,0:T(8,128)}) custom-call(s32[3]{0:T(128)} %pad_add_fusion.place_ref, f32[1024,768]{1,0:T(8,128)} %get-tuple-element.303.refs_0_, bf16[1024,3072]{1,0:T(8,128)(2,1)} %get-tuple-element.304.refs_1_, ...), custom_call_target="tpu_custom_call" | custom-call | flops 2415000 | bytes 7560 | tf_op jit(solution)/shard_map/feed_back/pallas_call | solution.py:230
  260.6 11.3 %grads_up.2 = (bf16[768,768]{1,0:T(8,128)(2,1)}, bf16[768,768]{1,0:T(8,128)(2,1)}, bf16[768,768]{1,0:T(8,128)(2,1)}, bf16[768,768]{1,0:T(8,128)(2,1)}) custom-call(s32[3]{0:T(128)} %pad_add_fusion.place_ref, bf16[1024,768]{1,0:T(8,128)(2,1)} %get-tuple-element.313.refs_0_, bf16[1024,3072]{1,0:T(8,128)(2,1)} %get-tuple-element.314.refs_1_), custom_call_target="tpu_custom_call" | custom-call | flops 920000 | bytes 2880 | tf_op jit(solution)/shard_map/grads_up/pallas_call | solution.py:230
  273.4 24.9 %attend_back.2 = (bf16[1024,576]{1,0:T(8,128)(2,1)}, bf16[1024,576]{1,0:T(8,128)(2,1)}, bf16[1024,576]{1,0:T(8,128)(2,1)}, bf16[1024,576]{1,0:T(8,128)(2,1)}, bf...) custom-call(s32[3]{0:T(128)} %pad_add_fusion.place_ref, ...), custom_call_target="tpu_custom_call" | custom-call | flops 2875000 | bytes 9000 | tf_op jit(solution)/shard_map/attend_back/pallas_call | solution.py:230
  305.7 12.7 %grads_attn.2 = (bf16[768,768]{1,0:T(8,128)(2,1)}, bf16[768,768]{1,0:T(8,128)(2,1)}, bf16[768,768]{1,0:T(8,128)(2,1)}, bf16[768,768]{1,0:T(8,128)(2,1)}) custom-call(s32[3]{0:T(128)} %pad_add_fusion.place_ref, bf16[1024,768]{1,0:T(8,128)(2,1)} %get-tuple-element.344.refs_0_, bf16[1024,768]{1,0:T(8,128)(2,1)} %get-tuple-element.345.refs_1_, ...), custom_call_target="tpu_custom_call" | custom-call | flops 920000 | bytes 2880 | tf_op jit(solution)/shard_map/grads_attn/pallas_call | solution.py:230
  318.4 4.9 collective-permute-done.28
  327.2 20.4 %feed_back.3 = (bf16[1024,3072]{1,0:T(8,128)(2,1)}, f32[1024,768]{1,0:T(8,128)}, bf16[1024,768]{1,0:T(8,128)(2,1)}, bf16[1024,768]{1,0:T(8,128)(2,1)}, f32[8,768]{1,0:T(8,128)}) custom-call(s32[3]{0:T(128)} %pad_add_fusion.place_ref, bf16[4,64,768]{2,1,0:T(8,128)(2,1)} %bitcast.42, bf16[4,64,768]{2,1,0:T(8,128)(2,1)} %bitcast.43, ...), custom_call_target="tpu_custom_call" | custom-call | flops 2415000 | bytes 7560 | tf_op jit(solution)/shard_map/feed_back/pallas_call | solution.py:230
  347.6 11.2 %grads_down.3 = (bf16[768,768]{1,0:T(8,128)(2,1)}, bf16[768,768]{1,0:T(8,128)(2,1)}, bf16[768,768]{1,0:T(8,128)(2,1)}, bf16[768,768]{1,0:T(8,128)(2,1)}) custom-call(s32[3]{0:T(128)} %pad_add_fusion.place_ref, bf16[1024,3072]{1,0:T(8,128)(2,1)} %get-tuple-element.375.refs_0_, bf16[1024,768]{1,0:T(8,128)(2,1)} %get-tuple-element.376.refs_1_), custom_call_target="tpu_custom_call" | custom-call | flops 920000 | bytes 2880 | tf_op jit(solution)/shard_map/grads_down/pallas_call | solution.py:230
  365.3 2.6 collective-permute-start.37
  367.9 11.2 %grads_up.3 = (bf16[768,768]{1,0:T(8,128)(2,1)}, bf16[768,768]{1,0:T(8,128)(2,1)}, bf16[768,768]{1,0:T(8,128)(2,1)}, bf16[768,768]{1,0:T(8,128)(2,1)}) custom-call(s32[3]{0:T(128)} %pad_add_fusion.place_ref, bf16[1024,768]{1,0:T(8,128)(2,1)} %get-tuple-element.386.refs_0_, bf16[1024,3072]{1,0:T(8,128)(2,1)} %get-tuple-element.387.refs_1_), custom_call_target="tpu_custom_call" | custom-call | flops 920000 | bytes 2880 | tf_op jit(solution)/shard_map/grads_up/pallas_call | solution.py:230
  379.1 25.8 %attend_back.3 = (bf16[1024,576]{1,0:T(8,128)(2,1)}, bf16[1024,576]{1,0:T(8,128)(2,1)}, bf16[1024,576]{1,0:T(8,128)(2,1)}, bf16[1024,576]{1,0:T(8,128)(2,1)}, f32[1024,768]{1,0:T(8,128)}, /*index=5*/f32[8,768]{1,0:T(8,128)}) custom-call(s32[3]{0:T(128)} %pad_add_fusion.place_ref, f32[1024,768]{1,0:T(8,128)} %get-tuple-element.389.refs_0_, ...), custom_call_target="tpu_custom_call" | custom-call | flops 2875000 | bytes 9000 | tf_op jit(solution)/shard_map/attend_back/pallas_call | solution.py:230
  412.9 11.9 %collective-permute-done.39 = bf16[384,768]{1,0:T(8,128)(2,1)S(1)} collective-permute-done((bf16[384,768]{1,0:T(8,128)(2,1)S(1)}, bf16[384,768]{1,0:T(8,128)(2,1)S(1)}, u32[]{:S(2)}, u32[]{:S(2)}) %collective-permute-start.39) | collective-permute-done | bytes 589856 | tf_op jit(solution)/shard_map/ppermute | solution.py:729
  426.1 12.6 %grads_attn.3 = (bf16[768,768]{1,0:T(8,128)(2,1)}, bf16[768,768]{1,0:T(8,128)(2,1)}, bf16[768,768]{1,0:T(8,128)(2,1)}, bf16[768,768]{1,0:T(8,128)(2,1)}) custom-call(s32[3]{0:T(128)} %pad_add_fusion.place_ref, bf16[1024,768]{1,0:T(8,128)(2,1)} %get-tuple-element.425.refs_0_, bf16[1024,768]{1,0:T(8,128)(2,1)} %get-tuple-element.426.refs_1_, ...), custom_call_target="tpu_custom_call" | custom-call | flops 920000 | bytes 2880 | tf_op jit(solution)/shard_map/grads_attn/pallas_call | solution.py:230
  446.4 4.0 collective-permute-done.45
  452.0 19.5 %collective-permute-done.46 = bf16[384,768]{1,0:T(8,128)(2,1)S(1)} collective-permute-done((bf16[384,768]{1,0:T(8,128)(2,1)S(1)}, bf16[384,768]{1,0:T(8,128)(2,1)S(1)}, u32[]{:S(2)}, u32[]{:S(2)}) %collective-permute-start.46) | collective-permute-done | bytes 589856 | tf_op jit(solution)/shard_map/ppermute | solution.py:729
  472.8 4.1 collective-permute-done.47
  476.9 8.3 %collective-permute-done.48 = bf16[384,768]{1,0:T(8,128)(2,1)S(1)} collective-permute-done((bf16[384,768]{1,0:T(8,128)(2,1)S(1)}, bf16[384,768]{1,0:T(8,128)(2,1)S(1)}, u32[]{:S(2)}, u32[]{:S(2)}) %collective-permute-start.48) | collective-permute-done | bytes 589856 | tf_op jit(solution)/shard_map/ppermute | solution.py:729
  487.6 2.3 collective-permute-start.56
  490.4 2.9 collective-permute-start.54
  494.6 22.1 %collective-permute-done.52 = f32[40,768]{1,0:T(8,128)S(1)} collective-permute-done((f32[40,768]{1,0:T(8,128)S(1)}, f32[40,768]{1,0:T(8,128)S(1)}, u32[]{:S(2)}, u32[]{:S(2)}) %collective-permute-start.52) | collective-permute-done | bytes 122912 | tf_op jit(solution)/shard_map/ppermute | solution.py:724
  518.0 11.2 %collective-permute-done.57.refs_1_ = bf16[384,768]{1,0:T(8,128)(2,1)S(1)} collective-permute-done((bf16[384,768]{1,0:T(8,128)(2,1)S(1)}, bf16[384,768]{1,0:T(8,128)(2,1)S(1)}, u32[]{:S(2)}, u32[]{:S(2)}) %collective-permute-start.57) | collective-permute-done | bytes 589856 | tf_op jit(solution)/shard_map/ppermute | solution.py:729
  530.7 5.0 collective-permute-start.60
  539.1 23.9 %collective-permute-done.58 = f32[40,768]{1,0:T(8,128)S(1)} collective-permute-done((f32[40,768]{1,0:T(8,128)S(1)}, f32[40,768]{1,0:T(8,128)S(1)}, u32[]{:S(2)}, u32[]{:S(2)}) %collective-permute-start.58) | collective-permute-done | bytes 122912 | tf_op jit(solution)/shard_map/ppermute | solution.py:729
  567.9 23.0 %collective-permute-done.63 = f32[40,768]{1,0:T(8,128)S(1)} collective-permute-done((f32[40,768]{1,0:T(8,128)S(1)}, f32[40,768]{1,0:T(8,128)S(1)}, u32[]{:S(2)}, u32[]{:S(2)}) %collective-permute-start.63) | collective-permute-done | bytes 122912 | tf_op jit(solution)/shard_map/ppermute | solution.py:729
  596.1 3.4 emit.10.refs_2_
  599.5 3.4 emit.8.refs_2_
  603.0 3.8 emit.6
  606.8 3.4 emit.11
  610.3 11.8 %collective-permute-done.67 = f32[40,768]{1,0:T(8,128)S(1)} collective-permute-done((f32[40,768]{1,0:T(8,128)S(1)}, f32[40,768]{1,0:T(8,128)S(1)}, u32[]{:S(2)}, u32[]{:S(2)}) %collective-permute-start.67) | collective-permute-done | bytes 122912 | tf_op jit(solution)/shard_map/ppermute | solution.py:729
  628.0 3.5 emit.9
  631.5 6.1 collective-permute-done.70.refs_1_
  638.5 3.8 emit.7
  642.3 5.6 copy.31
  (335 shorter events, 87.6 us)
Async XLA Ops:
  7.2 77.7 %all-gather.3.cloned.1.call-start = ((), (), s32[]{:S(2)}) async-start(), calls=%async_computation | async-start | bytes 2654208 | tf_op jit(solution)/shard_map/all_gather | solution.py:850
  20.9 156.0 %all-gather.5.cloned.1.call-start = ((), (), s32[]{:S(2)}) async-start(), calls=%async_computation.1 | async-start | bytes 2654208 | tf_op jit(solution)/shard_map/all_gather | solution.py:850
  26.2 26.7 %collective-permute-start.5 = (bf16[768,768]{1,0:T(8,128)(2,1)S(1)}, bf16[768,768]{1,0:T(8,128)(2,1)}, u32[]{:S(2)}, u32[]{:S(2)}) collective-permute-start(bf16[768,768]{1,0:T(8,128)(2,1)S(1)} %pad_maximum_fusion.refs_8_.refs_2_.refs_6_), channel_id=1, source_target_pairs={{0,2},{1,3},{2,0},{3,1},{4,6},{5,7},{6,4},{7,5},{8,10},{9,11},{10,... | collective-permute-start | bytes 3538952 | tf_op jit(solution)/shard_map/ppermute | solution.py:724
  26.5 30.9 %collective-permute-start.4 = (bf16[768,768]{1,0:T(8,128)(2,1)S(1)}, bf16[768,768]{1,0:T(8,128)(2,1)}, u32[]{:S(2)}, u32[]{:S(2)}) collective-permute-start(bf16[768,768]{1,0:T(8,128)(2,1)S(1)} %pad_maximum_fusion.refs_8_.refs_2_.refs_6_), channel_id=1, source_target_pairs={{0,1},{1,0},{2,3},{3,2},{4,5},{5,4},{6,7},{7,6},{8,9},{9,8},{10,11... | collective-permute-start | bytes 3538952 | tf_op jit(solution)/shard_map/ppermute | solution.py:724
  84.3 30.4 %collective-permute-start.7 = (bf16[2,768,768]{2,1,0:T(8,128)(2,1)S(1)}, bf16[2,768,768]{2,1,0:T(8,128)(2,1)}, u32[]{:S(2)}, u32[]{:S(2)}) collective-permute-start(bf16[2,768,768]{2,1,0:T(8,128)(2,1)S(1)} %copy-done), channel_id=1, source_target_pairs={{0,1},{1,0},{2,3},{3,2},{4,5},{5,4},{6,7},{7,6},{8,9},{9,8},{10,11... | collective-permute-start | bytes 7077896 | tf_op jit(solution)/shard_map/ppermute | solution.py:724
  84.3 30.3 %collective-permute-start.9 = (bf16[2,768,768]{2,1,0:T(8,128)(2,1)}, bf16[2,768,768]{2,1,0:T(8,128)(2,1)}, u32[]{:S(2)}, u32[]{:S(2)}) collective-permute-start(bf16[2,768,768]{2,1,0:T(8,128)(2,1)} %refs_11_.1), channel_id=1, source_target_pairs={{0,1},{1,0},{2,3},{3,2},{4,5},{5,4},{6,7},{7,6},{8,9},{9,8},{10,11... | collective-permute-start | bytes 7077896 | tf_op jit(solution)/shard_map/ppermute | solution.py:724
  84.8 29.8 %collective-permute-start.8 = (bf16[1536,768]{1,0:T(8,128)(2,1)}, bf16[1536,768]{1,0:T(8,128)(2,1)S(1)}, u32[]{:S(2)}, u32[]{:S(2)}) collective-permute-start(bf16[1536,768]{1,0:T(8,128)(2,1)} %all-gather.3.cloned.1.call-done.refs_15_.refs_19_.refs_9_.refs_13_), channel_id=1, source_target_pairs={{0,1},{1,0},{2,3},{3,2},{4,5},{5,4},{6,7},{7,6},{8,9},{9,8},{10,11... | collective-permute-start | bytes 7077896 | tf_op jit(solution)/shard_map/ppermute | solution.py:724
  86.3 28.4 %collective-permute-start.15 = (bf16[768,768]{1,0:T(8,128)(2,1)S(1)}, bf16[768,768]{1,0:T(8,128)(2,1)S(1)}, u32[]{:S(2)}, u32[]{:S(2)}) collective-permute-start(bf16[768,768]{1,0:T(8,128)(2,1)S(1)} %pad_maximum_fusion.1.refs_10_.refs_2_.refs_6_), channel_id=1, source_target_pairs={{0,2},{1,3},{2,0},{3,1},{4,6},{5,7},{6,4},{7,5},{8,10},{9,11},{10,... | collective-permute-start | bytes 3538952 | tf_op jit(solution)/shard_map/ppermute | solution.py:724
  86.9 72.6 %collective-permute-start.14 = (bf16[768,768]{1,0:T(8,128)(2,1)S(1)}, bf16[768,768]{1,0:T(8,128)(2,1)S(1)}, u32[]{:S(2)}, u32[]{:S(2)}) collective-permute-start(bf16[768,768]{1,0:T(8,128)(2,1)S(1)} %pad_maximum_fusion.1.refs_10_.refs_2_.refs_6_), channel_id=1, source_target_pairs={{0,1},{1,0},{2,3},{3,2},{4,5},{5,4},{6,7},{7,6},{8,9},{9,8},{10,11... | collective-permute-start | bytes 3538952 | tf_op jit(solution)/shard_map/ppermute | solution.py:724
  114.7 45.0 %collective-permute-start.16 = (bf16[768,768]{1,0:T(8,128)(2,1)S(1)}, bf16[768,768]{1,0:T(8,128)(2,1)}, u32[]{:S(2)}, u32[]{:S(2)}) collective-permute-start(bf16[768,768]{1,0:T(8,128)(2,1)S(1)} %collective-permute-done.15.refs_12_.refs_4_.refs_8_), channel_id=1, source_target_pairs={{0,1},{1,0},{2,3},{3,2},{4,5},{5,4},{6,7},{7,6},{8,9},{9,8},{10,11... | collective-permute-start | bytes 3538952 | tf_op jit(solution)/shard_map/ppermute | solution.py:724
  177.0 29.7 %collective-permute-start.18 = (f32[4,64]{1,0:T(4,128)S(1)}, f32[4,64]{1,0:T(4,128)S(1)}, u32[]{:S(2)}, u32[]{:S(2)}) collective-permute-start(f32[4,64]{1,0:T(4,128)S(1)} %copy-done.71), channel_id=1, source_target_pairs={{0,1},{1,0},{2,3},{3,2},{4,5},{5,4},{6,7},{7,6},{8,9},{9,8},{10,11... | collective-permute-start | bytes 3080 | tf_op jit(solution)/shard_map/ppermute | solution.py:724
  177.5 29.2 %collective-permute-start.19 = (f32[4,64]{1,0:T(4,128)S(1)}, f32[4,64]{1,0:T(4,128)S(1)}, u32[]{:S(2)}, u32[]{:S(2)}) collective-permute-start(f32[4,64]{1,0:T(4,128)S(1)} %copy-done.70), channel_id=1, source_target_pairs={{0,2},{1,3},{2,0},{3,1},{4,6},{5,7},{6,4},{7,5},{8,10},{9,11},{10,... | collective-permute-start | bytes 3080 | tf_op jit(solution)/shard_map/ppermute | solution.py:724
  178.1 28.6 %collective-permute-start.20 = (f32[4,64]{1,0:T(4,128)S(1)}, f32[4,64]{1,0:T(4,128)S(1)}, u32[]{:S(2)}, u32[]{:S(2)}) collective-permute-start(f32[4,64]{1,0:T(4,128)S(1)} %copy-done.69), channel_id=1, source_target_pairs={{0,3},{1,2},{2,1},{3,0},{4,7},{5,6},{6,5},{7,4},{8,11},{9,10},{10,... | collective-permute-start | bytes 3080 | tf_op jit(solution)/shard_map/ppermute | solution.py:724
  229.1 30.4 %collective-permute-start.22 = (bf16[768,768]{1,0:T(8,128)(2,1)}, bf16[768,768]{1,0:T(8,128)(2,1)S(1)}, u32[]{:S(2)}, u32[]{:S(2)}) collective-permute-start(bf16[768,768]{1,0:T(8,128)(2,1)} %get-tuple-element.312), channel_id=1, source_target_pairs={{0,1},{1,0},{2,3},{3,2},{4,5},{5,4},{6,7},{7,6},{8,9},{9,8},{10,11... | collective-permute-start | bytes 3538952 | tf_op jit(solution)/shard_map/ppermute | solution.py:724
  229.3 30.2 %collective-permute-start.21 = (bf16[768,768]{1,0:T(8,128)(2,1)}, bf16[768,768]{1,0:T(8,128)(2,1)S(1)}, u32[]{:S(2)}, u32[]{:S(2)}) collective-permute-start(bf16[768,768]{1,0:T(8,128)(2,1)} %get-tuple-element.309), channel_id=1, source_target_pairs={{0,1},{1,0},{2,3},{3,2},{4,5},{5,4},{6,7},{7,6},{8,9},{9,8},{10,11... | collective-permute-start | bytes 3538952 | tf_op jit(solution)/shard_map/ppermute | solution.py:724
  272.2 28.2 %collective-permute-start.23 = (bf16[768,768]{1,0:T(8,128)(2,1)S(1)}, bf16[768,768]{1,0:T(8,128)(2,1)}, u32[]{:S(2)}, u32[]{:S(2)}) collective-permute-start(bf16[768,768]{1,0:T(8,128)(2,1)S(1)} %add_convert_fusion.5), channel_id=1, source_target_pairs={{0,2},{1,3},{2,0},{3,1},{4,6},{5,7},{6,4},{7,5},{8,10},{9,11},{10,... | collective-permute-start | bytes 3538952 | tf_op jit(solution)/shard_map/ppermute | solution.py:724
  272.9 27.5 %collective-permute-start.24 = (bf16[768,768]{1,0:T(8,128)(2,1)}, bf16[768,768]{1,0:T(8,128)(2,1)S(1)}, u32[]{:S(2)}, u32[]{:S(2)}) collective-permute-start(bf16[768,768]{1,0:T(8,128)(2,1)} %get-tuple-element.326), channel_id=1, source_target_pairs={{0,1},{1,0},{2,3},{3,2},{4,5},{5,4},{6,7},{7,6},{8,9},{9,8},{10,11... | collective-permute-start | bytes 3538952 | tf_op jit(solution)/shard_map/ppermute | solution.py:724
  272.9 27.5 %collective-permute-start.25 = (bf16[768,768]{1,0:T(8,128)(2,1)}, bf16[768,768]{1,0:T(8,128)(2,1)S(1)}, u32[]{:S(2)}, u32[]{:S(2)}) collective-permute-start(bf16[768,768]{1,0:T(8,128)(2,1)} %get-tuple-element.328), channel_id=1, source_target_pairs={{0,1},{1,0},{2,3},{3,2},{4,5},{5,4},{6,7},{7,6},{8,9},{9,8},{10,11... | collective-permute-start | bytes 3538952 | tf_op jit(solution)/shard_map/ppermute | solution.py:724
  324.5 34.3 %collective-permute-start.31 = (bf16[768,768]{1,0:T(8,128)(2,1)S(1)}, bf16[768,768]{1,0:T(8,128)(2,1)S(1)}, u32[]{:S(2)}, u32[]{:S(2)}) collective-permute-start(bf16[768,768]{1,0:T(8,128)(2,1)S(1)} %add_convert_fusion.4), channel_id=1, source_target_pairs={{0,2},{1,3},{2,0},{3,1},{4,6},{5,7},{6,4},{7,5},{8,10},{9,11},{10,... | collective-permute-start | bytes 3538952 | tf_op jit(solution)/shard_map/ppermute | solution.py:724
  325.1 33.7 %collective-permute-start.32 = (bf16[768,768]{1,0:T(8,128)(2,1)}, bf16[768,768]{1,0:T(8,128)(2,1)S(1)}, u32[]{:S(2)}, u32[]{:S(2)}) collective-permute-start(bf16[768,768]{1,0:T(8,128)(2,1)} %get-tuple-element.372), channel_id=1, source_target_pairs={{0,1},{1,0},{2,3},{3,2},{4,5},{5,4},{6,7},{7,6},{8,9},{9,8},{10,11... | collective-permute-start | bytes 3538952 | tf_op jit(solution)/shard_map/ppermute | solution.py:724
  325.1 33.7 %collective-permute-start.33 = (bf16[768,768]{1,0:T(8,128)(2,1)}, bf16[768,768]{1,0:T(8,128)(2,1)S(1)}, u32[]{:S(2)}, u32[]{:S(2)}) collective-permute-start(bf16[768,768]{1,0:T(8,128)(2,1)} %get-tuple-element.378), channel_id=1, source_target_pairs={{0,1},{1,0},{2,3},{3,2},{4,5},{5,4},{6,7},{7,6},{8,9},{9,8},{10,11... | collective-permute-start | bytes 3538952 | tf_op jit(solution)/shard_map/ppermute | solution.py:724
  325.6 33.2 %collective-permute-start.30 = (bf16[384,768]{1,0:T(8,128)(2,1)S(1)}, bf16[384,768]{1,0:T(8,128)(2,1)S(1)}, u32[]{:S(2)}, u32[]{:S(2)}) collective-permute-start(bf16[384,768]{1,0:T(8,128)(2,1)S(1)} %add_convert_fusion.23), channel_id=1, source_target_pairs={{0,8},{4,12},{8,0},{12,4},{16,24},{20,28},{24,16},{28,20},{1,9},{5... | collective-permute-start | bytes 1769480 | tf_op jit(solution)/shard_map/ppermute | solution.py:729
  362.5 42.4 %collective-permute-start.35 = (bf16[768,768]{1,0:T(8,128)(2,1)S(1)}, bf16[768,768]{1,0:T(8,128)(2,1)S(1)}, u32[]{:S(2)}, u32[]{:S(2)}) collective-permute-start(bf16[768,768]{1,0:T(8,128)(2,1)S(1)} %add_convert_fusion.3), channel_id=1, source_target_pairs={{0,2},{1,3},{2,0},{3,1},{4,6},{5,7},{6,4},{7,5},{8,10},{9,11},{10,... | collective-permute-start | bytes 3538952 | tf_op jit(solution)/shard_map/ppermute | solution.py:724
  364.1 40.9 %collective-permute-start.36 = (bf16[768,768]{1,0:T(8,128)(2,1)}, bf16[768,768]{1,0:T(8,128)(2,1)S(1)}, u32[]{:S(2)}, u32[]{:S(2)}) collective-permute-start(bf16[768,768]{1,0:T(8,128)(2,1)} %get-tuple-element.401), channel_id=1, source_target_pairs={{0,1},{1,0},{2,3},{3,2},{4,5},{5,4},{6,7},{7,6},{8,9},{9,8},{10,11... | collective-permute-start | bytes 3538952 | tf_op jit(solution)/shard_map/ppermute | solution.py:724
  364.1 40.9 %collective-permute-start.38 = (bf16[768,768]{1,0:T(8,128)(2,1)}, bf16[768,768]{1,0:T(8,128)(2,1)S(1)}, u32[]{:S(2)}, u32[]{:S(2)}) collective-permute-start(bf16[768,768]{1,0:T(8,128)(2,1)} %get-tuple-element.404), channel_id=1, source_target_pairs={{0,1},{1,0},{2,3},{3,2},{4,5},{5,4},{6,7},{7,6},{8,9},{9,8},{10,11... | collective-permute-start | bytes 3538952 | tf_op jit(solution)/shard_map/ppermute | solution.py:724
  364.6 40.4 %collective-permute-start.34 = (bf16[384,768]{1,0:T(8,128)(2,1)}, bf16[384,768]{1,0:T(8,128)(2,1)S(1)}, u32[]{:S(2)}, u32[]{:S(2)}) collective-permute-start(bf16[384,768]{1,0:T(8,128)(2,1)} %get-tuple-element.396), channel_id=1, source_target_pairs={{0,4},{4,0},{8,12},{12,8},{16,20},{20,16},{24,28},{28,24},{1,5},{5... | collective-permute-start | bytes 1769480 | tf_op jit(solution)/shard_map/ppermute | solution.py:729
  365.3 39.6 %collective-permute-start.37 = (bf16[384,768]{1,0:T(8,128)(2,1)S(1)}, bf16[384,768]{1,0:T(8,128)(2,1)S(1)}, u32[]{:S(2)}, u32[]{:S(2)}) collective-permute-start(bf16[384,768]{1,0:T(8,128)(2,1)S(1)} %add_convert_fusion.22), channel_id=1, source_target_pairs={{0,16},{4,20},{8,24},{12,28},{16,0},{20,4},{24,8},{28,12},{1,17},{... | collective-permute-start | bytes 1769480 | tf_op jit(solution)/shard_map/ppermute | solution.py:729
  410.6 29.1 %collective-permute-start.41 = (bf16[768,768]{1,0:T(8,128)(2,1)S(1)}, bf16[768,768]{1,0:T(8,128)(2,1)}, u32[]{:S(2)}, u32[]{:S(2)}) collective-permute-start(bf16[768,768]{1,0:T(8,128)(2,1)S(1)} %add_convert_fusion.2), channel_id=1, source_target_pairs={{0,2},{1,3},{2,0},{3,1},{4,6},{5,7},{6,4},{7,5},{8,10},{9,11},{10,... | collective-permute-start | bytes 3538952 | tf_op jit(solution)/shard_map/ppermute | solution.py:724
  411.1 28.6 %collective-permute-start.42 = (bf16[768,768]{1,0:T(8,128)(2,1)}, bf16[768,768]{1,0:T(8,128)(2,1)S(1)}, u32[]{:S(2)}, u32[]{:S(2)}) collective-permute-start(bf16[768,768]{1,0:T(8,128)(2,1)} %get-tuple-element.420), channel_id=1, source_target_pairs={{0,1},{1,0},{2,3},{3,2},{4,5},{5,4},{6,7},{7,6},{8,9},{9,8},{10,11... | collective-permute-start | bytes 3538952 | tf_op jit(solution)/shard_map/ppermute | solution.py:724
  411.1 28.6 %collective-permute-start.43 = (bf16[768,768]{1,0:T(8,128)(2,1)}, bf16[768,768]{1,0:T(8,128)(2,1)S(1)}, u32[]{:S(2)}, u32[]{:S(2)}) collective-permute-start(bf16[768,768]{1,0:T(8,128)(2,1)} %get-tuple-element.433), channel_id=1, source_target_pairs={{0,1},{1,0},{2,3},{3,2},{4,5},{5,4},{6,7},{7,6},{8,9},{9,8},{10,11... | collective-permute-start | bytes 3538952 | tf_op jit(solution)/shard_map/ppermute | solution.py:724
  411.6 27.1 %collective-permute-start.40 = (bf16[384,768]{1,0:T(8,128)(2,1)}, bf16[384,768]{1,0:T(8,128)(2,1)S(1)}, u32[]{:S(2)}, u32[]{:S(2)}) collective-permute-start(bf16[384,768]{1,0:T(8,128)(2,1)} %get-tuple-element.415), channel_id=1, source_target_pairs={{0,4},{4,0},{8,12},{12,8},{16,20},{20,16},{24,28},{28,24},{1,5},{5... | collective-permute-start | bytes 1769480 | tf_op jit(solution)/shard_map/ppermute | solution.py:729
  443.8 27.7 %collective-permute-start.46 = (bf16[384,768]{1,0:T(8,128)(2,1)S(1)}, bf16[384,768]{1,0:T(8,128)(2,1)S(1)}, u32[]{:S(2)}, u32[]{:S(2)}) collective-permute-start(bf16[384,768]{1,0:T(8,128)(2,1)S(1)} %add_convert_fusion.18), channel_id=1, source_target_pairs={{0,16},{4,20},{8,24},{12,28},{16,0},{20,4},{24,8},{28,12},{1,17},{... | collective-permute-start | bytes 1769480 | tf_op jit(solution)/shard_map/ppermute | solution.py:729
  444.2 41.1 %collective-permute-start.49 = (bf16[768,768]{1,0:T(8,128)(2,1)S(1)}, bf16[768,768]{1,0:T(8,128)(2,1)S(1)}, u32[]{:S(2)}, u32[]{:S(2)}) collective-permute-start(bf16[768,768]{1,0:T(8,128)(2,1)S(1)} %add_convert_fusion.1), channel_id=1, source_target_pairs={{0,2},{1,3},{2,0},{3,1},{4,6},{5,7},{6,4},{7,5},{8,10},{9,11},{10,... | collective-permute-start | bytes 3538952 | tf_op jit(solution)/shard_map/ppermute | solution.py:724
  445.7 39.6 %collective-permute-start.50 = (bf16[768,768]{1,0:T(8,128)(2,1)S(1)}, bf16[768,768]{1,0:T(8,128)(2,1)S(1)}, u32[]{:S(2)}, u32[]{:S(2)}) collective-permute-start(bf16[768,768]{1,0:T(8,128)(2,1)S(1)} %copy-done.65), channel_id=1, source_target_pairs={{0,1},{1,0},{2,3},{3,2},{4,5},{5,4},{6,7},{7,6},{8,9},{9,8},{10,11... | collective-permute-start | bytes 3538952 | tf_op jit(solution)/shard_map/ppermute | solution.py:724
  445.7 39.6 %collective-permute-start.51 = (bf16[768,768]{1,0:T(8,128)(2,1)S(1)}, bf16[768,768]{1,0:T(8,128)(2,1)S(1)}, u32[]{:S(2)}, u32[]{:S(2)}) collective-permute-start(bf16[768,768]{1,0:T(8,128)(2,1)S(1)} %copy-done.64), channel_id=1, source_target_pairs={{0,1},{1,0},{2,3},{3,2},{4,5},{5,4},{6,7},{7,6},{8,9},{9,8},{10,11... | collective-permute-start | bytes 3538952 | tf_op jit(solution)/shard_map/ppermute | solution.py:724
  450.4 26.5 %collective-permute-start.47 = (bf16[384,768]{1,0:T(8,128)(2,1)S(1)}, bf16[384,768]{1,0:T(8,128)(2,1)S(1)}, u32[]{:S(2)}, u32[]{:S(2)}) collective-permute-start(bf16[384,768]{1,0:T(8,128)(2,1)S(1)} %add_convert_fusion.19), channel_id=1, source_target_pairs={{0,8},{4,12},{8,0},{12,4},{16,24},{20,28},{24,16},{28,20},{1,9},{5... | collective-permute-start | bytes 1769480 | tf_op jit(solution)/shard_map/ppermute | solution.py:729
  487.6 41.6 %collective-permute-start.56 = (bf16[768,768]{1,0:T(8,128)(2,1)S(1)}, bf16[768,768]{1,0:T(8,128)(2,1)S(1)}, u32[]{:S(2)}, u32[]{:S(2)}) collective-permute-start(bf16[768,768]{1,0:T(8,128)(2,1)S(1)} %add_convert_fusion), channel_id=1, source_target_pairs={{0,2},{1,3},{2,0},{3,1},{4,6},{5,7},{6,4},{7,5},{8,10},{9,11},{10,... | collective-permute-start | bytes 3538952 | tf_op jit(solution)/shard_map/ppermute | solution.py:724
  489.9 26.7 %collective-permute-start.52 = (f32[40,768]{1,0:T(8,128)S(1)}, f32[40,768]{1,0:T(8,128)S(1)}, u32[]{:S(2)}, u32[]{:S(2)}) collective-permute-start(f32[40,768]{1,0:T(8,128)S(1)} %add.164), channel_id=1, source_target_pairs={{0,2},{1,3},{2,0},{3,1},{4,6},{5,7},{6,4},{7,5},{8,10},{9,11},{10,... | collective-permute-start | bytes 368648 | tf_op jit(solution)/shard_map/ppermute | solution.py:724
  490.3 27.7 %collective-permute-start.53 = (bf16[384,768]{1,0:T(8,128)(2,1)S(1)}, bf16[384,768]{1,0:T(8,128)(2,1)S(1)}, u32[]{:S(2)}, u32[]{:S(2)}) collective-permute-start(bf16[384,768]{1,0:T(8,128)(2,1)S(1)} %add_convert_fusion.16), channel_id=1, source_target_pairs={{0,16},{4,20},{8,24},{12,28},{16,0},{20,4},{24,8},{28,12},{1,17},{... | collective-permute-start | bytes 1769480 | tf_op jit(solution)/shard_map/ppermute | solution.py:729
  490.4 27.6 %collective-permute-start.54 = (bf16[384,768]{1,0:T(8,128)(2,1)S(1)}, bf16[384,768]{1,0:T(8,128)(2,1)S(1)}, u32[]{:S(2)}, u32[]{:S(2)}) collective-permute-start(bf16[384,768]{1,0:T(8,128)(2,1)S(1)} %add_convert_fusion.17), channel_id=1, source_target_pairs={{0,8},{4,12},{8,0},{12,4},{16,24},{20,28},{24,16},{28,20},{1,9},{5... | collective-permute-start | bytes 1769480 | tf_op jit(solution)/shard_map/ppermute | solution.py:729
  530.6 32.5 %collective-permute-start.59 = (bf16[384,768]{1,0:T(8,128)(2,1)S(1)}, bf16[384,768]{1,0:T(8,128)(2,1)S(1)}, u32[]{:S(2)}, u32[]{:S(2)}) collective-permute-start(bf16[384,768]{1,0:T(8,128)(2,1)S(1)} %add_convert_fusion.13), channel_id=1, source_target_pairs={{0,16},{4,20},{8,24},{12,28},{16,0},{20,4},{24,8},{28,12},{1,17},{... | collective-permute-start | bytes 1769480 | tf_op jit(solution)/shard_map/ppermute | solution.py:729
  530.7 32.4 %collective-permute-start.60 = (bf16[384,768]{1,0:T(8,128)(2,1)S(1)}, bf16[384,768]{1,0:T(8,128)(2,1)S(1)}, u32[]{:S(2)}, u32[]{:S(2)}) collective-permute-start(bf16[384,768]{1,0:T(8,128)(2,1)S(1)} %add_convert_fusion.14), channel_id=1, source_target_pairs={{0,8},{4,12},{8,0},{12,4},{16,24},{20,28},{24,16},{28,20},{1,9},{5... | collective-permute-start | bytes 1769480 | tf_op jit(solution)/shard_map/ppermute | solution.py:729
  535.7 27.4 %collective-permute-start.61 = (bf16[384,768]{1,0:T(8,128)(2,1)S(1)}, bf16[384,768]{1,0:T(8,128)(2,1)S(1)}, u32[]{:S(2)}, u32[]{:S(2)}) collective-permute-start(bf16[384,768]{1,0:T(8,128)(2,1)S(1)} %get-tuple-element.484), channel_id=1, source_target_pairs={{0,4},{4,0},{8,12},{12,8},{16,20},{20,16},{24,28},{28,24},{1,5},{5... | collective-permute-start | bytes 1769480 | tf_op jit(solution)/shard_map/ppermute | solution.py:729
  564.1 26.9 %collective-permute-start.64 = (bf16[384,768]{1,0:T(8,128)(2,1)S(1)}, bf16[384,768]{1,0:T(8,128)(2,1)S(1)}, u32[]{:S(2)}, u32[]{:S(2)}) collective-permute-start(bf16[384,768]{1,0:T(8,128)(2,1)S(1)} %add_convert_fusion.10), channel_id=1, source_target_pairs={{0,16},{4,20},{8,24},{12,28},{16,0},{20,4},{24,8},{28,12},{1,17},{... | collective-permute-start | bytes 1769480 | tf_op jit(solution)/shard_map/ppermute | solution.py:729
  564.5 26.4 %collective-permute-start.65 = (bf16[384,768]{1,0:T(8,128)(2,1)S(1)}, bf16[384,768]{1,0:T(8,128)(2,1)S(1)}, u32[]{:S(2)}, u32[]{:S(2)}) collective-permute-start(bf16[384,768]{1,0:T(8,128)(2,1)S(1)} %add_convert_fusion.11), channel_id=1, source_target_pairs={{0,8},{4,12},{8,0},{12,4},{16,24},{20,28},{24,16},{28,20},{1,9},{5... | collective-permute-start | bytes 1769480 | tf_op jit(solution)/shard_map/ppermute | solution.py:729
  591.8 30.3 %collective-permute-start.68 = (bf16[384,768]{1,0:T(8,128)(2,1)S(1)}, bf16[384,768]{1,0:T(8,128)(2,1)S(1)}, u32[]{:S(2)}, u32[]{:S(2)}) collective-permute-start(bf16[384,768]{1,0:T(8,128)(2,1)S(1)} %add_convert_fusion.8), channel_id=1, source_target_pairs={{0,16},{4,20},{8,24},{12,28},{16,0},{20,4},{24,8},{28,12},{1,17},{... | collective-permute-start | bytes 1769480 | tf_op jit(solution)/shard_map/ppermute | solution.py:729
  594.0 28.2 %collective-permute-start.69 = (bf16[384,768]{1,0:T(8,128)(2,1)S(1)}, bf16[384,768]{1,0:T(8,128)(2,1)S(1)}, u32[]{:S(2)}, u32[]{:S(2)}) collective-permute-start(bf16[384,768]{1,0:T(8,128)(2,1)S(1)} %add_convert_fusion.7.refs_0_), channel_id=1, source_target_pairs={{0,4},{4,0},{8,12},{12,8},{16,20},{20,16},{24,28},{28,24},{1,5},{5... | collective-permute-start | bytes 1769480 | tf_op jit(solution)/shard_map/ppermute | solution.py:729
  595.3 26.8 %collective-permute-start.67 = (f32[40,768]{1,0:T(8,128)S(1)}, f32[40,768]{1,0:T(8,128)S(1)}, u32[]{:S(2)}, u32[]{:S(2)}) collective-permute-start(f32[40,768]{1,0:T(8,128)S(1)} %add.181), channel_id=1, source_target_pairs={{0,16},{4,20},{8,24},{12,28},{16,0},{20,4},{24,8},{28,12},{1,17},{... | collective-permute-start | bytes 368648 | tf_op jit(solution)/shard_map/ppermute | solution.py:729
  (97 other events, 1135.6 us)
Sparse Core Ops, SparseCore 0:
  21.0 53.5 all-gather.2
  84.4 52.3 all-gather.4

commit v3 on v2

--- a/solution.py
+++ b/solution.py
@@ -72,6 +72,23 @@
         acc_ref[...] += parts
 
 
+ORDER = (1, 3, 0, 2)
+
+
+def step_rows():
+    return pl.ds(pl.multiple_of(pl.program_id(0) * WINDOW, WINDOW), WINDOW)
+
+
+def put_parts(leaving_ref, staying_ref, gradient_of):
+    for n, k in enumerate(ORDER):
+        (leaving_ref if n < 2 else staying_ref)[n % 2] = gradient_of(k).astype(bf16)
+
+
+def parts_outs(width):
+    spec = pl.BlockSpec((2, width, width), lambda i, s: (0, 0, 0))
+    return [((2, width, width), bf16, spec)] * 2
+
+
 def last_step():
     return pl.program_id(0) == pl.num_programs(0) - 1
 
@@ -137,7 +154,7 @@
     return jnp.concatenate([jnp.where(low, pair, zero), jnp.where(low, zero, pair)], axis=0)
 
 
-def attend_core(qkv, allowed, att_ref, lse_ref):
+def attend_core(qkv, allowed, att_ref, lse_ref, part_ref):
     width = att_ref.shape[1]
     pairs = width // PAIR
 
@@ -166,6 +183,9 @@
             lse_ref[head : head + 1, :] = top + jnp.log(total)
         out = dot_tn(jnp.concatenate(probs, axis=0), stack_heads(part(2, pair)))
         att_ref[:, pair * PAIR : (pair + 1) * PAIR] = out.astype(bf16)
+    share = width // 4
+    for k in range(4):
+        part_ref[k] = att_ref[:, k * share : (k + 1) * share]
 
 
 def attend_kernel(layer, place_ref, *refs):
@@ -178,7 +198,7 @@
         stream = jnp.concatenate(
             [p[...].reshape(BAND, p.shape[-1]) for p in pieces], axis=0
         ).astype(f32)
-    gain_ref, shift_ref, s0, s1, s2, s3, p0, p1, p2, p3, x_ref, normed_ref, qkv_ref, att_ref, lse_ref, *refs = refs
+    gain_ref, shift_ref, s0, s1, s2, s3, p0, p1, p2, p3, x_ref, normed_ref, qkv_ref, att_ref, lse_ref, part_ref, *refs = refs
     *mark_refs, scratch = refs
     share = scratch.shape[1] // 4
 
@@ -206,7 +226,7 @@
     qkv = (dot_nt(normed, scratch[...]) + bias).astype(bf16)
     qkv_ref[...] = qkv
     allowed = allowed_of(place_ref) if layer == 1 else None
-    attend_core(qkv, allowed, att_ref, lse_ref)
+    attend_core(qkv, allowed, att_ref, lse_ref, part_ref)
 
 
 def whole(array):
@@ -216,6 +236,10 @@
 
 def rows_of(columns, rows=WINDOW):
     return pl.BlockSpec((rows, columns), lambda i, s: (i, 0))
+
+
+def parts_of(columns):
+    return pl.BlockSpec((4, WINDOW, columns), lambda i, s: (0, i, 0))
 
 
 def tube_of(columns):
@@ -259,6 +283,7 @@
         ((rows, 3 * width), bf16, rows_of(3 * width)),
         ((rows, width), bf16, rows_of(width)),
         ((4 * LSE_ROWS, WINDOW), f32, rows_of(WINDOW, LSE_ROWS)),
+        ((4, rows, width // 4), bf16, parts_of(width // 4)),
     ]
     if layer == 0:
         outs += [((4, BAND), f32, pl.BlockSpec((4, BAND), lambda i, s: (0, 0)))] * 4
@@ -315,12 +340,21 @@
 
 def attend_back_kernel(layer, place_ref, *refs):
     (stream_ref, g1_ref, x_ref, qkv_ref, lse_ref, gain_ref, p0, p1, p2, p3, *outs) = refs
-    d0, d1, d2, d3, *outs = outs
     if layer == 1:
+        side_ref, *outs = outs
         pieces, outs = outs[:4], outs[4:]
+        sums_ref, scratch, out_scratch, acc = outs
+        rows = slice(None)
     else:
-        (final_ref, *outs) = outs
-    sums_ref, scratch, out_scratch, acc = outs
+        (
+            normed_ref, part_ref, final_ref, sums_ref, leaving_ref, staying_ref,
+            scratch, out_scratch, acc, side_ref, all_normed, all_parts, all_g1,
+        ) = outs
+        rows = step_rows()
+        all_normed[rows, :] = normed_ref[...]
+        all_g1[rows, :] = g1_ref[...]
+        for k in range(4):
+            all_parts[k, rows, :] = part_ref[k]
     width = stream_ref.shape[1]
     share = width // 4
 
@@ -332,9 +366,9 @@
     grad_att = dot_nt(g1_ref[...], out_scratch[...]).astype(bf16)
     allowed = allowed_of(place_ref) if layer == 1 else None
     parts = attend_back_core(qkv_ref[...], grad_att, lse_ref, allowed)
-    for k, ref in enumerate((d0, d1, d2, d3)):
+    for k in range(4):
         for j in range(3):
-            ref[:, j * share : (j + 1) * share] = parts[j][:, k * share : (k + 1) * share]
+            side_ref[k, rows, j * share : (j + 1) * share] = parts[j][:, k * share : (k + 1) * share]
     joined = jnp.concatenate(parts, axis=1)
     grad_normed = dot(joined, scratch[...])
     inner, scaled = norm_back(x_ref[...].astype(f32), gain_ref[layer, 0:1], grad_normed)
@@ -361,9 +395,17 @@
             sums_ref[pl.ds(place_ref[0] ^ k, 1), : 2 * share] = jnp.concatenate([query, value], axis=1)
         sums_ref[4:5, :] = total[:, 2 * width : 3 * width]
         sums_ref[5:6, :] = total[:, 3 * width :]
-
-
-def attend_back(layer, place, stream, g1, x, qkv, lse, gain, packs):
+        if layer == 0:
+
+            def gradient_of(k):
+                upper = dot_tn(side_ref[k], all_normed[...])
+                lower = dot_tn(all_parts[k], all_g1[...])
+                return jnp.concatenate([upper, lower], axis=0)
+
+            put_parts(leaving_ref, staying_ref, gradient_of)
+
+
+def attend_back(layer, place, stream, g1, x, qkv, lse, gain, packs, normed, attended):
     rows, width = stream.shape
     share = width // 4
     operands = [
@@ -373,16 +415,21 @@
         (qkv, rows_of(3 * width)),
         (lse, rows_of(WINDOW, LSE_ROWS)),
     ] + [(a, whole(a)) for a in (gain, *packs)]
-    outs = [((rows, 3 * share), bf16, rows_of(3 * share))] * 4
+    sums = [((8, width), f32, sums_of(width))]
+    scratch = [
+        pltpu.VMEM((3 * width, width), bf16), pltpu.VMEM((width, width), bf16), pltpu.VMEM((8, 4 * width), f32)
+    ]
     if layer == 1:
-        outs = outs + [((4, 4, CELL, width), bf16, tube_of(width))] * 4
+        outs = [((4, rows, 3 * share), bf16, parts_of(3 * share))]
+        outs = outs + [((4, 4, CELL, width), bf16, tube_of(width))] * 4 + sums
     else:
-        outs = outs + [((rows, width), f32, rows_of(width))]
-    outs = outs + [((8, width), f32, sums_of(width))]
-    return call(
-        partial(attend_back_kernel, layer), "attend_back", place, 4, operands, outs,
-        [pltpu.VMEM((3 * width, width), bf16), pltpu.VMEM((width, width), bf16), pltpu.VMEM((8, 4 * width), f32)],
-    )
+        operands += [(normed, rows_of(width)), (attended, parts_of(share))]
+        outs = [((rows, width), f32, rows_of(width))] + sums + parts_outs(width)
+        scratch += [
+            pltpu.VMEM((4, rows, 3 * share), bf16), pltpu.VMEM((rows, width), bf16),
+            pltpu.VMEM((4, rows, share), bf16), pltpu.VMEM((rows, width), bf16),
+        ]
+    return call(partial(attend_back_kernel, layer), "attend_back", place, 4, operands, outs, scratch)
 
 
 def feed_kernel(layer, place_ref, *refs):
@@ -426,21 +473,16 @@
 
 
 def feed_specs(layer, packs):
-    ups, downs, across = packs
-    width = across[0].shape[1]
-    block = (width, width)
+    ups, downs, ups_across, downs_across = packs
 
     def of_layer(a):
-        return (a, pl.BlockSpec((None, *block), lambda i, s: (layer, 0, 0)))
-
-    def of_half(a, half):
-        return (a, pl.BlockSpec(block, lambda i, s: (half, 0)))
+        return (a, pl.BlockSpec((None, *a.shape[1:]), lambda i, s: (layer, 0, 0)))
 
     return [
         *[of_layer(a) for a in ups],
-        *[of_half(a, 0) for a in across],
+        *[(a, whole(a)) for a in ups_across],
         *[of_layer(a) for a in downs],
-        *[of_half(a, 1) for a in across],
+        *[(a, whole(a)) for a in downs_across],
     ]
 
 
@@ -471,7 +513,10 @@
     )
 
 
-def loss_kernel(place_ref, final_ref, head_ref, m0, m1, m2, m3, grad_ref, g2_ref, loss_ref, acc):
+def loss_kernel(
+    place_ref, final_ref, head_ref, m0, m1, m2, m3, active_ref, grad_ref, loss_ref, leaving_ref, staying_ref,
+    acc, all_active, all_g2,
+):
     logits = dot(final_ref[...], head_ref[...])
     spread = jnp.concatenate(
         [jnp.broadcast_to(m[f : f + 1, :], (CELL, BAND)) for m in (m0, m1, m2, m3) for f in range(4)],
@@ -495,26 +540,33 @@
     grad_logits = (weight * (soft - jnp.where(chosen, 1.0, 0.0))).astype(bf16)
     grad = dot_nt(grad_logits, head_ref[...])
     grad_ref[...] = grad
-    g2_ref[...] = grad.astype(bf16)
+    all_g2[step_rows(), :] = grad.astype(bf16)
+    all_active[step_rows(), :] = active_ref[...]
     gather_sums(acc, [jnp.broadcast_to(entry, (WINDOW, PAIR))])
 
     @pl.when(last_step())
     def _():
         total = jnp.sum(acc[...], axis=0, keepdims=True)
         loss_ref[...] = jnp.broadcast_to(total[:, :1], loss_ref.shape)
-
-
-def code_loss(place, final, code_head, marks):
+        width = grad_ref.shape[1]
+        put_parts(
+            leaving_ref, staying_ref,
+            lambda k: dot_tn(all_active[:, k * width : (k + 1) * width], all_g2[...]),
+        )
+
+
+def code_loss(place, final, code_head, marks, active):
     rows, width = final.shape
     operands = [(final, rows_of(width))] + [(a, whole(a)) for a in (code_head, *marks)]
+    operands += [(active, rows_of(active.shape[1]))]
     outs = [
         ((rows, width), f32, rows_of(width)),
-        ((rows, width), bf16, rows_of(width)),
         ((8, width), f32, sums_of(width)),
+    ] + parts_outs(width)
+    scratch = [
+        pltpu.VMEM((8, PAIR), f32), pltpu.VMEM(active.shape, bf16), pltpu.VMEM((rows, width), bf16)
     ]
-    return call(
-        loss_kernel, "code_loss", place, 4, operands, outs, [pltpu.VMEM((8, PAIR), f32)]
-    )
+    return call(loss_kernel, "code_loss", place, 4, operands, outs, scratch)
 
 
 def feed_back_kernel(layer, place_ref, *refs):
@@ -522,19 +574,14 @@
         grad_ref, *refs = refs
         grad = grad_ref[...]
     else:
-        pieces, refs = refs[:4], refs[4:]
-        grad = jnp.concatenate(
-            [p[...].reshape(BAND, p.shape[-1]) for p in pieces], axis=0
-        ).astype(f32)
+        grad_ref, *refs = refs
+        grad = grad_ref[...].astype(f32)
     (
-        slope_ref, stream_ref, gain_ref, u0, u1, u2, u3, d0, d1, d2, d3, hidden_ref, next_ref, g1_ref, *outs
+        slope_ref, stream_ref, normed_ref, gain_ref, u0, u1, u2, u3, d0, d1, d2, d3, next_ref, g1_ref,
+        sums_ref, leaving_ref, staying_ref, acc, all_hidden, all_normed,
     ) = refs
-    if layer == 0:
-        (g2_ref, *outs) = outs
-    sums_ref, acc = outs
+    all_normed[step_rows(), :] = normed_ref[...]
     g2 = grad.astype(bf16)
-    if layer == 0:
-        g2_ref[...] = g2
     units = u0.shape[1]
     grad_normed = jnp.zeros(grad.shape, f32)
     sums = []
@@ -546,7 +593,7 @@
             ahead = dot_nt(g2, downs[k + 1][...])
         cut = slice(k * units, (k + 1) * units)
         grad_hidden = (grad_active * slope_ref[:, cut].astype(f32)).astype(bf16)
-        hidden_ref[:, cut] = grad_hidden
+        all_hidden[step_rows(), cut] = grad_hidden
         sums.append(grad_hidden.astype(f32))
         grad_normed = grad_normed + dot_nt(grad_hidden, ups[k][...])
     inner, scaled = norm_back(stream_ref[...], gain_ref[layer, 1:2], grad_normed)
@@ -563,159 +610,116 @@
             sums_ref[pl.ds(place_ref[0] ^ k, 1), :] = total[:, k * units : (k + 1) * units]
             start = 4 * units + k * grad.shape[1]
             sums_ref[4 + k : 5 + k, :] = total[:, start : start + grad.shape[1]]
-
-
-def feed_back(layer, place, grad, slope, stream, gain, packs):
+        put_parts(
+            leaving_ref, staying_ref,
+            lambda k: dot_tn(all_normed[...], all_hidden[:, k * units : (k + 1) * units]),
+        )
+
+
+def feed_back(layer, place, grad, slope, stream, normed, gain, packs):
     rows, width = stream.shape
     units = packs[0][0].shape[2]
-    if layer == 1:
-        first = [(grad, rows_of(width))]
-    else:
-        piece = pl.BlockSpec((1, BAND, width), lambda i, s: (i, 0, 0))
-        first = [(p, piece) for p in grad]
     operands = (
-        first
-        + [(slope, rows_of(4 * units)), (stream, rows_of(width))]
+        [(grad, rows_of(width)), (slope, rows_of(4 * units)), (stream, rows_of(width)), (normed, rows_of(width))]
         + [(gain, whole(gain))]
         + feed_specs(layer, packs)
     )
     outs = [
-        ((rows, 4 * units), bf16, rows_of(4 * units)),
         ((rows, width), f32, rows_of(width)),
         ((rows, width), bf16, rows_of(width)),
+        ((8, width), f32, sums_of(width)),
+    ] + parts_outs(width)
+    scratch = [
+        pltpu.VMEM((8, 4 * units + 4 * width), f32),
+        pltpu.VMEM((rows, 4 * units), bf16),
+        pltpu.VMEM((rows, width), bf16),
     ]
-    if layer == 0:
-        outs = outs + [((rows, width), bf16, rows_of(width))]
-    outs = outs + [((8, width), f32, sums_of(width))]
-    return call(
-        partial(feed_back_kernel, layer), "feed_back", place, 4, operands, outs,
-        [pltpu.VMEM((8, 4 * units + 4 * width), f32)],
-    )
-
-
-ORDER = (1, 3, 2, 0)
+    return call(partial(feed_back_kernel, layer), "feed_back", place, 4, operands, outs, scratch)
 
 
 def grad_kernel(kind, place_ref, *refs):
-    refs = list(refs)
-
-    def take(count):
-        taken = refs[:count]
-        del refs[:count]
-        return taken
-
-    sources = {"attn": 7, "up": 2, "down": 2}[kind]
-    arrays = take(sources)
-    outs = take(4)
-    bufs = take(7 if kind == "attn" else 5)
-    out_bufs = take(4)
-    in_sem, out_sem = refs
-    width = out_bufs[0].shape[-1]
-    copies = []
-
-    def fetch(source, buf):
-        copy = pltpu.make_async_copy(source, buf, in_sem.at[len(copies)])
-        copy.start()
-        copies.append(copy)
-        return [copy, buf]
-
-    def ready(item):
-        if item[0] is not None:
-            item[0].wait()
-            item[0] = None
-        return item[1]
-
-    def columns(ref, k):
-        return ref.at[:, pl.ds(k * width, width)]
-
+    *inputs, leaving_ref, staying_ref = refs
     if kind == "attn":
-        normed = fetch(arrays[0], bufs[0])
-        sides = [fetch(arrays[3], bufs[3])]
-        g1 = fetch(arrays[1], bufs[1])
-        att = fetch(arrays[2], bufs[2])
-        sides += [fetch(arrays[3 + n], bufs[3 + n]) for n in range(1, 4)]
-        plan = [(normed, side) for side in sides]
+        side_ref, normed_ref, part_ref, g1_ref = inputs
+        upper = dot_tn(side_ref[...], normed_ref[...])
+        lower = dot_tn(part_ref[...], g1_ref[...])
+        value = jnp.concatenate([upper, lower], axis=0)
     else:
-        fixed, split = (arrays[1], arrays[0]) if kind == "down" else (arrays[0], arrays[1])
-        fixed = fetch(fixed, bufs[4])
-        split = [fetch(columns(split, k), bufs[n]) for n, k in enumerate(ORDER)]
-        plan = [(s, fixed) if kind == "down" else (fixed, s) for s in split]
-    sent = []
-    for n, (left, right) in enumerate(plan):
-        value = dot_tn(ready(left)[...], ready(right)[...])
-        if kind == "attn":
-            share = width // 4
-            k = ORDER[n]
-            beside = dot_tn(ready(g1)[...], ready(att)[:, k * share : (k + 1) * share])
-            value = jnp.concatenate([value, beside], axis=1)
-        out_bufs[n][...] = value.astype(bf16)
-        copy = pltpu.make_async_copy(out_bufs[n], outs[n], out_sem.at[n])
-        copy.start()
-        sent.append(copy)
-    for copy in sent:
-        copy.wait()
+        left_ref, right_ref = inputs
+        value = dot_tn(left_ref[...], right_ref[...])
+    value = value.astype(bf16)
+    step = pl.program_id(0)
+
+    @pl.when(step < 2)
+    def _():
+        leaving_ref[...] = value
+
+    @pl.when(step >= 2)
+    def _():
+        staying_ref[...] = value
 
 
 def grads(kind, place, arrays, width):
     rows = arrays[1].shape[0]
+
+    def part_at(i):
+        return jnp.where(i < 2, 2 * i + 1, 2 * i - 4)
+
+    part = pl.BlockSpec((rows, width), lambda i, s: (0, part_at(i)))
+
+    def of_part(a):
+        return pl.BlockSpec((None, *a.shape[1:]), lambda i, s: (part_at(i), 0, 0))
+
     if kind == "attn":
-        arrays = list(arrays[:3]) + [arrays[3][k] for k in ORDER]
-        loads = [a.shape for a in arrays]
+        side, normed, attended, g1 = arrays
+        specs = [of_part(side), whole(normed), of_part(attended), whole(g1)]
+    elif kind == "up":
+        specs = [whole(arrays[0]), part]
     else:
-        loads = [(rows, width)] * 5
-    anywhere = pl.BlockSpec(memory_space=pl.ANY)
-    scratch = (
-        [pltpu.VMEM(shape, bf16) for shape in loads]
-        + [pltpu.VMEM((width, width), bf16)] * 4
-        + [pltpu.SemaphoreType.DMA((len(loads),)), pltpu.SemaphoreType.DMA((4,))]
-    )
-    operands = [(a, anywhere) for a in arrays]
-    outs = [((width, width), bf16, anywhere)] * 4
-    return call(partial(grad_kernel, kind), "grads_" + kind, place, 1, operands, outs, scratch)
-
-
-def emit_kernel(attention, split, aliased, place_ref, *refs):
-    if split:
-        mine_ref, other_ref, *refs = refs
-        mine = pl.program_id(0) == place_ref[2]
-        value = jnp.where(mine, mine_ref[...].astype(f32), other_ref[...].astype(f32))
-    else:
-        whole_ref, *refs = refs
-        value = whole_ref[...].astype(f32)
+        specs = [part, whole(arrays[1])]
+    block = (None, width, width)
+    outs = [
+        ((2, width, width), bf16, pl.BlockSpec(block, lambda i, s: (jnp.minimum(i, 1), 0, 0))),
+        ((2, width, width), bf16, pl.BlockSpec(block, lambda i, s: (jnp.maximum(i - 2, 0), 0, 0))),
+    ]
+    return call(
+        partial(grad_kernel, kind), "grads_" + kind, place, 4, list(zip(arrays, specs)), outs
+    )
+
+
+def emit_kernel(attention, aliased, place_ref, mine_ref, other_ref, *refs):
     outs = refs[aliased:]
+    half, width = mine_ref.shape
+    upper = place_ref[2] == 1
+    mine, other = mine_ref[...].astype(f32), other_ref[...].astype(f32)
+    low, high = jnp.where(upper, other, mine), jnp.where(upper, mine, other)
     if attention:
         qkv_ref, out_ref = outs
-        share = qkv_ref.shape[-1]
-        for j in range(3):
-            qkv_ref[0, j] = value[:, j * share : (j + 1) * share]
-        out_ref[0] = value[:, 3 * share :].T
+        share = width // 4
+        qkv_ref[0, 0], qkv_ref[0, 1] = low[:share], low[share:]
+        qkv_ref[0, 2], out_ref[0] = high[:share], high[share:]
     else:
-        outs[0][0] = value
+        outs[0][0, :half] = low
+        outs[0][0, half:] = high
 
 
 def emit(place, layer, attention, summed, earlier):
-    split = len(summed) == 2
     width = summed[0].shape[1]
-    half = width // 2
     share = width // 4
     if attention:
         outs = [
-            ((2, 3, width, share), f32, pl.BlockSpec((1, 3, half, share), lambda i, s: (layer, 0, i, 0))),
-            ((2, share, width), f32, pl.BlockSpec((1, share, half), lambda i, s: (layer, 0, i))),
+            ((2, 3, share, width), f32, pl.BlockSpec((1, 3, share, width), lambda i, s: (layer, 0, 0, 0))),
+            ((2, share, width), f32, pl.BlockSpec((1, share, width), lambda i, s: (layer, 0, 0))),
         ]
     else:
-        outs = [((2, width, width), f32, pl.BlockSpec((1, half, width), lambda i, s: (layer, i, 0)))]
-    if split:
-        operands = [(a, whole(a)) for a in summed]
-    else:
-        operands = [(summed[0], pl.BlockSpec((half, width), lambda i, s: (i, 0)))]
+        outs = [((2, width, width), f32, pl.BlockSpec((1, width, width), lambda i, s: (layer, 0, 0)))]
+    operands = [(a, whole(a)) for a in summed]
     aliases = {}
     if earlier is not None:
-        aliases = {1 + len(operands) + n: n for n in range(len(earlier))}
+        aliases = {3 + n: n for n in range(len(earlier))}
         operands += [(e, pl.BlockSpec(memory_space=pl.ANY)) for e in earlier]
     return call(
-        partial(emit_kernel, attention, split, len(aliases)), "emit", place, 2, operands, outs,
-        aliases=aliases,
+        partial(emit_kernel, attention, len(aliases)), "emit", place, 1, operands, outs, aliases=aliases
     )
 
 
@@ -751,55 +755,79 @@
         self.pending = []
 
 
+def split_halves(total, upper):
+    half = total.shape[0] // 2
+    low, high = total[:half], total[half:]
+    return jnp.where(upper, low, high).astype(bf16), jnp.where(upper, high, low).astype(bf16)
+
+
+def join_halves(mine, other, upper):
+    return jnp.concatenate(
+        [jnp.where(upper, other, mine), jnp.where(upper, mine, other)], axis=0
+    )
+
+
 class Pack:
-    def __init__(self, order, place, kind, arrays, width):
+    def __init__(self, order, leaving, staying):
         self.order = order
-        self.upper = place[2] == 1
-        self.parts = order.run(lambda *a: grads(kind, place, a, width), *arrays)
-        count = lax.axis_size("clip")
-        self.distances = [1 << n for n in range(count.bit_length() - 1)] + [1]
-        self.stage = 0
+        self.out, self.kept = leaving, staying
+        levels = lax.axis_size("clip").bit_length() - 1
+        clip = lax.axis_index("clip")
+        self.uppers = [((clip >> n) & 1) == 1 for n in range(levels)]
+        down = [("halve", n) for n in range(levels - 1)]
+        up = [("join", n) for n in reversed(range(levels - 1))]
+        self.stages = ["core", "across"] + down + [("all", levels - 1)] + up
+        self.at = 0
+
+    def total(self):
+        if self.at == 2:
+            return (self.kept[0].astype(f32) + self.near[0].astype(f32)) + self.moved.astype(f32)
+        return self.sum.astype(f32) + self.moved.astype(f32)
 
     def prepare(self):
+        stage = self.stages[self.at]
         run = self.order.run
-        if self.stage == 1:
-
-            def add(part, beyond):
-                return (part.astype(f32) + beyond.astype(f32)).astype(bf16)
-
-            self.leaving = run(add, self.parts[2], self.beyond)
-        elif self.stage == 2:
-
-            def add(part, beside, across):
-                total = part.astype(f32) + beside.astype(f32) + across.astype(f32)
-                half = total.shape[0] // 2
-                low, high = total[:half], total[half:]
-                return (
-                    jnp.where(self.upper, low, high).astype(bf16),
-                    jnp.where(self.upper, high, low).astype(bf16),
+        if stage == "core":
+            self.leaving = self.out
+        elif stage == "across":
+            self.leaving = run(
+                lambda kept, near: (kept[1].astype(f32) + near[1].astype(f32)).astype(bf16),
+                self.kept, self.near,
+            )
+        else:
+            kind, level = stage
+            upper = self.uppers[level]
+            if self.at == 2:
+                start = lambda kept, near, moved: (
+                    kept[0].astype(f32) + near[0].astype(f32) + moved.astype(f32)
                 )
-
-            self.leaving, self.sum = run(add, self.parts[3], self.beside, self.moved)
-        elif self.stage > 2:
-
-            def add(total, moved):
-                return (total.astype(f32) + moved.astype(f32)).astype(bf16)
-
-            self.leaving = self.sum = run(add, self.sum, self.moved)
+                values = (self.kept, self.near, self.moved)
+            else:
+                start = lambda total, moved: total.astype(f32) + moved.astype(f32)
+                values = (self.sum, self.moved)
+            if kind == "halve":
+                self.leaving, self.sum = run(lambda *v: split_halves(start(*v), upper), *values)
+            elif kind == "all" or self.stages[self.at - 1][0] == "all":
+                self.leaving = self.sum = run(lambda *v: start(*v).astype(bf16), *values)
+            else:
+                before = self.uppers[self.stages[self.at - 1][1]]
+                self.leaving = self.sum = run(
+                    lambda mine, other: join_halves(mine, other, before), self.sum, self.moved
+                )
 
     def launch(self):
+        stage = self.stages[self.at]
         send = self.order.send
-        if self.stage == 0:
-            self.beside = send(head_swap, self.parts[0], 1)
-            self.beyond = send(head_swap, self.parts[1], 1)
-        elif self.stage == 1:
+        if stage == "core":
+            self.near = send(head_swap, self.leaving, 1)
+        elif stage == "across":
             self.moved = send(head_swap, self.leaving, 2)
         else:
-            self.moved = send(clip_swap, self.leaving, self.distances[self.stage - 2])
-        self.stage += 1
+            self.moved = send(clip_swap, self.leaving, 1 << stage[1])
+        self.at += 1
 
     def done(self):
-        return self.stage == 2 + len(self.distances)
+        return self.at == len(self.stages)
 
     def whole(self):
         assert self.done()
@@ -836,18 +864,33 @@
 
     clip_count = lax.axis_size("clip")
     own_small = jnp.concatenate([up_bias, qv_bias.reshape(1, width)], axis=0)
-    piece = (w_up.shape[1] + w_down.shape[1]) // clip_count
-    first_row = lax.axis_index("clip") * piece
-
-    def chunk(layer):
-        halves = [w_up[layer], w_down[layer]]
-        rows = halves[0].shape[0]
-        start = first_row % rows
-        parts = [lax.dynamic_slice_in_dim(h, start, piece, 0) for h in halves]
-        return jnp.where(first_row < rows, parts[0], parts[1])
-
-    def gather_feed(chunk_across):
+    clip_index = lax.axis_index("clip")
+
+    def chunk(matrix):
+        piece = matrix.shape[0] // clip_count
+        return lax.dynamic_slice_in_dim(matrix, clip_index * piece, piece, 0)
+
+    def over_clips(chunk_across):
         return lax.all_gather(chunk_across, "clip", axis=0, tiled=True)
+
+    y_place, z_place = clip_index & 1, (clip_index >> 1) & 1
+
+    def quarter(matrix):
+        rows = matrix.shape[0] // 4
+        return lax.dynamic_slice_in_dim(matrix, (2 * y_place + z_place) * rows, rows, 0)
+
+    def over_neighbours(first):
+        second = clip_swap(first, 1)
+        others = clip_swap(jnp.concatenate([first, second], axis=0), 2)
+        rows = first.shape[0]
+        pieces = []
+        for y in range(2):
+            for z in range(2):
+                same = z_place == z
+                mine = jnp.where(same, first, others[:rows])
+                next_one = jnp.where(same, second, others[rows:])
+                pieces.append(jnp.where(y_place == y, mine, next_one))
+        return jnp.concatenate(pieces, axis=0)
 
     def attn_pack(layer):
         transposed = w_qkv[layer].swapaxes(1, 2).reshape(-1, width)
@@ -856,60 +899,85 @@
     def spread(own, across):
         return [own, head_swap(own, 1), across, head_swap(across, 1)]
 
-    chunk_0 = head_swap(chunk(0), 2)
+    chunk_0 = head_swap(quarter(w_up[0]), 2)
     smalls = spread(own_small, head_swap(own_small, 2))
     own = tied(attn_pack(0), chunk_0, smalls[2])
-    attn = [spread(own, head_swap(own, 2)), None]
-    feed_across = [gather_feed(chunk_0), None]
-    ups = [w_up, head_swap(tied(w_up, attn[0][2]), 1)]
-    downs = [w_down, head_swap(tied(w_down, attn[0][2]), 1)]
+    later = jnp.concatenate([chunk(w_up[1]), chunk(w_down[1])], axis=0)
+    marks = (2 * targets + token_mask).astype(f32).reshape(-1, 1)
+    across, first_down, later, marks, place, up_across = lax.optimization_barrier(
+        (head_swap(own, 2), w_down[0], later, marks, place, over_neighbours(chunk_0))
+    )
+    attn = [spread(own, across), None]
+    order.last = (attn[0][2],)
+    down_across = order.send(head_swap, first_down, 2)
+    order.last = (smalls[1], smalls[3], attn[0][1], attn[0][3])
+    ups = [w_up, order.send(head_swap, w_up, 1)]
+    downs = [w_down, order.send(head_swap, w_down, 1)]
+    up_diagonal = order.send(head_swap, up_across, 1)
     packs = [None, None]
 
-    marks = (2 * targets + token_mask).astype(f32).reshape(-1, 1)
     kept = []
     inputs = (tokens, marks)
     for layer in range(2):
-        x, normed, qkv, att, lse, *mark_pieces = order.run(
+        x, normed, qkv, att, lse, att_parts, *mark_pieces = order.run(
             lambda *a: attend(layer, place, a, norm_gain, norm_bias, smalls, attn[layer]), *inputs
         )
+        order.close()
         if layer == 0:
             marks = [mark_pieces[0]] + [head_swap(mark_pieces[k], k) for k in (1, 2, 3)]
-            chunk_1 = head_swap(tied(chunk(1), x), 2)
-            own = tied(attn_pack(1), chunk_1)
-            attn[1] = spread(own, head_swap(own, 2))
-            feed_across[1] = gather_feed(chunk_1)
-        across = tied(feed_across[layer], x)
-        packs[layer] = (ups, downs, [across, head_swap(across, 1)])
+            chunk_1 = order.send(head_swap, later, 2)
+            up_x, down_x = up_across, down_across
+            up_pair = [up_x, up_diagonal]
+        else:
+            pieces = gathered.reshape(clip_count, 2, -1, width)
+            up_x, down_x = tied((pieces[:, 0].reshape(-1, width), pieces[:, 1].reshape(-1, width)), x)
+            up_pair = [up_x, order.send(head_swap, up_x, 1)]
+        packs[layer] = (
+            ups, downs,
+            up_pair,
+            [down_x, order.send(head_swap, down_x, 1)],
+        )
+        order.close()
+        if layer == 0:
+            gathered = over_clips(tied(chunk_1, up_across))
+            own = attn_pack(1)
+            attn_across = order.send(head_swap, own, 2)
+            attn[1] = [own, head_swap(own, 1), attn_across]
         stream, normed2, active, slope, *outs = order.run(
             lambda a, b: feed(
                 layer, place, a, b, attn[layer], vec_bias, norm_gain, norm_bias, smalls, packs[layer]
             ),
             x, att,
         )
-        kept.append((x, normed, qkv, att, lse, stream, normed2, active, slope))
+        kept.append((x, normed, qkv, att_parts, lse, stream, normed2, active, slope))
         if layer == 0:
+            order.close()
+            attn[1].append(order.send(head_swap, attn_across, 1))
             inputs = [outs[0]] + [order.send(head_swap, outs[k], k) for k in (1, 2, 3)]
             inputs = [p.reshape(4, 4, CELL, width) for p in inputs]
             order.close()
-    grad, g2, loss_sum = order.run(lambda a: code_loss(place, a, code_head, marks), outs[0])
+    grad, loss_sum, *parts = order.run(
+        lambda a: code_loss(place, a, code_head, marks, active), outs[0]
+    )
+    down_1 = Pack(order, *parts)
 
     def run_feed_back(layer, grad):
         x, normed, qkv, att, lse, stream, normed2, active, slope = kept[layer]
         return order.run(
-            lambda a: feed_back(layer, place, a, slope, stream, norm_gain, packs[layer]), grad
+            lambda a: feed_back(layer, place, a, slope, stream, normed2, norm_gain, packs[layer]), grad
         )
 
     def run_attend_back(layer, grad_next, g1):
         x, normed, qkv, att, lse, *_ = kept[layer]
         return order.run(
             lambda a, b: attend_back(
-                layer, place, a, b, x, qkv, lse, norm_gain, attn[layer]
+                layer, place, a, b, x, qkv, lse, norm_gain, attn[layer], normed, att
             ),
             grad_next, g1,
         )
 
     def pack(kind, *arrays):
-        return Pack(order, place, kind, arrays, width)
+        return Pack(order, *order.run(lambda *a: grads(kind, place, a, width), *arrays))
 
     def move(*ones):
         for one in ones:
@@ -917,54 +985,66 @@
         for one in ones:
             one.launch()
 
-    normed, att, normed2, active = kept[1][1], kept[1][3], kept[1][6], kept[1][7]
-    down_1 = pack("down", active, g2)
     move(down_1)
-    grad_hidden, grad_next, g1, feed_sum_1 = run_feed_back(1, grad)
     order.close()
-
-    up_1 = pack("up", normed2, grad_hidden)
-    move(down_1, up_1)
-    *rest, attn_sum_1 = run_attend_back(1, grad_next, g1)
+    move(down_1)
+    grad_next, g1, feed_sum_1, *parts = run_feed_back(1, grad)
+    up_1 = Pack(order, *parts)
     order.close()
-
-    sides, outs = rest[:4], rest[4:]
+    move(up_1)
+    order.close()
+    move(up_1, down_1)
+    side, *outs, attn_sum_1 = run_attend_back(1, grad_next, g1)
+    order.close()
+
     grad = [outs[0]] + [order.send(head_swap, outs[k], k) for k in (1, 2, 3)]
     grad = [p.reshape(4, BAND, width) for p in grad]
-    move(down_1)
-    attn_1 = pack("attn", normed, g1, att, sides)
+    move(up_1, down_1)
+    attn_1 = pack("attn", side, kept[1][1], kept[1][3], g1)
     order.close()
 
-    normed, att, normed2, active = kept[0][1], kept[0][3], kept[0][6], kept[0][7]
-    move(up_1, attn_1, down_1)
-    grad_hidden, grad_next, g1, g2, feed_sum_0 = run_feed_back(0, grad)
-    down_0 = pack("down", active, g2)
+    move(attn_1, up_1)
+    g2 = jnp.stack(grad, axis=1).reshape(-1, width)
+    down_0 = pack("down", kept[0][7], g2)
     order.close()
-
-    move(attn_1, up_1, down_1, down_0)
-    up_0 = pack("up", normed2, grad_hidden)
-    *rest, attn_sum_0 = run_attend_back(0, grad_next, g1)
-    sides, (grad_input,) = rest[:4], rest[4:]
+    move(attn_1, down_0, down_1, up_1)
+    grad_next, g1, feed_sum_0, *parts = run_feed_back(0, g2)
+    up_0 = Pack(order, *parts)
     order.close()
-
-    move(down_0, up_0, attn_1, up_1, down_1)
-    attn_0 = pack("attn", normed, g1, att, sides)
+    move(down_0, up_0, attn_1, down_1, up_1)
+    grad_input, attn_sum_0, *parts = run_attend_back(0, grad_next, g1)
+    attn_0 = Pack(order, *parts)
+    order.close()
+    move(up_0, attn_0, down_0, attn_1, down_1)
+    order.close()
+    move(attn_0, up_0, down_0, attn_1, up_1)
+    order.close()
+
     packed = jnp.concatenate([feed_sum_0, feed_sum_1, attn_sum_0, attn_sum_1, loss_sum], axis=0)
-    order.close()
-
     swaps = [(head_swap, 1), (head_swap, 2)]
     swaps += [(clip_swap, 1 << n) for n in range(clip_count.bit_length() - 1)]
+
+    def pack_step():
+        swap, distance = swaps.pop(0)
+        return packed + order.send(swap, packed, distance)
+
+    early = [(up_1, False), (down_1, False), (attn_1, True)]
+    ready = {}
     moving = [attn_0, up_0, down_0, attn_1, up_1, down_1]
-    while not attn_0.done() or swaps:
+    while swaps or not all(one.done() for one in moving):
         move(*[one for one in moving if not one.done()])
         if swaps:
-            swap, distance = swaps.pop(0)
-            packed = packed + order.send(swap, packed, distance)
+            packed = pack_step()
+        if early and early[0][0].done():
+            one, attention = early.pop(0)
+            ready[one] = order.run(lambda *a: emit(place, 1, attention, a, None), *one.whole())
         order.close()
-
-    attn_out = emit(place, 0, True, attn_0.whole(), emit(place, 1, True, attn_1.whole(), None))
-    up_out = emit(place, 0, False, up_0.whole(), emit(place, 1, False, up_1.whole(), None))
-    down_out = emit(place, 0, False, down_0.whole(), emit(place, 1, False, down_1.whole(), None))
+    for one, attention in early:
+        ready[one] = emit(place, 1, attention, one.whole(), None)
+
+    attn_out = emit(place, 0, True, attn_0.whole(), ready[attn_1])
+    up_out = emit(place, 0, False, up_0.whole(), ready[up_1])
+    down_out = emit(place, 0, False, down_0.whole(), ready[down_1])
 
     feed_sums = packed[:16].reshape(2, 8, width)
     attn_sums = packed[16:32].reshape(2, 8, width)
@@ -978,7 +1058,7 @@
         grad_input,
         jnp.stack([attn_sums[:, 4], feed_sums[:, 4]], axis=1),
         jnp.stack([attn_sums[:, 5], feed_sums[:, 5]], axis=1),
-        attn_out[0],
+        attn_out[0].swapaxes(2, 3),
         own_attn[:, : 2 * share].reshape(2, 2, share),
         attn_out[1],
         jnp.stack([feed_sums[:, 7], feed_sums[:, 6]], axis=1),

time: 667 us -> 575 us (0.86); the launches traced: 656 us -> 571 us
  waiting for transfers between devices: 245 us -> 172 us
  Pallas kernels: 283 us -> 254 us
  other arithmetic: 17.6 us -> 33.4 us
    ppermute x44 -> x41, waiting for transfers between devices: 123 us -> 69.7 us  [head_swap(): lax.ppermute(values, 'head', [(i, i ^ distance) for i in range(count)])]
    pallas_call x21 -> x17, Pallas kernels: 283 us -> 254 us  [call(): pl.pallas_call(kernel, grid_spec=pltpu.PrefetchScalarGridSpec(num_scalar_...]
    ppermute x27 -> x35, waiting for transfers between devices: 121 us -> 103 us  [clip_swap(): lax.ppermute(values, 'clip', [(i, i ^ distance) for i in range(count)])]
    unnamed x151 -> x144, local copies, waits for them, and re-layouts: 24 us -> 14.5 us
    convert_element_type x30, other arithmetic: 6.48 us -> 13.2 us  [the longest x6 6.44 us: prepare(): (kept[1].astype(f32) + near[1].astype(f32)).astype(bf16)]
    ppermute x27 -> x35, starting transfers between devices: 36.3 us -> 40.3 us  [clip_swap(): lax.ppermute(values, 'clip', [(i, i ^ distance) for i in range(count)])]
    ppermute x44 -> x41, starting transfers between devices: 24.7 us -> 25.4 us  [head_swap(): lax.ppermute(values, 'head', [(i, i ^ distance) for i in range(count)])]
  transfers between devices with their start and end apart: 73 -> 77, of which waited for: 21 -> 34; matrix products, arithmetic and copies ran while one was open for 2% -> 3% of each run, Pallas kernels for 37% -> 41%
where the time goes in v3:
time: 575 us; the launch traced here: 571 us
  Pallas kernels  254 us (44%)
  waiting for transfers between devices  172 us (30%)
  starting transfers between devices  65.7 us (11%)
  other arithmetic  33.4 us (6%)
  local copies, waits for them, and re-layouts  27.1 us (5%)
  between operations  18.2 us (3%)
    pallas_call x17, Pallas kernels, call(): pl.pallas_call(kernel, grid_spec=pltpu.PrefetchScalarGridSpec(num_scalar_...  254 us
    ppermute x35, waiting for transfers between devices, clip_swap(): lax.ppermute(values, 'clip', [(i, i ^ distance) for i in range(count)])  103 us
    ppermute x41, waiting for transfers between devices, head_swap(): lax.ppermute(values, 'head', [(i, i ^ distance) for i in range(count)])  69.7 us
    ppermute x35, starting transfers between devices, clip_swap(): lax.ppermute(values, 'clip', [(i, i ^ distance) for i in range(count)])  40.3 us
    ppermute x41, starting transfers between devices, head_swap(): lax.ppermute(values, 'head', [(i, i ^ distance) for i in range(count)])  25.4 us
    unnamed x144, local copies, waits for them, and re-layouts  14.5 us
  transfers between devices with their start and end apart: 77, of which 34 were waited for; matrix products, arithmetic and copies ran while one was open for 3% of the time, Pallas kernels for 41%

profile of v3, /device:TPU:0, one launch (start us, length us, event | category | flops | bytes accessed | tf_op | source)
XLA Modules:
  0.0 571.1 jit_solution(8707004978223723286)
XLA Ops:
  7.3 2.9 fusion.7
  10.2 3.0 collective-permute-start
  14.5 5.9 %collective-permute-done = bf16[192,768]{1,0:T(8,128)(2,1)S(1)} collective-permute-done((bf16[192,768]{1,0:T(8,128)(2,1)S(1)}, bf16[192,768]{1,0:T(8,128)(2,1)S(1)}, u32[]{:S(2)}, u32[]{:S(2)}) %collective-permute-start) | collective-permute-done | bytes 294944 | tf_op jit(solution)/shard_map/ppermute | solution.py:728
  24.6 3.8 collective-permute-done.3
  30.0 2.8 fusion.8
  36.5 5.6 collective-permute-done.4
  44.4 5.3 collective-permute-done.2.refs_10_.refs_4_.refs_8_
  56.4 17.7 %attend.2 = (bf16[1024,768]{1,0:T(8,128)(2,1)}, bf16[1024,768]{1,0:T(8,128)(2,1)}, bf16[1024,2304]{1,0:T(8,128)(2,1)}, bf16[1024,768]{1,0:T(8,128)(2,1)}, f32[64...) custom-call(s32[3]{0:T(128)} %pad_add_fusion.place_ref, ...), custom_call_target="tpu_custom_call" | custom-call | flops 1955000 | bytes 6120 | tf_op jit(solution)/shard_map/attend/pallas_call | solution.py:254
  74.2 8.0 %collective-permute-done.9.refs_19_.refs_11_ = bf16[768,768]{1,0:T(8,128)(2,1)S(1)} collective-permute-done((bf16[768,768]{1,0:T(8,128)(2,1)}, bf16[768,768]{1,0:T(8,128)(2,1)S(1)}, u32[]{:S(2)}, u32[]{:S(2)}) %collective-permute-start.9) | collective-permute-done | bytes 1179680 | tf_op jit(solution)/shard_map/ppermute | solution.py:728
  83.7 6.7 %collective-permute-done.13 = bf16[192,768]{1,0:T(8,128)(2,1)S(1)} collective-permute-done((bf16[192,768]{1,0:T(8,128)(2,1)S(1)}, bf16[192,768]{1,0:T(8,128)(2,1)S(1)}, u32[]{:S(2)}, u32[]{:S(2)}) %collective-permute-start.13) | collective-permute-done | bytes 294944 | tf_op jit(solution)/shard_map/ppermute | solution.py:728
  95.6 23.5 %feed.2 = (f32[1024,768]{1,0:T(8,128)}, bf16[1024,768]{1,0:T(8,128)(2,1)}, bf16[1024,3072]{1,0:T(8,128)(2,1)}, bf16[1024,3072]{1,0:T(8,128)(2,1)}, bf16[4,64,768...) custom-call(s32[3]{0:T(128)} %pad_add_fusion.place_ref, ...), custom_call_target="tpu_custom_call" | custom-call | flops 2645000 | bytes 8280 | tf_op jit(solution)/shard_map/feed/pallas_call | solution.py:254
  119.1 3.0 collective-permute-done.15.refs_12_.refs_4_.refs_8_
  124.5 9.5 %collective-permute-done.18 = bf16[4,64,768]{2,1,0:T(8,128)(2,1)S(1)} collective-permute-done((bf16[4,64,768]{2,1,0:T(8,128)(2,1)}, bf16[4,64,768]{2,1,0:T(8,128)(2,1)S(1)}, u32[]{:S(2)}, u32[]{:S(2)}) %collective-permute-start.18) | collective-permute-done | bytes 393248 | tf_op jit(solution)/shard_map/ppermute | solution.py:728
  134.0 8.7 %collective-permute-done.17 = bf16[4,64,768]{2,1,0:T(8,128)(2,1)S(1)} collective-permute-done((bf16[4,64,768]{2,1,0:T(8,128)(2,1)}, bf16[4,64,768]{2,1,0:T(8,128)(2,1)S(1)}, u32[]{:S(2)}, u32[]{:S(2)}) %collective-permute-start.17) | collective-permute-done | bytes 393248 | tf_op jit(solution)/shard_map/ppermute | solution.py:728
  145.1 17.3 %attend.3 = (bf16[1024,768]{1,0:T(8,128)(2,1)}, bf16[1024,768]{1,0:T(8,128)(2,1)}, bf16[1024,2304]{1,0:T(8,128)(2,1)}, bf16[1024,768]{1,0:T(8,128)(2,1)}, f32[64...) custom-call(s32[3]{0:T(128)} %pad_add_fusion.place_ref, bf16[4,4,16,768]{3,2,1,0:T(8,128)(2,1)} %bitcast.96, ...), custom_call_target="tpu_custom_call" | custom-call | flops 1955000 | bytes 6120 | tf_op jit(solution)/shard_map/attend/pallas_call | solution.py:254
  169.8 23.5 %feed.3 = (f32[1024,768]{1,0:T(8,128)}, bf16[1024,768]{1,0:T(8,128)(2,1)}, bf16[1024,3072]{1,0:T(8,128)(2,1)}, bf16[1024,3072]{1,0:T(8,128)(2,1)}, bf16[1024,768]{1,0:T(8,128)(2,1)}) custom-call(s32[3]{0:T(128)} %pad_add_fusion.place_ref, bf16[1024,768]{1,0:T(8,128)(2,1)} %get-tuple-element.292.refs_0_.refs_2_, ...), custom_call_target="tpu_custom_call" | custom-call | flops 2645000 | bytes 8280 | tf_op jit(solution)/shard_map/feed/pallas_call | solution.py:254
  194.0 17.8 %code_loss.1 = (f32[1024,768]{1,0:T(8,128)}, f32[8,768]{1,0:T(8,128)}, bf16[2,768,768]{2,1,0:T(8,128)(2,1)}, bf16[2,768,768]{2,1,0:T(8,128)(2,1)}) custom-call(s32[3]{0:T(128)} %pad_add_fusion.place_ref, bf16[1024,768]{1,0:T(8,128)(2,1)} %get-tuple-element.296.final_ref, bf16[768,1024]{1,0:T(8,128)(2,1)} %head_ref.1, f32[4,64]{1,0:T(4,128)} %get-tuple-element.297.m0, ...), custom_call_target="tpu_custom_call" | custom-call | flops 1150000 | bytes 3600 | tf_op jit(solution)/shard_map/code_loss/pallas_call | solution.py:254
  211.9 4.6 collective-permute-done.26
  220.6 27.0 %feed_back.2 = (f32[1024,768]{1,0:T(8,128)}, bf16[1024,768]{1,0:T(8,128)(2,1)}, f32[8,768]{1,0:T(8,128)}, bf16[2,768,768]{2,1,0:T(8,128)(2,1)}, bf16[2,768,768]{2,1,0:T(8,128)(2,1)}) custom-call(s32[3]{0:T(128)} %pad_add_fusion.place_ref, f32[1024,768]{1,0:T(8,128)} %get-tuple-element.308.refs_0_, bf16[1024,3072]{1,0:T(8,128)(2,1)} %get-tuple-element.309.refs_1_, ...), custom_call_target="tpu_custom_call" | custom-call | flops 2415000 | bytes 7560 | tf_op jit(solution)/shard_map/feed_back/pallas_call | solution.py:254
  247.7 4.7 collective-permute-done.28
  258.4 24.7 %attend_back.2 = (bf16[4,1024,576]{2,1,0:T(8,128)(2,1)}, bf16[4,4,16,768]{3,2,1,0:T(8,128)(2,1)}, bf16[4,4,16,768]{3,2,1,0:T(8,128)(2,1)}, bf16[4,4,16,768]{3,2,...) custom-call(s32[3]{0:T(128)} %pad_add_fusion.place_ref, f32[1024,768]{1,0:T(8,128)} %get-tuple-element.322.refs_0_, ...), custom_call_target="tpu_custom_call" | custom-call | flops 2875000 | bytes 9000 | tf_op jit(solution)/shard_map/attend_back/pallas_call | solution.py:254
  290.7 11.1 %grads_attn.1 = (bf16[2,768,768]{2,1,0:T(8,128)(2,1)}, bf16[2,768,768]{2,1,0:T(8,128)(2,1)}) custom-call(s32[3]{0:T(128)} %pad_add_fusion.place_ref, bf16[4,1024,576]{2,1,0:T(8,128)(2,1)} %get-tuple-element.344.refs_0_, bf16[1024,768]{1,0:T(8,128)(2,1)} %get-tuple-element.345.refs_1_, bf16[4,1024,192]{2,1,0:T(8,128)(2,1)} %get-tuple-element.346.refs_2_, ...), custom_call_target="tpu_custom_call" | custom-call | flops 920000 | bytes 2880 | tf_op jit(solution)/shard_map/grads_attn/pallas_call | solution.py:254
  301.8 5.0 collective-permute-done.33
  310.3 10.7 %grads_down.1 = (bf16[2,768,768]{2,1,0:T(8,128)(2,1)}, bf16[2,768,768]{2,1,0:T(8,128)(2,1)}) custom-call(s32[3]{0:T(128)} %pad_add_fusion.place_ref, bf16[1024,3072]{1,0:T(8,128)(2,1)} %get-tuple-element.356.refs_0_, bf16[1024,768]{1,0:T(8,128)(2,1)} %bitcast.81), custom_call_target="tpu_custom_call" | custom-call | flops 920000 | bytes 2880 | tf_op jit(solution)/shard_map/grads_down/pallas_call | solution.py:254
  325.2 2.6 collective-permute-start.38
  328.1 27.2 %feed_back.3 = (f32[1024,768]{1,0:T(8,128)}, bf16[1024,768]{1,0:T(8,128)(2,1)}, f32[8,768]{1,0:T(8,128)}, bf16[2,768,768]{2,1,0:T(8,128)(2,1)}, bf16[2,768,768]{2,1,0:T(8,128)(2,1)}) custom-call(s32[3]{0:T(128)} %pad_add_fusion.place_ref, bf16[1024,768]{1,0:T(8,128)(2,1)} %bitcast.82, bf16[1024,3072]{1,0:T(8,128)(2,1)} %get-tuple-element.366.refs_1_, ...), custom_call_target="tpu_custom_call" | custom-call | flops 2415000 | bytes 7560 | tf_op jit(solution)/shard_map/feed_back/pallas_call | solution.py:254
  367.8 32.4 %attend_back.3 = (f32[1024,768]{1,0:T(8,128)}, f32[8,768]{1,0:T(8,128)}, bf16[2,768,768]{2,1,0:T(8,128)(2,1)}, bf16[2,768,768]{2,1,0:T(8,128)(2,1)}) custom-call(s32[3]{0:T(128)} %pad_add_fusion.place_ref, f32[1024,768]{1,0:T(8,128)} %get-tuple-element.386.refs_0_, bf16[1024,768]{1,0:T(8,128)(2,1)} %get-tuple-element.387.refs_1_, ...), custom_call_target="tpu_custom_call" | custom-call | flops 2875000 | bytes 9000 | tf_op jit(solution)/shard_map/attend_back/pallas_call | solution.py:254
  410.0 8.1 %collective-permute-done.47 = bf16[192,768]{1,0:T(8,128)(2,1)S(1)} collective-permute-done((bf16[192,768]{1,0:T(8,128)(2,1)S(1)}, bf16[192,768]{1,0:T(8,128)(2,1)S(1)}, u32[]{:S(2)}, u32[]{:S(2)}) %collective-permute-start.47) | collective-permute-done | bytes 294944 | tf_op jit(solution)/shard_map/ppermute | solution.py:733
  418.1 5.6 collective-permute-done.48
  423.7 11.9 %collective-permute-done.51.other_ref = bf16[384,768]{1,0:T(8,128)(2,1)S(1)} collective-permute-done((bf16[384,768]{1,0:T(8,128)(2,1)S(1)}, bf16[384,768]{1,0:T(8,128)(2,1)S(1)}, u32[]{:S(2)}, u32[]{:S(2)}) %collective-permute-start.51) | collective-permute-done | bytes 589856 | tf_op jit(solution)/shard_map/ppermute | solution.py:733
  441.4 2.6 collective-permute-start.52
  444.5 11.5 %collective-permute-done.52 = bf16[192,768]{1,0:T(8,128)(2,1)S(1)} collective-permute-done((bf16[192,768]{1,0:T(8,128)(2,1)S(1)}, bf16[192,768]{1,0:T(8,128)(2,1)S(1)}, u32[]{:S(2)}, u32[]{:S(2)}) %collective-permute-start.52) | collective-permute-done | bytes 294944 | tf_op jit(solution)/shard_map/ppermute | solution.py:733
  457.3 9.0 %collective-permute-done.56.other_ref = bf16[384,768]{1,0:T(8,128)(2,1)S(1)} collective-permute-done((bf16[384,768]{1,0:T(8,128)(2,1)S(1)}, bf16[384,768]{1,0:T(8,128)(2,1)S(1)}, u32[]{:S(2)}, u32[]{:S(2)}) %collective-permute-start.56) | collective-permute-done | bytes 589856 | tf_op jit(solution)/shard_map/ppermute | solution.py:733
  473.0 3.6 emit.6.refs_0_
  476.6 6.1 %collective-permute-done.58 = bf16[192,768]{1,0:T(8,128)(2,1)S(1)} collective-permute-done((bf16[192,768]{1,0:T(8,128)(2,1)S(1)}, bf16[192,768]{1,0:T(8,128)(2,1)S(1)}, u32[]{:S(2)}, u32[]{:S(2)}) %collective-permute-start.58) | collective-permute-done | bytes 294944 | tf_op jit(solution)/shard_map/ppermute | solution.py:733
  482.8 5.2 collective-permute-done.60
  490.2 2.6 collective-permute-start.64
  495.4 3.6 emit.7.refs_0_
  499.3 5.5 collective-permute-done.63
  504.8 5.3 collective-permute-done.65
  514.8 3.5 emit.8
  518.3 9.5 %collective-permute-done.67 = f32[40,768]{1,0:T(8,128)S(1)} collective-permute-done((f32[40,768]{1,0:T(8,128)S(1)}, f32[40,768]{1,0:T(8,128)S(1)}, u32[]{:S(2)}, u32[]{:S(2)}) %collective-permute-start.67) | collective-permute-done | bytes 122912 | tf_op jit(solution)/shard_map/ppermute | solution.py:733
  531.4 7.3 %collective-permute-done.71 = f32[40,768]{1,0:T(8,128)S(1)} collective-permute-done((f32[40,768]{1,0:T(8,128)S(1)}, f32[40,768]{1,0:T(8,128)S(1)}, u32[]{:S(2)}, u32[]{:S(2)}) %collective-permute-start.71) | collective-permute-done | bytes 122912 | tf_op jit(solution)/shard_map/ppermute | solution.py:733
  538.7 3.3 collective-permute-done.73.other_ref
  542.2 3.6 emit.11
  546.5 3.6 emit.10
  554.5 3.8 collective-permute-done.75.other_ref
  559.1 3.5 emit.9
  (356 shorter events, 119.4 us)
Async XLA Ops:
  7.2 155.2 %all-gather.2.cloned.1.call-start = ((), (), s32[]{:S(2)}) async-start(), calls=%async_computation | async-start | bytes 2654208 | tf_op jit(solution)/shard_map/all_gather | solution.py:874
  23.0 26.6 %collective-permute-start.2 = (bf16[768,768]{1,0:T(8,128)(2,1)S(1)}, bf16[768,768]{1,0:T(8,128)(2,1)}, u32[]{:S(2)}, u32[]{:S(2)}) collective-permute-start(bf16[768,768]{1,0:T(8,128)(2,1)S(1)} %pad_maximum_fusion.1.refs_8_.refs_2_.refs_6_), channel_id=1, source_target_pairs={{0,2},{1,3},{2,0},{3,1},{4,6},{5,7},{6,4},{7,5},{8,10},{9,11},{10,... | collective-permute-start | bytes 3538952 | tf_op jit(solution)/shard_map/ppermute | solution.py:728
  36.4 16.0 %collective-permute-start.7 = (bf16[768,768]{1,0:T(8,128)(2,1)S(1)}, bf16[768,768]{1,0:T(8,128)(2,1)S(1)}, u32[]{:S(2)}, u32[]{:S(2)}) collective-permute-start(bf16[768,768]{1,0:T(8,128)(2,1)S(1)} %pad_maximum_fusion.1.refs_8_.refs_2_.refs_6_), channel_id=1, source_target_pairs={{0,1},{1,0},{2,3},{3,2},{4,5},{5,4},{6,7},{7,6},{8,9},{9,8},{10,11... | collective-permute-start | bytes 3538952 | tf_op jit(solution)/shard_map/ppermute | solution.py:728
  52.7 29.5 %collective-permute-start.10 = (bf16[2,768,768]{2,1,0:T(8,128)(2,1)S(1)}, bf16[2,768,768]{2,1,0:T(8,128)(2,1)}, u32[]{:S(2)}, u32[]{:S(2)}) collective-permute-start(bf16[2,768,768]{2,1,0:T(8,128)(2,1)S(1)} %copy-done), channel_id=1, source_target_pairs={{0,1},{1,0},{2,3},{3,2},{4,5},{5,4},{6,7},{7,6},{8,9},{9,8},{10,11... | collective-permute-start | bytes 7077896 | tf_op jit(solution)/shard_map/ppermute | solution.py:728
  53.6 28.6 %collective-permute-start.11 = (bf16[2,768,768]{2,1,0:T(8,128)(2,1)}, bf16[2,768,768]{2,1,0:T(8,128)(2,1)}, u32[]{:S(2)}, u32[]{:S(2)}) collective-permute-start(bf16[2,768,768]{2,1,0:T(8,128)(2,1)} %refs_9_.3), channel_id=1, source_target_pairs={{0,1},{1,0},{2,3},{3,2},{4,5},{5,4},{6,7},{7,6},{8,9},{9,8},{10,11... | collective-permute-start | bytes 7077896 | tf_op jit(solution)/shard_map/ppermute | solution.py:728
  53.9 28.2 %collective-permute-start.9 = (bf16[768,768]{1,0:T(8,128)(2,1)}, bf16[768,768]{1,0:T(8,128)(2,1)S(1)}, u32[]{:S(2)}, u32[]{:S(2)}) collective-permute-start(bf16[768,768]{1,0:T(8,128)(2,1)} %get-tuple-element.261), channel_id=1, source_target_pairs={{0,2},{1,3},{2,0},{3,1},{4,6},{5,7},{6,4},{7,5},{8,10},{9,11},{10,... | collective-permute-start | bytes 3538952 | tf_op jit(solution)/shard_map/ppermute | solution.py:728
  55.4 26.7 %collective-permute-start.12 = (bf16[768,768]{1,0:T(8,128)(2,1)}, bf16[768,768]{1,0:T(8,128)(2,1)}, u32[]{:S(2)}, u32[]{:S(2)}) collective-permute-start(bf16[768,768]{1,0:T(8,128)(2,1)} %pad_maximum_fusion.2.refs_15_.refs_7_), channel_id=1, source_target_pairs={{0,1},{1,0},{2,3},{3,2},{4,5},{5,4},{6,7},{7,6},{8,9},{9,8},{10,11... | collective-permute-start | bytes 3538952 | tf_op jit(solution)/shard_map/ppermute | solution.py:728
  94.1 28.0 %collective-permute-start.15 = (bf16[768,768]{1,0:T(8,128)(2,1)S(1)}, bf16[768,768]{1,0:T(8,128)(2,1)S(1)}, u32[]{:S(2)}, u32[]{:S(2)}) collective-permute-start(bf16[768,768]{1,0:T(8,128)(2,1)S(1)} %pad_maximum_fusion.3.refs_10_.refs_2_.refs_6_), channel_id=1, source_target_pairs={{0,2},{1,3},{2,0},{3,1},{4,6},{5,7},{6,4},{7,5},{8,10},{9,11},{10,... | collective-permute-start | bytes 3538952 | tf_op jit(solution)/shard_map/ppermute | solution.py:728
  122.1 20.6 %collective-permute-start.19 = (bf16[768,768]{1,0:T(8,128)(2,1)S(1)}, bf16[768,768]{1,0:T(8,128)(2,1)S(1)}, u32[]{:S(2)}, u32[]{:S(2)}) collective-permute-start(bf16[768,768]{1,0:T(8,128)(2,1)S(1)} %collective-permute-done.15.refs_12_.refs_4_.refs_8_), channel_id=1, source_target_pairs={{0,1},{1,0},{2,3},{3,2},{4,5},{5,4},{6,7},{7,6},{8,9},{9,8},{10,11... | collective-permute-start | bytes 3538952 | tf_op jit(solution)/shard_map/ppermute | solution.py:728
  122.1 20.6 %collective-permute-start.20 = (bf16[768,768]{1,0:T(8,128)(2,1)S(1)}, bf16[768,768]{1,0:T(8,128)(2,1)S(1)}, u32[]{:S(2)}, u32[]{:S(2)}) collective-permute-start(bf16[768,768]{1,0:T(8,128)(2,1)S(1)} %pad_maximum_fusion.3.refs_10_.refs_2_.refs_6_), channel_id=1, source_target_pairs={{0,1},{1,0},{2,3},{3,2},{4,5},{5,4},{6,7},{7,6},{8,9},{9,8},{10,11... | collective-permute-start | bytes 3538952 | tf_op jit(solution)/shard_map/ppermute | solution.py:728
  123.8 18.9 %collective-permute-start.17 = (bf16[4,64,768]{2,1,0:T(8,128)(2,1)}, bf16[4,64,768]{2,1,0:T(8,128)(2,1)S(1)}, u32[]{:S(2)}, u32[]{:S(2)}) collective-permute-start(bf16[4,64,768]{2,1,0:T(8,128)(2,1)} %get-tuple-element.277), channel_id=1, source_target_pairs={{0,2},{1,3},{2,0},{3,1},{4,6},{5,7},{6,4},{7,5},{8,10},{9,11},{10,... | collective-permute-start | bytes 1179656 | tf_op jit(solution)/shard_map/ppermute | solution.py:728
  124.4 18.4 %collective-permute-start.16 = (bf16[4,64,768]{2,1,0:T(8,128)(2,1)}, bf16[4,64,768]{2,1,0:T(8,128)(2,1)S(1)}, u32[]{:S(2)}, u32[]{:S(2)}) collective-permute-start(bf16[4,64,768]{2,1,0:T(8,128)(2,1)} %get-tuple-element.275), channel_id=1, source_target_pairs={{0,1},{1,0},{2,3},{3,2},{4,5},{5,4},{6,7},{7,6},{8,9},{9,8},{10,11... | collective-permute-start | bytes 1179656 | tf_op jit(solution)/shard_map/ppermute | solution.py:728
  164.8 28.6 %collective-permute-start.23 = (f32[4,64]{1,0:T(4,128)S(1)}, f32[4,64]{1,0:T(4,128)S(1)}, u32[]{:S(2)}, u32[]{:S(2)}) collective-permute-start(f32[4,64]{1,0:T(4,128)S(1)} %copy-done.68), channel_id=1, source_target_pairs={{0,1},{1,0},{2,3},{3,2},{4,5},{5,4},{6,7},{7,6},{8,9},{9,8},{10,11... | collective-permute-start | bytes 3080 | tf_op jit(solution)/shard_map/ppermute | solution.py:728
  164.8 28.5 %collective-permute-start.24 = (f32[4,64]{1,0:T(4,128)S(1)}, f32[4,64]{1,0:T(4,128)S(1)}, u32[]{:S(2)}, u32[]{:S(2)}) collective-permute-start(f32[4,64]{1,0:T(4,128)S(1)} %copy-done.67), channel_id=1, source_target_pairs={{0,2},{1,3},{2,0},{3,1},{4,6},{5,7},{6,4},{7,5},{8,10},{9,11},{10,... | collective-permute-start | bytes 3080 | tf_op jit(solution)/shard_map/ppermute | solution.py:728
  166.3 27.0 %collective-permute-start.25 = (f32[4,64]{1,0:T(4,128)S(1)}, f32[4,64]{1,0:T(4,128)S(1)}, u32[]{:S(2)}, u32[]{:S(2)}) collective-permute-start(f32[4,64]{1,0:T(4,128)S(1)} %copy-done.66), channel_id=1, source_target_pairs={{0,3},{1,2},{2,1},{3,0},{4,7},{5,6},{6,5},{7,4},{8,11},{9,10},{10,... | collective-permute-start | bytes 3080 | tf_op jit(solution)/shard_map/ppermute | solution.py:728
  219.0 28.6 %collective-permute-start.27 = (bf16[768,768]{1,0:T(8,128)(2,1)S(1)}, bf16[768,768]{1,0:T(8,128)(2,1)S(1)}, u32[]{:S(2)}, u32[]{:S(2)}) collective-permute-start(bf16[768,768]{1,0:T(8,128)(2,1)S(1)} %fusion), channel_id=1, source_target_pairs={{0,2},{1,3},{2,0},{3,1},{4,6},{5,7},{6,4},{7,5},{8,10},{9,11},{10,... | collective-permute-start | bytes 3538952 | tf_op jit(solution)/shard_map/ppermute | solution.py:728
  257.0 28.0 %collective-permute-start.29 = (bf16[768,768]{1,0:T(8,128)(2,1)S(1)}, bf16[768,768]{1,0:T(8,128)(2,1)S(1)}, u32[]{:S(2)}, u32[]{:S(2)}) collective-permute-start(bf16[768,768]{1,0:T(8,128)(2,1)S(1)} %fusion.1), channel_id=1, source_target_pairs={{0,2},{1,3},{2,0},{3,1},{4,6},{5,7},{6,4},{7,5},{8,10},{9,11},{10,... | collective-permute-start | bytes 3538952 | tf_op jit(solution)/shard_map/ppermute | solution.py:728
  257.9 25.2 %collective-permute-start.30 = (bf16[384,768]{1,0:T(8,128)(2,1)}, bf16[384,768]{1,0:T(8,128)(2,1)S(1)}, u32[]{:S(2)}, u32[]{:S(2)}) collective-permute-start(bf16[384,768]{1,0:T(8,128)(2,1)} %get-tuple-element.330), channel_id=1, source_target_pairs={{0,4},{4,0},{8,12},{12,8},{16,20},{20,16},{24,28},{28,24},{1,5},{5... | collective-permute-start | bytes 1769480 | tf_op jit(solution)/shard_map/ppermute | solution.py:733
  286.7 20.1 %collective-permute-start.34 = (bf16[384,768]{1,0:T(8,128)(2,1)S(1)}, bf16[384,768]{1,0:T(8,128)(2,1)S(1)}, u32[]{:S(2)}, u32[]{:S(2)}) collective-permute-start(bf16[384,768]{1,0:T(8,128)(2,1)S(1)} %get-tuple-element.341), channel_id=1, source_target_pairs={{0,4},{4,0},{8,12},{12,8},{16,20},{20,16},{24,28},{28,24},{1,5},{5... | collective-permute-start | bytes 1769480 | tf_op jit(solution)/shard_map/ppermute | solution.py:733
  287.3 14.5 %collective-permute-start.31 = (bf16[4,4,16,768]{3,2,1,0:T(8,128)(2,1)S(1)}, bf16[4,4,16,768]{3,2,1,0:T(8,128)(2,1)S(1)}, u32[]{:S(2)}, u32[]{:S(2)}) collective-permute-start(bf16[4,4,16,768]{3,2,1,0:T(8,128)(2,1)S(1)} %copy-done.65), channel_id=1, source_target_pairs={{0,1},{1,0},{2,3},{3,2},{4,5},{5,4},{6,7},{7,6},{8,9},{9,8},{10,11... | collective-permute-start | bytes 1179656 | tf_op jit(solution)/shard_map/ppermute | solution.py:728
  287.3 14.5 %collective-permute-start.32 = (bf16[4,4,16,768]{3,2,1,0:T(8,128)(2,1)S(1)}, bf16[4,4,16,768]{3,2,1,0:T(8,128)(2,1)S(1)}, u32[]{:S(2)}, u32[]{:S(2)}) collective-permute-start(bf16[4,4,16,768]{3,2,1,0:T(8,128)(2,1)S(1)} %copy-done.64), channel_id=1, source_target_pairs={{0,2},{1,3},{2,0},{3,1},{4,6},{5,7},{6,4},{7,5},{8,10},{9,11},{10,... | collective-permute-start | bytes 1179656 | tf_op jit(solution)/shard_map/ppermute | solution.py:728
  288.4 18.4 %collective-permute-start.33 = (bf16[4,4,16,768]{3,2,1,0:T(8,128)(2,1)S(1)}, bf16[4,4,16,768]{3,2,1,0:T(8,128)(2,1)S(1)}, u32[]{:S(2)}, u32[]{:S(2)}) collective-permute-start(bf16[4,4,16,768]{3,2,1,0:T(8,128)(2,1)S(1)} %copy-done.63), channel_id=1, source_target_pairs={{0,3},{1,2},{2,1},{3,0},{4,7},{5,6},{6,5},{7,4},{8,11},{9,10},{10,... | collective-permute-start | bytes 1179656 | tf_op jit(solution)/shard_map/ppermute | solution.py:728
  324.1 31.2 %collective-permute-start.41 = (bf16[2,768,768]{2,1,0:T(8,128)(2,1)}, bf16[2,768,768]{2,1,0:T(8,128)(2,1)S(1)}, u32[]{:S(2)}, u32[]{:S(2)}) collective-permute-start(bf16[2,768,768]{2,1,0:T(8,128)(2,1)} %get-tuple-element.376), channel_id=1, source_target_pairs={{0,1},{1,0},{2,3},{3,2},{4,5},{5,4},{6,7},{7,6},{8,9},{9,8},{10,11... | collective-permute-start | bytes 7077896 | tf_op jit(solution)/shard_map/ppermute | solution.py:728
  324.1 31.2 %collective-permute-start.40 = (bf16[768,768]{1,0:T(8,128)(2,1)S(1)}, bf16[768,768]{1,0:T(8,128)(2,1)}, u32[]{:S(2)}, u32[]{:S(2)}) collective-permute-start(bf16[768,768]{1,0:T(8,128)(2,1)S(1)} %fusion.2), channel_id=1, source_target_pairs={{0,2},{1,3},{2,0},{3,1},{4,6},{5,7},{6,4},{7,5},{8,10},{9,11},{10,... | collective-permute-start | bytes 3538952 | tf_op jit(solution)/shard_map/ppermute | solution.py:728
  325.2 30.1 %collective-permute-start.38 = (bf16[192,768]{1,0:T(8,128)(2,1)}, bf16[192,768]{1,0:T(8,128)(2,1)}, u32[]{:S(2)}, u32[]{:S(2)}) collective-permute-start(bf16[192,768]{1,0:T(8,128)(2,1)} %add_convert_fusion.16), channel_id=1, source_target_pairs={{0,16},{4,20},{8,24},{12,28},{16,0},{20,4},{24,8},{28,12},{1,17},{... | collective-permute-start | bytes 884744 | tf_op jit(solution)/shard_map/ppermute | solution.py:733
  327.7 27.6 %collective-permute-start.39 = (bf16[192,768]{1,0:T(8,128)(2,1)}, bf16[192,768]{1,0:T(8,128)(2,1)}, u32[]{:S(2)}, u32[]{:S(2)}) collective-permute-start(bf16[192,768]{1,0:T(8,128)(2,1)} %add_convert_fusion.17), channel_id=1, source_target_pairs={{0,16},{4,20},{8,24},{12,28},{16,0},{20,4},{24,8},{28,12},{1,17},{... | collective-permute-start | bytes 884744 | tf_op jit(solution)/shard_map/ppermute | solution.py:733
  363.2 37.1 %collective-permute-start.44 = (bf16[2,768,768]{2,1,0:T(8,128)(2,1)}, bf16[2,768,768]{2,1,0:T(8,128)(2,1)S(1)}, u32[]{:S(2)}, u32[]{:S(2)}) collective-permute-start(bf16[2,768,768]{2,1,0:T(8,128)(2,1)} %get-tuple-element.399), channel_id=1, source_target_pairs={{0,1},{1,0},{2,3},{3,2},{4,5},{5,4},{6,7},{7,6},{8,9},{9,8},{10,11... | collective-permute-start | bytes 7077896 | tf_op jit(solution)/shard_map/ppermute | solution.py:728
  363.2 37.0 %collective-permute-start.43 = (bf16[768,768]{1,0:T(8,128)(2,1)}, bf16[768,768]{1,0:T(8,128)(2,1)}, u32[]{:S(2)}, u32[]{:S(2)}) collective-permute-start(bf16[768,768]{1,0:T(8,128)(2,1)} %fusion.3), channel_id=1, source_target_pairs={{0,2},{1,3},{2,0},{3,1},{4,6},{5,7},{6,4},{7,5},{8,10},{9,11},{10,... | collective-permute-start | bytes 3538952 | tf_op jit(solution)/shard_map/ppermute | solution.py:728
  364.3 36.0 %collective-permute-start.42 = (bf16[384,768]{1,0:T(8,128)(2,1)}, bf16[384,768]{1,0:T(8,128)(2,1)}, u32[]{:S(2)}, u32[]{:S(2)}) collective-permute-start(bf16[384,768]{1,0:T(8,128)(2,1)} %get-tuple-element.395), channel_id=1, source_target_pairs={{0,4},{4,0},{8,12},{12,8},{16,20},{20,16},{24,28},{28,24},{1,5},{5... | collective-permute-start | bytes 1769480 | tf_op jit(solution)/shard_map/ppermute | solution.py:733
  365.8 34.4 %collective-permute-start.45 = (bf16[192,768]{1,0:T(8,128)(2,1)S(1)}, bf16[192,768]{1,0:T(8,128)(2,1)}, u32[]{:S(2)}, u32[]{:S(2)}) collective-permute-start(bf16[192,768]{1,0:T(8,128)(2,1)S(1)} %add_convert_fusion.15), channel_id=1, source_target_pairs={{0,8},{4,12},{8,0},{12,4},{16,24},{20,28},{24,16},{28,20},{1,9},{5... | collective-permute-start | bytes 884744 | tf_op jit(solution)/shard_map/ppermute | solution.py:733
  366.2 34.0 %collective-permute-start.46 = (bf16[192,768]{1,0:T(8,128)(2,1)S(1)}, bf16[192,768]{1,0:T(8,128)(2,1)}, u32[]{:S(2)}, u32[]{:S(2)}) collective-permute-start(bf16[192,768]{1,0:T(8,128)(2,1)S(1)} %add_convert_fusion.14), channel_id=1, source_target_pairs={{0,8},{4,12},{8,0},{12,4},{16,24},{20,28},{24,16},{28,20},{1,9},{5... | collective-permute-start | bytes 884744 | tf_op jit(solution)/shard_map/ppermute | solution.py:733
  406.4 29.1 %collective-permute-start.50 = (bf16[2,768,768]{2,1,0:T(8,128)(2,1)S(1)}, bf16[2,768,768]{2,1,0:T(8,128)(2,1)S(1)}, u32[]{:S(2)}, u32[]{:S(2)}) collective-permute-start(bf16[2,768,768]{2,1,0:T(8,128)(2,1)S(1)} %copy-done.62), channel_id=1, source_target_pairs={{0,1},{1,0},{2,3},{3,2},{4,5},{5,4},{6,7},{7,6},{8,9},{9,8},{10,11... | collective-permute-start | bytes 7077896 | tf_op jit(solution)/shard_map/ppermute | solution.py:728
  406.5 29.0 %collective-permute-start.49 = (bf16[768,768]{1,0:T(8,128)(2,1)S(1)}, bf16[768,768]{1,0:T(8,128)(2,1)S(1)}, u32[]{:S(2)}, u32[]{:S(2)}) collective-permute-start(bf16[768,768]{1,0:T(8,128)(2,1)S(1)} %fusion.4), channel_id=1, source_target_pairs={{0,2},{1,3},{2,0},{3,1},{4,6},{5,7},{6,4},{7,5},{8,10},{9,11},{10,... | collective-permute-start | bytes 3538952 | tf_op jit(solution)/shard_map/ppermute | solution.py:728
  407.5 16.2 %collective-permute-start.48 = (bf16[384,768]{1,0:T(8,128)(2,1)S(1)}, bf16[384,768]{1,0:T(8,128)(2,1)S(1)}, u32[]{:S(2)}, u32[]{:S(2)}) collective-permute-start(bf16[384,768]{1,0:T(8,128)(2,1)S(1)} %get-tuple-element.413), channel_id=1, source_target_pairs={{0,4},{4,0},{8,12},{12,8},{16,20},{20,16},{24,28},{28,24},{1,5},{5... | collective-permute-start | bytes 1769480 | tf_op jit(solution)/shard_map/ppermute | solution.py:733
  408.2 27.4 %collective-permute-start.51 = (bf16[384,768]{1,0:T(8,128)(2,1)S(1)}, bf16[384,768]{1,0:T(8,128)(2,1)S(1)}, u32[]{:S(2)}, u32[]{:S(2)}) collective-permute-start(bf16[384,768]{1,0:T(8,128)(2,1)S(1)} %pad_maximum_fusion.5.mine_ref), channel_id=1, source_target_pairs={{0,4},{4,0},{8,12},{12,8},{16,20},{20,16},{24,28},{28,24},{1,5},{5... | collective-permute-start | bytes 1769480 | tf_op jit(solution)/shard_map/ppermute | solution.py:733
  438.2 28.1 %collective-permute-start.55 = (bf16[768,768]{1,0:T(8,128)(2,1)S(1)}, bf16[768,768]{1,0:T(8,128)(2,1)S(1)}, u32[]{:S(2)}, u32[]{:S(2)}) collective-permute-start(bf16[768,768]{1,0:T(8,128)(2,1)S(1)} %fusion.5), channel_id=1, source_target_pairs={{0,2},{1,3},{2,0},{3,1},{4,6},{5,7},{6,4},{7,5},{8,10},{9,11},{10,... | collective-permute-start | bytes 3538952 | tf_op jit(solution)/shard_map/ppermute | solution.py:728
  439.4 17.9 %collective-permute-start.54 = (bf16[384,768]{1,0:T(8,128)(2,1)S(1)}, bf16[384,768]{1,0:T(8,128)(2,1)S(1)}, u32[]{:S(2)}, u32[]{:S(2)}) collective-permute-start(bf16[384,768]{1,0:T(8,128)(2,1)S(1)} %get-tuple-element.432), channel_id=1, source_target_pairs={{0,4},{4,0},{8,12},{12,8},{16,20},{20,16},{24,28},{28,24},{1,5},{5... | collective-permute-start | bytes 1769480 | tf_op jit(solution)/shard_map/ppermute | solution.py:733
  439.9 26.4 %collective-permute-start.56 = (bf16[384,768]{1,0:T(8,128)(2,1)S(1)}, bf16[384,768]{1,0:T(8,128)(2,1)S(1)}, u32[]{:S(2)}, u32[]{:S(2)}) collective-permute-start(bf16[384,768]{1,0:T(8,128)(2,1)S(1)} %pad_maximum_fusion.6.mine_ref), channel_id=1, source_target_pairs={{0,4},{4,0},{8,12},{12,8},{16,20},{20,16},{24,28},{28,24},{1,5},{5... | collective-permute-start | bytes 1769480 | tf_op jit(solution)/shard_map/ppermute | solution.py:733
  441.4 14.6 %collective-permute-start.52 = (bf16[192,768]{1,0:T(8,128)(2,1)S(1)}, bf16[192,768]{1,0:T(8,128)(2,1)S(1)}, u32[]{:S(2)}, u32[]{:S(2)}) collective-permute-start(bf16[192,768]{1,0:T(8,128)(2,1)S(1)} %add_convert_fusion.13), channel_id=1, source_target_pairs={{0,16},{4,20},{8,24},{12,28},{16,0},{20,4},{24,8},{28,12},{1,17},{... | collective-permute-start | bytes 884744 | tf_op jit(solution)/shard_map/ppermute | solution.py:733
  467.6 20.3 %collective-permute-start.61 = (bf16[384,768]{1,0:T(8,128)(2,1)S(1)}, bf16[384,768]{1,0:T(8,128)(2,1)S(1)}, u32[]{:S(2)}, u32[]{:S(2)}) collective-permute-start(bf16[384,768]{1,0:T(8,128)(2,1)S(1)} %get-tuple-element.448), channel_id=1, source_target_pairs={{0,4},{4,0},{8,12},{12,8},{16,20},{20,16},{24,28},{28,24},{1,5},{5... | collective-permute-start | bytes 1769480 | tf_op jit(solution)/shard_map/ppermute | solution.py:733
  471.3 16.6 %collective-permute-start.60 = (bf16[192,768]{1,0:T(8,128)(2,1)S(1)}, bf16[192,768]{1,0:T(8,128)(2,1)S(1)}, u32[]{:S(2)}, u32[]{:S(2)}) collective-permute-start(bf16[192,768]{1,0:T(8,128)(2,1)S(1)} %get-tuple-element.447), channel_id=1, source_target_pairs={{0,8},{4,12},{8,0},{12,4},{16,24},{20,28},{24,16},{28,20},{1,9},{5... | collective-permute-start | bytes 884744 | tf_op jit(solution)/shard_map/ppermute | solution.py:733
  488.4 21.6 %collective-permute-start.66 = (bf16[384,768]{1,0:T(8,128)(2,1)S(1)}, bf16[384,768]{1,0:T(8,128)(2,1)S(1)}, u32[]{:S(2)}, u32[]{:S(2)}) collective-permute-start(bf16[384,768]{1,0:T(8,128)(2,1)S(1)} %pad_maximum_fusion.7.mine_ref), channel_id=1, source_target_pairs={{0,4},{4,0},{8,12},{12,8},{16,20},{20,16},{24,28},{28,24},{1,5},{5... | collective-permute-start | bytes 1769480 | tf_op jit(solution)/shard_map/ppermute | solution.py:733
  489.8 15.0 %collective-permute-start.63 = (bf16[192,768]{1,0:T(8,128)(2,1)S(1)}, bf16[192,768]{1,0:T(8,128)(2,1)S(1)}, u32[]{:S(2)}, u32[]{:S(2)}) collective-permute-start(bf16[192,768]{1,0:T(8,128)(2,1)S(1)} %add_convert_fusion.9), channel_id=1, source_target_pairs={{0,8},{4,12},{8,0},{12,4},{16,24},{20,28},{24,16},{28,20},{1,9},{5... | collective-permute-start | bytes 884744 | tf_op jit(solution)/shard_map/ppermute | solution.py:733
  490.2 14.6 %collective-permute-start.64 = (bf16[192,768]{1,0:T(8,128)(2,1)S(1)}, bf16[192,768]{1,0:T(8,128)(2,1)S(1)}, u32[]{:S(2)}, u32[]{:S(2)}) collective-permute-start(bf16[192,768]{1,0:T(8,128)(2,1)S(1)} %add_convert_fusion.10), channel_id=1, source_target_pairs={{0,16},{4,20},{8,24},{12,28},{16,0},{20,4},{24,8},{28,12},{1,17},{... | collective-permute-start | bytes 884744 | tf_op jit(solution)/shard_map/ppermute | solution.py:733
  492.8 17.2 %collective-permute-start.65 = (bf16[192,768]{1,0:T(8,128)(2,1)S(1)}, bf16[192,768]{1,0:T(8,128)(2,1)S(1)}, u32[]{:S(2)}, u32[]{:S(2)}) collective-permute-start(bf16[192,768]{1,0:T(8,128)(2,1)S(1)} %get-tuple-element.462), channel_id=1, source_target_pairs={{0,8},{4,12},{8,0},{12,4},{16,24},{20,28},{24,16},{28,20},{1,9},{5... | collective-permute-start | bytes 884744 | tf_op jit(solution)/shard_map/ppermute | solution.py:733
  510.8 16.9 %collective-permute-start.70 = (bf16[384,768]{1,0:T(8,128)(2,1)S(1)}, bf16[384,768]{1,0:T(8,128)(2,1)S(1)}, u32[]{:S(2)}, u32[]{:S(2)}) collective-permute-start(bf16[384,768]{1,0:T(8,128)(2,1)S(1)} %pad_maximum_fusion.8.mine_ref), channel_id=1, source_target_pairs={{0,4},{4,0},{8,12},{12,8},{16,20},{20,16},{24,28},{28,24},{1,5},{5... | collective-permute-start | bytes 1769480 | tf_op jit(solution)/shard_map/ppermute | solution.py:733
  511.5 16.2 %collective-permute-start.68 = (bf16[192,768]{1,0:T(8,128)(2,1)S(1)}, bf16[192,768]{1,0:T(8,128)(2,1)S(1)}, u32[]{:S(2)}, u32[]{:S(2)}) collective-permute-start(bf16[192,768]{1,0:T(8,128)(2,1)S(1)} %add_convert_fusion.7), channel_id=1, source_target_pairs={{0,8},{4,12},{8,0},{12,4},{16,24},{20,28},{24,16},{28,20},{1,9},{5... | collective-permute-start | bytes 884744 | tf_op jit(solution)/shard_map/ppermute | solution.py:733
  511.8 15.9 %collective-permute-start.69 = (bf16[192,768]{1,0:T(8,128)(2,1)S(1)}, bf16[192,768]{1,0:T(8,128)(2,1)S(1)}, u32[]{:S(2)}, u32[]{:S(2)}) collective-permute-start(bf16[192,768]{1,0:T(8,128)(2,1)S(1)} %add_convert_fusion.8), channel_id=1, source_target_pairs={{0,16},{4,20},{8,24},{12,28},{16,0},{20,4},{24,8},{28,12},{1,17},{... | collective-permute-start | bytes 884744 | tf_op jit(solution)/shard_map/ppermute | solution.py:733
  (98 other events, 773.3 us)
Sparse Core Ops, SparseCore 0:
  91.3 52.3 all-gather.1

commit v4 on v3

--- a/solution.py
+++ b/solution.py
@@ -768,23 +768,24 @@
 
 
 class Pack:
-    def __init__(self, order, leaving, staying):
+    def __init__(self, order, leaving, staying, halving=True):
         self.order = order
         self.out, self.kept = leaving, staying
         levels = lax.axis_size("clip").bit_length() - 1
         clip = lax.axis_index("clip")
         self.uppers = [((clip >> n) & 1) == 1 for n in range(levels)]
-        down = [("halve", n) for n in range(levels - 1)]
-        up = [("join", n) for n in reversed(range(levels - 1))]
-        self.stages = ["core", "across"] + down + [("all", levels - 1)] + up
+        depth = levels - 1 if halving else 1
+        down = [("halve", n) for n in range(depth)]
+        level = [("all", n) for n in range(depth, levels)]
+        up = [("join", n) for n in reversed(range(depth))]
+        self.stages = ["core", "across"] + down + level + up
         self.at = 0
-
-    def total(self):
-        if self.at == 2:
-            return (self.kept[0].astype(f32) + self.near[0].astype(f32)) + self.moved.astype(f32)
-        return self.sum.astype(f32) + self.moved.astype(f32)
+        self.prepared = False
 
     def prepare(self):
+        if self.prepared:
+            return
+        self.prepared = True
         stage = self.stages[self.at]
         run = self.order.run
         if stage == "core":
@@ -825,6 +826,7 @@
         else:
             self.moved = send(clip_swap, self.leaving, 1 << stage[1])
         self.at += 1
+        self.prepared = False
 
     def done(self):
         return self.at == len(self.stages)
@@ -879,16 +881,17 @@
         rows = matrix.shape[0] // 4
         return lax.dynamic_slice_in_dim(matrix, (2 * y_place + z_place) * rows, rows, 0)
 
-    def over_neighbours(first):
-        second = clip_swap(first, 1)
-        others = clip_swap(jnp.concatenate([first, second], axis=0), 2)
-        rows = first.shape[0]
+    def along_y(first):
+        return jnp.concatenate([first, clip_swap(first, 1)], axis=0)
+
+    def by_place(pair, others):
+        rows = pair.shape[0] // 2
         pieces = []
         for y in range(2):
             for z in range(2):
                 same = z_place == z
-                mine = jnp.where(same, first, others[:rows])
-                next_one = jnp.where(same, second, others[rows:])
+                mine = jnp.where(same, pair[:rows], others[:rows])
+                next_one = jnp.where(same, pair[rows:], others[rows:])
                 pieces.append(jnp.where(y_place == y, mine, next_one))
         return jnp.concatenate(pieces, axis=0)
 
@@ -899,22 +902,34 @@
     def spread(own, across):
         return [own, head_swap(own, 1), across, head_swap(across, 1)]
 
-    chunk_0 = head_swap(quarter(w_up[0]), 2)
+    quarters = jnp.concatenate([quarter(w_up[0]), quarter(w_down[0])], axis=0)
+    quarters = head_swap(quarters, 2)
     smalls = spread(own_small, head_swap(own_small, 2))
-    own = tied(attn_pack(0), chunk_0, smalls[2])
+    own = tied(attn_pack(0), quarters, smalls[2])
     later = jnp.concatenate([chunk(w_up[1]), chunk(w_down[1])], axis=0)
     marks = (2 * targets + token_mask).astype(f32).reshape(-1, 1)
-    across, first_down, later, marks, place, up_across = lax.optimization_barrier(
-        (head_swap(own, 2), w_down[0], later, marks, place, over_neighbours(chunk_0))
+    rows = quarters.shape[0] // 2
+    beyond_y = clip_swap(quarters, 1)
+    up_pair = jnp.concatenate([quarters[:rows], beyond_y[:rows]], axis=0)
+    down_pair = jnp.concatenate([quarters[rows:], beyond_y[rows:]], axis=0)
+    across, later, marks, place, up_pair, up_others, down_pair = lax.optimization_barrier(
+        (head_swap(own, 2), later, marks, place, up_pair, clip_swap(up_pair, 2), down_pair)
     )
     attn = [spread(own, across), None]
-    order.last = (attn[0][2],)
-    down_across = order.send(head_swap, first_down, 2)
+    order.last = (across,)
+    down_others = order.send(clip_swap, down_pair, 2)
+    chunk_1 = order.send(head_swap, later, 2)
     order.last = (smalls[1], smalls[3], attn[0][1], attn[0][3])
     ups = [w_up, order.send(head_swap, w_up, 1)]
     downs = [w_down, order.send(head_swap, w_down, 1)]
-    up_diagonal = order.send(head_swap, up_across, 1)
     packs = [None, None]
+
+    def feed_packs(up_x, down_x):
+        return (
+            ups, downs,
+            [up_x, order.send(head_swap, up_x, 1)],
+            [down_x, order.send(head_swap, down_x, 1)],
+        )
 
     kept = []
     inputs = (tokens, marks)
@@ -924,22 +939,14 @@
         )
         order.close()
         if layer == 0:
+            gathered = over_clips(tied(chunk_1, x))
             marks = [mark_pieces[0]] + [head_swap(mark_pieces[k], k) for k in (1, 2, 3)]
-            chunk_1 = order.send(head_swap, later, 2)
-            up_x, down_x = up_across, down_across
-            up_pair = [up_x, up_diagonal]
-        else:
-            pieces = gathered.reshape(clip_count, 2, -1, width)
-            up_x, down_x = tied((pieces[:, 0].reshape(-1, width), pieces[:, 1].reshape(-1, width)), x)
-            up_pair = [up_x, order.send(head_swap, up_x, 1)]
-        packs[layer] = (
-            ups, downs,
-            up_pair,
-            [down_x, order.send(head_swap, down_x, 1)],
-        )
-        order.close()
-        if layer == 0:
-            gathered = over_clips(tied(chunk_1, up_across))
+            up_x, down_x = order.run(
+                lambda a, b, c, d: (by_place(a, b), by_place(c, d)),
+                up_pair, up_others, down_pair, down_others,
+            )
+            packs[0] = feed_packs(up_x, down_x)
+            order.close()
             own = attn_pack(1)
             attn_across = order.send(head_swap, own, 2)
             attn[1] = [own, head_swap(own, 1), attn_across]
@@ -952,14 +959,16 @@
         kept.append((x, normed, qkv, att_parts, lse, stream, normed2, active, slope))
         if layer == 0:
             order.close()
+            pieces = gathered.reshape(clip_count, 2, -1, width)
             attn[1].append(order.send(head_swap, attn_across, 1))
             inputs = [outs[0]] + [order.send(head_swap, outs[k], k) for k in (1, 2, 3)]
             inputs = [p.reshape(4, 4, CELL, width) for p in inputs]
             order.close()
+            packs[1] = feed_packs(pieces[:, 0].reshape(-1, width), pieces[:, 1].reshape(-1, width))
     grad, loss_sum, *parts = order.run(
         lambda a: code_loss(place, a, code_head, marks, active), outs[0]
     )
-    down_1 = Pack(order, *parts)
+    down_1 = Pack(order, *parts, halving=False)
 
     def run_feed_back(layer, grad):
         x, normed, qkv, att, lse, stream, normed2, active, slope = kept[layer]
@@ -976,8 +985,9 @@
             grad_next, g1,
         )
 
-    def pack(kind, *arrays):
-        return Pack(order, *order.run(lambda *a: grads(kind, place, a, width), *arrays))
+    def pack(kind, *arrays, halving=True):
+        parts = order.run(lambda *a: grads(kind, place, a, width), *arrays)
+        return Pack(order, *parts, halving=halving)
 
     def move(*ones):
         for one in ones:
@@ -989,9 +999,10 @@
     order.close()
     move(down_1)
     grad_next, g1, feed_sum_1, *parts = run_feed_back(1, grad)
-    up_1 = Pack(order, *parts)
+    up_1 = Pack(order, *parts, halving=False)
     order.close()
     move(up_1)
+    down_1.prepare()
     order.close()
     move(up_1, down_1)
     side, *outs, attn_sum_1 = run_attend_back(1, grad_next, g1)
@@ -1000,10 +1011,10 @@
     grad = [outs[0]] + [order.send(head_swap, outs[k], k) for k in (1, 2, 3)]
     grad = [p.reshape(4, BAND, width) for p in grad]
     move(up_1, down_1)
-    attn_1 = pack("attn", side, kept[1][1], kept[1][3], g1)
+    attn_1 = pack("attn", side, kept[1][1], kept[1][3], g1, halving=False)
     order.close()
 
-    move(attn_1, up_1)
+    move(attn_1)
     g2 = jnp.stack(grad, axis=1).reshape(-1, width)
     down_0 = pack("down", kept[0][7], g2)
     order.close()
@@ -1015,9 +1026,9 @@
     grad_input, attn_sum_0, *parts = run_attend_back(0, grad_next, g1)
     attn_0 = Pack(order, *parts)
     order.close()
-    move(up_0, attn_0, down_0, attn_1, down_1)
+    move(up_0, attn_0, down_0, attn_1, up_1)
     order.close()
-    move(attn_0, up_0, down_0, attn_1, up_1)
+    move(attn_0, up_0, down_0, attn_1)
     order.close()
 
     packed = jnp.concatenate([feed_sum_0, feed_sum_1, attn_sum_0, attn_sum_1, loss_sum], axis=0)
@@ -1028,23 +1039,43 @@
         swap, distance = swaps.pop(0)
         return packed + order.send(swap, packed, distance)
 
-    early = [(up_1, False), (down_1, False), (attn_1, True)]
     ready = {}
-    moving = [attn_0, up_0, down_0, attn_1, up_1, down_1]
-    while swaps or not all(one.done() for one in moving):
-        move(*[one for one in moving if not one.done()])
+
+    def write(one, layer, attention, earlier):
+        ready[one] = order.run(lambda *a: emit(place, layer, attention, a, earlier), *one.whole())
+
+    late = [down_1, up_1]
+    moving = [attn_0, up_0, down_0]
+    wait = 0
+    while swaps or not all(one.done() for one in moving + late + [attn_1]):
+        move(*[one for one in moving + late if not one.done()])
+        if wait:
+            move(*[one for one in [attn_1] if not one.done()])
+        wait += 1
         if swaps:
             packed = pack_step()
-        if early and early[0][0].done():
-            one, attention = early.pop(0)
-            ready[one] = order.run(lambda *a: emit(place, 1, attention, a, None), *one.whole())
+        for one in late:
+            if one.done() and one not in ready:
+                write(one, 1, False, None)
+                break
+        if attn_1.done() and wait > 2 and attn_1 not in ready:
+            write(attn_1, 1, True, None)
+        for one, earlier in ((down_0, down_1), (up_0, up_1)):
+            if one.done() and one not in ready and earlier in ready and one.closed:
+                write(one, 0, False, ready[earlier])
+                break
         order.close()
-    for one, attention in early:
-        ready[one] = emit(place, 1, attention, one.whole(), None)
-
-    attn_out = emit(place, 0, True, attn_0.whole(), ready[attn_1])
-    up_out = emit(place, 0, False, up_0.whole(), ready[up_1])
-    down_out = emit(place, 0, False, down_0.whole(), ready[down_1])
+        for one in moving:
+            one.closed = one.done()
+
+    for one, layer, attention, earlier in (
+        (down_1, 1, False, None), (up_1, 1, False, None), (attn_1, 1, True, None),
+        (down_0, 0, False, down_1), (up_0, 0, False, up_1), (attn_0, 0, True, attn_1),
+    ):
+        if one not in ready:
+            write(one, layer, attention, ready.get(earlier))
+
+    attn_out, up_out, down_out = ready[attn_0], ready[up_0], ready[down_0]
 
     feed_sums = packed[:16].reshape(2, 8, width)
     attn_sums = packed[16:32].reshape(2, 8, width)

time: 575 us -> 553 us (0.962)
  waiting for transfers between devices: 172 us -> 162 us
    ppermute x41 -> x40, waiting for transfers between devices: 69.7 us -> 41.5 us  [head_swap(): lax.ppermute(values, 'head', [(i, i ^ distance) for i in range(count)])]
    all_gather x1, waiting for transfers between devices: 0.02 us -> 11.7 us  [over_clips(): return lax.all_gather(chunk_across, 'clip', axis=0, tiled=True)]
    ppermute x35 -> x33, waiting for transfers between devices: 103 us -> 109 us  [clip_swap(): lax.ppermute(values, 'clip', [(i, i ^ distance) for i in range(count)])]
    ppermute x35 -> x33, starting transfers between devices: 40.3 us -> 36.2 us  [clip_swap(): lax.ppermute(values, 'clip', [(i, i ^ distance) for i in range(count)])]
    ppermute x41 -> x40, starting transfers between devices: 25.4 us -> 23.8 us  [head_swap(): lax.ppermute(values, 'head', [(i, i ^ distance) for i in range(count)])]
  transfers between devices with their start and end apart: 77 -> 74, of which waited for: 34 -> 31; matrix products, arithmetic and copies ran while one was open for 3% -> 4% of each run, Pallas kernels for 41% -> 42%
where the time goes in v4:
time: 553 us; the launch traced here: 550 us
  Pallas kernels  254 us (46%)
  waiting for transfers between devices  162 us (29%)
  starting transfers between devices  60 us (11%)
  other arithmetic  31.8 us (6%)
  local copies, waits for them, and re-layouts  23.7 us (4%)
  between operations  18.2 us (3%)
    pallas_call x17, Pallas kernels, call(): pl.pallas_call(kernel, grid_spec=pltpu.PrefetchScalarGridSpec(num_scalar_...  254 us
    ppermute x33, waiting for transfers between devices, clip_swap(): lax.ppermute(values, 'clip', [(i, i ^ distance) for i in range(count)])  109 us
    ppermute x40, waiting for transfers between devices, head_swap(): lax.ppermute(values, 'head', [(i, i ^ distance) for i in range(count)])  41.5 us
    ppermute x33, starting transfers between devices, clip_swap(): lax.ppermute(values, 'clip', [(i, i ^ distance) for i in range(count)])  36.2 us
    ppermute x40, starting transfers between devices, head_swap(): lax.ppermute(values, 'head', [(i, i ^ distance) for i in range(count)])  23.8 us
    all_gather x1, waiting for transfers between devices, over_clips(): return lax.all_gather(chunk_across, 'clip', axis=0, tiled=True)  11.7 us
  transfers between devices with their start and end apart: 74, of which 31 were waited for; matrix products, arithmetic and copies ran while one was open for 4% of the time, Pallas kernels for 42%

profile of v4, /device:TPU:0, one launch (start us, length us, event | category | flops | bytes accessed | tf_op | source)
XLA Modules:
  0.0 549.7 jit_solution(1831769097558426848)
XLA Ops:
  7.2 2.8 fusion.7
  10.0 2.8 fusion.8
  12.9 3.0 collective-permute-start
  16.6 2.5 fusion.9
  19.1 10.3 %collective-permute-done = bf16[384,768]{1,0:T(8,128)(2,1)S(1)} collective-permute-done((bf16[384,768]{1,0:T(8,128)(2,1)S(1)}, bf16[384,768]{1,0:T(8,128)(2,1)S(1)}, u32[]{:S(2)}, u32[]{:S(2)}) %collective-permute-start) | collective-permute-done | bytes 589856 | tf_op jit(solution)/shard_map/ppermute | solution.py:728
  34.9 8.9 %collective-permute-done.3 = bf16[384,768]{1,0:T(8,128)(2,1)S(1)} collective-permute-done((bf16[384,768]{1,0:T(8,128)(2,1)S(1)}, bf16[384,768]{1,0:T(8,128)(2,1)S(1)}, u32[]{:S(2)}, u32[]{:S(2)}) %collective-permute-start.3) | collective-permute-done | bytes 589856 | tf_op jit(solution)/shard_map/ppermute | solution.py:733
  48.3 9.1 %collective-permute-done.4 = bf16[384,768]{1,0:T(8,128)(2,1)S(1)} collective-permute-done((bf16[384,768]{1,0:T(8,128)(2,1)S(1)}, bf16[384,768]{1,0:T(8,128)(2,1)S(1)}, u32[]{:S(2)}, u32[]{:S(2)}) %collective-permute-start.4) | collective-permute-done | bytes 589856 | tf_op jit(solution)/shard_map/ppermute | solution.py:733
  57.4 2.4 collective-permute-done.2.refs_10_.refs_4_.refs_8_
  60.4 2.3 collective-permute-done.5.refs_5_.refs_10_.refs_7_
  68.1 17.7 %attend.2 = (bf16[1024,768]{1,0:T(8,128)(2,1)}, bf16[1024,768]{1,0:T(8,128)(2,1)}, bf16[1024,2304]{1,0:T(8,128)(2,1)}, bf16[1024,768]{1,0:T(8,128)(2,1)}, f32[64...) custom-call(s32[3]{0:T(128)} %pad_add_fusion.place_ref, ...), custom_call_target="tpu_custom_call" | custom-call | flops 1955000 | bytes 6120 | tf_op jit(solution)/shard_map/attend/pallas_call | solution.py:254
  95.0 23.3 %feed.2 = (f32[1024,768]{1,0:T(8,128)}, bf16[1024,768]{1,0:T(8,128)(2,1)}, bf16[1024,3072]{1,0:T(8,128)(2,1)}, bf16[1024,3072]{1,0:T(8,128)(2,1)}, bf16[4,64,768...) custom-call(s32[3]{0:T(128)} %pad_add_fusion.place_ref, ...), custom_call_target="tpu_custom_call" | custom-call | flops 2645000 | bytes 8280 | tf_op jit(solution)/shard_map/feed/pallas_call | solution.py:254
  118.2 3.7 collective-permute-done.15.refs_12_.refs_4_.refs_8_
  124.6 11.7 %all-gather.2.cloned.1.call-done = bf16[1536,768]{1,0:T(8,128)(2,1)} async-done(((bf16[192,768]{1,0:T(8,128)(2,1)}), bf16[1536,768]{1,0:T(8,128)(2,1)}) %all-gather.2.cloned.1.call-update) | async-done | bytes 2359312 | tf_op jit(solution)/shard_map/all_gather | solution.py:876
  138.1 4.0 collective-permute-done.17
  144.6 17.2 %attend.3 = (bf16[1024,768]{1,0:T(8,128)(2,1)}, bf16[1024,768]{1,0:T(8,128)(2,1)}, bf16[1024,2304]{1,0:T(8,128)(2,1)}, bf16[1024,768]{1,0:T(8,128)(2,1)}, f32[64...) custom-call(s32[3]{0:T(128)} %pad_add_fusion.place_ref, bf16[4,4,16,768]{3,2,1,0:T(8,128)(2,1)} %bitcast.93, ...), custom_call_target="tpu_custom_call" | custom-call | flops 1955000 | bytes 6120 | tf_op jit(solution)/shard_map/attend/pallas_call | solution.py:254
  163.3 23.5 %feed.3 = (f32[1024,768]{1,0:T(8,128)}, bf16[1024,768]{1,0:T(8,128)(2,1)}, bf16[1024,3072]{1,0:T(8,128)(2,1)}, bf16[1024,3072]{1,0:T(8,128)(2,1)}, bf16[1024,768]{1,0:T(8,128)(2,1)}) custom-call(s32[3]{0:T(128)} %pad_add_fusion.place_ref, bf16[1024,768]{1,0:T(8,128)(2,1)} %get-tuple-element.295.refs_0_.refs_2_, ...), custom_call_target="tpu_custom_call" | custom-call | flops 2645000 | bytes 8280 | tf_op jit(solution)/shard_map/feed/pallas_call | solution.py:254
  187.4 17.9 %code_loss.1 = (f32[1024,768]{1,0:T(8,128)}, f32[8,768]{1,0:T(8,128)}, bf16[2,768,768]{2,1,0:T(8,128)(2,1)}, bf16[2,768,768]{2,1,0:T(8,128)(2,1)}) custom-call(s32[3]{0:T(128)} %pad_add_fusion.place_ref, bf16[1024,768]{1,0:T(8,128)(2,1)} %get-tuple-element.299.final_ref, bf16[768,1024]{1,0:T(8,128)(2,1)} %head_ref.1, f32[4,64]{1,0:T(4,128)} %get-tuple-element.300.m0, ...), custom_call_target="tpu_custom_call" | custom-call | flops 1150000 | bytes 3600 | tf_op jit(solution)/shard_map/code_loss/pallas_call | solution.py:254
  205.6 4.4 collective-permute-done.26
  210.0 2.5 fusion
  213.1 27.0 %feed_back.2 = (f32[1024,768]{1,0:T(8,128)}, bf16[1024,768]{1,0:T(8,128)(2,1)}, f32[8,768]{1,0:T(8,128)}, bf16[2,768,768]{2,1,0:T(8,128)(2,1)}, bf16[2,768,768]{2,1,0:T(8,128)(2,1)}) custom-call(s32[3]{0:T(128)} %pad_add_fusion.place_ref, f32[1024,768]{1,0:T(8,128)} %get-tuple-element.311.refs_0_, bf16[1024,3072]{1,0:T(8,128)(2,1)} %get-tuple-element.312.refs_1_, ...), custom_call_target="tpu_custom_call" | custom-call | flops 2415000 | bytes 7560 | tf_op jit(solution)/shard_map/feed_back/pallas_call | solution.py:254
  247.3 24.5 %attend_back.2 = (bf16[4,1024,576]{2,1,0:T(8,128)(2,1)}, bf16[4,4,16,768]{3,2,1,0:T(8,128)(2,1)}, bf16[4,4,16,768]{3,2,1,0:T(8,128)(2,1)}, bf16[4,4,16,768]{3,2,...) custom-call(s32[3]{0:T(128)} %pad_add_fusion.place_ref, f32[1024,768]{1,0:T(8,128)} %get-tuple-element.325.refs_0_, ...), custom_call_target="tpu_custom_call" | custom-call | flops 2875000 | bytes 9000 | tf_op jit(solution)/shard_map/attend_back/pallas_call | solution.py:254
  277.5 11.2 %grads_attn.1 = (bf16[2,768,768]{2,1,0:T(8,128)(2,1)}, bf16[2,768,768]{2,1,0:T(8,128)(2,1)}) custom-call(s32[3]{0:T(128)} %pad_add_fusion.place_ref, bf16[4,1024,576]{2,1,0:T(8,128)(2,1)} %get-tuple-element.348.refs_0_, bf16[1024,768]{1,0:T(8,128)(2,1)} %get-tuple-element.349.refs_1_, bf16[4,1024,192]{2,1,0:T(8,128)(2,1)} %get-tuple-element.350.refs_2_, ...), custom_call_target="tpu_custom_call" | custom-call | flops 920000 | bytes 2880 | tf_op jit(solution)/shard_map/grads_attn/pallas_call | solution.py:254
  288.7 6.4 %collective-permute-done.33 = bf16[4,4,16,768]{3,2,1,0:T(8,128)(2,1)S(1)} collective-permute-done((bf16[4,4,16,768]{3,2,1,0:T(8,128)(2,1)S(1)}, bf16[4,4,16,768]{3,2,1,0:T(8,128)(2,1)S(1)}, u32[]{:S(2)}, u32[]{:S(2)}) %collective-permute-start.33) | collective-permute-done | bytes 393248 | tf_op jit(solution)/shard_map/ppermute | solution.py:728
  296.7 10.7 %grads_down.1 = (bf16[2,768,768]{2,1,0:T(8,128)(2,1)}, bf16[2,768,768]{2,1,0:T(8,128)(2,1)}) custom-call(s32[3]{0:T(128)} %pad_add_fusion.place_ref, bf16[1024,3072]{1,0:T(8,128)(2,1)} %get-tuple-element.356.refs_0_, bf16[1024,768]{1,0:T(8,128)(2,1)} %bitcast.81), custom_call_target="tpu_custom_call" | custom-call | flops 920000 | bytes 2880 | tf_op jit(solution)/shard_map/grads_down/pallas_call | solution.py:254
  310.8 2.6 collective-permute-start.38
  313.4 26.8 %feed_back.3 = (f32[1024,768]{1,0:T(8,128)}, bf16[1024,768]{1,0:T(8,128)(2,1)}, f32[8,768]{1,0:T(8,128)}, bf16[2,768,768]{2,1,0:T(8,128)(2,1)}, bf16[2,768,768]{2,1,0:T(8,128)(2,1)}) custom-call(s32[3]{0:T(128)} %pad_add_fusion.place_ref, bf16[1024,768]{1,0:T(8,128)(2,1)} %bitcast.82, bf16[1024,3072]{1,0:T(8,128)(2,1)} %get-tuple-element.366.refs_1_, ...), custom_call_target="tpu_custom_call" | custom-call | flops 2415000 | bytes 7560 | tf_op jit(solution)/shard_map/feed_back/pallas_call | solution.py:254
  350.2 32.5 %attend_back.3 = (f32[1024,768]{1,0:T(8,128)}, f32[8,768]{1,0:T(8,128)}, bf16[2,768,768]{2,1,0:T(8,128)(2,1)}, bf16[2,768,768]{2,1,0:T(8,128)(2,1)}) custom-call(s32[3]{0:T(128)} %pad_add_fusion.place_ref, f32[1024,768]{1,0:T(8,128)} %get-tuple-element.386.refs_0_, bf16[1024,768]{1,0:T(8,128)(2,1)} %get-tuple-element.387.refs_1_, ...), custom_call_target="tpu_custom_call" | custom-call | flops 2875000 | bytes 9000 | tf_op jit(solution)/shard_map/attend_back/pallas_call | solution.py:254
  384.6 2.0 bitcast_add_fusion.2
  394.1 12.6 %collective-permute-done.46 = bf16[384,768]{1,0:T(8,128)(2,1)S(1)} collective-permute-done((bf16[384,768]{1,0:T(8,128)(2,1)S(1)}, bf16[384,768]{1,0:T(8,128)(2,1)S(1)}, u32[]{:S(2)}, u32[]{:S(2)}) %collective-permute-start.46) | collective-permute-done | bytes 589856 | tf_op jit(solution)/shard_map/ppermute | solution.py:733
  407.2 11.4 %collective-permute-done.50.other_ref = bf16[384,768]{1,0:T(8,128)(2,1)S(1)} collective-permute-done((bf16[384,768]{1,0:T(8,128)(2,1)S(1)}, bf16[384,768]{1,0:T(8,128)(2,1)S(1)}, u32[]{:S(2)}, u32[]{:S(2)}) %collective-permute-start.50) | collective-permute-done | bytes 589856 | tf_op jit(solution)/shard_map/ppermute | solution.py:733
  424.3 2.6 collective-permute-start.54
  427.4 17.4 %collective-permute-done.51 = bf16[192,768]{1,0:T(8,128)(2,1)S(1)} collective-permute-done((bf16[192,768]{1,0:T(8,128)(2,1)S(1)}, bf16[192,768]{1,0:T(8,128)(2,1)S(1)}, u32[]{:S(2)}, u32[]{:S(2)}) %collective-permute-start.51) | collective-permute-done | bytes 294944 | tf_op jit(solution)/shard_map/ppermute | solution.py:733
  444.8 7.1 %collective-permute-done.54 = bf16[384,768]{1,0:T(8,128)(2,1)S(1)} collective-permute-done((bf16[384,768]{1,0:T(8,128)(2,1)S(1)}, bf16[384,768]{1,0:T(8,128)(2,1)S(1)}, u32[]{:S(2)}, u32[]{:S(2)}) %collective-permute-start.54) | collective-permute-done | bytes 589856 | tf_op jit(solution)/shard_map/ppermute | solution.py:733
  454.1 2.4 collective-permute-start.57
  456.6 3.6 emit.6.refs_0_
  460.2 8.3 %collective-permute-done.56 = bf16[192,768]{1,0:T(8,128)(2,1)S(1)} collective-permute-done((bf16[192,768]{1,0:T(8,128)(2,1)S(1)}, bf16[192,768]{1,0:T(8,128)(2,1)S(1)}, u32[]{:S(2)}, u32[]{:S(2)}) %collective-permute-start.56) | collective-permute-done | bytes 294944 | tf_op jit(solution)/shard_map/ppermute | solution.py:733
  470.5 2.1 collective-permute-start.61
  473.9 3.6 emit.7.refs_0_
  477.8 8.5 %collective-permute-done.60 = bf16[192,768]{1,0:T(8,128)(2,1)S(1)} collective-permute-done((bf16[192,768]{1,0:T(8,128)(2,1)S(1)}, bf16[192,768]{1,0:T(8,128)(2,1)S(1)}, u32[]{:S(2)}, u32[]{:S(2)}) %collective-permute-start.60) | collective-permute-done | bytes 294944 | tf_op jit(solution)/shard_map/ppermute | solution.py:733
  486.3 5.3 collective-permute-done.62
  496.5 3.5 emit.8
  500.1 9.4 %collective-permute-done.64 = f32[40,768]{1,0:T(8,128)S(1)} collective-permute-done((f32[40,768]{1,0:T(8,128)S(1)}, f32[40,768]{1,0:T(8,128)S(1)}, u32[]{:S(2)}, u32[]{:S(2)}) %collective-permute-start.64) | collective-permute-done | bytes 122912 | tf_op jit(solution)/shard_map/ppermute | solution.py:733
  513.1 3.6 emit.9
  516.7 3.7 collective-permute-done.68
  520.5 3.2 collective-permute-done.70.other_ref
  525.2 3.6 emit.10
  528.8 2.2 collective-permute-done.71
  537.7 3.5 emit.11
  (349 shorter events, 100.6 us)
Async XLA Ops:
  7.2 129.1 %all-gather.2.cloned.1.call-start = ((), (), s32[]{:S(2)}) async-start(), calls=%async_computation | async-start | bytes 2654208 | tf_op jit(solution)/shard_map/all_gather | solution.py:876
  12.9 16.5 %collective-permute-start = (bf16[384,768]{1,0:T(8,128)(2,1)S(1)}, bf16[384,768]{1,0:T(8,128)(2,1)S(1)}, u32[]{:S(2)}, u32[]{:S(2)}) collective-permute-start(bf16[384,768]{1,0:T(8,128)(2,1)S(1)} %pad_maximum_fusion.5), channel_id=1, source_target_pairs={{0,2},{1,3},{2,0},{3,1},{4,6},{5,7},{6,4},{7,5},{8,10},{9,11},{10,... | collective-permute-start | bytes 1769480 | tf_op jit(solution)/shard_map/ppermute | solution.py:728
  16.0 17.3 %collective-permute-start.1 = (f32[3,768]{1,0:T(4,128)S(1)}, f32[3,768]{1,0:T(4,128)}, u32[]{:S(2)}, u32[]{:S(2)}) collective-permute-start(f32[3,768]{1,0:T(4,128)S(1)} %pad_maximum_fusion.12.refs_4_.refs_9_.refs_6_), channel_id=1, source_target_pairs={{0,2},{1,3},{2,0},{3,1},{4,6},{5,7},{6,4},{7,5},{8,10},{9,11},{10,... | collective-permute-start | bytes 27656 | tf_op jit(solution)/shard_map/ppermute | solution.py:728
  33.4 26.4 %collective-permute-start.2 = (bf16[768,768]{1,0:T(8,128)(2,1)S(1)}, bf16[768,768]{1,0:T(8,128)(2,1)S(1)}, u32[]{:S(2)}, u32[]{:S(2)}) collective-permute-start(bf16[768,768]{1,0:T(8,128)(2,1)S(1)} %pad_maximum_fusion.1.refs_8_.refs_2_.refs_6_), channel_id=1, source_target_pairs={{0,2},{1,3},{2,0},{3,1},{4,6},{5,7},{6,4},{7,5},{8,10},{9,11},{10,... | collective-permute-start | bytes 3538952 | tf_op jit(solution)/shard_map/ppermute | solution.py:728
  62.9 23.0 %collective-permute-start.11 = (bf16[2,768,768]{2,1,0:T(8,128)(2,1)S(1)}, bf16[2,768,768]{2,1,0:T(8,128)(2,1)}, u32[]{:S(2)}, u32[]{:S(2)}) collective-permute-start(bf16[2,768,768]{2,1,0:T(8,128)(2,1)S(1)} %copy-done), channel_id=1, source_target_pairs={{0,1},{1,0},{2,3},{3,2},{4,5},{5,4},{6,7},{7,6},{8,9},{9,8},{10,11... | collective-permute-start | bytes 7077896 | tf_op jit(solution)/shard_map/ppermute | solution.py:728
  63.1 22.8 %collective-permute-start.12 = (bf16[2,768,768]{2,1,0:T(8,128)(2,1)}, bf16[2,768,768]{2,1,0:T(8,128)(2,1)}, u32[]{:S(2)}, u32[]{:S(2)}) collective-permute-start(bf16[2,768,768]{2,1,0:T(8,128)(2,1)} %refs_9_.3), channel_id=1, source_target_pairs={{0,1},{1,0},{2,3},{3,2},{4,5},{5,4},{6,7},{7,6},{8,9},{9,8},{10,11... | collective-permute-start | bytes 7077896 | tf_op jit(solution)/shard_map/ppermute | solution.py:728
  63.9 22.0 %collective-permute-start.9 = (bf16[384,768]{1,0:T(8,128)(2,1)}, bf16[384,768]{1,0:T(8,128)(2,1)}, u32[]{:S(2)}, u32[]{:S(2)}) collective-permute-start(bf16[384,768]{1,0:T(8,128)(2,1)} %pad_maximum_fusion.7), channel_id=1, source_target_pairs={{0,8},{4,12},{8,0},{12,4},{16,24},{20,28},{24,16},{28,20},{1,9},{5... | collective-permute-start | bytes 1769480 | tf_op jit(solution)/shard_map/ppermute | solution.py:733
  65.5 20.3 %collective-permute-start.10 = (bf16[192,768]{1,0:T(8,128)(2,1)}, bf16[192,768]{1,0:T(8,128)(2,1)}, u32[]{:S(2)}, u32[]{:S(2)}) collective-permute-start(bf16[192,768]{1,0:T(8,128)(2,1)} %pad_maximum_fusion.11), channel_id=1, source_target_pairs={{0,2},{1,3},{2,0},{3,1},{4,6},{5,7},{6,4},{7,5},{8,10},{9,11},{10,... | collective-permute-start | bytes 884744 | tf_op jit(solution)/shard_map/ppermute | solution.py:728
  93.9 28.0 %collective-permute-start.15 = (bf16[768,768]{1,0:T(8,128)(2,1)S(1)}, bf16[768,768]{1,0:T(8,128)(2,1)S(1)}, u32[]{:S(2)}, u32[]{:S(2)}) collective-permute-start(bf16[768,768]{1,0:T(8,128)(2,1)S(1)} %pad_maximum_fusion.4.refs_10_.refs_2_.refs_6_), channel_id=1, source_target_pairs={{0,2},{1,3},{2,0},{3,1},{4,6},{5,7},{6,4},{7,5},{8,10},{9,11},{10,... | collective-permute-start | bytes 3538952 | tf_op jit(solution)/shard_map/ppermute | solution.py:728
  121.9 20.2 %collective-permute-start.19 = (bf16[768,768]{1,0:T(8,128)(2,1)S(1)}, bf16[768,768]{1,0:T(8,128)(2,1)S(1)}, u32[]{:S(2)}, u32[]{:S(2)}) collective-permute-start(bf16[768,768]{1,0:T(8,128)(2,1)S(1)} %collective-permute-done.15.refs_12_.refs_4_.refs_8_), channel_id=1, source_target_pairs={{0,1},{1,0},{2,3},{3,2},{4,5},{5,4},{6,7},{7,6},{8,9},{9,8},{10,11... | collective-permute-start | bytes 3538952 | tf_op jit(solution)/shard_map/ppermute | solution.py:728
  121.9 16.2 %collective-permute-start.18 = (bf16[4,64,768]{2,1,0:T(8,128)(2,1)}, bf16[4,64,768]{2,1,0:T(8,128)(2,1)}, u32[]{:S(2)}, u32[]{:S(2)}) collective-permute-start(bf16[4,64,768]{2,1,0:T(8,128)(2,1)} %get-tuple-element.284), channel_id=1, source_target_pairs={{0,3},{1,2},{2,1},{3,0},{4,7},{5,6},{6,5},{7,4},{8,11},{9,10},{10,... | collective-permute-start | bytes 1179656 | tf_op jit(solution)/shard_map/ppermute | solution.py:728
  122.6 19.5 %collective-permute-start.17 = (bf16[4,64,768]{2,1,0:T(8,128)(2,1)}, bf16[4,64,768]{2,1,0:T(8,128)(2,1)}, u32[]{:S(2)}, u32[]{:S(2)}) collective-permute-start(bf16[4,64,768]{2,1,0:T(8,128)(2,1)} %get-tuple-element.282), channel_id=1, source_target_pairs={{0,2},{1,3},{2,0},{3,1},{4,6},{5,7},{6,4},{7,5},{8,10},{9,11},{10,... | collective-permute-start | bytes 1179656 | tf_op jit(solution)/shard_map/ppermute | solution.py:728
  124.1 18.0 %collective-permute-start.16 = (bf16[4,64,768]{2,1,0:T(8,128)(2,1)}, bf16[4,64,768]{2,1,0:T(8,128)(2,1)}, u32[]{:S(2)}, u32[]{:S(2)}) collective-permute-start(bf16[4,64,768]{2,1,0:T(8,128)(2,1)} %get-tuple-element.280), channel_id=1, source_target_pairs={{0,1},{1,0},{2,3},{3,2},{4,5},{5,4},{6,7},{7,6},{8,9},{9,8},{10,11... | collective-permute-start | bytes 1179656 | tf_op jit(solution)/shard_map/ppermute | solution.py:728
  124.1 19.2 %collective-permute-start.20 = (bf16[768,768]{1,0:T(8,128)(2,1)S(1)}, bf16[768,768]{1,0:T(8,128)(2,1)}, u32[]{:S(2)}, u32[]{:S(2)}) collective-permute-start(bf16[768,768]{1,0:T(8,128)(2,1)S(1)} %pad_maximum_fusion.4.refs_10_.refs_2_.refs_6_), channel_id=1, source_target_pairs={{0,1},{1,0},{2,3},{3,2},{4,5},{5,4},{6,7},{7,6},{8,9},{9,8},{10,11... | collective-permute-start | bytes 3538952 | tf_op jit(solution)/shard_map/ppermute | solution.py:728
  142.1 19.7 %collective-permute-start.21 = (bf16[768,768]{1,0:T(8,128)(2,1)S(1)}, bf16[768,768]{1,0:T(8,128)(2,1)S(1)}, u32[]{:S(2)}, u32[]{:S(2)}) collective-permute-start(bf16[768,768]{1,0:T(8,128)(2,1)S(1)} %bitcast.86), channel_id=1, source_target_pairs={{0,1},{1,0},{2,3},{3,2},{4,5},{5,4},{6,7},{7,6},{8,9},{9,8},{10,11... | collective-permute-start | bytes 3538952 | tf_op jit(solution)/shard_map/ppermute | solution.py:728
  142.2 19.6 %collective-permute-start.22 = (bf16[768,768]{1,0:T(8,128)(2,1)S(1)}, bf16[768,768]{1,0:T(8,128)(2,1)S(1)}, u32[]{:S(2)}, u32[]{:S(2)}) collective-permute-start(bf16[768,768]{1,0:T(8,128)(2,1)S(1)} %bitcast.83), channel_id=1, source_target_pairs={{0,1},{1,0},{2,3},{3,2},{4,5},{5,4},{6,7},{7,6},{8,9},{9,8},{10,11... | collective-permute-start | bytes 3538952 | tf_op jit(solution)/shard_map/ppermute | solution.py:728
  142.7 44.1 %collective-permute-start.23 = (f32[4,64]{1,0:T(4,128)S(1)}, f32[4,64]{1,0:T(4,128)S(1)}, u32[]{:S(2)}, u32[]{:S(2)}) collective-permute-start(f32[4,64]{1,0:T(4,128)S(1)} %copy-done.68), channel_id=1, source_target_pairs={{0,1},{1,0},{2,3},{3,2},{4,5},{5,4},{6,7},{7,6},{8,9},{9,8},{10,11... | collective-permute-start | bytes 3080 | tf_op jit(solution)/shard_map/ppermute | solution.py:728
  142.8 44.0 %collective-permute-start.24 = (f32[4,64]{1,0:T(4,128)S(1)}, f32[4,64]{1,0:T(4,128)S(1)}, u32[]{:S(2)}, u32[]{:S(2)}) collective-permute-start(f32[4,64]{1,0:T(4,128)S(1)} %copy-done.67), channel_id=1, source_target_pairs={{0,2},{1,3},{2,0},{3,1},{4,6},{5,7},{6,4},{7,5},{8,10},{9,11},{10,... | collective-permute-start | bytes 3080 | tf_op jit(solution)/shard_map/ppermute | solution.py:728
  143.3 43.5 %collective-permute-start.25 = (f32[4,64]{1,0:T(4,128)S(1)}, f32[4,64]{1,0:T(4,128)S(1)}, u32[]{:S(2)}, u32[]{:S(2)}) collective-permute-start(f32[4,64]{1,0:T(4,128)S(1)} %copy-done.66), channel_id=1, source_target_pairs={{0,3},{1,2},{2,1},{3,0},{4,7},{5,6},{6,5},{7,4},{8,11},{9,10},{10,... | collective-permute-start | bytes 3080 | tf_op jit(solution)/shard_map/ppermute | solution.py:728
  212.5 28.3 %collective-permute-start.27 = (bf16[768,768]{1,0:T(8,128)(2,1)S(1)}, bf16[768,768]{1,0:T(8,128)(2,1)S(1)}, u32[]{:S(2)}, u32[]{:S(2)}) collective-permute-start(bf16[768,768]{1,0:T(8,128)(2,1)S(1)} %fusion), channel_id=1, source_target_pairs={{0,2},{1,3},{2,0},{3,1},{4,6},{5,7},{6,4},{7,5},{8,10},{9,11},{10,... | collective-permute-start | bytes 3538952 | tf_op jit(solution)/shard_map/ppermute | solution.py:728
  245.8 28.1 %collective-permute-start.29 = (bf16[768,768]{1,0:T(8,128)(2,1)S(1)}, bf16[768,768]{1,0:T(8,128)(2,1)S(1)}, u32[]{:S(2)}, u32[]{:S(2)}) collective-permute-start(bf16[768,768]{1,0:T(8,128)(2,1)S(1)} %fusion.1), channel_id=1, source_target_pairs={{0,2},{1,3},{2,0},{3,1},{4,6},{5,7},{6,4},{7,5},{8,10},{9,11},{10,... | collective-permute-start | bytes 3538952 | tf_op jit(solution)/shard_map/ppermute | solution.py:728
  246.8 25.0 %collective-permute-start.30 = (bf16[384,768]{1,0:T(8,128)(2,1)}, bf16[384,768]{1,0:T(8,128)(2,1)S(1)}, u32[]{:S(2)}, u32[]{:S(2)}) collective-permute-start(bf16[384,768]{1,0:T(8,128)(2,1)} %get-tuple-element.333), channel_id=1, source_target_pairs={{0,4},{4,0},{8,12},{12,8},{16,20},{20,16},{24,28},{28,24},{1,5},{5... | collective-permute-start | bytes 1769480 | tf_op jit(solution)/shard_map/ppermute | solution.py:733
  274.6 20.5 %collective-permute-start.34 = (bf16[384,768]{1,0:T(8,128)(2,1)S(1)}, bf16[384,768]{1,0:T(8,128)(2,1)S(1)}, u32[]{:S(2)}, u32[]{:S(2)}) collective-permute-start(bf16[384,768]{1,0:T(8,128)(2,1)S(1)} %get-tuple-element.344), channel_id=1, source_target_pairs={{0,4},{4,0},{8,12},{12,8},{16,20},{20,16},{24,28},{28,24},{1,5},{5... | collective-permute-start | bytes 1769480 | tf_op jit(solution)/shard_map/ppermute | solution.py:733
  275.2 20.0 %collective-permute-start.35 = (bf16[384,768]{1,0:T(8,128)(2,1)S(1)}, bf16[384,768]{1,0:T(8,128)(2,1)S(1)}, u32[]{:S(2)}, u32[]{:S(2)}) collective-permute-start(bf16[384,768]{1,0:T(8,128)(2,1)S(1)} %add_convert_fusion.14), channel_id=1, source_target_pairs={{0,8},{4,12},{8,0},{12,4},{16,24},{20,28},{24,16},{28,20},{1,9},{5... | collective-permute-start | bytes 1769480 | tf_op jit(solution)/shard_map/ppermute | solution.py:733
  276.6 18.5 %collective-permute-start.33 = (bf16[4,4,16,768]{3,2,1,0:T(8,128)(2,1)S(1)}, bf16[4,4,16,768]{3,2,1,0:T(8,128)(2,1)S(1)}, u32[]{:S(2)}, u32[]{:S(2)}) collective-permute-start(bf16[4,4,16,768]{3,2,1,0:T(8,128)(2,1)S(1)} %copy-done.63), channel_id=1, source_target_pairs={{0,3},{1,2},{2,1},{3,0},{4,7},{5,6},{6,5},{7,4},{8,11},{9,10},{10,... | collective-permute-start | bytes 1179656 | tf_op jit(solution)/shard_map/ppermute | solution.py:728
  308.0 32.3 %collective-permute-start.40 = (bf16[2,768,768]{2,1,0:T(8,128)(2,1)}, bf16[2,768,768]{2,1,0:T(8,128)(2,1)}, u32[]{:S(2)}, u32[]{:S(2)}) collective-permute-start(bf16[2,768,768]{2,1,0:T(8,128)(2,1)} %get-tuple-element.376), channel_id=1, source_target_pairs={{0,1},{1,0},{2,3},{3,2},{4,5},{5,4},{6,7},{7,6},{8,9},{9,8},{10,11... | collective-permute-start | bytes 7077896 | tf_op jit(solution)/shard_map/ppermute | solution.py:728
  308.3 32.0 %collective-permute-start.39 = (bf16[768,768]{1,0:T(8,128)(2,1)S(1)}, bf16[768,768]{1,0:T(8,128)(2,1)}, u32[]{:S(2)}, u32[]{:S(2)}) collective-permute-start(bf16[768,768]{1,0:T(8,128)(2,1)S(1)} %fusion.2), channel_id=1, source_target_pairs={{0,2},{1,3},{2,0},{3,1},{4,6},{5,7},{6,4},{7,5},{8,10},{9,11},{10,... | collective-permute-start | bytes 3538952 | tf_op jit(solution)/shard_map/ppermute | solution.py:728
  309.2 31.0 %collective-permute-start.37 = (bf16[384,768]{1,0:T(8,128)(2,1)S(1)}, bf16[384,768]{1,0:T(8,128)(2,1)S(1)}, u32[]{:S(2)}, u32[]{:S(2)}) collective-permute-start(bf16[384,768]{1,0:T(8,128)(2,1)S(1)} %add_convert_fusion.12), channel_id=1, source_target_pairs={{0,8},{4,12},{8,0},{12,4},{16,24},{20,28},{24,16},{28,20},{1,9},{5... | collective-permute-start | bytes 1769480 | tf_op jit(solution)/shard_map/ppermute | solution.py:733
  310.8 29.5 %collective-permute-start.38 = (bf16[384,768]{1,0:T(8,128)(2,1)S(1)}, bf16[384,768]{1,0:T(8,128)(2,1)S(1)}, u32[]{:S(2)}, u32[]{:S(2)}) collective-permute-start(bf16[384,768]{1,0:T(8,128)(2,1)S(1)} %add_convert_fusion.13), channel_id=1, source_target_pairs={{0,16},{4,20},{8,24},{12,28},{16,0},{20,4},{24,8},{28,12},{1,17},{... | collective-permute-start | bytes 1769480 | tf_op jit(solution)/shard_map/ppermute | solution.py:733
  346.6 36.2 %collective-permute-start.42 = (bf16[2,768,768]{2,1,0:T(8,128)(2,1)}, bf16[2,768,768]{2,1,0:T(8,128)(2,1)}, u32[]{:S(2)}, u32[]{:S(2)}) collective-permute-start(bf16[2,768,768]{2,1,0:T(8,128)(2,1)} %get-tuple-element.398), channel_id=1, source_target_pairs={{0,1},{1,0},{2,3},{3,2},{4,5},{5,4},{6,7},{7,6},{8,9},{9,8},{10,11... | collective-permute-start | bytes 7077896 | tf_op jit(solution)/shard_map/ppermute | solution.py:728
  346.7 36.1 %collective-permute-start.41 = (bf16[768,768]{1,0:T(8,128)(2,1)S(1)}, bf16[768,768]{1,0:T(8,128)(2,1)}, u32[]{:S(2)}, u32[]{:S(2)}) collective-permute-start(bf16[768,768]{1,0:T(8,128)(2,1)S(1)} %fusion.3), channel_id=1, source_target_pairs={{0,2},{1,3},{2,0},{3,1},{4,6},{5,7},{6,4},{7,5},{8,10},{9,11},{10,... | collective-permute-start | bytes 3538952 | tf_op jit(solution)/shard_map/ppermute | solution.py:728
  347.8 34.9 %collective-permute-start.43 = (bf16[384,768]{1,0:T(8,128)(2,1)}, bf16[384,768]{1,0:T(8,128)(2,1)}, u32[]{:S(2)}, u32[]{:S(2)}) collective-permute-start(bf16[384,768]{1,0:T(8,128)(2,1)} %get-tuple-element.400), channel_id=1, source_target_pairs={{0,4},{4,0},{8,12},{12,8},{16,20},{20,16},{24,28},{28,24},{1,5},{5... | collective-permute-start | bytes 1769480 | tf_op jit(solution)/shard_map/ppermute | solution.py:733
  349.4 33.4 %collective-permute-start.44 = (bf16[384,768]{1,0:T(8,128)(2,1)S(1)}, bf16[384,768]{1,0:T(8,128)(2,1)S(1)}, u32[]{:S(2)}, u32[]{:S(2)}) collective-permute-start(bf16[384,768]{1,0:T(8,128)(2,1)S(1)} %add_convert_fusion.11.mine_ref), channel_id=1, source_target_pairs={{0,4},{4,0},{8,12},{12,8},{16,20},{20,16},{24,28},{28,24},{1,5},{5... | collective-permute-start | bytes 1769480 | tf_op jit(solution)/shard_map/ppermute | solution.py:733
  349.9 32.9 %collective-permute-start.45 = (bf16[384,768]{1,0:T(8,128)(2,1)S(1)}, bf16[384,768]{1,0:T(8,128)(2,1)}, u32[]{:S(2)}, u32[]{:S(2)}) collective-permute-start(bf16[384,768]{1,0:T(8,128)(2,1)S(1)} %add_convert_fusion.10), channel_id=1, source_target_pairs={{0,16},{4,20},{8,24},{12,28},{16,0},{20,4},{24,8},{28,12},{1,17},{... | collective-permute-start | bytes 1769480 | tf_op jit(solution)/shard_map/ppermute | solution.py:733
  389.4 29.1 %collective-permute-start.48 = (bf16[2,768,768]{2,1,0:T(8,128)(2,1)S(1)}, bf16[2,768,768]{2,1,0:T(8,128)(2,1)S(1)}, u32[]{:S(2)}, u32[]{:S(2)}) collective-permute-start(bf16[2,768,768]{2,1,0:T(8,128)(2,1)S(1)} %copy-done.62), channel_id=1, source_target_pairs={{0,1},{1,0},{2,3},{3,2},{4,5},{5,4},{6,7},{7,6},{8,9},{9,8},{10,11... | collective-permute-start | bytes 7077896 | tf_op jit(solution)/shard_map/ppermute | solution.py:728
  389.5 29.0 %collective-permute-start.47 = (bf16[768,768]{1,0:T(8,128)(2,1)S(1)}, bf16[768,768]{1,0:T(8,128)(2,1)S(1)}, u32[]{:S(2)}, u32[]{:S(2)}) collective-permute-start(bf16[768,768]{1,0:T(8,128)(2,1)S(1)} %fusion.4), channel_id=1, source_target_pairs={{0,2},{1,3},{2,0},{3,1},{4,6},{5,7},{6,4},{7,5},{8,10},{9,11},{10,... | collective-permute-start | bytes 3538952 | tf_op jit(solution)/shard_map/ppermute | solution.py:728
  390.5 16.2 %collective-permute-start.46 = (bf16[384,768]{1,0:T(8,128)(2,1)S(1)}, bf16[384,768]{1,0:T(8,128)(2,1)S(1)}, u32[]{:S(2)}, u32[]{:S(2)}) collective-permute-start(bf16[384,768]{1,0:T(8,128)(2,1)S(1)} %get-tuple-element.412), channel_id=1, source_target_pairs={{0,4},{4,0},{8,12},{12,8},{16,20},{20,16},{24,28},{28,24},{1,5},{5... | collective-permute-start | bytes 1769480 | tf_op jit(solution)/shard_map/ppermute | solution.py:733
  393.6 24.9 %collective-permute-start.50 = (bf16[384,768]{1,0:T(8,128)(2,1)S(1)}, bf16[384,768]{1,0:T(8,128)(2,1)S(1)}, u32[]{:S(2)}, u32[]{:S(2)}) collective-permute-start(bf16[384,768]{1,0:T(8,128)(2,1)S(1)} %add_convert_fusion.8.mine_ref), channel_id=1, source_target_pairs={{0,4},{4,0},{8,12},{12,8},{16,20},{20,16},{24,28},{28,24},{1,5},{5... | collective-permute-start | bytes 1769480 | tf_op jit(solution)/shard_map/ppermute | solution.py:733
  421.6 30.3 %collective-permute-start.53 = (bf16[768,768]{1,0:T(8,128)(2,1)S(1)}, bf16[768,768]{1,0:T(8,128)(2,1)S(1)}, u32[]{:S(2)}, u32[]{:S(2)}) collective-permute-start(bf16[768,768]{1,0:T(8,128)(2,1)S(1)} %fusion.5), channel_id=1, source_target_pairs={{0,2},{1,3},{2,0},{3,1},{4,6},{5,7},{6,4},{7,5},{8,10},{9,11},{10,... | collective-permute-start | bytes 3538952 | tf_op jit(solution)/shard_map/ppermute | solution.py:728
  422.8 22.0 %collective-permute-start.52 = (bf16[384,768]{1,0:T(8,128)(2,1)S(1)}, bf16[384,768]{1,0:T(8,128)(2,1)S(1)}, u32[]{:S(2)}, u32[]{:S(2)}) collective-permute-start(bf16[384,768]{1,0:T(8,128)(2,1)S(1)} %get-tuple-element.429), channel_id=1, source_target_pairs={{0,4},{4,0},{8,12},{12,8},{16,20},{20,16},{24,28},{28,24},{1,5},{5... | collective-permute-start | bytes 1769480 | tf_op jit(solution)/shard_map/ppermute | solution.py:733
  424.3 27.5 %collective-permute-start.54 = (bf16[384,768]{1,0:T(8,128)(2,1)S(1)}, bf16[384,768]{1,0:T(8,128)(2,1)S(1)}, u32[]{:S(2)}, u32[]{:S(2)}) collective-permute-start(bf16[384,768]{1,0:T(8,128)(2,1)S(1)} %add_convert_fusion.7), channel_id=1, source_target_pairs={{0,16},{4,20},{8,24},{12,28},{16,0},{20,4},{24,8},{28,12},{1,17},{... | collective-permute-start | bytes 1769480 | tf_op jit(solution)/shard_map/ppermute | solution.py:733
  426.9 17.9 %collective-permute-start.51 = (bf16[192,768]{1,0:T(8,128)(2,1)S(1)}, bf16[192,768]{1,0:T(8,128)(2,1)S(1)}, u32[]{:S(2)}, u32[]{:S(2)}) collective-permute-start(bf16[192,768]{1,0:T(8,128)(2,1)S(1)} %get-tuple-element.428), channel_id=1, source_target_pairs={{0,8},{4,12},{8,0},{12,4},{16,24},{20,28},{24,16},{28,20},{1,9},{5... | collective-permute-start | bytes 884744 | tf_op jit(solution)/shard_map/ppermute | solution.py:733
  452.8 15.8 %collective-permute-start.58 = (bf16[384,768]{1,0:T(8,128)(2,1)S(1)}, bf16[384,768]{1,0:T(8,128)(2,1)S(1)}, u32[]{:S(2)}, u32[]{:S(2)}) collective-permute-start(bf16[384,768]{1,0:T(8,128)(2,1)S(1)} %get-tuple-element.442), channel_id=1, source_target_pairs={{0,4},{4,0},{8,12},{12,8},{16,20},{20,16},{24,28},{28,24},{1,5},{5... | collective-permute-start | bytes 1769480 | tf_op jit(solution)/shard_map/ppermute | solution.py:733
  469.2 22.4 %collective-permute-start.63 = (bf16[384,768]{1,0:T(8,128)(2,1)S(1)}, bf16[384,768]{1,0:T(8,128)(2,1)S(1)}, u32[]{:S(2)}, u32[]{:S(2)}) collective-permute-start(bf16[384,768]{1,0:T(8,128)(2,1)S(1)} %add_convert_fusion.6.mine_ref), channel_id=1, source_target_pairs={{0,4},{4,0},{8,12},{12,8},{16,20},{20,16},{24,28},{28,24},{1,5},{5... | collective-permute-start | bytes 1769480 | tf_op jit(solution)/shard_map/ppermute | solution.py:733
  472.6 19.0 %collective-permute-start.62 = (bf16[192,768]{1,0:T(8,128)(2,1)S(1)}, bf16[192,768]{1,0:T(8,128)(2,1)S(1)}, u32[]{:S(2)}, u32[]{:S(2)}) collective-permute-start(bf16[192,768]{1,0:T(8,128)(2,1)S(1)} %get-tuple-element.456), channel_id=1, source_target_pairs={{0,8},{4,12},{8,0},{12,4},{16,24},{20,28},{24,16},{28,20},{1,9},{5... | collective-permute-start | bytes 884744 | tf_op jit(solution)/shard_map/ppermute | solution.py:733
  492.4 17.0 %collective-permute-start.67 = (bf16[384,768]{1,0:T(8,128)(2,1)S(1)}, bf16[384,768]{1,0:T(8,128)(2,1)S(1)}, u32[]{:S(2)}, u32[]{:S(2)}) collective-permute-start(bf16[384,768]{1,0:T(8,128)(2,1)S(1)} %pad_maximum_fusion.8.mine_ref), channel_id=1, source_target_pairs={{0,4},{4,0},{8,12},{12,8},{16,20},{20,16},{24,28},{28,24},{1,5},{5... | collective-permute-start | bytes 1769480 | tf_op jit(solution)/shard_map/ppermute | solution.py:733
  493.3 16.2 %collective-permute-start.65 = (bf16[192,768]{1,0:T(8,128)(2,1)S(1)}, bf16[192,768]{1,0:T(8,128)(2,1)S(1)}, u32[]{:S(2)}, u32[]{:S(2)}) collective-permute-start(bf16[192,768]{1,0:T(8,128)(2,1)S(1)} %add_convert_fusion.16), channel_id=1, source_target_pairs={{0,8},{4,12},{8,0},{12,4},{16,24},{20,28},{24,16},{28,20},{1,9},{5... | collective-permute-start | bytes 884744 | tf_op jit(solution)/shard_map/ppermute | solution.py:733
  493.6 15.8 %collective-permute-start.66 = (bf16[192,768]{1,0:T(8,128)(2,1)S(1)}, bf16[192,768]{1,0:T(8,128)(2,1)S(1)}, u32[]{:S(2)}, u32[]{:S(2)}) collective-permute-start(bf16[192,768]{1,0:T(8,128)(2,1)S(1)} %add_convert_fusion.17), channel_id=1, source_target_pairs={{0,16},{4,20},{8,24},{12,28},{16,0},{20,4},{24,8},{28,12},{1,17},{... | collective-permute-start | bytes 884744 | tf_op jit(solution)/shard_map/ppermute | solution.py:733
  (95 other events, 816.2 us)
Sparse Core Ops, SparseCore 0:
  86.0 50.2 all-gather.1

commit v5 on v4

--- a/solution.py
+++ b/solution.py
@@ -207,8 +207,11 @@
         assemble_qkv((p0, p1, p2, p3), scratch)
 
     if layer == 0:
-        chosen = shuffle_of(place_ref, 1).astype(f32)
-        marks = jnp.sum(chosen * marks_ref[...], axis=0, keepdims=True)
+        given = marks_ref[pl.ds(pl.program_id(0), 1), :]
+        high = given >> 4
+        both = jnp.concatenate([high, given - 16 * high], axis=0).astype(f32).astype(bf16)
+        both = dot(both, shuffle_of(place_ref, 1))
+        marks = 16.0 * both[0:1] + both[1:2]
         for k in range(4):
             mark_refs[k][pl.ds(pl.program_id(0), 1), :] = marks[:, k * BAND : (k + 1) * BAND]
     x_ref[...] = stream.astype(bf16)
@@ -273,7 +276,7 @@
     rows = 4 * WINDOW
     if layer == 0:
         tokens, marks = inputs
-        first = [(tokens, rows_of(width)), (marks, rows_of(1))]
+        first = [(tokens, rows_of(width)), (marks, whole(marks))]
     else:
         first = [(p, tube_of(width)) for p in inputs]
     operands = first + [(a, whole(a)) for a in (gain, shift, *smalls, *packs)]
@@ -756,8 +759,8 @@
 
 
 def split_halves(total, upper):
-    half = total.shape[0] // 2
-    low, high = total[:half], total[half:]
+    half = total.shape[-2] // 2
+    low, high = total[..., :half, :], total[..., half:, :]
     return jnp.where(upper, low, high).astype(bf16), jnp.where(upper, high, low).astype(bf16)
 
 
@@ -768,8 +771,9 @@
 
 
 class Pack:
-    def __init__(self, order, leaving, staying, halving=True):
+    def __init__(self, order, leaving, staying, halving=True, late=False):
         self.order = order
+        self.late = late
         self.out, self.kept = leaving, staying
         levels = lax.axis_size("clip").bit_length() - 1
         clip = lax.axis_index("clip")
@@ -778,7 +782,10 @@
         down = [("halve", n) for n in range(depth)]
         level = [("all", n) for n in range(depth, levels)]
         up = [("join", n) for n in reversed(range(depth))]
-        self.stages = ["core", "across"] + down + level + up
+        if late:
+            self.stages = ["core"] + down + ["across"] + level + up
+        else:
+            self.stages = ["core", "across"] + down + level + up
         self.at = 0
         self.prepared = False
 
@@ -790,6 +797,20 @@
         run = self.order.run
         if stage == "core":
             self.leaving = self.out
+        elif self.late and stage == "across":
+
+            def parted(total, moved):
+                total = total.astype(f32) + moved.astype(f32)
+                return total[1].astype(bf16), total[0].astype(bf16)
+
+            self.leaving, self.sum = run(parted, self.sum, self.moved)
+        elif self.late and self.at == 1:
+            upper = self.uppers[stage[1]]
+
+            def halved(kept, near):
+                return split_halves(kept.astype(f32) + near.astype(f32), upper)
+
+            self.leaving, self.sum = run(halved, self.kept, self.near)
         elif stage == "across":
             self.leaving = run(
                 lambda kept, near: (kept[1].astype(f32) + near[1].astype(f32)).astype(bf16),
@@ -798,7 +819,7 @@
         else:
             kind, level = stage
             upper = self.uppers[level]
-            if self.at == 2:
+            if self.at == 2 and not self.late:
                 start = lambda kept, near, moved: (
                     kept[0].astype(f32) + near[0].astype(f32) + moved.astype(f32)
                 )
@@ -902,18 +923,18 @@
     def spread(own, across):
         return [own, head_swap(own, 1), across, head_swap(across, 1)]
 
-    quarters = jnp.concatenate([quarter(w_up[0]), quarter(w_down[0])], axis=0)
-    quarters = head_swap(quarters, 2)
+    up_quarter = head_swap(quarter(w_up[0]), 2)
+    down_quarter = head_swap(quarter(w_down[0]), 2)
+    up_quarter, down_quarter, own, own_small = lax.optimization_barrier(
+        (up_quarter, down_quarter, attn_pack(0), own_small)
+    )
     smalls = spread(own_small, head_swap(own_small, 2))
-    own = tied(attn_pack(0), quarters, smalls[2])
     later = jnp.concatenate([chunk(w_up[1]), chunk(w_down[1])], axis=0)
-    marks = (2 * targets + token_mask).astype(f32).reshape(-1, 1)
-    rows = quarters.shape[0] // 2
-    beyond_y = clip_swap(quarters, 1)
-    up_pair = jnp.concatenate([quarters[:rows], beyond_y[:rows]], axis=0)
-    down_pair = jnp.concatenate([quarters[rows:], beyond_y[rows:]], axis=0)
-    across, later, marks, place, up_pair, up_others, down_pair = lax.optimization_barrier(
-        (head_swap(own, 2), later, marks, place, up_pair, clip_swap(up_pair, 2), down_pair)
+    marks = (2 * targets + token_mask).reshape(4, WINDOW)
+    up_pair, down_pair = along_y(up_quarter), along_y(down_quarter)
+    up_x = by_place(up_pair, clip_swap(up_pair, 2))
+    across, later, marks, place, up_x, down_pair = lax.optimization_barrier(
+        (head_swap(own, 2), later, marks, place, up_x, down_pair)
     )
     attn = [spread(own, across), None]
     order.last = (across,)
@@ -922,6 +943,7 @@
     order.last = (smalls[1], smalls[3], attn[0][1], attn[0][3])
     ups = [w_up, order.send(head_swap, w_up, 1)]
     downs = [w_down, order.send(head_swap, w_down, 1)]
+    up_diagonal = order.send(head_swap, up_x, 1)
     packs = [None, None]
 
     def feed_packs(up_x, down_x):
@@ -941,11 +963,8 @@
         if layer == 0:
             gathered = over_clips(tied(chunk_1, x))
             marks = [mark_pieces[0]] + [head_swap(mark_pieces[k], k) for k in (1, 2, 3)]
-            up_x, down_x = order.run(
-                lambda a, b, c, d: (by_place(a, b), by_place(c, d)),
-                up_pair, up_others, down_pair, down_others,
-            )
-            packs[0] = feed_packs(up_x, down_x)
+            down_x = order.run(by_place, down_pair, down_others)
+            packs[0] = (ups, downs, [up_x, up_diagonal], [down_x, order.send(head_swap, down_x, 1)])
             order.close()
             own = attn_pack(1)
             attn_across = order.send(head_swap, own, 2)
@@ -985,9 +1004,9 @@
             grad_next, g1,
         )
 
-    def pack(kind, *arrays, halving=True):
+    def pack(kind, *arrays, **options):
         parts = order.run(lambda *a: grads(kind, place, a, width), *arrays)
-        return Pack(order, *parts, halving=halving)
+        return Pack(order, *parts, **options)
 
     def move(*ones):
         for one in ones:
@@ -1011,24 +1030,35 @@
     grad = [outs[0]] + [order.send(head_swap, outs[k], k) for k in (1, 2, 3)]
     grad = [p.reshape(4, BAND, width) for p in grad]
     move(up_1, down_1)
-    attn_1 = pack("attn", side, kept[1][1], kept[1][3], g1, halving=False)
+    attn_1 = pack("attn", side, kept[1][1], kept[1][3], g1, late=True)
     order.close()
 
     move(attn_1)
     g2 = jnp.stack(grad, axis=1).reshape(-1, width)
     down_0 = pack("down", kept[0][7], g2)
     order.close()
-    move(attn_1, down_0, down_1, up_1)
+    move(down_0)
+    for one in (attn_1, down_1, up_1):
+        one.prepare()
+    order.close()
+    move(down_0, attn_1, down_1, up_1)
     grad_next, g1, feed_sum_0, *parts = run_feed_back(0, g2)
     up_0 = Pack(order, *parts)
     order.close()
-    move(down_0, up_0, attn_1, down_1, up_1)
+    move(up_0)
+    for one in (down_0, attn_1, up_1, down_1):
+        one.prepare()
+    order.close()
+    move(up_0, down_0, attn_1, up_1, down_1)
     grad_input, attn_sum_0, *parts = run_attend_back(0, grad_next, g1)
     attn_0 = Pack(order, *parts)
     order.close()
-    move(up_0, attn_0, down_0, attn_1, up_1)
+    move(attn_0)
+    move(attn_1)
+    for one in (up_0, down_0, up_1):
+        one.prepare()
     order.close()
-    move(attn_0, up_0, down_0, attn_1)
+    move(attn_0, up_0, down_0, attn_1, up_1)
     order.close()
 
     packed = jnp.concatenate([feed_sum_0, feed_sum_1, attn_sum_0, attn_sum_1, loss_sum], axis=0)
@@ -1048,9 +1078,7 @@
     moving = [attn_0, up_0, down_0]
     wait = 0
     while swaps or not all(one.done() for one in moving + late + [attn_1]):
-        move(*[one for one in moving + late if not one.done()])
-        if wait:
-            move(*[one for one in [attn_1] if not one.done()])
+        move(*[one for one in moving + [attn_1] + late if not one.done()])
         wait += 1
         if swaps:
             packed = pack_step()

time: 553 us -> 534 us (0.966)
  waiting for transfers between devices: 162 us -> 130 us
  starting transfers between devices: 60 us -> 69.4 us
    ppermute x33 -> x35, waiting for transfers between devices: 109 us -> 70.2 us  [clip_swap(): lax.ppermute(values, 'clip', [(i, i ^ distance) for i in range(count)])]
    ppermute x33 -> x35, starting transfers between devices: 36.2 us -> 45.4 us  [clip_swap(): lax.ppermute(values, 'clip', [(i, i ^ distance) for i in range(count)])]
    ppermute x40 -> x41, waiting for transfers between devices: 41.5 us -> 45.7 us  [head_swap(): lax.ppermute(values, 'head', [(i, i ^ distance) for i in range(count)])]
    unnamed x144 -> x138, local copies, waits for them, and re-layouts: 9.43 us -> 12.9 us
    ppermute x40 -> x41, starting transfers between devices: 23.8 us -> 24 us  [head_swap(): lax.ppermute(values, 'head', [(i, i ^ distance) for i in range(count)])]
  transfers between devices with their start and end apart: 74 -> 77, of which waited for: 31 -> 32; matrix products, arithmetic and copies ran while one was open for 4% -> 7% of each run, Pallas kernels for 42% -> 44%
where the time goes in v5:
time: 534 us; the launch traced here: 529 us
  Pallas kernels  254 us (48%)
  waiting for transfers between devices  130 us (24%)
  starting transfers between devices  69.4 us (13%)
  other arithmetic  32.6 us (6%)
  local copies, waits for them, and re-layouts  25.5 us (5%)
  between operations  17.8 us (3%)
    pallas_call x17, Pallas kernels, call(): pl.pallas_call(kernel, grid_spec=pltpu.PrefetchScalarGridSpec(num_scalar_...  254 us
    ppermute x35, waiting for transfers between devices, clip_swap(): lax.ppermute(values, 'clip', [(i, i ^ distance) for i in range(count)])  70.2 us
    ppermute x41, waiting for transfers between devices, head_swap(): lax.ppermute(values, 'head', [(i, i ^ distance) for i in range(count)])  45.7 us
    ppermute x35, starting transfers between devices, clip_swap(): lax.ppermute(values, 'clip', [(i, i ^ distance) for i in range(count)])  45.4 us
    ppermute x41, starting transfers between devices, head_swap(): lax.ppermute(values, 'head', [(i, i ^ distance) for i in range(count)])  24 us
    all_gather x1, waiting for transfers between devices, over_clips(): return lax.all_gather(chunk_across, 'clip', axis=0, tiled=True)  13.8 us
    unnamed x138, local copies, waits for them, and re-layouts  12.9 us
  transfers between devices with their start and end apart: 77, of which 32 were waited for; matrix products, arithmetic and copies ran while one was open for 7% of the time, Pallas kernels for 44%

profile of v5, /device:TPU:0, one launch (start us, length us, event | category | flops | bytes accessed | tf_op | source)
XLA Modules:
  0.0 528.7 jit_solution(13779632342076685499)
XLA Ops:
  9.8 2.9 collective-permute-start
  12.7 2.9 fusion.7
  18.5 2.4 collective-permute-done
  20.8 5.5 %collective-permute-done.1 = bf16[192,768]{1,0:T(8,128)(2,1)} collective-permute-done((bf16[192,768]{1,0:T(8,128)(2,1)}, bf16[192,768]{1,0:T(8,128)(2,1)}, u32[]{:S(2)}, u32[]{:S(2)}) %collective-permute-start.1) | collective-permute-done | bytes 294944 | tf_op jit(solution)/shard_map/ppermute | solution.py:731
  30.9 3.9 collective-permute-done.3
  40.5 3.9 collective-permute-done.5
  46.2 3.3 collective-permute-done.4
  51.7 3.1 collective-permute-done.2.refs_10_.refs_4_.refs_8_
  63.5 17.5 %attend.2 = (bf16[1024,768]{1,0:T(8,128)(2,1)}, bf16[1024,768]{1,0:T(8,128)(2,1)}, bf16[1024,2304]{1,0:T(8,128)(2,1)}, bf16[1024,768]{1,0:T(8,128)(2,1)}, f32[64...) custom-call(s32[3]{0:T(128)} %pad_add_fusion.place_ref, ...), custom_call_target="tpu_custom_call" | custom-call | flops 1955000 | bytes 6120 | tf_op jit(solution)/shard_map/attend/pallas_call | solution.py:257
  88.3 23.2 %feed.2 = (f32[1024,768]{1,0:T(8,128)}, bf16[1024,768]{1,0:T(8,128)(2,1)}, bf16[1024,3072]{1,0:T(8,128)(2,1)}, bf16[1024,3072]{1,0:T(8,128)(2,1)}, bf16[4,64,768...) custom-call(s32[3]{0:T(128)} %pad_add_fusion.place_ref, ...), custom_call_target="tpu_custom_call" | custom-call | flops 2645000 | bytes 8280 | tf_op jit(solution)/shard_map/feed/pallas_call | solution.py:257
  111.5 3.7 collective-permute-done.17.refs_12_.refs_4_.refs_8_
  117.9 13.8 %all-gather.2.cloned.1.call-done = bf16[1536,768]{1,0:T(8,128)(2,1)} async-done(((bf16[192,768]{1,0:T(8,128)(2,1)}), bf16[1536,768]{1,0:T(8,128)(2,1)}) %all-gather.2.cloned.1.call-update) | async-done | bytes 2359312 | tf_op jit(solution)/shard_map/all_gather | solution.py:897
  137.9 17.2 %attend.3 = (bf16[1024,768]{1,0:T(8,128)(2,1)}, bf16[1024,768]{1,0:T(8,128)(2,1)}, bf16[1024,2304]{1,0:T(8,128)(2,1)}, bf16[1024,768]{1,0:T(8,128)(2,1)}, f32[64...) custom-call(s32[3]{0:T(128)} %pad_add_fusion.place_ref, bf16[4,4,16,768]{3,2,1,0:T(8,128)(2,1)} %bitcast.92, ...), custom_call_target="tpu_custom_call" | custom-call | flops 1955000 | bytes 6120 | tf_op jit(solution)/shard_map/attend/pallas_call | solution.py:257
  156.6 23.5 %feed.3 = (f32[1024,768]{1,0:T(8,128)}, bf16[1024,768]{1,0:T(8,128)(2,1)}, bf16[1024,3072]{1,0:T(8,128)(2,1)}, bf16[1024,3072]{1,0:T(8,128)(2,1)}, bf16[1024,768]{1,0:T(8,128)(2,1)}) custom-call(s32[3]{0:T(128)} %pad_add_fusion.place_ref, bf16[1024,768]{1,0:T(8,128)(2,1)} %get-tuple-element.297.refs_0_.refs_2_, ...), custom_call_target="tpu_custom_call" | custom-call | flops 2645000 | bytes 8280 | tf_op jit(solution)/shard_map/feed/pallas_call | solution.py:257
  180.8 17.9 %code_loss.1 = (f32[1024,768]{1,0:T(8,128)}, f32[8,768]{1,0:T(8,128)}, bf16[2,768,768]{2,1,0:T(8,128)(2,1)}, bf16[2,768,768]{2,1,0:T(8,128)(2,1)}) custom-call(s32[3]{0:T(128)} %pad_add_fusion.place_ref, bf16[1024,768]{1,0:T(8,128)(2,1)} %get-tuple-element.301.final_ref, bf16[768,1024]{1,0:T(8,128)(2,1)} %head_ref.1, f32[4,64]{1,0:T(4,128)} %get-tuple-element.302.m0, ...), custom_call_target="tpu_custom_call" | custom-call | flops 1150000 | bytes 3600 | tf_op jit(solution)/shard_map/code_loss/pallas_call | solution.py:257
  199.0 4.4 collective-permute-done.28
  207.0 27.1 %feed_back.2 = (f32[1024,768]{1,0:T(8,128)}, bf16[1024,768]{1,0:T(8,128)(2,1)}, f32[8,768]{1,0:T(8,128)}, bf16[2,768,768]{2,1,0:T(8,128)(2,1)}, bf16[2,768,768]{2,1,0:T(8,128)(2,1)}) custom-call(s32[3]{0:T(128)} %pad_add_fusion.place_ref, f32[1024,768]{1,0:T(8,128)} %get-tuple-element.313.refs_0_, bf16[1024,3072]{1,0:T(8,128)(2,1)} %get-tuple-element.314.refs_1_, ...), custom_call_target="tpu_custom_call" | custom-call | flops 2415000 | bytes 7560 | tf_op jit(solution)/shard_map/feed_back/pallas_call | solution.py:257
  234.6 2.0 bitcast_add_fusion.4
  241.2 24.5 %attend_back.2 = (bf16[4,1024,576]{2,1,0:T(8,128)(2,1)}, bf16[4,4,16,768]{3,2,1,0:T(8,128)(2,1)}, bf16[4,4,16,768]{3,2,1,0:T(8,128)(2,1)}, bf16[4,4,16,768]{3,2,...) custom-call(s32[3]{0:T(128)} %pad_add_fusion.place_ref, f32[1024,768]{1,0:T(8,128)} %get-tuple-element.327.refs_0_, ...), custom_call_target="tpu_custom_call" | custom-call | flops 2875000 | bytes 9000 | tf_op jit(solution)/shard_map/attend_back/pallas_call | solution.py:257
  271.3 11.2 %grads_attn.1 = (bf16[2,768,768]{2,1,0:T(8,128)(2,1)}, bf16[2,768,768]{2,1,0:T(8,128)(2,1)}) custom-call(s32[3]{0:T(128)} %pad_add_fusion.place_ref, bf16[4,1024,576]{2,1,0:T(8,128)(2,1)} %get-tuple-element.349.refs_0_, bf16[1024,768]{1,0:T(8,128)(2,1)} %get-tuple-element.350.refs_1_, bf16[4,1024,192]{2,1,0:T(8,128)(2,1)} %get-tuple-element.351.refs_2_, ...), custom_call_target="tpu_custom_call" | custom-call | flops 920000 | bytes 2880 | tf_op jit(solution)/shard_map/grads_attn/pallas_call | solution.py:257
  282.5 6.4 %collective-permute-done.35 = bf16[4,4,16,768]{3,2,1,0:T(8,128)(2,1)S(1)} collective-permute-done((bf16[4,4,16,768]{3,2,1,0:T(8,128)(2,1)S(1)}, bf16[4,4,16,768]{3,2,1,0:T(8,128)(2,1)S(1)}, u32[]{:S(2)}, u32[]{:S(2)}) %collective-permute-start.35) | collective-permute-done | bytes 393248 | tf_op jit(solution)/shard_map/ppermute | solution.py:731
  290.6 10.7 %grads_down.1 = (bf16[2,768,768]{2,1,0:T(8,128)(2,1)}, bf16[2,768,768]{2,1,0:T(8,128)(2,1)}) custom-call(s32[3]{0:T(128)} %pad_add_fusion.place_ref, bf16[1024,3072]{1,0:T(8,128)(2,1)} %get-tuple-element.356.refs_0_, bf16[1024,768]{1,0:T(8,128)(2,1)} %bitcast.80), custom_call_target="tpu_custom_call" | custom-call | flops 920000 | bytes 2880 | tf_op jit(solution)/shard_map/grads_down/pallas_call | solution.py:257
  302.5 3.5 collective-permute-done.39
  310.2 2.6 collective-permute-start.42
  314.3 26.8 %feed_back.3 = (f32[1024,768]{1,0:T(8,128)}, bf16[1024,768]{1,0:T(8,128)(2,1)}, f32[8,768]{1,0:T(8,128)}, bf16[2,768,768]{2,1,0:T(8,128)(2,1)}, bf16[2,768,768]{2,1,0:T(8,128)(2,1)}) custom-call(s32[3]{0:T(128)} %pad_add_fusion.place_ref, bf16[1024,768]{1,0:T(8,128)(2,1)} %bitcast.81, bf16[1024,3072]{1,0:T(8,128)(2,1)} %get-tuple-element.372.refs_1_, ...), custom_call_target="tpu_custom_call" | custom-call | flops 2415000 | bytes 7560 | tf_op jit(solution)/shard_map/feed_back/pallas_call | solution.py:257
  342.4 2.0 bitcast_add_fusion.2
  354.1 32.6 %attend_back.3 = (f32[1024,768]{1,0:T(8,128)}, f32[8,768]{1,0:T(8,128)}, bf16[2,768,768]{2,1,0:T(8,128)(2,1)}, bf16[2,768,768]{2,1,0:T(8,128)(2,1)}) custom-call(s32[3]{0:T(128)} %pad_add_fusion.place_ref, f32[1024,768]{1,0:T(8,128)} %get-tuple-element.396.refs_0_, bf16[1024,768]{1,0:T(8,128)(2,1)} %get-tuple-element.397.refs_1_, ...), custom_call_target="tpu_custom_call" | custom-call | flops 2875000 | bytes 9000 | tf_op jit(solution)/shard_map/attend_back/pallas_call | solution.py:257
  393.5 5.8 %collective-permute-done.50 = bf16[192,768]{1,0:T(8,128)(2,1)S(1)} collective-permute-done((bf16[192,768]{1,0:T(8,128)(2,1)S(1)}, bf16[192,768]{1,0:T(8,128)(2,1)S(1)}, u32[]{:S(2)}, u32[]{:S(2)}) %collective-permute-start.50) | collective-permute-done | bytes 294944 | tf_op jit(solution)/shard_map/ppermute | solution.py:731
  406.3 11.6 %collective-permute-done.52 = bf16[192,768]{1,0:T(8,128)(2,1)S(1)} collective-permute-done((bf16[192,768]{1,0:T(8,128)(2,1)S(1)}, bf16[192,768]{1,0:T(8,128)(2,1)S(1)}, u32[]{:S(2)}, u32[]{:S(2)}) %collective-permute-start.52) | collective-permute-done | bytes 294944 | tf_op jit(solution)/shard_map/ppermute | solution.py:736
  418.1 10.0 %collective-permute-done.56.other_ref = bf16[384,768]{1,0:T(8,128)(2,1)S(1)} collective-permute-done((bf16[384,768]{1,0:T(8,128)(2,1)S(1)}, bf16[384,768]{1,0:T(8,128)(2,1)S(1)}, u32[]{:S(2)}, u32[]{:S(2)}) %collective-permute-start.56) | collective-permute-done | bytes 589856 | tf_op jit(solution)/shard_map/ppermute | solution.py:736
  431.0 2.6 collective-permute-start.59
  434.1 3.6 emit.6.refs_0_
  437.7 7.7 %collective-permute-done.58 = bf16[192,768]{1,0:T(8,128)(2,1)S(1)} collective-permute-done((bf16[192,768]{1,0:T(8,128)(2,1)S(1)}, bf16[192,768]{1,0:T(8,128)(2,1)S(1)}, u32[]{:S(2)}, u32[]{:S(2)}) %collective-permute-start.58) | collective-permute-done | bytes 294944 | tf_op jit(solution)/shard_map/ppermute | solution.py:736
  445.4 4.7 collective-permute-done.60
  452.8 2.6 collective-permute-start.64
  456.9 3.6 emit.7.refs_0_
  460.8 6.6 %collective-permute-done.63 = bf16[192,768]{1,0:T(8,128)(2,1)S(1)} collective-permute-done((bf16[192,768]{1,0:T(8,128)(2,1)S(1)}, bf16[192,768]{1,0:T(8,128)(2,1)S(1)}, u32[]{:S(2)}, u32[]{:S(2)}) %collective-permute-start.63) | collective-permute-done | bytes 294944 | tf_op jit(solution)/shard_map/ppermute | solution.py:736
  467.4 4.3 collective-permute-done.65
  473.8 3.4 collective-permute-start.69
  478.6 3.5 emit.8
  482.1 6.4 %collective-permute-done.67 = f32[40,768]{1,0:T(8,128)S(1)} collective-permute-done((f32[40,768]{1,0:T(8,128)S(1)}, f32[40,768]{1,0:T(8,128)S(1)}, u32[]{:S(2)}, u32[]{:S(2)}) %collective-permute-start.67) | collective-permute-done | bytes 122912 | tf_op jit(solution)/shard_map/ppermute | solution.py:736
  493.4 3.6 emit.9
  497.0 2.3 collective-permute-done.71
  499.3 2.4 collective-permute-done.73.other_ref
  502.5 2.6 collective-permute-start.74
  505.9 3.6 emit.10
  513.8 2.4 collective-permute-done.75.other_ref
  517.1 3.5 emit.11
  (350 shorter events, 115.5 us)
Async XLA Ops:
  7.2 124.5 %all-gather.2.cloned.1.call-start = ((), (), s32[]{:S(2)}) async-start(), calls=%async_computation | async-start | bytes 2654208 | tf_op jit(solution)/shard_map/all_gather | solution.py:897
  28.1 26.7 %collective-permute-start.2 = (bf16[768,768]{1,0:T(8,128)(2,1)S(1)}, bf16[768,768]{1,0:T(8,128)(2,1)}, u32[]{:S(2)}, u32[]{:S(2)}) collective-permute-start(bf16[768,768]{1,0:T(8,128)(2,1)S(1)} %pad_maximum_fusion.1.refs_8_.refs_2_.refs_6_), channel_id=1, source_target_pairs={{0,2},{1,3},{2,0},{3,1},{4,6},{5,7},{6,4},{7,5},{8,10},{9,11},{10,... | collective-permute-start | bytes 3538952 | tf_op jit(solution)/shard_map/ppermute | solution.py:731
  40.4 19.2 %collective-permute-start.9 = (bf16[768,768]{1,0:T(8,128)(2,1)S(1)}, bf16[768,768]{1,0:T(8,128)(2,1)S(1)}, u32[]{:S(2)}, u32[]{:S(2)}) collective-permute-start(bf16[768,768]{1,0:T(8,128)(2,1)S(1)} %pad_maximum_fusion.1.refs_8_.refs_2_.refs_6_), channel_id=1, source_target_pairs={{0,1},{1,0},{2,3},{3,2},{4,5},{5,4},{6,7},{7,6},{8,9},{9,8},{10,11... | collective-permute-start | bytes 3538952 | tf_op jit(solution)/shard_map/ppermute | solution.py:731
  59.7 21.4 %collective-permute-start.13 = (bf16[2,768,768]{2,1,0:T(8,128)(2,1)S(1)}, bf16[2,768,768]{2,1,0:T(8,128)(2,1)}, u32[]{:S(2)}, u32[]{:S(2)}) collective-permute-start(bf16[2,768,768]{2,1,0:T(8,128)(2,1)S(1)} %copy-done), channel_id=1, source_target_pairs={{0,1},{1,0},{2,3},{3,2},{4,5},{5,4},{6,7},{7,6},{8,9},{9,8},{10,11... | collective-permute-start | bytes 7077896 | tf_op jit(solution)/shard_map/ppermute | solution.py:731
  59.9 21.2 %collective-permute-start.14 = (bf16[2,768,768]{2,1,0:T(8,128)(2,1)}, bf16[2,768,768]{2,1,0:T(8,128)(2,1)}, u32[]{:S(2)}, u32[]{:S(2)}) collective-permute-start(bf16[2,768,768]{2,1,0:T(8,128)(2,1)} %refs_9_.3), channel_id=1, source_target_pairs={{0,1},{1,0},{2,3},{3,2},{4,5},{5,4},{6,7},{7,6},{8,9},{9,8},{10,11... | collective-permute-start | bytes 7077896 | tf_op jit(solution)/shard_map/ppermute | solution.py:731
  60.3 20.8 %collective-permute-start.15 = (bf16[768,768]{1,0:T(8,128)(2,1)}, bf16[768,768]{1,0:T(8,128)(2,1)S(1)}, u32[]{:S(2)}, u32[]{:S(2)}) collective-permute-start(bf16[768,768]{1,0:T(8,128)(2,1)} %pad_maximum_fusion.2.refs_15_.refs_7_), channel_id=1, source_target_pairs={{0,1},{1,0},{2,3},{3,2},{4,5},{5,4},{6,7},{7,6},{8,9},{9,8},{10,11... | collective-permute-start | bytes 3538952 | tf_op jit(solution)/shard_map/ppermute | solution.py:731
  60.4 20.7 %collective-permute-start.11 = (bf16[384,768]{1,0:T(8,128)(2,1)}, bf16[384,768]{1,0:T(8,128)(2,1)}, u32[]{:S(2)}, u32[]{:S(2)}) collective-permute-start(bf16[384,768]{1,0:T(8,128)(2,1)} %pad_maximum_fusion.6), channel_id=1, source_target_pairs={{0,8},{4,12},{8,0},{12,4},{16,24},{20,28},{24,16},{28,20},{1,9},{5... | collective-permute-start | bytes 1769480 | tf_op jit(solution)/shard_map/ppermute | solution.py:736
  62.0 19.1 %collective-permute-start.12 = (bf16[192,768]{1,0:T(8,128)(2,1)S(1)}, bf16[192,768]{1,0:T(8,128)(2,1)}, u32[]{:S(2)}, u32[]{:S(2)}) collective-permute-start(bf16[192,768]{1,0:T(8,128)(2,1)S(1)} %pad_maximum_fusion.11), channel_id=1, source_target_pairs={{0,2},{1,3},{2,0},{3,1},{4,6},{5,7},{6,4},{7,5},{8,10},{9,11},{10,... | collective-permute-start | bytes 884744 | tf_op jit(solution)/shard_map/ppermute | solution.py:731
  87.2 28.0 %collective-permute-start.17 = (bf16[768,768]{1,0:T(8,128)(2,1)S(1)}, bf16[768,768]{1,0:T(8,128)(2,1)S(1)}, u32[]{:S(2)}, u32[]{:S(2)}) collective-permute-start(bf16[768,768]{1,0:T(8,128)(2,1)S(1)} %pad_maximum_fusion.4.refs_10_.refs_2_.refs_6_), channel_id=1, source_target_pairs={{0,2},{1,3},{2,0},{3,1},{4,6},{5,7},{6,4},{7,5},{8,10},{9,11},{10,... | collective-permute-start | bytes 3538952 | tf_op jit(solution)/shard_map/ppermute | solution.py:731
  115.2 20.2 %collective-permute-start.21 = (bf16[768,768]{1,0:T(8,128)(2,1)S(1)}, bf16[768,768]{1,0:T(8,128)(2,1)S(1)}, u32[]{:S(2)}, u32[]{:S(2)}) collective-permute-start(bf16[768,768]{1,0:T(8,128)(2,1)S(1)} %collective-permute-done.17.refs_12_.refs_4_.refs_8_), channel_id=1, source_target_pairs={{0,1},{1,0},{2,3},{3,2},{4,5},{5,4},{6,7},{7,6},{8,9},{9,8},{10,11... | collective-permute-start | bytes 3538952 | tf_op jit(solution)/shard_map/ppermute | solution.py:731
  115.2 18.3 %collective-permute-start.20 = (bf16[4,64,768]{2,1,0:T(8,128)(2,1)}, bf16[4,64,768]{2,1,0:T(8,128)(2,1)}, u32[]{:S(2)}, u32[]{:S(2)}) collective-permute-start(bf16[4,64,768]{2,1,0:T(8,128)(2,1)} %get-tuple-element.286), channel_id=1, source_target_pairs={{0,3},{1,2},{2,1},{3,0},{4,7},{5,6},{6,5},{7,4},{8,11},{9,10},{10,... | collective-permute-start | bytes 1179656 | tf_op jit(solution)/shard_map/ppermute | solution.py:731
  115.9 19.5 %collective-permute-start.19 = (bf16[4,64,768]{2,1,0:T(8,128)(2,1)}, bf16[4,64,768]{2,1,0:T(8,128)(2,1)}, u32[]{:S(2)}, u32[]{:S(2)}) collective-permute-start(bf16[4,64,768]{2,1,0:T(8,128)(2,1)} %get-tuple-element.284), channel_id=1, source_target_pairs={{0,2},{1,3},{2,0},{3,1},{4,6},{5,7},{6,4},{7,5},{8,10},{9,11},{10,... | collective-permute-start | bytes 1179656 | tf_op jit(solution)/shard_map/ppermute | solution.py:731
  117.4 18.0 %collective-permute-start.18 = (bf16[4,64,768]{2,1,0:T(8,128)(2,1)}, bf16[4,64,768]{2,1,0:T(8,128)(2,1)}, u32[]{:S(2)}, u32[]{:S(2)}) collective-permute-start(bf16[4,64,768]{2,1,0:T(8,128)(2,1)} %get-tuple-element.282), channel_id=1, source_target_pairs={{0,1},{1,0},{2,3},{3,2},{4,5},{5,4},{6,7},{7,6},{8,9},{9,8},{10,11... | collective-permute-start | bytes 1179656 | tf_op jit(solution)/shard_map/ppermute | solution.py:731
  117.4 19.2 %collective-permute-start.22 = (bf16[768,768]{1,0:T(8,128)(2,1)S(1)}, bf16[768,768]{1,0:T(8,128)(2,1)}, u32[]{:S(2)}, u32[]{:S(2)}) collective-permute-start(bf16[768,768]{1,0:T(8,128)(2,1)S(1)} %pad_maximum_fusion.4.refs_10_.refs_2_.refs_6_), channel_id=1, source_target_pairs={{0,1},{1,0},{2,3},{3,2},{4,5},{5,4},{6,7},{7,6},{8,9},{9,8},{10,11... | collective-permute-start | bytes 3538952 | tf_op jit(solution)/shard_map/ppermute | solution.py:731
  135.4 19.7 %collective-permute-start.23 = (bf16[768,768]{1,0:T(8,128)(2,1)S(1)}, bf16[768,768]{1,0:T(8,128)(2,1)S(1)}, u32[]{:S(2)}, u32[]{:S(2)}) collective-permute-start(bf16[768,768]{1,0:T(8,128)(2,1)S(1)} %bitcast.85), channel_id=1, source_target_pairs={{0,1},{1,0},{2,3},{3,2},{4,5},{5,4},{6,7},{7,6},{8,9},{9,8},{10,11... | collective-permute-start | bytes 3538952 | tf_op jit(solution)/shard_map/ppermute | solution.py:731
  135.5 19.6 %collective-permute-start.24 = (bf16[768,768]{1,0:T(8,128)(2,1)S(1)}, bf16[768,768]{1,0:T(8,128)(2,1)S(1)}, u32[]{:S(2)}, u32[]{:S(2)}) collective-permute-start(bf16[768,768]{1,0:T(8,128)(2,1)S(1)} %bitcast.82), channel_id=1, source_target_pairs={{0,1},{1,0},{2,3},{3,2},{4,5},{5,4},{6,7},{7,6},{8,9},{9,8},{10,11... | collective-permute-start | bytes 3538952 | tf_op jit(solution)/shard_map/ppermute | solution.py:731
  136.0 44.1 %collective-permute-start.25 = (f32[4,64]{1,0:T(4,128)S(1)}, f32[4,64]{1,0:T(4,128)S(1)}, u32[]{:S(2)}, u32[]{:S(2)}) collective-permute-start(f32[4,64]{1,0:T(4,128)S(1)} %copy-done.65), channel_id=1, source_target_pairs={{0,1},{1,0},{2,3},{3,2},{4,5},{5,4},{6,7},{7,6},{8,9},{9,8},{10,11... | collective-permute-start | bytes 3080 | tf_op jit(solution)/shard_map/ppermute | solution.py:731
  136.1 44.1 %collective-permute-start.26 = (f32[4,64]{1,0:T(4,128)S(1)}, f32[4,64]{1,0:T(4,128)S(1)}, u32[]{:S(2)}, u32[]{:S(2)}) collective-permute-start(f32[4,64]{1,0:T(4,128)S(1)} %copy-done.64), channel_id=1, source_target_pairs={{0,2},{1,3},{2,0},{3,1},{4,6},{5,7},{6,4},{7,5},{8,10},{9,11},{10,... | collective-permute-start | bytes 3080 | tf_op jit(solution)/shard_map/ppermute | solution.py:731
  136.6 43.6 %collective-permute-start.27 = (f32[4,64]{1,0:T(4,128)S(1)}, f32[4,64]{1,0:T(4,128)S(1)}, u32[]{:S(2)}, u32[]{:S(2)}) collective-permute-start(f32[4,64]{1,0:T(4,128)S(1)} %copy-done.63), channel_id=1, source_target_pairs={{0,3},{1,2},{2,1},{3,0},{4,7},{5,6},{6,5},{7,4},{8,11},{9,10},{10,... | collective-permute-start | bytes 3080 | tf_op jit(solution)/shard_map/ppermute | solution.py:731
  206.4 28.3 %collective-permute-start.29 = (bf16[768,768]{1,0:T(8,128)(2,1)S(1)}, bf16[768,768]{1,0:T(8,128)(2,1)S(1)}, u32[]{:S(2)}, u32[]{:S(2)}) collective-permute-start(bf16[768,768]{1,0:T(8,128)(2,1)S(1)} %fusion), channel_id=1, source_target_pairs={{0,2},{1,3},{2,0},{3,1},{4,6},{5,7},{6,4},{7,5},{8,10},{9,11},{10,... | collective-permute-start | bytes 3538952 | tf_op jit(solution)/shard_map/ppermute | solution.py:731
  239.7 28.1 %collective-permute-start.31 = (bf16[768,768]{1,0:T(8,128)(2,1)S(1)}, bf16[768,768]{1,0:T(8,128)(2,1)S(1)}, u32[]{:S(2)}, u32[]{:S(2)}) collective-permute-start(bf16[768,768]{1,0:T(8,128)(2,1)S(1)} %fusion.1), channel_id=1, source_target_pairs={{0,2},{1,3},{2,0},{3,1},{4,6},{5,7},{6,4},{7,5},{8,10},{9,11},{10,... | collective-permute-start | bytes 3538952 | tf_op jit(solution)/shard_map/ppermute | solution.py:731
  240.7 25.0 %collective-permute-start.32 = (bf16[384,768]{1,0:T(8,128)(2,1)}, bf16[384,768]{1,0:T(8,128)(2,1)S(1)}, u32[]{:S(2)}, u32[]{:S(2)}) collective-permute-start(bf16[384,768]{1,0:T(8,128)(2,1)} %get-tuple-element.335), channel_id=1, source_target_pairs={{0,4},{4,0},{8,12},{12,8},{16,20},{20,16},{24,28},{28,24},{1,5},{5... | collective-permute-start | bytes 1769480 | tf_op jit(solution)/shard_map/ppermute | solution.py:736
  268.4 20.5 %collective-permute-start.36 = (bf16[384,768]{1,0:T(8,128)(2,1)S(1)}, bf16[384,768]{1,0:T(8,128)(2,1)S(1)}, u32[]{:S(2)}, u32[]{:S(2)}) collective-permute-start(bf16[384,768]{1,0:T(8,128)(2,1)S(1)} %get-tuple-element.354), channel_id=1, source_target_pairs={{0,4},{4,0},{8,12},{12,8},{16,20},{20,16},{24,28},{28,24},{1,5},{5... | collective-permute-start | bytes 1769480 | tf_op jit(solution)/shard_map/ppermute | solution.py:736
  269.0 20.0 %collective-permute-start.37 = (bf16[384,768]{1,0:T(8,128)(2,1)S(1)}, bf16[384,768]{1,0:T(8,128)(2,1)S(1)}, u32[]{:S(2)}, u32[]{:S(2)}) collective-permute-start(bf16[384,768]{1,0:T(8,128)(2,1)S(1)} %add_convert_fusion.11), channel_id=1, source_target_pairs={{0,8},{4,12},{8,0},{12,4},{16,24},{20,28},{24,16},{28,20},{1,9},{5... | collective-permute-start | bytes 1769480 | tf_op jit(solution)/shard_map/ppermute | solution.py:736
  270.5 18.4 %collective-permute-start.35 = (bf16[4,4,16,768]{3,2,1,0:T(8,128)(2,1)S(1)}, bf16[4,4,16,768]{3,2,1,0:T(8,128)(2,1)S(1)}, u32[]{:S(2)}, u32[]{:S(2)}) collective-permute-start(bf16[4,4,16,768]{3,2,1,0:T(8,128)(2,1)S(1)} %copy-done.60), channel_id=1, source_target_pairs={{0,3},{1,2},{2,1},{3,0},{4,7},{5,6},{6,5},{7,4},{8,11},{9,10},{10,... | collective-permute-start | bytes 1179656 | tf_op jit(solution)/shard_map/ppermute | solution.py:731
  307.6 33.6 %collective-permute-start.40 = (bf16[768,768]{1,0:T(8,128)(2,1)}, bf16[768,768]{1,0:T(8,128)(2,1)}, u32[]{:S(2)}, u32[]{:S(2)}) collective-permute-start(bf16[768,768]{1,0:T(8,128)(2,1)} %fusion.2), channel_id=1, source_target_pairs={{0,2},{1,3},{2,0},{3,1},{4,6},{5,7},{6,4},{7,5},{8,10},{9,11},{10,... | collective-permute-start | bytes 3538952 | tf_op jit(solution)/shard_map/ppermute | solution.py:731
  308.6 32.6 %collective-permute-start.41 = (bf16[2,384,768]{2,1,0:T(8,128)(2,1)S(1)}, bf16[2,384,768]{2,1,0:T(8,128)(2,1)S(1)}, u32[]{:S(2)}, u32[]{:S(2)}) collective-permute-start(bf16[2,384,768]{2,1,0:T(8,128)(2,1)S(1)} %get-tuple-element.381), channel_id=1, source_target_pairs={{0,4},{4,0},{8,12},{12,8},{16,20},{20,16},{24,28},{28,24},{1,5},{5... | collective-permute-start | bytes 3538952 | tf_op jit(solution)/shard_map/ppermute | solution.py:736
  310.2 31.0 %collective-permute-start.42 = (bf16[384,768]{1,0:T(8,128)(2,1)S(1)}, bf16[384,768]{1,0:T(8,128)(2,1)S(1)}, u32[]{:S(2)}, u32[]{:S(2)}) collective-permute-start(bf16[384,768]{1,0:T(8,128)(2,1)S(1)} %add_convert_fusion.10), channel_id=1, source_target_pairs={{0,16},{4,20},{8,24},{12,28},{16,0},{20,4},{24,8},{28,12},{1,17},{... | collective-permute-start | bytes 1769480 | tf_op jit(solution)/shard_map/ppermute | solution.py:736
  312.7 28.4 %collective-permute-start.43 = (bf16[384,768]{1,0:T(8,128)(2,1)S(1)}, bf16[384,768]{1,0:T(8,128)(2,1)S(1)}, u32[]{:S(2)}, u32[]{:S(2)}) collective-permute-start(bf16[384,768]{1,0:T(8,128)(2,1)S(1)} %add_convert_fusion.9), channel_id=1, source_target_pairs={{0,8},{4,12},{8,0},{12,4},{16,24},{20,28},{24,16},{28,20},{1,9},{5... | collective-permute-start | bytes 1769480 | tf_op jit(solution)/shard_map/ppermute | solution.py:736
  349.5 37.2 %collective-permute-start.46 = (bf16[768,768]{1,0:T(8,128)(2,1)S(1)}, bf16[768,768]{1,0:T(8,128)(2,1)}, u32[]{:S(2)}, u32[]{:S(2)}) collective-permute-start(bf16[768,768]{1,0:T(8,128)(2,1)S(1)} %fusion.3), channel_id=1, source_target_pairs={{0,2},{1,3},{2,0},{3,1},{4,6},{5,7},{6,4},{7,5},{8,10},{9,11},{10,... | collective-permute-start | bytes 3538952 | tf_op jit(solution)/shard_map/ppermute | solution.py:731
  350.6 36.1 %collective-permute-start.45 = (bf16[2,192,768]{2,1,0:T(8,128)(2,1)}, bf16[2,192,768]{2,1,0:T(8,128)(2,1)}, u32[]{:S(2)}, u32[]{:S(2)}) collective-permute-start(bf16[2,192,768]{2,1,0:T(8,128)(2,1)} %get-tuple-element.405), channel_id=1, source_target_pairs={{0,8},{4,12},{8,0},{12,4},{16,24},{20,28},{24,16},{28,20},{1,9},{5... | collective-permute-start | bytes 1769480 | tf_op jit(solution)/shard_map/ppermute | solution.py:736
  351.0 35.6 %collective-permute-start.47 = (bf16[384,768]{1,0:T(8,128)(2,1)}, bf16[384,768]{1,0:T(8,128)(2,1)}, u32[]{:S(2)}, u32[]{:S(2)}) collective-permute-start(bf16[384,768]{1,0:T(8,128)(2,1)} %get-tuple-element.408), channel_id=1, source_target_pairs={{0,4},{4,0},{8,12},{12,8},{16,20},{20,16},{24,28},{28,24},{1,5},{5... | collective-permute-start | bytes 1769480 | tf_op jit(solution)/shard_map/ppermute | solution.py:736
  351.5 35.1 %collective-permute-start.48 = (bf16[384,768]{1,0:T(8,128)(2,1)S(1)}, bf16[384,768]{1,0:T(8,128)(2,1)}, u32[]{:S(2)}, u32[]{:S(2)}) collective-permute-start(bf16[384,768]{1,0:T(8,128)(2,1)S(1)} %add_convert_fusion.8), channel_id=1, source_target_pairs={{0,16},{4,20},{8,24},{12,28},{16,0},{20,4},{24,8},{28,12},{1,17},{... | collective-permute-start | bytes 1769480 | tf_op jit(solution)/shard_map/ppermute | solution.py:736
  352.6 34.1 %collective-permute-start.49 = (bf16[384,768]{1,0:T(8,128)(2,1)S(1)}, bf16[384,768]{1,0:T(8,128)(2,1)}, u32[]{:S(2)}, u32[]{:S(2)}) collective-permute-start(bf16[384,768]{1,0:T(8,128)(2,1)S(1)} %add_convert_fusion.7.mine_ref), channel_id=1, source_target_pairs={{0,4},{4,0},{8,12},{12,8},{16,20},{20,16},{24,28},{28,24},{1,5},{5... | collective-permute-start | bytes 1769480 | tf_op jit(solution)/shard_map/ppermute | solution.py:736
  399.7 28.4 %collective-permute-start.55 = (bf16[768,768]{1,0:T(8,128)(2,1)S(1)}, bf16[768,768]{1,0:T(8,128)(2,1)S(1)}, u32[]{:S(2)}, u32[]{:S(2)}) collective-permute-start(bf16[768,768]{1,0:T(8,128)(2,1)S(1)} %fusion.4), channel_id=1, source_target_pairs={{0,2},{1,3},{2,0},{3,1},{4,6},{5,7},{6,4},{7,5},{8,10},{9,11},{10,... | collective-permute-start | bytes 3538952 | tf_op jit(solution)/shard_map/ppermute | solution.py:731
  400.8 17.3 %collective-permute-start.54 = (bf16[384,768]{1,0:T(8,128)(2,1)S(1)}, bf16[384,768]{1,0:T(8,128)(2,1)S(1)}, u32[]{:S(2)}, u32[]{:S(2)}) collective-permute-start(bf16[384,768]{1,0:T(8,128)(2,1)S(1)} %get-tuple-element.430), channel_id=1, source_target_pairs={{0,4},{4,0},{8,12},{12,8},{16,20},{20,16},{24,28},{28,24},{1,5},{5... | collective-permute-start | bytes 1769480 | tf_op jit(solution)/shard_map/ppermute | solution.py:736
  401.3 26.8 %collective-permute-start.56 = (bf16[384,768]{1,0:T(8,128)(2,1)S(1)}, bf16[384,768]{1,0:T(8,128)(2,1)S(1)}, u32[]{:S(2)}, u32[]{:S(2)}) collective-permute-start(bf16[384,768]{1,0:T(8,128)(2,1)S(1)} %add_convert_fusion.5.mine_ref), channel_id=1, source_target_pairs={{0,4},{4,0},{8,12},{12,8},{16,20},{20,16},{24,28},{28,24},{1,5},{5... | collective-permute-start | bytes 1769480 | tf_op jit(solution)/shard_map/ppermute | solution.py:736
  402.8 15.1 %collective-permute-start.52 = (bf16[192,768]{1,0:T(8,128)(2,1)S(1)}, bf16[192,768]{1,0:T(8,128)(2,1)S(1)}, u32[]{:S(2)}, u32[]{:S(2)}) collective-permute-start(bf16[192,768]{1,0:T(8,128)(2,1)S(1)} %add_convert_fusion.19), channel_id=1, source_target_pairs={{0,16},{4,20},{8,24},{12,28},{16,0},{20,4},{24,8},{28,12},{1,17},{... | collective-permute-start | bytes 884744 | tf_op jit(solution)/shard_map/ppermute | solution.py:736
  429.4 20.7 %collective-permute-start.61 = (bf16[384,768]{1,0:T(8,128)(2,1)S(1)}, bf16[384,768]{1,0:T(8,128)(2,1)S(1)}, u32[]{:S(2)}, u32[]{:S(2)}) collective-permute-start(bf16[384,768]{1,0:T(8,128)(2,1)S(1)} %get-tuple-element.446), channel_id=1, source_target_pairs={{0,4},{4,0},{8,12},{12,8},{16,20},{20,16},{24,28},{28,24},{1,5},{5... | collective-permute-start | bytes 1769480 | tf_op jit(solution)/shard_map/ppermute | solution.py:736
  430.0 15.4 %collective-permute-start.58 = (bf16[192,768]{1,0:T(8,128)(2,1)S(1)}, bf16[192,768]{1,0:T(8,128)(2,1)S(1)}, u32[]{:S(2)}, u32[]{:S(2)}) collective-permute-start(bf16[192,768]{1,0:T(8,128)(2,1)S(1)} %add_convert_fusion.17), channel_id=1, source_target_pairs={{0,8},{4,12},{8,0},{12,4},{16,24},{20,28},{24,16},{28,20},{1,9},{5... | collective-permute-start | bytes 884744 | tf_op jit(solution)/shard_map/ppermute | solution.py:736
  433.5 16.5 %collective-permute-start.60 = (bf16[192,768]{1,0:T(8,128)(2,1)S(1)}, bf16[192,768]{1,0:T(8,128)(2,1)S(1)}, u32[]{:S(2)}, u32[]{:S(2)}) collective-permute-start(bf16[192,768]{1,0:T(8,128)(2,1)S(1)} %get-tuple-element.445), channel_id=1, source_target_pairs={{0,8},{4,12},{8,0},{12,4},{16,24},{20,28},{24,16},{28,20},{1,9},{5... | collective-permute-start | bytes 884744 | tf_op jit(solution)/shard_map/ppermute | solution.py:736
  450.6 21.1 %collective-permute-start.66 = (bf16[384,768]{1,0:T(8,128)(2,1)S(1)}, bf16[384,768]{1,0:T(8,128)(2,1)S(1)}, u32[]{:S(2)}, u32[]{:S(2)}) collective-permute-start(bf16[384,768]{1,0:T(8,128)(2,1)S(1)} %pad_maximum_fusion.7.mine_ref), channel_id=1, source_target_pairs={{0,4},{4,0},{8,12},{12,8},{16,20},{20,16},{24,28},{28,24},{1,5},{5... | collective-permute-start | bytes 1769480 | tf_op jit(solution)/shard_map/ppermute | solution.py:736
  451.9 15.5 %collective-permute-start.63 = (bf16[192,768]{1,0:T(8,128)(2,1)S(1)}, bf16[192,768]{1,0:T(8,128)(2,1)S(1)}, u32[]{:S(2)}, u32[]{:S(2)}) collective-permute-start(bf16[192,768]{1,0:T(8,128)(2,1)S(1)} %add_convert_fusion.15), channel_id=1, source_target_pairs={{0,8},{4,12},{8,0},{12,4},{16,24},{20,28},{24,16},{28,20},{1,9},{5... | collective-permute-start | bytes 884744 | tf_op jit(solution)/shard_map/ppermute | solution.py:736
  452.8 14.6 %collective-permute-start.64 = (bf16[192,768]{1,0:T(8,128)(2,1)S(1)}, bf16[192,768]{1,0:T(8,128)(2,1)S(1)}, u32[]{:S(2)}, u32[]{:S(2)}) collective-permute-start(bf16[192,768]{1,0:T(8,128)(2,1)S(1)} %add_convert_fusion.16), channel_id=1, source_target_pairs={{0,16},{4,20},{8,24},{12,28},{16,0},{20,4},{24,8},{28,12},{1,17},{... | collective-permute-start | bytes 884744 | tf_op jit(solution)/shard_map/ppermute | solution.py:736
  455.4 16.2 %collective-permute-start.65 = (bf16[192,768]{1,0:T(8,128)(2,1)S(1)}, bf16[192,768]{1,0:T(8,128)(2,1)S(1)}, u32[]{:S(2)}, u32[]{:S(2)}) collective-permute-start(bf16[192,768]{1,0:T(8,128)(2,1)S(1)} %get-tuple-element.460), channel_id=1, source_target_pairs={{0,8},{4,12},{8,0},{12,4},{16,24},{20,28},{24,16},{28,20},{1,9},{5... | collective-permute-start | bytes 884744 | tf_op jit(solution)/shard_map/ppermute | solution.py:736
  472.5 16.6 %collective-permute-start.70 = (bf16[384,768]{1,0:T(8,128)(2,1)S(1)}, bf16[384,768]{1,0:T(8,128)(2,1)S(1)}, u32[]{:S(2)}, u32[]{:S(2)}) collective-permute-start(bf16[384,768]{1,0:T(8,128)(2,1)S(1)} %pad_maximum_fusion.8.mine_ref), channel_id=1, source_target_pairs={{0,4},{4,0},{8,12},{12,8},{16,20},{20,16},{24,28},{28,24},{1,5},{5... | collective-permute-start | bytes 1769480 | tf_op jit(solution)/shard_map/ppermute | solution.py:736
  473.3 15.2 %collective-permute-start.68 = (bf16[192,768]{1,0:T(8,128)(2,1)S(1)}, bf16[192,768]{1,0:T(8,128)(2,1)S(1)}, u32[]{:S(2)}, u32[]{:S(2)}) collective-permute-start(bf16[192,768]{1,0:T(8,128)(2,1)S(1)} %add_convert_fusion.13), channel_id=1, source_target_pairs={{0,8},{4,12},{8,0},{12,4},{16,24},{20,28},{24,16},{28,20},{1,9},{5... | collective-permute-start | bytes 884744 | tf_op jit(solution)/shard_map/ppermute | solution.py:736
  473.8 15.3 %collective-permute-start.69 = (bf16[192,768]{1,0:T(8,128)(2,1)S(1)}, bf16[192,768]{1,0:T(8,128)(2,1)S(1)}, u32[]{:S(2)}, u32[]{:S(2)}) collective-permute-start(bf16[192,768]{1,0:T(8,128)(2,1)S(1)} %add_convert_fusion.14), channel_id=1, source_target_pairs={{0,16},{4,20},{8,24},{12,28},{16,0},{20,4},{24,8},{28,12},{1,17},{... | collective-permute-start | bytes 884744 | tf_op jit(solution)/shard_map/ppermute | solution.py:736
  (95 other events, 646.4 us)
Sparse Core Ops, SparseCore 0:
  81.2 50.4 all-gather.1

commit v6 on v5

--- a/solution.py
+++ b/solution.py
@@ -16,17 +16,18 @@
 BAND = 64
 CELL = 16
 LSE_ROWS = 16
+SMALLS = 3
 
 epsilon = 1e-06
 masked_score = -1e30
 f32 = jnp.float32
 bf16 = jnp.bfloat16
-VMEM_LIMIT = 56 * 1024 * 1024
+VMEM_LIMIT = 44 * 1024 * 1024
 TIMES = {
-    "attend": 17, "feed": 23, "code_loss": 10, "feed_back": 21, "attend_back": 25,
-    "grads_down": 8, "grads_up": 8, "grads_attn": 8, "emit": 3,
+    "attend": 17, "feed": 23, "code_loss": 18, "feed_back": 26, "attend_back": 25,
+    "grads_down": 10, "grads_attn": 11, "emit": 3,
 }
-SCALE = 0.0001
+SCALE = 1.0
 
 
 def cost_of(name):
@@ -79,14 +80,24 @@
     return pl.ds(pl.multiple_of(pl.program_id(0) * WINDOW, WINDOW), WINDOW)
 
 
-def put_parts(leaving_ref, staying_ref, gradient_of):
+def put_parts(leaving_ref, staying_ref, buf, sem, gradient_of):
+    copies = []
     for n, k in enumerate(ORDER):
-        (leaving_ref if n < 2 else staying_ref)[n % 2] = gradient_of(k).astype(bf16)
+        buf[n] = gradient_of(k).astype(bf16)
+        target = (leaving_ref if n < 2 else staying_ref).at[n % 2]
+        copy = pltpu.make_async_copy(buf.at[n], target, sem.at[n])
+        copy.start()
+        copies.append(copy)
+    for copy in copies:
+        copy.wait()
 
 
 def parts_outs(width):
-    spec = pl.BlockSpec((2, width, width), lambda i, s: (0, 0, 0))
-    return [((2, width, width), bf16, spec)] * 2
+    return [((2, width, width), bf16, pl.BlockSpec(memory_space=pl.ANY))] * 2
+
+
+def parts_scratch(width):
+    return [pltpu.VMEM((4, width, width), bf16), pltpu.SemaphoreType.DMA((4,))]
 
 
 def last_step():
@@ -133,6 +144,16 @@
     return (source == plain).astype(f32).astype(bf16)
 
 
+def small_rows(ref, start, count=1):
+    terms = [ref[SMALLS * n + start : SMALLS * n + start + count, :].astype(f32) for n in range(3)]
+    return terms[0] + terms[1] + terms[2]
+
+
+def small_of(a):
+    rows, width = a.shape
+    return pl.BlockSpec((CELL, width), lambda i, s: (rows // CELL - 1, 0))
+
+
 def assemble_qkv(packs, scratch):
     width = scratch.shape[1]
     share = width // 4
@@ -145,7 +166,7 @@
 def assemble_out(packs, scratch):
     share = scratch.shape[0] // 4
     for k in range(4):
-        scratch[k * share : (k + 1) * share, :] = packs[k][3 * share :, :]
+        scratch[k * share : (k + 1) * share, :] = packs[k][3 * share : 4 * share, :]
 
 
 def stack_heads(pair):
@@ -219,11 +240,11 @@
     normed = (normal * gain_ref[layer, 0:1] + shift_ref[layer, 0:1]).astype(bf16)
     normed_ref[...] = normed
     start = 2 * layer * share
-    smalls = (s0, s1, s2, s3)
+    smalls = [small_rows(r, 2) for r in (s0, s1, s2, s3)]
     bias = jnp.concatenate(
-        [r[2:3, start : start + share] for r in smalls]
+        [r[:, start : start + share] for r in smalls]
         + [jnp.zeros((1, 4 * share), f32)]
-        + [r[2:3, start + share : start + 2 * share] for r in smalls],
+        + [r[:, start + share : start + 2 * share] for r in smalls],
         axis=1,
     )
     qkv = (dot_nt(normed, scratch[...]) + bias).astype(bf16)
@@ -234,7 +255,7 @@
 
 def whole(array):
     zeros = (0,) * array.ndim
-    return pl.BlockSpec(array.shape, lambda i, s: zeros)
+    return pl.BlockSpec(array.shape, lambda i, s: zeros, pipeline_mode=pl.Buffered(1))
 
 
 def rows_of(columns, rows=WINDOW):
@@ -279,7 +300,8 @@
         first = [(tokens, rows_of(width)), (marks, whole(marks))]
     else:
         first = [(p, tube_of(width)) for p in inputs]
-    operands = first + [(a, whole(a)) for a in (gain, shift, *smalls, *packs)]
+    operands = first + [(a, whole(a)) for a in (gain, shift)]
+    operands += [(a, small_of(a)) for a in smalls] + [(a, whole(a)) for a in packs]
     outs = [
         ((rows, width), bf16, rows_of(width)),
         ((rows, width), bf16, rows_of(width)),
@@ -351,7 +373,7 @@
     else:
         (
             normed_ref, part_ref, final_ref, sums_ref, leaving_ref, staying_ref,
-            scratch, out_scratch, acc, side_ref, all_normed, all_parts, all_g1,
+            scratch, out_scratch, acc, side_ref, all_normed, all_parts, all_g1, buf, sem,
         ) = outs
         rows = step_rows()
         all_normed[rows, :] = normed_ref[...]
@@ -405,7 +427,7 @@
                 lower = dot_tn(all_parts[k], all_g1[...])
                 return jnp.concatenate([upper, lower], axis=0)
 
-            put_parts(leaving_ref, staying_ref, gradient_of)
+            put_parts(leaving_ref, staying_ref, buf, sem, gradient_of)
 
 
 def attend_back(layer, place, stream, g1, x, qkv, lse, gain, packs, normed, attended):
@@ -431,7 +453,7 @@
         scratch += [
             pltpu.VMEM((4, rows, 3 * share), bf16), pltpu.VMEM((rows, width), bf16),
             pltpu.VMEM((4, rows, share), bf16), pltpu.VMEM((rows, width), bf16),
-        ]
+        ] + parts_scratch(width)
     return call(partial(attend_back_kernel, layer), "attend_back", place, 4, operands, outs, scratch)
 
 
@@ -463,7 +485,7 @@
         if k < 3:
             ahead = dot(normed, ups[k + 1][...])
         cut = slice(k * units, (k + 1) * units)
-        active, slope = gelu_both(hidden + (s0, s1, s2, s3)[k][layer : layer + 1, :])
+        active, slope = gelu_both(hidden + small_rows((s0, s1, s2, s3)[k], layer))
         active_ref[:, cut] = active
         slope_ref[:, cut] = slope
         total = total + dot(active, downs[k][...])
@@ -479,7 +501,9 @@
     ups, downs, ups_across, downs_across = packs
 
     def of_layer(a):
-        return (a, pl.BlockSpec((None, *a.shape[1:]), lambda i, s: (layer, 0, 0)))
+        return (a, pl.BlockSpec(
+            (None, *a.shape[1:]), lambda i, s: (layer, 0, 0), pipeline_mode=pl.Buffered(1)
+        ))
 
     return [
         *[of_layer(a) for a in ups],
@@ -496,7 +520,8 @@
     operands = (
         [(x, rows_of(width)), (att, rows_of(width))]
         + [(a, last) for a in attn_packs]
-        + [(a, whole(a)) for a in (vecs, gain, shift, *smalls)]
+        + [(a, whole(a)) for a in (vecs, gain, shift)]
+        + [(a, small_of(a)) for a in smalls]
         + feed_specs(layer, packs)
     )
     outs = [
@@ -518,7 +543,7 @@
 
 def loss_kernel(
     place_ref, final_ref, head_ref, m0, m1, m2, m3, active_ref, grad_ref, loss_ref, leaving_ref, staying_ref,
-    acc, all_active, all_g2,
+    acc, all_active, all_g2, buf, sem,
 ):
     logits = dot(final_ref[...], head_ref[...])
     spread = jnp.concatenate(
@@ -553,7 +578,7 @@
         loss_ref[...] = jnp.broadcast_to(total[:, :1], loss_ref.shape)
         width = grad_ref.shape[1]
         put_parts(
-            leaving_ref, staying_ref,
+            leaving_ref, staying_ref, buf, sem,
             lambda k: dot_tn(all_active[:, k * width : (k + 1) * width], all_g2[...]),
         )
 
@@ -568,7 +593,7 @@
     ] + parts_outs(width)
     scratch = [
         pltpu.VMEM((8, PAIR), f32), pltpu.VMEM(active.shape, bf16), pltpu.VMEM((rows, width), bf16)
-    ]
+    ] + parts_scratch(width)
     return call(loss_kernel, "code_loss", place, 4, operands, outs, scratch)
 
 
@@ -581,7 +606,7 @@
         grad = grad_ref[...].astype(f32)
     (
         slope_ref, stream_ref, normed_ref, gain_ref, u0, u1, u2, u3, d0, d1, d2, d3, next_ref, g1_ref,
-        sums_ref, leaving_ref, staying_ref, acc, all_hidden, all_normed,
+        sums_ref, leaving_ref, staying_ref, acc, all_hidden, all_normed, buf, sem,
     ) = refs
     all_normed[step_rows(), :] = normed_ref[...]
     g2 = grad.astype(bf16)
@@ -614,7 +639,7 @@
             start = 4 * units + k * grad.shape[1]
             sums_ref[4 + k : 5 + k, :] = total[:, start : start + grad.shape[1]]
         put_parts(
-            leaving_ref, staying_ref,
+            leaving_ref, staying_ref, buf, sem,
             lambda k: dot_tn(all_normed[...], all_hidden[:, k * units : (k + 1) * units]),
         )
 
@@ -636,7 +661,7 @@
         pltpu.VMEM((8, 4 * units + 4 * width), f32),
         pltpu.VMEM((rows, 4 * units), bf16),
         pltpu.VMEM((rows, width), bf16),
-    ]
+    ] + parts_scratch(width)
     return call(partial(feed_back_kernel, layer), "feed_back", place, 4, operands, outs, scratch)
 
 
@@ -925,10 +950,14 @@
 
     up_quarter = head_swap(quarter(w_up[0]), 2)
     down_quarter = head_swap(quarter(w_down[0]), 2)
-    up_quarter, down_quarter, own, own_small = lax.optimization_barrier(
-        (up_quarter, down_quarter, attn_pack(0), own_small)
-    )
-    smalls = spread(own_small, head_swap(own_small, 2))
+    terms, left = [], own_small
+    for _ in range(3):
+        term = lax.reduce_precision(left, 8, 7)
+        terms.append(term.astype(bf16))
+        left = left - term
+    fill = jnp.zeros((CELL - 3 * SMALLS, width), bf16)
+    own = jnp.concatenate([attn_pack(0), *terms, fill], axis=0)
+    up_quarter, down_quarter, own = lax.optimization_barrier((up_quarter, down_quarter, own))
     later = jnp.concatenate([chunk(w_up[1]), chunk(w_down[1])], axis=0)
     marks = (2 * targets + token_mask).reshape(4, WINDOW)
     up_pair, down_pair = along_y(up_quarter), along_y(down_quarter)
@@ -940,7 +969,8 @@
     order.last = (across,)
     down_others = order.send(clip_swap, down_pair, 2)
     chunk_1 = order.send(head_swap, later, 2)
-    order.last = (smalls[1], smalls[3], attn[0][1], attn[0][3])
+    smalls = attn[0]
+    order.last = (attn[0][1], attn[0][3])
     ups = [w_up, order.send(head_swap, w_up, 1)]
     downs = [w_down, order.send(head_swap, w_down, 1)]
     up_diagonal = order.send(head_swap, up_x, 1)
@@ -1054,11 +1084,11 @@
     attn_0 = Pack(order, *parts)
     order.close()
     move(attn_0)
-    move(attn_1)
-    for one in (up_0, down_0, up_1):
+    move(attn_1, down_0)
+    for one in (up_0, up_1):
         one.prepare()
     order.close()
-    move(attn_0, up_0, down_0, attn_1, up_1)
+    move(down_0, attn_0, attn_1, up_0, up_1)
     order.close()
 
     packed = jnp.concatenate([feed_sum_0, feed_sum_1, attn_sum_0, attn_sum_1, loss_sum], axis=0)
@@ -1076,32 +1106,30 @@
 
     late = [down_1, up_1]
     moving = [attn_0, up_0, down_0]
+    everyone = moving + late + [attn_1]
+    closed = [one for one in everyone if one.done()]
+    jobs = [
+        (down_1, 1, False, None), (up_1, 1, False, None), (down_0, 0, False, down_1),
+        (attn_1, 1, True, None), (up_0, 0, False, up_1), (attn_0, 0, True, attn_1),
+    ]
     wait = 0
     while swaps or not all(one.done() for one in moving + late + [attn_1]):
-        move(*[one for one in moving + [attn_1] + late if not one.done()])
+        held = [attn_1] if wait == 1 else []
+        move(*[one for one in moving + [attn_1] + late if not one.done() and one not in held])
         wait += 1
         if swaps:
             packed = pack_step()
-        for one in late:
-            if one.done() and one not in ready:
-                write(one, 1, False, None)
-                break
-        if attn_1.done() and wait > 2 and attn_1 not in ready:
-            write(attn_1, 1, True, None)
-        for one, earlier in ((down_0, down_1), (up_0, up_1)):
-            if one.done() and one not in ready and earlier in ready and one.closed:
-                write(one, 0, False, ready[earlier])
+        for job in jobs:
+            one, layer, attention, earlier = job
+            if one in closed and (earlier is None or earlier in ready):
+                write(one, layer, attention, ready.get(earlier))
+                jobs.remove(job)
                 break
         order.close()
-        for one in moving:
-            one.closed = one.done()
-
-    for one, layer, attention, earlier in (
-        (down_1, 1, False, None), (up_1, 1, False, None), (attn_1, 1, True, None),
-        (down_0, 0, False, down_1), (up_0, 0, False, up_1), (attn_0, 0, True, attn_1),
-    ):
-        if one not in ready:
-            write(one, layer, attention, ready.get(earlier))
+        closed = [one for one in everyone if one.done()]
+
+    for one, layer, attention, earlier in jobs:
+        write(one, layer, attention, ready.get(earlier))
 
     attn_out, up_out, down_out = ready[attn_0], ready[up_0], ready[down_0]
 

time: 534 us -> 532 us (level)
  Pallas kernels: 254 us -> 231 us
  waiting for transfers between devices: 130 us -> 152 us
    pallas_call x17, Pallas kernels: 254 us -> 231 us  [call(): pl.pallas_call(kernel, grid_spec=pltpu.PrefetchScalarGridSpec(num_scalar_...]
    ppermute x35, waiting for transfers between devices: 70.2 us -> 91.8 us  [clip_swap(): lax.ppermute(values, 'clip', [(i, i ^ distance) for i in range(count)])]
    ppermute x41 -> x38, waiting for transfers between devices: 45.7 us -> 43.8 us  [head_swap(): lax.ppermute(values, 'head', [(i, i ^ distance) for i in range(count)])]
    unnamed x138 -> x112, local copies, waits for them, and re-layouts: 12.9 us -> 11.6 us
    ppermute x41 -> x38, starting transfers between devices: 24 us -> 24.7 us  [head_swap(): lax.ppermute(values, 'head', [(i, i ^ distance) for i in range(count)])]
  transfers between devices with their start and end apart: 77 -> 74, of which waited for: 32 -> 30; matrix products, arithmetic and copies ran while one was open for 7% -> 6% of each run, Pallas kernels for 44% -> 40%
where the time goes in v6:
time: 532 us; the launch traced here: 524 us
  Pallas kernels  231 us (43%)
  waiting for transfers between devices  152 us (29%)
  starting transfers between devices  66.3 us (12%)
  other arithmetic  30.1 us (6%)
  local copies, waits for them, and re-layouts  26 us (5%)
  between operations  18 us (3%)
    pallas_call x17, Pallas kernels, call(): pl.pallas_call(kernel, grid_spec=pltpu.PrefetchScalarGridSpec(num_scalar_...  231 us
    ppermute x35, waiting for transfers between devices, clip_swap(): lax.ppermute(values, 'clip', [(i, i ^ distance) for i in range(count)])  91.8 us
    ppermute x38, waiting for transfers between devices, head_swap(): lax.ppermute(values, 'head', [(i, i ^ distance) for i in range(count)])  43.8 us
    ppermute x35, starting transfers between devices, clip_swap(): lax.ppermute(values, 'clip', [(i, i ^ distance) for i in range(count)])  41.5 us
    ppermute x38, starting transfers between devices, head_swap(): lax.ppermute(values, 'head', [(i, i ^ distance) for i in range(count)])  24.7 us
    all_gather x1, waiting for transfers between devices, over_clips(): return lax.all_gather(chunk_across, 'clip', axis=0, tiled=True)  16.9 us
    unnamed x112, local copies, waits for them, and re-layouts  11.6 us
  transfers between devices with their start and end apart: 74, of which 30 were waited for; matrix products, arithmetic and copies ran while one was open for 6% of the time, Pallas kernels for 40%

profile of v6, /device:TPU:0, one launch (start us, length us, event | category | flops | bytes accessed | tf_op | source)
XLA Modules:
  0.0 524.0 jit_solution(2176933421266271373)
XLA Ops:
  7.2 2.8 fusion.8
  10.1 3.0 collective-permute-start
  13.1 2.8 fusion.9
  16.9 2.5 fusion.10
  20.9 5.6 %collective-permute-done.1 = bf16[192,768]{1,0:T(8,128)(2,1)} collective-permute-done((bf16[192,768]{1,0:T(8,128)(2,1)S(1)}, bf16[192,768]{1,0:T(8,128)(2,1)}, u32[]{:S(2)}, u32[]{:S(2)}) %collective-permute-start.1) | collective-permute-done | bytes 294944 | tf_op jit(solution)/shard_map/ppermute | solution.py:756
  30.5 4.3 collective-permute-done.3
  39.9 4.4 collective-permute-done.5
  45.3 3.2 collective-permute-done.4
  48.7 6.7 %collective-permute-done.2.refs_6_.refs_10_.refs_4_.refs_11_.refs_8_ = bf16[784,768]{1,0:T(8,128)(2,1)} collective-permute-done((bf16[784,768]{1,0:T(8,128)(2,1)S(1)}, bf16[784,768]{1,0:T(8,128)(2,1)}, u32[]{:S(2)}, u32[]{:S(2)}) %collective-permute-start.2) | collective-permute-done | bytes 1204256 | tf_op jit(solution)/shard_map/ppermute | solution.py:756
  55.5 3.1 collective-permute-done.7.refs_7_.refs_11_.refs_5_.refs_12_.refs_9_
  62.2 15.6 %attend.2 = (bf16[1024,768]{1,0:T(8,128)(2,1)S(1)}, bf16[1024,768]{1,0:T(8,128)(2,1)S(1)}, bf16[1024,2304]{1,0:T(8,128)(2,1)}, bf16[1024,768]{1,0:T(8,128)(2,1)S...) custom-call(s32[3]{0:T(128)S(1)} %pad_add_fusion.place_ref, ...), custom_call_target="tpu_custom_call" | custom-call | flops 19549999104 | bytes 61200000 | tf_op jit(solution)/shard_map/attend/pallas_call | solution.py:278
  85.1 2.4 pad_maximum_fusion.3.refs_10_.refs_2_.refs_6_
  88.5 23.2 %feed.2 = (f32[1024,768]{1,0:T(8,128)}, bf16[1024,768]{1,0:T(8,128)(2,1)}, bf16[1024,3072]{1,0:T(8,128)(2,1)}, bf16[1024,3072]{1,0:T(8,128)(2,1)}, bf16[4,64,768...) custom-call(s32[3]{0:T(128)S(1)} %pad_add_fusion.place_ref, ...), custom_call_target="tpu_custom_call" | custom-call | flops 26449999872 | bytes 82800000 | tf_op jit(solution)/shard_map/feed/pallas_call | solution.py:278
  112.4 4.1 collective-permute-done.14.refs_12_.refs_4_.refs_8_
  118.8 16.9 %all-gather.2.cloned.1.call-done = bf16[1536,768]{1,0:T(8,128)(2,1)} async-done(((bf16[192,768]{1,0:T(8,128)(2,1)}), bf16[1536,768]{1,0:T(8,128)(2,1)}) %all-gather.2.cloned.1.call-update) | async-done | bytes 2359312 | tf_op jit(solution)/shard_map/all_gather | solution.py:922
  140.1 17.1 %attend.3 = (bf16[1024,768]{1,0:T(8,128)(2,1)}, bf16[1024,768]{1,0:T(8,128)(2,1)}, bf16[1024,2304]{1,0:T(8,128)(2,1)}, bf16[1024,768]{1,0:T(8,128)(2,1)}, f32[64...) custom-call(s32[3]{0:T(128)S(1)} %pad_add_fusion.place_ref, bf16[4,4,16,768]{3,2,1,0:T(8,128)(2,1)S(1)} %bitcast.91, ...), custom_call_target="tpu_custom_call" | custom-call | flops 19549999104 | bytes 61200000 | tf_op jit(solution)/shard_map/attend/pallas_call | solution.py:278
  157.3 22.8 %feed.3 = (f32[1024,768]{1,0:T(8,128)}, bf16[1024,768]{1,0:T(8,128)(2,1)}, bf16[1024,3072]{1,0:T(8,128)(2,1)}, bf16[1024,3072]{1,0:T(8,128)(2,1)}, bf16[1024,768]{1,0:T(8,128)(2,1)}) custom-call(s32[3]{0:T(128)S(1)} %pad_add_fusion.place_ref, bf16[1024,768]{1,0:T(8,128)(2,1)} %get-tuple-element.295.refs_0_.refs_2_, ...), custom_call_target="tpu_custom_call" | custom-call | flops 26449999872 | bytes 82800000 | tf_op jit(solution)/shard_map/feed/pallas_call | solution.py:278
  181.6 19.0 %code_loss.1 = (f32[1024,768]{1,0:T(8,128)}, f32[8,768]{1,0:T(8,128)S(1)}, bf16[2,768,768]{2,1,0:T(8,128)(2,1)S(1)}, bf16[2,768,768]{2,1,0:T(8,128)(2,1)S(1)}) custom-call(s32[3]{0:T(128)S(1)} %pad_add_fusion.place_ref, bf16[1024,768]{1,0:T(8,128)(2,1)S(1)} %copy-done.30, bf16[768,1024]{1,0:T(8,128)(2,1)S(1)} %copy-done.4, ...), custom_call_target="tpu_custom_call" | custom-call | flops 20700000256 | bytes 64800000 | tf_op jit(solution)/shard_map/code_loss/pallas_call | solution.py:278
  200.9 4.2 collective-permute-done.25
  207.6 25.0 %feed_back.2 = (f32[1024,768]{1,0:T(8,128)}, bf16[1024,768]{1,0:T(8,128)(2,1)S(1)}, f32[8,768]{1,0:T(8,128)S(1)}, bf16[2,768,768]{2,1,0:T(8,128)(2,1)}, bf16[2,768,768]{2,1,0:T(8,128)(2,1)}) custom-call(s32[3]{0:T(128)S(1)} %pad_add_fusion.place_ref, f32[1024,768]{1,0:T(8,128)} %get-tuple-element.311.refs_0_, bf16[1024,3072]{1,0:T(8,128)(2,1)} %get-tuple-element.312.refs_1_, ...), custom_call_target="tpu_custom_call" | custom-call | flops 29899999232 | bytes 93600000 | tf_op jit(solution)/shard_map/feed_back/pallas_call | solution.py:278
  237.3 2.4 collective-permute-done.27
  243.5 23.6 %attend_back.2 = (bf16[4,1024,576]{2,1,0:T(8,128)(2,1)}, bf16[4,4,16,768]{3,2,1,0:T(8,128)(2,1)S(1)}, bf16[4,4,16,768]{3,2,1,0:T(8,128)(2,1)S(1)}, bf16[4,4,16,7...) custom-call(s32[3]{0:T(128)S(1)} %pad_add_fusion.place_ref, ...), custom_call_target="tpu_custom_call" | custom-call | flops 28750000128 | bytes 90000000 | tf_op jit(solution)/shard_map/attend_back/pallas_call | solution.py:278
  267.1 2.8 collective-permute-done.28
  276.9 8.0 %grads_attn.1 = (bf16[2,768,768]{2,1,0:T(8,128)(2,1)S(1)}, bf16[2,768,768]{2,1,0:T(8,128)(2,1)S(1)}) custom-call(s32[3]{0:T(128)S(1)} %pad_add_fusion.place_ref, bf16[4,1024,576]{2,1,0:T(8,128)(2,1)} %get-tuple-element.347.refs_0_, bf16[1024,768]{1,0:T(8,128)(2,1)S(1)} %copy-done.21, bf16[4,1024,192]{2,1,0:T(8,128)(2,1)S(1)} %copy-done.20, ...), custom_call_target="tpu_custom_call" | custom-call | flops 12650000384 | bytes 39600000 | tf_op jit(solution)/shard_map/grads_attn/pallas_call | solution.py:278
  284.9 6.6 %collective-permute-done.32 = bf16[4,4,16,768]{3,2,1,0:T(8,128)(2,1)S(1)} collective-permute-done((bf16[4,4,16,768]{3,2,1,0:T(8,128)(2,1)S(1)}, bf16[4,4,16,768]{3,2,1,0:T(8,128)(2,1)S(1)}, u32[]{:S(2)}, u32[]{:S(2)}) %collective-permute-start.32) | collective-permute-done | bytes 393248 | tf_op jit(solution)/shard_map/ppermute | solution.py:756
  292.5 8.3 %grads_down.1 = (bf16[2,768,768]{2,1,0:T(8,128)(2,1)S(1)}, bf16[2,768,768]{2,1,0:T(8,128)(2,1)S(1)}) custom-call(s32[3]{0:T(128)S(1)} %pad_add_fusion.place_ref, bf16[1024,3072]{1,0:T(8,128)(2,1)} %get-tuple-element.354.refs_0_, bf16[1024,768]{1,0:T(8,128)(2,1)S(1)} %bitcast.80), custom_call_target="tpu_custom_call" | custom-call | flops 11500000256 | bytes 36000000 | tf_op jit(solution)/shard_map/grads_down/pallas_call | solution.py:278
  312.2 25.0 %feed_back.3 = (f32[1024,768]{1,0:T(8,128)}, bf16[1024,768]{1,0:T(8,128)(2,1)S(1)}, f32[8,768]{1,0:T(8,128)S(1)}, bf16[2,768,768]{2,1,0:T(8,128)(2,1)}, bf16[2,768,768]{2,1,0:T(8,128)(2,1)}) custom-call(s32[3]{0:T(128)S(1)} %pad_add_fusion.place_ref, bf16[1024,768]{1,0:T(8,128)(2,1)S(1)} %bitcast.81, bf16[1024,3072]{1,0:T(8,128)(2,1)} %get-tuple-element.370.refs_1_, ...), custom_call_target="tpu_custom_call" | custom-call | flops 29899999232 | bytes 93600000 | tf_op jit(solution)/shard_map/feed_back/pallas_call | solution.py:278
  338.2 2.2 bitcast_add_fusion.2
  352.5 30.2 %attend_back.3 = (f32[1024,768]{1,0:T(8,128)}, f32[8,768]{1,0:T(8,128)S(1)}, bf16[2,768,768]{2,1,0:T(8,128)(2,1)}, bf16[2,768,768]{2,1,0:T(8,128)(2,1)}) custom-call(s32[3]{0:T(128)S(1)} %pad_add_fusion.place_ref, f32[1024,768]{1,0:T(8,128)} %get-tuple-element.394.refs_0_, bf16[1024,768]{1,0:T(8,128)(2,1)S(1)} %get-tuple-element.395.refs_1_, ...), custom_call_target="tpu_custom_call" | custom-call | flops 28750000128 | bytes 90000000 | tf_op jit(solution)/shard_map/attend_back/pallas_call | solution.py:278
  387.0 5.7 %collective-permute-done.47 = bf16[192,768]{1,0:T(8,128)(2,1)S(1)} collective-permute-done((bf16[192,768]{1,0:T(8,128)(2,1)S(1)}, bf16[192,768]{1,0:T(8,128)(2,1)S(1)}, u32[]{:S(2)}, u32[]{:S(2)}) %collective-permute-start.47) | collective-permute-done | bytes 294944 | tf_op jit(solution)/shard_map/ppermute | solution.py:756
  400.0 19.2 %collective-permute-done.50 = bf16[192,768]{1,0:T(8,128)(2,1)S(1)} collective-permute-done((bf16[192,768]{1,0:T(8,128)(2,1)S(1)}, bf16[192,768]{1,0:T(8,128)(2,1)S(1)}, u32[]{:S(2)}, u32[]{:S(2)}) %collective-permute-start.50) | collective-permute-done | bytes 294944 | tf_op jit(solution)/shard_map/ppermute | solution.py:761
  419.2 5.2 collective-permute-done.51
  429.2 2.2 emit.6.refs_0_
  431.4 5.4 %collective-permute-done.56 = bf16[192,768]{1,0:T(8,128)(2,1)S(1)} collective-permute-done((bf16[192,768]{1,0:T(8,128)(2,1)S(1)}, bf16[192,768]{1,0:T(8,128)(2,1)S(1)}, u32[]{:S(2)}, u32[]{:S(2)}) %collective-permute-start.56) | collective-permute-done | bytes 294944 | tf_op jit(solution)/shard_map/ppermute | solution.py:761
  436.9 6.3 %collective-permute-done.57 = bf16[192,768]{1,0:T(8,128)(2,1)S(1)} collective-permute-done((bf16[192,768]{1,0:T(8,128)(2,1)S(1)}, bf16[192,768]{1,0:T(8,128)(2,1)S(1)}, u32[]{:S(2)}, u32[]{:S(2)}) %collective-permute-start.57) | collective-permute-done | bytes 294944 | tf_op jit(solution)/shard_map/ppermute | solution.py:761
  443.2 5.9 %collective-permute-done.59 = bf16[192,768]{1,0:T(8,128)(2,1)S(1)} collective-permute-done((bf16[192,768]{1,0:T(8,128)(2,1)S(1)}, bf16[192,768]{1,0:T(8,128)(2,1)S(1)}, u32[]{:S(2)}, u32[]{:S(2)}) %collective-permute-start.59) | collective-permute-done | bytes 294944 | tf_op jit(solution)/shard_map/ppermute | solution.py:761
  454.0 2.2 emit.7.refs_0_
  456.2 10.5 %collective-permute-done.61 = bf16[192,768]{1,0:T(8,128)(2,1)S(1)} collective-permute-done((bf16[192,768]{1,0:T(8,128)(2,1)S(1)}, bf16[192,768]{1,0:T(8,128)(2,1)S(1)}, u32[]{:S(2)}, u32[]{:S(2)}) %collective-permute-start.61) | collective-permute-done | bytes 294944 | tf_op jit(solution)/shard_map/ppermute | solution.py:761
  469.3 2.3 collective-permute-start.66
  471.6 2.2 emit.8
  473.8 11.1 %collective-permute-done.64 = f32[40,768]{1,0:T(8,128)S(1)} collective-permute-done((f32[40,768]{1,0:T(8,128)S(1)}, f32[40,768]{1,0:T(8,128)S(1)}, u32[]{:S(2)}, u32[]{:S(2)}) %collective-permute-start.64) | collective-permute-done | bytes 122912 | tf_op jit(solution)/shard_map/ppermute | solution.py:761
  488.8 2.2 emit.9
  493.0 4.1 collective-permute-done.69
  497.2 2.4 collective-permute-done.70.other_ref
  501.3 2.2 emit.10
  503.6 2.5 collective-permute-done.71
  510.4 3.0 collective-permute-done.72.other_ref
  513.3 2.2 emit.11
  (319 shorter events, 111.5 us)
Async XLA Ops:
  7.2 128.5 %all-gather.2.cloned.1.call-start = ((), (), s32[]{:S(2)}) async-start(), calls=%async_computation | async-start | bytes 2654208 | tf_op jit(solution)/shard_map/all_gather | solution.py:922
  28.3 27.2 %collective-permute-start.2 = (bf16[784,768]{1,0:T(8,128)(2,1)S(1)}, bf16[784,768]{1,0:T(8,128)(2,1)}, u32[]{:S(2)}, u32[]{:S(2)}) collective-permute-start(bf16[784,768]{1,0:T(8,128)(2,1)S(1)} %concatenate.40.refs_4_.refs_8_.refs_2_.refs_9_.refs_6_), channel_id=1, source_target_pairs={{0,2},{1,3},{2,0},{3,1},{4,6},{5,7},{6,4},{7,5},{8,10},{9,11},{10,... | collective-permute-start | bytes 3612680 | tf_op jit(solution)/shard_map/ppermute | solution.py:756
  39.9 15.6 %collective-permute-start.6 = (bf16[784,768]{1,0:T(8,128)(2,1)S(1)}, bf16[784,768]{1,0:T(8,128)(2,1)S(1)}, u32[]{:S(2)}, u32[]{:S(2)}) collective-permute-start(bf16[784,768]{1,0:T(8,128)(2,1)S(1)} %concatenate.40.refs_4_.refs_8_.refs_2_.refs_9_.refs_6_), channel_id=1, source_target_pairs={{0,1},{1,0},{2,3},{3,2},{4,5},{5,4},{6,7},{7,6},{8,9},{9,8},{10,11... | collective-permute-start | bytes 3612680 | tf_op jit(solution)/shard_map/ppermute | solution.py:756
  58.6 22.6 %collective-permute-start.10 = (bf16[2,768,768]{2,1,0:T(8,128)(2,1)}, bf16[2,768,768]{2,1,0:T(8,128)(2,1)}, u32[]{:S(2)}, u32[]{:S(2)}) collective-permute-start(bf16[2,768,768]{2,1,0:T(8,128)(2,1)} %refs_5_.8), channel_id=1, source_target_pairs={{0,1},{1,0},{2,3},{3,2},{4,5},{5,4},{6,7},{7,6},{8,9},{9,8},{10,11... | collective-permute-start | bytes 7077896 | tf_op jit(solution)/shard_map/ppermute | solution.py:756
  58.7 22.5 %collective-permute-start.11 = (bf16[2,768,768]{2,1,0:T(8,128)(2,1)}, bf16[2,768,768]{2,1,0:T(8,128)(2,1)}, u32[]{:S(2)}, u32[]{:S(2)}) collective-permute-start(bf16[2,768,768]{2,1,0:T(8,128)(2,1)} %refs_9_.3), channel_id=1, source_target_pairs={{0,1},{1,0},{2,3},{3,2},{4,5},{5,4},{6,7},{7,6},{8,9},{9,8},{10,11... | collective-permute-start | bytes 7077896 | tf_op jit(solution)/shard_map/ppermute | solution.py:756
  59.1 22.1 %collective-permute-start.9 = (bf16[192,768]{1,0:T(8,128)(2,1)S(1)}, bf16[192,768]{1,0:T(8,128)(2,1)}, u32[]{:S(2)}, u32[]{:S(2)}) collective-permute-start(bf16[192,768]{1,0:T(8,128)(2,1)S(1)} %pad_maximum_fusion.10), channel_id=1, source_target_pairs={{0,2},{1,3},{2,0},{3,1},{4,6},{5,7},{6,4},{7,5},{8,10},{9,11},{10,... | collective-permute-start | bytes 884744 | tf_op jit(solution)/shard_map/ppermute | solution.py:756
  60.6 20.6 %collective-permute-start.8 = (bf16[384,768]{1,0:T(8,128)(2,1)S(1)}, bf16[384,768]{1,0:T(8,128)(2,1)}, u32[]{:S(2)}, u32[]{:S(2)}) collective-permute-start(bf16[384,768]{1,0:T(8,128)(2,1)S(1)} %pad_maximum_fusion.5), channel_id=1, source_target_pairs={{0,8},{4,12},{8,0},{12,4},{16,24},{20,28},{24,16},{28,20},{1,9},{5... | collective-permute-start | bytes 1769480 | tf_op jit(solution)/shard_map/ppermute | solution.py:761
  62.1 19.1 %collective-permute-start.12 = (bf16[768,768]{1,0:T(8,128)(2,1)S(1)}, bf16[768,768]{1,0:T(8,128)(2,1)}, u32[]{:S(2)}, u32[]{:S(2)}) collective-permute-start(bf16[768,768]{1,0:T(8,128)(2,1)S(1)} %pad_maximum_fusion.1.refs_15_.refs_7_), channel_id=1, source_target_pairs={{0,1},{1,0},{2,3},{3,2},{4,5},{5,4},{6,7},{7,6},{8,9},{9,8},{10,11... | collective-permute-start | bytes 3538952 | tf_op jit(solution)/shard_map/ppermute | solution.py:756
  87.9 28.6 %collective-permute-start.14 = (bf16[768,768]{1,0:T(8,128)(2,1)}, bf16[768,768]{1,0:T(8,128)(2,1)}, u32[]{:S(2)}, u32[]{:S(2)}) collective-permute-start(bf16[768,768]{1,0:T(8,128)(2,1)} %pad_maximum_fusion.3.refs_10_.refs_2_.refs_6_), channel_id=1, source_target_pairs={{0,2},{1,3},{2,0},{3,1},{4,6},{5,7},{6,4},{7,5},{8,10},{9,11},{10,... | collective-permute-start | bytes 3538952 | tf_op jit(solution)/shard_map/ppermute | solution.py:756
  116.5 23.1 %collective-permute-start.18 = (bf16[768,768]{1,0:T(8,128)(2,1)}, bf16[768,768]{1,0:T(8,128)(2,1)}, u32[]{:S(2)}, u32[]{:S(2)}) collective-permute-start(bf16[768,768]{1,0:T(8,128)(2,1)} %collective-permute-done.14.refs_12_.refs_4_.refs_8_), channel_id=1, source_target_pairs={{0,1},{1,0},{2,3},{3,2},{4,5},{5,4},{6,7},{7,6},{8,9},{9,8},{10,11... | collective-permute-start | bytes 3538952 | tf_op jit(solution)/shard_map/ppermute | solution.py:756
  116.5 23.5 %collective-permute-start.19 = (bf16[768,768]{1,0:T(8,128)(2,1)}, bf16[768,768]{1,0:T(8,128)(2,1)}, u32[]{:S(2)}, u32[]{:S(2)}) collective-permute-start(bf16[768,768]{1,0:T(8,128)(2,1)} %pad_maximum_fusion.3.refs_10_.refs_2_.refs_6_), channel_id=1, source_target_pairs={{0,1},{1,0},{2,3},{3,2},{4,5},{5,4},{6,7},{7,6},{8,9},{9,8},{10,11... | collective-permute-start | bytes 3538952 | tf_op jit(solution)/shard_map/ppermute | solution.py:756
  117.0 20.6 %collective-permute-start.17 = (bf16[4,64,768]{2,1,0:T(8,128)(2,1)}, bf16[4,64,768]{2,1,0:T(8,128)(2,1)S(1)}, u32[]{:S(2)}, u32[]{:S(2)}) collective-permute-start(bf16[4,64,768]{2,1,0:T(8,128)(2,1)} %get-tuple-element.284), channel_id=1, source_target_pairs={{0,3},{1,2},{2,1},{3,0},{4,7},{5,6},{6,5},{7,4},{8,11},{9,10},{10,... | collective-permute-start | bytes 1179656 | tf_op jit(solution)/shard_map/ppermute | solution.py:756
  117.1 20.6 %collective-permute-start.16 = (bf16[4,64,768]{2,1,0:T(8,128)(2,1)}, bf16[4,64,768]{2,1,0:T(8,128)(2,1)S(1)}, u32[]{:S(2)}, u32[]{:S(2)}) collective-permute-start(bf16[4,64,768]{2,1,0:T(8,128)(2,1)} %get-tuple-element.282), channel_id=1, source_target_pairs={{0,2},{1,3},{2,0},{3,1},{4,6},{5,7},{6,4},{7,5},{8,10},{9,11},{10,... | collective-permute-start | bytes 1179656 | tf_op jit(solution)/shard_map/ppermute | solution.py:756
  118.6 20.6 %collective-permute-start.15 = (bf16[4,64,768]{2,1,0:T(8,128)(2,1)}, bf16[4,64,768]{2,1,0:T(8,128)(2,1)}, u32[]{:S(2)}, u32[]{:S(2)}) collective-permute-start(bf16[4,64,768]{2,1,0:T(8,128)(2,1)} %get-tuple-element.280), channel_id=1, source_target_pairs={{0,1},{1,0},{2,3},{3,2},{4,5},{5,4},{6,7},{7,6},{8,9},{9,8},{10,11... | collective-permute-start | bytes 1179656 | tf_op jit(solution)/shard_map/ppermute | solution.py:756
  137.6 42.5 %collective-permute-start.22 = (f32[4,64]{1,0:T(4,128)S(1)}, f32[4,64]{1,0:T(4,128)S(1)}, u32[]{:S(2)}, u32[]{:S(2)}) collective-permute-start(f32[4,64]{1,0:T(4,128)S(1)} %get-tuple-element.301), channel_id=1, source_target_pairs={{0,1},{1,0},{2,3},{3,2},{4,5},{5,4},{6,7},{7,6},{8,9},{9,8},{10,11... | collective-permute-start | bytes 3080 | tf_op jit(solution)/shard_map/ppermute | solution.py:756
  137.7 42.4 %collective-permute-start.23 = (f32[4,64]{1,0:T(4,128)S(1)}, f32[4,64]{1,0:T(4,128)S(1)}, u32[]{:S(2)}, u32[]{:S(2)}) collective-permute-start(f32[4,64]{1,0:T(4,128)S(1)} %get-tuple-element.302), channel_id=1, source_target_pairs={{0,2},{1,3},{2,0},{3,1},{4,6},{5,7},{6,4},{7,5},{8,10},{9,11},{10,... | collective-permute-start | bytes 3080 | tf_op jit(solution)/shard_map/ppermute | solution.py:756
  139.2 40.9 %collective-permute-start.24 = (f32[4,64]{1,0:T(4,128)S(1)}, f32[4,64]{1,0:T(4,128)S(1)}, u32[]{:S(2)}, u32[]{:S(2)}) collective-permute-start(f32[4,64]{1,0:T(4,128)S(1)} %get-tuple-element.303), channel_id=1, source_target_pairs={{0,3},{1,2},{2,1},{3,0},{4,7},{5,6},{6,5},{7,4},{8,11},{9,10},{10,... | collective-permute-start | bytes 3080 | tf_op jit(solution)/shard_map/ppermute | solution.py:756
  139.6 17.7 %collective-permute-start.20 = (bf16[768,768]{1,0:T(8,128)(2,1)S(1)}, bf16[768,768]{1,0:T(8,128)(2,1)S(1)}, u32[]{:S(2)}, u32[]{:S(2)}) collective-permute-start(bf16[768,768]{1,0:T(8,128)(2,1)S(1)} %bitcast.85), channel_id=1, source_target_pairs={{0,1},{1,0},{2,3},{3,2},{4,5},{5,4},{6,7},{7,6},{8,9},{9,8},{10,11... | collective-permute-start | bytes 3538952 | tf_op jit(solution)/shard_map/ppermute | solution.py:756
  139.9 17.3 %collective-permute-start.21 = (bf16[768,768]{1,0:T(8,128)(2,1)S(1)}, bf16[768,768]{1,0:T(8,128)(2,1)S(1)}, u32[]{:S(2)}, u32[]{:S(2)}) collective-permute-start(bf16[768,768]{1,0:T(8,128)(2,1)S(1)} %bitcast.82), channel_id=1, source_target_pairs={{0,1},{1,0},{2,3},{3,2},{4,5},{5,4},{6,7},{7,6},{8,9},{9,8},{10,11... | collective-permute-start | bytes 3538952 | tf_op jit(solution)/shard_map/ppermute | solution.py:756
  205.5 28.3 %collective-permute-start.26 = (bf16[768,768]{1,0:T(8,128)(2,1)S(1)}, bf16[768,768]{1,0:T(8,128)(2,1)S(1)}, u32[]{:S(2)}, u32[]{:S(2)}) collective-permute-start(bf16[768,768]{1,0:T(8,128)(2,1)S(1)} %fusion), channel_id=1, source_target_pairs={{0,2},{1,3},{2,0},{3,1},{4,6},{5,7},{6,4},{7,5},{8,10},{9,11},{10,... | collective-permute-start | bytes 3538952 | tf_op jit(solution)/shard_map/ppermute | solution.py:756
  241.4 25.7 %collective-permute-start.29 = (bf16[384,768]{1,0:T(8,128)(2,1)S(1)}, bf16[384,768]{1,0:T(8,128)(2,1)S(1)}, u32[]{:S(2)}, u32[]{:S(2)}) collective-permute-start(bf16[384,768]{1,0:T(8,128)(2,1)S(1)} %get-tuple-element.333), channel_id=1, source_target_pairs={{0,4},{4,0},{8,12},{12,8},{16,20},{20,16},{24,28},{28,24},{1,5},{5... | collective-permute-start | bytes 1769480 | tf_op jit(solution)/shard_map/ppermute | solution.py:761
  242.0 27.9 %collective-permute-start.28 = (bf16[768,768]{1,0:T(8,128)(2,1)S(1)}, bf16[768,768]{1,0:T(8,128)(2,1)S(1)}, u32[]{:S(2)}, u32[]{:S(2)}) collective-permute-start(bf16[768,768]{1,0:T(8,128)(2,1)S(1)} %fusion.1), channel_id=1, source_target_pairs={{0,2},{1,3},{2,0},{3,1},{4,6},{5,7},{6,4},{7,5},{8,10},{9,11},{10,... | collective-permute-start | bytes 3538952 | tf_op jit(solution)/shard_map/ppermute | solution.py:756
  273.6 18.0 %collective-permute-start.32 = (bf16[4,4,16,768]{3,2,1,0:T(8,128)(2,1)S(1)}, bf16[4,4,16,768]{3,2,1,0:T(8,128)(2,1)S(1)}, u32[]{:S(2)}, u32[]{:S(2)}) collective-permute-start(bf16[4,4,16,768]{3,2,1,0:T(8,128)(2,1)S(1)} %get-tuple-element.338), channel_id=1, source_target_pairs={{0,3},{1,2},{2,1},{3,0},{4,7},{5,6},{6,5},{7,4},{8,11},{9,10},{10,... | collective-permute-start | bytes 1179656 | tf_op jit(solution)/shard_map/ppermute | solution.py:756
  273.9 17.6 %collective-permute-start.33 = (bf16[384,768]{1,0:T(8,128)(2,1)S(1)}, bf16[384,768]{1,0:T(8,128)(2,1)S(1)}, u32[]{:S(2)}, u32[]{:S(2)}) collective-permute-start(bf16[384,768]{1,0:T(8,128)(2,1)S(1)} %get-tuple-element.352), channel_id=1, source_target_pairs={{0,4},{4,0},{8,12},{12,8},{16,20},{20,16},{24,28},{28,24},{1,5},{5... | collective-permute-start | bytes 1769480 | tf_op jit(solution)/shard_map/ppermute | solution.py:761
  275.4 16.2 %collective-permute-start.34 = (bf16[384,768]{1,0:T(8,128)(2,1)S(1)}, bf16[384,768]{1,0:T(8,128)(2,1)S(1)}, u32[]{:S(2)}, u32[]{:S(2)}) collective-permute-start(bf16[384,768]{1,0:T(8,128)(2,1)S(1)} %add_convert_fusion.11), channel_id=1, source_target_pairs={{0,8},{4,12},{8,0},{12,4},{16,24},{20,28},{24,16},{28,20},{1,9},{5... | collective-permute-start | bytes 1769480 | tf_op jit(solution)/shard_map/ppermute | solution.py:761
  306.8 30.3 %collective-permute-start.39 = (bf16[384,768]{1,0:T(8,128)(2,1)S(1)}, bf16[384,768]{1,0:T(8,128)(2,1)S(1)}, u32[]{:S(2)}, u32[]{:S(2)}) collective-permute-start(bf16[384,768]{1,0:T(8,128)(2,1)S(1)} %add_convert_fusion.10), channel_id=1, source_target_pairs={{0,16},{4,20},{8,24},{12,28},{16,0},{20,4},{24,8},{28,12},{1,17},{... | collective-permute-start | bytes 1769480 | tf_op jit(solution)/shard_map/ppermute | solution.py:761
  308.7 28.5 %collective-permute-start.40 = (bf16[384,768]{1,0:T(8,128)(2,1)S(1)}, bf16[384,768]{1,0:T(8,128)(2,1)}, u32[]{:S(2)}, u32[]{:S(2)}) collective-permute-start(bf16[384,768]{1,0:T(8,128)(2,1)S(1)} %add_convert_fusion.9), channel_id=1, source_target_pairs={{0,8},{4,12},{8,0},{12,4},{16,24},{20,28},{24,16},{28,20},{1,9},{5... | collective-permute-start | bytes 1769480 | tf_op jit(solution)/shard_map/ppermute | solution.py:761
  309.2 27.9 %collective-permute-start.37 = (bf16[768,768]{1,0:T(8,128)(2,1)}, bf16[768,768]{1,0:T(8,128)(2,1)}, u32[]{:S(2)}, u32[]{:S(2)}) collective-permute-start(bf16[768,768]{1,0:T(8,128)(2,1)} %fusion.2), channel_id=1, source_target_pairs={{0,2},{1,3},{2,0},{3,1},{4,6},{5,7},{6,4},{7,5},{8,10},{9,11},{10,... | collective-permute-start | bytes 3538952 | tf_op jit(solution)/shard_map/ppermute | solution.py:756
  310.7 27.5 %collective-permute-start.38 = (bf16[2,384,768]{2,1,0:T(8,128)(2,1)}, bf16[2,384,768]{2,1,0:T(8,128)(2,1)S(1)}, u32[]{:S(2)}, u32[]{:S(2)}) collective-permute-start(bf16[2,384,768]{2,1,0:T(8,128)(2,1)} %get-tuple-element.379), channel_id=1, source_target_pairs={{0,4},{4,0},{8,12},{12,8},{16,20},{20,16},{24,28},{28,24},{1,5},{5... | collective-permute-start | bytes 3538952 | tf_op jit(solution)/shard_map/ppermute | solution.py:761
  347.4 35.3 %collective-permute-start.42 = (bf16[2,192,768]{2,1,0:T(8,128)(2,1)}, bf16[2,192,768]{2,1,0:T(8,128)(2,1)S(1)}, u32[]{:S(2)}, u32[]{:S(2)}) collective-permute-start(bf16[2,192,768]{2,1,0:T(8,128)(2,1)} %get-tuple-element.403), channel_id=1, source_target_pairs={{0,8},{4,12},{8,0},{12,4},{16,24},{20,28},{24,16},{28,20},{1,9},{5... | collective-permute-start | bytes 1769480 | tf_op jit(solution)/shard_map/ppermute | solution.py:761
  348.8 33.9 %collective-permute-start.44 = (bf16[384,768]{1,0:T(8,128)(2,1)}, bf16[384,768]{1,0:T(8,128)(2,1)S(1)}, u32[]{:S(2)}, u32[]{:S(2)}) collective-permute-start(bf16[384,768]{1,0:T(8,128)(2,1)} %get-tuple-element.406), channel_id=1, source_target_pairs={{0,4},{4,0},{8,12},{12,8},{16,20},{20,16},{24,28},{28,24},{1,5},{5... | collective-permute-start | bytes 1769480 | tf_op jit(solution)/shard_map/ppermute | solution.py:761
  350.3 32.4 %collective-permute-start.45 = (bf16[384,768]{1,0:T(8,128)(2,1)S(1)}, bf16[384,768]{1,0:T(8,128)(2,1)S(1)}, u32[]{:S(2)}, u32[]{:S(2)}) collective-permute-start(bf16[384,768]{1,0:T(8,128)(2,1)S(1)} %add_convert_fusion.8), channel_id=1, source_target_pairs={{0,16},{4,20},{8,24},{12,28},{16,0},{20,4},{24,8},{28,12},{1,17},{... | collective-permute-start | bytes 1769480 | tf_op jit(solution)/shard_map/ppermute | solution.py:761
  351.4 31.3 %collective-permute-start.46 = (bf16[384,768]{1,0:T(8,128)(2,1)S(1)}, bf16[384,768]{1,0:T(8,128)(2,1)S(1)}, u32[]{:S(2)}, u32[]{:S(2)}) collective-permute-start(bf16[384,768]{1,0:T(8,128)(2,1)S(1)} %add_convert_fusion.7.mine_ref), channel_id=1, source_target_pairs={{0,4},{4,0},{8,12},{12,8},{16,20},{20,16},{24,28},{28,24},{1,5},{5... | collective-permute-start | bytes 1769480 | tf_op jit(solution)/shard_map/ppermute | solution.py:761
  351.9 30.8 %collective-permute-start.43 = (bf16[768,768]{1,0:T(8,128)(2,1)S(1)}, bf16[768,768]{1,0:T(8,128)(2,1)S(1)}, u32[]{:S(2)}, u32[]{:S(2)}) collective-permute-start(bf16[768,768]{1,0:T(8,128)(2,1)S(1)} %fusion.3), channel_id=1, source_target_pairs={{0,2},{1,3},{2,0},{3,1},{4,6},{5,7},{6,4},{7,5},{8,10},{9,11},{10,... | collective-permute-start | bytes 3538952 | tf_op jit(solution)/shard_map/ppermute | solution.py:756
  394.4 30.0 %collective-permute-start.53 = (bf16[768,768]{1,0:T(8,128)(2,1)S(1)}, bf16[768,768]{1,0:T(8,128)(2,1)S(1)}, u32[]{:S(2)}, u32[]{:S(2)}) collective-permute-start(bf16[768,768]{1,0:T(8,128)(2,1)S(1)} %fusion.4), channel_id=1, source_target_pairs={{0,2},{1,3},{2,0},{3,1},{4,6},{5,7},{6,4},{7,5},{8,10},{9,11},{10,... | collective-permute-start | bytes 3538952 | tf_op jit(solution)/shard_map/ppermute | solution.py:756
  395.0 29.4 %collective-permute-start.52 = (bf16[384,768]{1,0:T(8,128)(2,1)S(1)}, bf16[384,768]{1,0:T(8,128)(2,1)S(1)}, u32[]{:S(2)}, u32[]{:S(2)}) collective-permute-start(bf16[384,768]{1,0:T(8,128)(2,1)S(1)} %get-tuple-element.431), channel_id=1, source_target_pairs={{0,4},{4,0},{8,12},{12,8},{16,20},{20,16},{24,28},{28,24},{1,5},{5... | collective-permute-start | bytes 1769480 | tf_op jit(solution)/shard_map/ppermute | solution.py:761
  396.5 27.9 %collective-permute-start.54 = (bf16[384,768]{1,0:T(8,128)(2,1)S(1)}, bf16[384,768]{1,0:T(8,128)(2,1)S(1)}, u32[]{:S(2)}, u32[]{:S(2)}) collective-permute-start(bf16[384,768]{1,0:T(8,128)(2,1)S(1)} %add_convert_fusion.5.mine_ref), channel_id=1, source_target_pairs={{0,4},{4,0},{8,12},{12,8},{16,20},{20,16},{24,28},{28,24},{1,5},{5... | collective-permute-start | bytes 1769480 | tf_op jit(solution)/shard_map/ppermute | solution.py:761
  397.1 22.1 %collective-permute-start.50 = (bf16[192,768]{1,0:T(8,128)(2,1)S(1)}, bf16[192,768]{1,0:T(8,128)(2,1)S(1)}, u32[]{:S(2)}, u32[]{:S(2)}) collective-permute-start(bf16[192,768]{1,0:T(8,128)(2,1)S(1)} %add_convert_fusion.18), channel_id=1, source_target_pairs={{0,16},{4,20},{8,24},{12,28},{16,0},{20,4},{24,8},{28,12},{1,17},{... | collective-permute-start | bytes 884744 | tf_op jit(solution)/shard_map/ppermute | solution.py:761
  398.9 25.5 %collective-permute-start.51 = (bf16[192,768]{1,0:T(8,128)(2,1)S(1)}, bf16[192,768]{1,0:T(8,128)(2,1)S(1)}, u32[]{:S(2)}, u32[]{:S(2)}) collective-permute-start(bf16[192,768]{1,0:T(8,128)(2,1)S(1)} %add_convert_fusion.19), channel_id=1, source_target_pairs={{0,16},{4,20},{8,24},{12,28},{16,0},{20,4},{24,8},{28,12},{1,17},{... | collective-permute-start | bytes 884744 | tf_op jit(solution)/shard_map/ppermute | solution.py:761
  425.4 23.7 %collective-permute-start.58 = (bf16[384,768]{1,0:T(8,128)(2,1)S(1)}, bf16[384,768]{1,0:T(8,128)(2,1)S(1)}, u32[]{:S(2)}, u32[]{:S(2)}) collective-permute-start(bf16[384,768]{1,0:T(8,128)(2,1)S(1)} %get-tuple-element.446), channel_id=1, source_target_pairs={{0,4},{4,0},{8,12},{12,8},{16,20},{20,16},{24,28},{28,24},{1,5},{5... | collective-permute-start | bytes 1769480 | tf_op jit(solution)/shard_map/ppermute | solution.py:761
  427.1 16.1 %collective-permute-start.57 = (bf16[192,768]{1,0:T(8,128)(2,1)S(1)}, bf16[192,768]{1,0:T(8,128)(2,1)S(1)}, u32[]{:S(2)}, u32[]{:S(2)}) collective-permute-start(bf16[192,768]{1,0:T(8,128)(2,1)S(1)} %get-tuple-element.445), channel_id=1, source_target_pairs={{0,8},{4,12},{8,0},{12,4},{16,24},{20,28},{24,16},{28,20},{1,9},{5... | collective-permute-start | bytes 884744 | tf_op jit(solution)/shard_map/ppermute | solution.py:761
  429.1 20.0 %collective-permute-start.59 = (bf16[192,768]{1,0:T(8,128)(2,1)S(1)}, bf16[192,768]{1,0:T(8,128)(2,1)S(1)}, u32[]{:S(2)}, u32[]{:S(2)}) collective-permute-start(bf16[192,768]{1,0:T(8,128)(2,1)S(1)} %add_convert_fusion.16), channel_id=1, source_target_pairs={{0,8},{4,12},{8,0},{12,4},{16,24},{20,28},{24,16},{28,20},{1,9},{5... | collective-permute-start | bytes 884744 | tf_op jit(solution)/shard_map/ppermute | solution.py:761
  449.5 17.3 %collective-permute-start.63 = (bf16[384,768]{1,0:T(8,128)(2,1)S(1)}, bf16[384,768]{1,0:T(8,128)(2,1)S(1)}, u32[]{:S(2)}, u32[]{:S(2)}) collective-permute-start(bf16[384,768]{1,0:T(8,128)(2,1)S(1)} %pad_maximum_fusion.6.mine_ref), channel_id=1, source_target_pairs={{0,4},{4,0},{8,12},{12,8},{16,20},{20,16},{24,28},{28,24},{1,5},{5... | collective-permute-start | bytes 1769480 | tf_op jit(solution)/shard_map/ppermute | solution.py:761
  451.6 15.1 %collective-permute-start.61 = (bf16[192,768]{1,0:T(8,128)(2,1)S(1)}, bf16[192,768]{1,0:T(8,128)(2,1)S(1)}, u32[]{:S(2)}, u32[]{:S(2)}) collective-permute-start(bf16[192,768]{1,0:T(8,128)(2,1)S(1)} %add_convert_fusion.15), channel_id=1, source_target_pairs={{0,16},{4,20},{8,24},{12,28},{16,0},{20,4},{24,8},{28,12},{1,17},{... | collective-permute-start | bytes 884744 | tf_op jit(solution)/shard_map/ppermute | solution.py:761
  467.0 18.0 %collective-permute-start.67 = (bf16[384,768]{1,0:T(8,128)(2,1)S(1)}, bf16[384,768]{1,0:T(8,128)(2,1)S(1)}, u32[]{:S(2)}, u32[]{:S(2)}) collective-permute-start(bf16[384,768]{1,0:T(8,128)(2,1)S(1)} %pad_maximum_fusion.7.mine_ref), channel_id=1, source_target_pairs={{0,4},{4,0},{8,12},{12,8},{16,20},{20,16},{24,28},{28,24},{1,5},{5... | collective-permute-start | bytes 1769480 | tf_op jit(solution)/shard_map/ppermute | solution.py:761
  468.6 16.4 %collective-permute-start.64 = (f32[40,768]{1,0:T(8,128)S(1)}, f32[40,768]{1,0:T(8,128)S(1)}, u32[]{:S(2)}, u32[]{:S(2)}) collective-permute-start(f32[40,768]{1,0:T(8,128)S(1)} %add.202), channel_id=1, source_target_pairs={{0,4},{4,0},{8,12},{12,8},{16,20},{20,16},{24,28},{28,24},{1,5},{5... | collective-permute-start | bytes 368648 | tf_op jit(solution)/shard_map/ppermute | solution.py:761
  469.2 15.8 %collective-permute-start.65 = (bf16[192,768]{1,0:T(8,128)(2,1)S(1)}, bf16[192,768]{1,0:T(8,128)(2,1)S(1)}, u32[]{:S(2)}, u32[]{:S(2)}) collective-permute-start(bf16[192,768]{1,0:T(8,128)(2,1)S(1)} %add_convert_fusion.13), channel_id=1, source_target_pairs={{0,8},{4,12},{8,0},{12,4},{16,24},{20,28},{24,16},{28,20},{1,9},{5... | collective-permute-start | bytes 884744 | tf_op jit(solution)/shard_map/ppermute | solution.py:761
  469.3 15.7 %collective-permute-start.66 = (bf16[192,768]{1,0:T(8,128)(2,1)S(1)}, bf16[192,768]{1,0:T(8,128)(2,1)S(1)}, u32[]{:S(2)}, u32[]{:S(2)}) collective-permute-start(bf16[192,768]{1,0:T(8,128)(2,1)S(1)} %add_convert_fusion.14), channel_id=1, source_target_pairs={{0,16},{4,20},{8,24},{12,28},{16,0},{20,4},{24,8},{28,12},{1,17},{... | collective-permute-start | bytes 884744 | tf_op jit(solution)/shard_map/ppermute | solution.py:761
  (79 other events, 749.4 us)
Sparse Core Ops, SparseCore 0:
  85.2 50.4 all-gather.1

commit v7 on v6

--- a/solution.py
+++ b/solution.py
@@ -23,6 +23,7 @@
 f32 = jnp.float32
 bf16 = jnp.bfloat16
 VMEM_LIMIT = 44 * 1024 * 1024
+LIMITS = {"emit": 20 * 1024 * 1024, "grads_down": 24 * 1024 * 1024, "grads_attn": 24 * 1024 * 1024}
 TIMES = {
     "attend": 17, "feed": 23, "code_loss": 18, "feed_back": 26, "attend_back": 25,
     "grads_down": 10, "grads_attn": 11, "emit": 3,
@@ -285,7 +286,7 @@
             scratch_shapes=list(scratch),
         ),
         out_shape=[jax.ShapeDtypeStruct(shape, dtype) for shape, dtype, _ in outs],
-        compiler_params=pltpu.CompilerParams(vmem_limit_bytes=VMEM_LIMIT),
+        compiler_params=pltpu.CompilerParams(vmem_limit_bytes=LIMITS.get(name, VMEM_LIMIT)),
         cost_estimate=cost_of(name),
         input_output_aliases=aliases,
         name=name,
@@ -1114,7 +1115,7 @@
     ]
     wait = 0
     while swaps or not all(one.done() for one in moving + late + [attn_1]):
-        held = [attn_1] if wait == 1 else []
+        held = [down_0] if wait == 0 else []
         move(*[one for one in moving + [attn_1] + late if not one.done() and one not in held])
         wait += 1
         if swaps:

time: 532 us -> 525 us (0.987)
  waiting for transfers between devices: 152 us -> 146 us
    ppermute x35, waiting for transfers between devices: 91.8 us -> 86.5 us  [clip_swap(): lax.ppermute(values, 'clip', [(i, i ^ distance) for i in range(count)])]
where the time goes in v7:
time: 525 us; the launch traced here: 517 us
  Pallas kernels  229 us (44%)
  waiting for transfers between devices  146 us (28%)
  starting transfers between devices  66.4 us (13%)
  other arithmetic  29.6 us (6%)
  local copies, waits for them, and re-layouts  27.9 us (5%)
  between operations  17.7 us (3%)
    pallas_call x17, Pallas kernels, call(): pl.pallas_call(kernel, grid_spec=pltpu.PrefetchScalarGridSpec(num_scalar_...  229 us
    ppermute x35, waiting for transfers between devices, clip_swap(): lax.ppermute(values, 'clip', [(i, i ^ distance) for i in range(count)])  86.5 us
    ppermute x38, waiting for transfers between devices, head_swap(): lax.ppermute(values, 'head', [(i, i ^ distance) for i in range(count)])  42.9 us
    ppermute x35, starting transfers between devices, clip_swap(): lax.ppermute(values, 'clip', [(i, i ^ distance) for i in range(count)])  41.7 us
    ppermute x38, starting transfers between devices, head_swap(): lax.ppermute(values, 'head', [(i, i ^ distance) for i in range(count)])  24.7 us
    all_gather x1, waiting for transfers between devices, over_clips(): return lax.all_gather(chunk_across, 'clip', axis=0, tiled=True)  16.9 us
    unnamed x112, local copies, waits for them, and re-layouts  13.4 us
  transfers between devices with their start and end apart: 74, of which 30 were waited for; matrix products, arithmetic and copies ran while one was open for 6% of the time, Pallas kernels for 40%

profile of v7, /device:TPU:0, one launch (start us, length us, event | category | flops | bytes accessed | tf_op | source)
XLA Modules:
  0.0 516.8 jit_solution(3740361548348125170)
XLA Ops:
  7.2 2.8 fusion.8
  10.1 3.0 collective-permute-start
  13.1 2.8 fusion.9
  16.9 2.5 fusion.10
  20.9 5.6 %collective-permute-done.1 = bf16[192,768]{1,0:T(8,128)(2,1)} collective-permute-done((bf16[192,768]{1,0:T(8,128)(2,1)S(1)}, bf16[192,768]{1,0:T(8,128)(2,1)}, u32[]{:S(2)}, u32[]{:S(2)}) %collective-permute-start.1) | collective-permute-done | bytes 294944 | tf_op jit(solution)/shard_map/ppermute | solution.py:757
  30.5 4.3 collective-permute-done.3
  39.9 4.4 collective-permute-done.5
  45.3 3.2 collective-permute-done.4
  48.7 6.7 %collective-permute-done.2.refs_6_.refs_10_.refs_4_.refs_11_.refs_8_ = bf16[784,768]{1,0:T(8,128)(2,1)} collective-permute-done((bf16[784,768]{1,0:T(8,128)(2,1)S(1)}, bf16[784,768]{1,0:T(8,128)(2,1)}, u32[]{:S(2)}, u32[]{:S(2)}) %collective-permute-start.2) | collective-permute-done | bytes 1204256 | tf_op jit(solution)/shard_map/ppermute | solution.py:757
  55.5 3.1 collective-permute-done.7.refs_7_.refs_11_.refs_5_.refs_12_.refs_9_
  62.2 15.6 %attend.2 = (bf16[1024,768]{1,0:T(8,128)(2,1)S(1)}, bf16[1024,768]{1,0:T(8,128)(2,1)S(1)}, bf16[1024,2304]{1,0:T(8,128)(2,1)}, bf16[1024,768]{1,0:T(8,128)(2,1)S...) custom-call(s32[3]{0:T(128)S(1)} %pad_add_fusion.place_ref, ...), custom_call_target="tpu_custom_call" | custom-call | flops 19549999104 | bytes 61200000 | tf_op jit(solution)/shard_map/attend/pallas_call | solution.py:279
  85.2 2.4 pad_maximum_fusion.3.refs_10_.refs_2_.refs_6_
  88.5 23.2 %feed.2 = (f32[1024,768]{1,0:T(8,128)}, bf16[1024,768]{1,0:T(8,128)(2,1)}, bf16[1024,3072]{1,0:T(8,128)(2,1)}, bf16[1024,3072]{1,0:T(8,128)(2,1)}, bf16[4,64,768...) custom-call(s32[3]{0:T(128)S(1)} %pad_add_fusion.place_ref, ...), custom_call_target="tpu_custom_call" | custom-call | flops 26449999872 | bytes 82800000 | tf_op jit(solution)/shard_map/feed/pallas_call | solution.py:279
  112.4 4.1 collective-permute-done.14.refs_12_.refs_4_.refs_8_
  118.8 16.9 %all-gather.2.cloned.1.call-done = bf16[1536,768]{1,0:T(8,128)(2,1)} async-done(((bf16[192,768]{1,0:T(8,128)(2,1)}), bf16[1536,768]{1,0:T(8,128)(2,1)}) %all-gather.2.cloned.1.call-update) | async-done | bytes 2359312 | tf_op jit(solution)/shard_map/all_gather | solution.py:923
  140.1 17.2 %attend.3 = (bf16[1024,768]{1,0:T(8,128)(2,1)}, bf16[1024,768]{1,0:T(8,128)(2,1)}, bf16[1024,2304]{1,0:T(8,128)(2,1)}, bf16[1024,768]{1,0:T(8,128)(2,1)}, f32[64...) custom-call(s32[3]{0:T(128)S(1)} %pad_add_fusion.place_ref, bf16[4,4,16,768]{3,2,1,0:T(8,128)(2,1)S(1)} %bitcast.91, ...), custom_call_target="tpu_custom_call" | custom-call | flops 19549999104 | bytes 61200000 | tf_op jit(solution)/shard_map/attend/pallas_call | solution.py:279
  157.3 22.8 %feed.3 = (f32[1024,768]{1,0:T(8,128)}, bf16[1024,768]{1,0:T(8,128)(2,1)}, bf16[1024,3072]{1,0:T(8,128)(2,1)}, bf16[1024,3072]{1,0:T(8,128)(2,1)}, bf16[1024,768]{1,0:T(8,128)(2,1)}) custom-call(s32[3]{0:T(128)S(1)} %pad_add_fusion.place_ref, bf16[1024,768]{1,0:T(8,128)(2,1)} %get-tuple-element.295.refs_0_.refs_2_, ...), custom_call_target="tpu_custom_call" | custom-call | flops 26449999872 | bytes 82800000 | tf_op jit(solution)/shard_map/feed/pallas_call | solution.py:279
  181.6 19.0 %code_loss.1 = (f32[1024,768]{1,0:T(8,128)}, f32[8,768]{1,0:T(8,128)S(1)}, bf16[2,768,768]{2,1,0:T(8,128)(2,1)S(1)}, bf16[2,768,768]{2,1,0:T(8,128)(2,1)S(1)}) custom-call(s32[3]{0:T(128)S(1)} %pad_add_fusion.place_ref, bf16[1024,768]{1,0:T(8,128)(2,1)S(1)} %copy-done.31, bf16[768,1024]{1,0:T(8,128)(2,1)S(1)} %copy-done.4, ...), custom_call_target="tpu_custom_call" | custom-call | flops 20700000256 | bytes 64800000 | tf_op jit(solution)/shard_map/code_loss/pallas_call | solution.py:279
  201.0 4.2 collective-permute-done.25
  207.7 25.0 %feed_back.2 = (f32[1024,768]{1,0:T(8,128)}, bf16[1024,768]{1,0:T(8,128)(2,1)S(1)}, f32[8,768]{1,0:T(8,128)S(1)}, bf16[2,768,768]{2,1,0:T(8,128)(2,1)}, bf16[2,768,768]{2,1,0:T(8,128)(2,1)}) custom-call(s32[3]{0:T(128)S(1)} %pad_add_fusion.place_ref, f32[1024,768]{1,0:T(8,128)} %get-tuple-element.311.refs_0_, bf16[1024,3072]{1,0:T(8,128)(2,1)} %get-tuple-element.312.refs_1_, ...), custom_call_target="tpu_custom_call" | custom-call | flops 29899999232 | bytes 93600000 | tf_op jit(solution)/shard_map/feed_back/pallas_call | solution.py:279
  237.4 2.4 collective-permute-done.27
  243.6 23.5 %attend_back.2 = (bf16[4,1024,576]{2,1,0:T(8,128)(2,1)}, bf16[4,4,16,768]{3,2,1,0:T(8,128)(2,1)S(1)}, bf16[4,4,16,768]{3,2,1,0:T(8,128)(2,1)S(1)}, bf16[4,4,16,7...) custom-call(s32[3]{0:T(128)S(1)} %pad_add_fusion.place_ref, ...), custom_call_target="tpu_custom_call" | custom-call | flops 28750000128 | bytes 90000000 | tf_op jit(solution)/shard_map/attend_back/pallas_call | solution.py:279
  267.1 2.9 collective-permute-done.28
  277.1 2.5 copy-done.20
  279.5 6.8 %grads_attn.1 = (bf16[2,768,768]{2,1,0:T(8,128)(2,1)S(1)}, bf16[2,768,768]{2,1,0:T(8,128)(2,1)S(1)}) custom-call(s32[3]{0:T(128)S(1)} %pad_add_fusion.place_ref, bf16[4,1024,576]{2,1,0:T(8,128)(2,1)S(1)} %copy-done.20, bf16[1024,768]{1,0:T(8,128)(2,1)S(1)} %copy-done.22, bf16[4,1024,192]{2,1,0:T(8,128)(2,1)S(1)} %copy-done.21, bf16[1024,768]{1,0:T(8,128)(2,1)S(1)} %copy-done.24), custom_call_target="tpu_custom_call" | custom-call | flops 12650000384 | bytes 39600000 | tf_op jit(solution)/shard_map/grads_attn/pallas_call | solution.py:279
  286.3 5.4 %collective-permute-done.32 = bf16[4,4,16,768]{3,2,1,0:T(8,128)(2,1)S(1)} collective-permute-done((bf16[4,4,16,768]{3,2,1,0:T(8,128)(2,1)S(1)}, bf16[4,4,16,768]{3,2,1,0:T(8,128)(2,1)S(1)}, u32[]{:S(2)}, u32[]{:S(2)}) %collective-permute-start.32) | collective-permute-done | bytes 393248 | tf_op jit(solution)/shard_map/ppermute | solution.py:757
  292.2 7.3 %grads_down.1 = (bf16[2,768,768]{2,1,0:T(8,128)(2,1)S(1)}, bf16[2,768,768]{2,1,0:T(8,128)(2,1)S(1)}) custom-call(s32[3]{0:T(128)S(1)} %pad_add_fusion.place_ref, bf16[1024,3072]{1,0:T(8,128)(2,1)S(1)} %bitcast.93, bf16[1024,768]{1,0:T(8,128)(2,1)S(1)} %bitcast.80), custom_call_target="tpu_custom_call" | custom-call | flops 11500000256 | bytes 36000000 | tf_op jit(solution)/shard_map/grads_down/pallas_call | solution.py:279
  301.9 2.2 collective-permute-done.36
  310.8 25.0 %feed_back.3 = (f32[1024,768]{1,0:T(8,128)}, bf16[1024,768]{1,0:T(8,128)(2,1)S(1)}, f32[8,768]{1,0:T(8,128)S(1)}, bf16[2,768,768]{2,1,0:T(8,128)(2,1)}, bf16[2,768,768]{2,1,0:T(8,128)(2,1)}) custom-call(s32[3]{0:T(128)S(1)} %pad_add_fusion.place_ref, bf16[1024,768]{1,0:T(8,128)(2,1)S(1)} %bitcast.81, bf16[1024,3072]{1,0:T(8,128)(2,1)} %get-tuple-element.370.refs_1_, ...), custom_call_target="tpu_custom_call" | custom-call | flops 29899999232 | bytes 93600000 | tf_op jit(solution)/shard_map/feed_back/pallas_call | solution.py:279
  336.8 2.2 bitcast_add_fusion.2
  349.4 30.4 %attend_back.3 = (f32[1024,768]{1,0:T(8,128)}, f32[8,768]{1,0:T(8,128)S(1)}, bf16[2,768,768]{2,1,0:T(8,128)(2,1)}, bf16[2,768,768]{2,1,0:T(8,128)(2,1)}) custom-call(s32[3]{0:T(128)S(1)} %pad_add_fusion.place_ref, f32[1024,768]{1,0:T(8,128)} %get-tuple-element.394.refs_0_, bf16[1024,768]{1,0:T(8,128)(2,1)S(1)} %get-tuple-element.395.refs_1_, ...), custom_call_target="tpu_custom_call" | custom-call | flops 28750000128 | bytes 90000000 | tf_op jit(solution)/shard_map/attend_back/pallas_call | solution.py:279
  386.0 5.0 collective-permute-done.47
  398.2 18.4 %collective-permute-done.50 = bf16[192,768]{1,0:T(8,128)(2,1)S(1)} collective-permute-done((bf16[192,768]{1,0:T(8,128)(2,1)S(1)}, bf16[192,768]{1,0:T(8,128)(2,1)S(1)}, u32[]{:S(2)}, u32[]{:S(2)}) %collective-permute-start.50) | collective-permute-done | bytes 294944 | tf_op jit(solution)/shard_map/ppermute | solution.py:762
  416.6 5.3 %collective-permute-done.53 = bf16[192,768]{1,0:T(8,128)(2,1)S(1)} collective-permute-done((bf16[192,768]{1,0:T(8,128)(2,1)S(1)}, bf16[192,768]{1,0:T(8,128)(2,1)S(1)}, u32[]{:S(2)}, u32[]{:S(2)}) %collective-permute-start.53) | collective-permute-done | bytes 294944 | tf_op jit(solution)/shard_map/ppermute | solution.py:762
  426.5 2.2 emit.6.refs_0_
  428.7 5.5 %collective-permute-done.56 = bf16[192,768]{1,0:T(8,128)(2,1)S(1)} collective-permute-done((bf16[192,768]{1,0:T(8,128)(2,1)S(1)}, bf16[192,768]{1,0:T(8,128)(2,1)S(1)}, u32[]{:S(2)}, u32[]{:S(2)}) %collective-permute-start.56) | collective-permute-done | bytes 294944 | tf_op jit(solution)/shard_map/ppermute | solution.py:762
  434.3 5.9 %collective-permute-done.57 = bf16[192,768]{1,0:T(8,128)(2,1)S(1)} collective-permute-done((bf16[192,768]{1,0:T(8,128)(2,1)S(1)}, bf16[192,768]{1,0:T(8,128)(2,1)S(1)}, u32[]{:S(2)}, u32[]{:S(2)}) %collective-permute-start.57) | collective-permute-done | bytes 294944 | tf_op jit(solution)/shard_map/ppermute | solution.py:762
  445.4 2.2 emit.7.refs_0_
  447.7 10.7 %collective-permute-done.60 = bf16[192,768]{1,0:T(8,128)(2,1)S(1)} collective-permute-done((bf16[192,768]{1,0:T(8,128)(2,1)S(1)}, bf16[192,768]{1,0:T(8,128)(2,1)S(1)}, u32[]{:S(2)}, u32[]{:S(2)}) %collective-permute-start.60) | collective-permute-done | bytes 294944 | tf_op jit(solution)/shard_map/ppermute | solution.py:762
  458.3 5.1 collective-permute-done.62
  468.2 2.2 emit.8
  470.5 10.0 %collective-permute-done.64 = f32[40,768]{1,0:T(8,128)S(1)} collective-permute-done((f32[40,768]{1,0:T(8,128)S(1)}, f32[40,768]{1,0:T(8,128)S(1)}, u32[]{:S(2)}, u32[]{:S(2)}) %collective-permute-start.64) | collective-permute-done | bytes 122912 | tf_op jit(solution)/shard_map/ppermute | solution.py:762
  484.3 2.2 emit.9
  488.3 3.1 collective-permute-done.69
  491.5 2.5 collective-permute-done.70.other_ref
  495.7 2.2 emit.10
  497.9 2.2 collective-permute-done.71
  506.5 2.2 emit.11
  (320 shorter events, 113.2 us)
Async XLA Ops:
  7.2 128.5 %all-gather.2.cloned.1.call-start = ((), (), s32[]{:S(2)}) async-start(), calls=%async_computation | async-start | bytes 2654208 | tf_op jit(solution)/shard_map/all_gather | solution.py:923
  28.3 27.2 %collective-permute-start.2 = (bf16[784,768]{1,0:T(8,128)(2,1)S(1)}, bf16[784,768]{1,0:T(8,128)(2,1)}, u32[]{:S(2)}, u32[]{:S(2)}) collective-permute-start(bf16[784,768]{1,0:T(8,128)(2,1)S(1)} %concatenate.40.refs_4_.refs_8_.refs_2_.refs_9_.refs_6_), channel_id=1, source_target_pairs={{0,2},{1,3},{2,0},{3,1},{4,6},{5,7},{6,4},{7,5},{8,10},{9,11},{10,... | collective-permute-start | bytes 3612680 | tf_op jit(solution)/shard_map/ppermute | solution.py:757
  39.9 15.6 %collective-permute-start.6 = (bf16[784,768]{1,0:T(8,128)(2,1)S(1)}, bf16[784,768]{1,0:T(8,128)(2,1)S(1)}, u32[]{:S(2)}, u32[]{:S(2)}) collective-permute-start(bf16[784,768]{1,0:T(8,128)(2,1)S(1)} %concatenate.40.refs_4_.refs_8_.refs_2_.refs_9_.refs_6_), channel_id=1, source_target_pairs={{0,1},{1,0},{2,3},{3,2},{4,5},{5,4},{6,7},{7,6},{8,9},{9,8},{10,11... | collective-permute-start | bytes 3612680 | tf_op jit(solution)/shard_map/ppermute | solution.py:757
  58.6 22.7 %collective-permute-start.10 = (bf16[2,768,768]{2,1,0:T(8,128)(2,1)}, bf16[2,768,768]{2,1,0:T(8,128)(2,1)}, u32[]{:S(2)}, u32[]{:S(2)}) collective-permute-start(bf16[2,768,768]{2,1,0:T(8,128)(2,1)} %refs_5_.8), channel_id=1, source_target_pairs={{0,1},{1,0},{2,3},{3,2},{4,5},{5,4},{6,7},{7,6},{8,9},{9,8},{10,11... | collective-permute-start | bytes 7077896 | tf_op jit(solution)/shard_map/ppermute | solution.py:757
  58.7 22.5 %collective-permute-start.11 = (bf16[2,768,768]{2,1,0:T(8,128)(2,1)}, bf16[2,768,768]{2,1,0:T(8,128)(2,1)}, u32[]{:S(2)}, u32[]{:S(2)}) collective-permute-start(bf16[2,768,768]{2,1,0:T(8,128)(2,1)} %refs_9_.3), channel_id=1, source_target_pairs={{0,1},{1,0},{2,3},{3,2},{4,5},{5,4},{6,7},{7,6},{8,9},{9,8},{10,11... | collective-permute-start | bytes 7077896 | tf_op jit(solution)/shard_map/ppermute | solution.py:757
  59.1 22.1 %collective-permute-start.9 = (bf16[192,768]{1,0:T(8,128)(2,1)S(1)}, bf16[192,768]{1,0:T(8,128)(2,1)}, u32[]{:S(2)}, u32[]{:S(2)}) collective-permute-start(bf16[192,768]{1,0:T(8,128)(2,1)S(1)} %pad_maximum_fusion.10), channel_id=1, source_target_pairs={{0,2},{1,3},{2,0},{3,1},{4,6},{5,7},{6,4},{7,5},{8,10},{9,11},{10,... | collective-permute-start | bytes 884744 | tf_op jit(solution)/shard_map/ppermute | solution.py:757
  60.6 20.6 %collective-permute-start.8 = (bf16[384,768]{1,0:T(8,128)(2,1)S(1)}, bf16[384,768]{1,0:T(8,128)(2,1)}, u32[]{:S(2)}, u32[]{:S(2)}) collective-permute-start(bf16[384,768]{1,0:T(8,128)(2,1)S(1)} %pad_maximum_fusion.5), channel_id=1, source_target_pairs={{0,8},{4,12},{8,0},{12,4},{16,24},{20,28},{24,16},{28,20},{1,9},{5... | collective-permute-start | bytes 1769480 | tf_op jit(solution)/shard_map/ppermute | solution.py:762
  62.1 19.1 %collective-permute-start.12 = (bf16[768,768]{1,0:T(8,128)(2,1)S(1)}, bf16[768,768]{1,0:T(8,128)(2,1)}, u32[]{:S(2)}, u32[]{:S(2)}) collective-permute-start(bf16[768,768]{1,0:T(8,128)(2,1)S(1)} %pad_maximum_fusion.1.refs_15_.refs_7_), channel_id=1, source_target_pairs={{0,1},{1,0},{2,3},{3,2},{4,5},{5,4},{6,7},{7,6},{8,9},{9,8},{10,11... | collective-permute-start | bytes 3538952 | tf_op jit(solution)/shard_map/ppermute | solution.py:757
  87.9 28.6 %collective-permute-start.14 = (bf16[768,768]{1,0:T(8,128)(2,1)}, bf16[768,768]{1,0:T(8,128)(2,1)}, u32[]{:S(2)}, u32[]{:S(2)}) collective-permute-start(bf16[768,768]{1,0:T(8,128)(2,1)} %pad_maximum_fusion.3.refs_10_.refs_2_.refs_6_), channel_id=1, source_target_pairs={{0,2},{1,3},{2,0},{3,1},{4,6},{5,7},{6,4},{7,5},{8,10},{9,11},{10,... | collective-permute-start | bytes 3538952 | tf_op jit(solution)/shard_map/ppermute | solution.py:757
  116.5 23.1 %collective-permute-start.18 = (bf16[768,768]{1,0:T(8,128)(2,1)}, bf16[768,768]{1,0:T(8,128)(2,1)}, u32[]{:S(2)}, u32[]{:S(2)}) collective-permute-start(bf16[768,768]{1,0:T(8,128)(2,1)} %collective-permute-done.14.refs_12_.refs_4_.refs_8_), channel_id=1, source_target_pairs={{0,1},{1,0},{2,3},{3,2},{4,5},{5,4},{6,7},{7,6},{8,9},{9,8},{10,11... | collective-permute-start | bytes 3538952 | tf_op jit(solution)/shard_map/ppermute | solution.py:757
  116.5 23.5 %collective-permute-start.19 = (bf16[768,768]{1,0:T(8,128)(2,1)}, bf16[768,768]{1,0:T(8,128)(2,1)}, u32[]{:S(2)}, u32[]{:S(2)}) collective-permute-start(bf16[768,768]{1,0:T(8,128)(2,1)} %pad_maximum_fusion.3.refs_10_.refs_2_.refs_6_), channel_id=1, source_target_pairs={{0,1},{1,0},{2,3},{3,2},{4,5},{5,4},{6,7},{7,6},{8,9},{9,8},{10,11... | collective-permute-start | bytes 3538952 | tf_op jit(solution)/shard_map/ppermute | solution.py:757
  117.0 20.6 %collective-permute-start.17 = (bf16[4,64,768]{2,1,0:T(8,128)(2,1)}, bf16[4,64,768]{2,1,0:T(8,128)(2,1)S(1)}, u32[]{:S(2)}, u32[]{:S(2)}) collective-permute-start(bf16[4,64,768]{2,1,0:T(8,128)(2,1)} %get-tuple-element.284), channel_id=1, source_target_pairs={{0,3},{1,2},{2,1},{3,0},{4,7},{5,6},{6,5},{7,4},{8,11},{9,10},{10,... | collective-permute-start | bytes 1179656 | tf_op jit(solution)/shard_map/ppermute | solution.py:757
  117.1 20.6 %collective-permute-start.16 = (bf16[4,64,768]{2,1,0:T(8,128)(2,1)}, bf16[4,64,768]{2,1,0:T(8,128)(2,1)S(1)}, u32[]{:S(2)}, u32[]{:S(2)}) collective-permute-start(bf16[4,64,768]{2,1,0:T(8,128)(2,1)} %get-tuple-element.282), channel_id=1, source_target_pairs={{0,2},{1,3},{2,0},{3,1},{4,6},{5,7},{6,4},{7,5},{8,10},{9,11},{10,... | collective-permute-start | bytes 1179656 | tf_op jit(solution)/shard_map/ppermute | solution.py:757
  118.6 20.6 %collective-permute-start.15 = (bf16[4,64,768]{2,1,0:T(8,128)(2,1)}, bf16[4,64,768]{2,1,0:T(8,128)(2,1)}, u32[]{:S(2)}, u32[]{:S(2)}) collective-permute-start(bf16[4,64,768]{2,1,0:T(8,128)(2,1)} %get-tuple-element.280), channel_id=1, source_target_pairs={{0,1},{1,0},{2,3},{3,2},{4,5},{5,4},{6,7},{7,6},{8,9},{9,8},{10,11... | collective-permute-start | bytes 1179656 | tf_op jit(solution)/shard_map/ppermute | solution.py:757
  137.6 42.5 %collective-permute-start.22 = (f32[4,64]{1,0:T(4,128)S(1)}, f32[4,64]{1,0:T(4,128)S(1)}, u32[]{:S(2)}, u32[]{:S(2)}) collective-permute-start(f32[4,64]{1,0:T(4,128)S(1)} %get-tuple-element.301), channel_id=1, source_target_pairs={{0,1},{1,0},{2,3},{3,2},{4,5},{5,4},{6,7},{7,6},{8,9},{9,8},{10,11... | collective-permute-start | bytes 3080 | tf_op jit(solution)/shard_map/ppermute | solution.py:757
  137.7 42.4 %collective-permute-start.23 = (f32[4,64]{1,0:T(4,128)S(1)}, f32[4,64]{1,0:T(4,128)S(1)}, u32[]{:S(2)}, u32[]{:S(2)}) collective-permute-start(f32[4,64]{1,0:T(4,128)S(1)} %get-tuple-element.302), channel_id=1, source_target_pairs={{0,2},{1,3},{2,0},{3,1},{4,6},{5,7},{6,4},{7,5},{8,10},{9,11},{10,... | collective-permute-start | bytes 3080 | tf_op jit(solution)/shard_map/ppermute | solution.py:757
  139.3 40.9 %collective-permute-start.24 = (f32[4,64]{1,0:T(4,128)S(1)}, f32[4,64]{1,0:T(4,128)S(1)}, u32[]{:S(2)}, u32[]{:S(2)}) collective-permute-start(f32[4,64]{1,0:T(4,128)S(1)} %get-tuple-element.303), channel_id=1, source_target_pairs={{0,3},{1,2},{2,1},{3,0},{4,7},{5,6},{6,5},{7,4},{8,11},{9,10},{10,... | collective-permute-start | bytes 3080 | tf_op jit(solution)/shard_map/ppermute | solution.py:757
  139.6 17.7 %collective-permute-start.20 = (bf16[768,768]{1,0:T(8,128)(2,1)S(1)}, bf16[768,768]{1,0:T(8,128)(2,1)S(1)}, u32[]{:S(2)}, u32[]{:S(2)}) collective-permute-start(bf16[768,768]{1,0:T(8,128)(2,1)S(1)} %bitcast.85), channel_id=1, source_target_pairs={{0,1},{1,0},{2,3},{3,2},{4,5},{5,4},{6,7},{7,6},{8,9},{9,8},{10,11... | collective-permute-start | bytes 3538952 | tf_op jit(solution)/shard_map/ppermute | solution.py:757
  139.9 17.3 %collective-permute-start.21 = (bf16[768,768]{1,0:T(8,128)(2,1)S(1)}, bf16[768,768]{1,0:T(8,128)(2,1)S(1)}, u32[]{:S(2)}, u32[]{:S(2)}) collective-permute-start(bf16[768,768]{1,0:T(8,128)(2,1)S(1)} %bitcast.82), channel_id=1, source_target_pairs={{0,1},{1,0},{2,3},{3,2},{4,5},{5,4},{6,7},{7,6},{8,9},{9,8},{10,11... | collective-permute-start | bytes 3538952 | tf_op jit(solution)/shard_map/ppermute | solution.py:757
  205.5 28.3 %collective-permute-start.26 = (bf16[768,768]{1,0:T(8,128)(2,1)S(1)}, bf16[768,768]{1,0:T(8,128)(2,1)S(1)}, u32[]{:S(2)}, u32[]{:S(2)}) collective-permute-start(bf16[768,768]{1,0:T(8,128)(2,1)S(1)} %fusion), channel_id=1, source_target_pairs={{0,2},{1,3},{2,0},{3,1},{4,6},{5,7},{6,4},{7,5},{8,10},{9,11},{10,... | collective-permute-start | bytes 3538952 | tf_op jit(solution)/shard_map/ppermute | solution.py:757
  241.5 25.7 %collective-permute-start.29 = (bf16[384,768]{1,0:T(8,128)(2,1)S(1)}, bf16[384,768]{1,0:T(8,128)(2,1)S(1)}, u32[]{:S(2)}, u32[]{:S(2)}) collective-permute-start(bf16[384,768]{1,0:T(8,128)(2,1)S(1)} %get-tuple-element.333), channel_id=1, source_target_pairs={{0,4},{4,0},{8,12},{12,8},{16,20},{20,16},{24,28},{28,24},{1,5},{5... | collective-permute-start | bytes 1769480 | tf_op jit(solution)/shard_map/ppermute | solution.py:762
  242.1 27.9 %collective-permute-start.28 = (bf16[768,768]{1,0:T(8,128)(2,1)S(1)}, bf16[768,768]{1,0:T(8,128)(2,1)S(1)}, u32[]{:S(2)}, u32[]{:S(2)}) collective-permute-start(bf16[768,768]{1,0:T(8,128)(2,1)S(1)} %fusion.1), channel_id=1, source_target_pairs={{0,2},{1,3},{2,0},{3,1},{4,6},{5,7},{6,4},{7,5},{8,10},{9,11},{10,... | collective-permute-start | bytes 3538952 | tf_op jit(solution)/shard_map/ppermute | solution.py:757
  273.8 17.9 %collective-permute-start.32 = (bf16[4,4,16,768]{3,2,1,0:T(8,128)(2,1)S(1)}, bf16[4,4,16,768]{3,2,1,0:T(8,128)(2,1)S(1)}, u32[]{:S(2)}, u32[]{:S(2)}) collective-permute-start(bf16[4,4,16,768]{3,2,1,0:T(8,128)(2,1)S(1)} %get-tuple-element.338), channel_id=1, source_target_pairs={{0,3},{1,2},{2,1},{3,0},{4,7},{5,6},{6,5},{7,4},{8,11},{9,10},{10,... | collective-permute-start | bytes 1179656 | tf_op jit(solution)/shard_map/ppermute | solution.py:757
  274.1 17.6 %collective-permute-start.33 = (bf16[384,768]{1,0:T(8,128)(2,1)S(1)}, bf16[384,768]{1,0:T(8,128)(2,1)S(1)}, u32[]{:S(2)}, u32[]{:S(2)}) collective-permute-start(bf16[384,768]{1,0:T(8,128)(2,1)S(1)} %get-tuple-element.352), channel_id=1, source_target_pairs={{0,4},{4,0},{8,12},{12,8},{16,20},{20,16},{24,28},{28,24},{1,5},{5... | collective-permute-start | bytes 1769480 | tf_op jit(solution)/shard_map/ppermute | solution.py:762
  275.6 16.2 %collective-permute-start.34 = (bf16[384,768]{1,0:T(8,128)(2,1)S(1)}, bf16[384,768]{1,0:T(8,128)(2,1)S(1)}, u32[]{:S(2)}, u32[]{:S(2)}) collective-permute-start(bf16[384,768]{1,0:T(8,128)(2,1)S(1)} %add_convert_fusion.11), channel_id=1, source_target_pairs={{0,8},{4,12},{8,0},{12,4},{16,24},{20,28},{24,16},{28,20},{1,9},{5... | collective-permute-start | bytes 1769480 | tf_op jit(solution)/shard_map/ppermute | solution.py:762
  305.5 30.4 %collective-permute-start.39 = (bf16[384,768]{1,0:T(8,128)(2,1)S(1)}, bf16[384,768]{1,0:T(8,128)(2,1)S(1)}, u32[]{:S(2)}, u32[]{:S(2)}) collective-permute-start(bf16[384,768]{1,0:T(8,128)(2,1)S(1)} %add_convert_fusion.10), channel_id=1, source_target_pairs={{0,16},{4,20},{8,24},{12,28},{16,0},{20,4},{24,8},{28,12},{1,17},{... | collective-permute-start | bytes 1769480 | tf_op jit(solution)/shard_map/ppermute | solution.py:762
  307.4 28.5 %collective-permute-start.40 = (bf16[384,768]{1,0:T(8,128)(2,1)S(1)}, bf16[384,768]{1,0:T(8,128)(2,1)S(1)}, u32[]{:S(2)}, u32[]{:S(2)}) collective-permute-start(bf16[384,768]{1,0:T(8,128)(2,1)S(1)} %add_convert_fusion.9), channel_id=1, source_target_pairs={{0,8},{4,12},{8,0},{12,4},{16,24},{20,28},{24,16},{28,20},{1,9},{5... | collective-permute-start | bytes 1769480 | tf_op jit(solution)/shard_map/ppermute | solution.py:762
  307.9 28.0 %collective-permute-start.37 = (bf16[768,768]{1,0:T(8,128)(2,1)}, bf16[768,768]{1,0:T(8,128)(2,1)}, u32[]{:S(2)}, u32[]{:S(2)}) collective-permute-start(bf16[768,768]{1,0:T(8,128)(2,1)} %fusion.2), channel_id=1, source_target_pairs={{0,2},{1,3},{2,0},{3,1},{4,6},{5,7},{6,4},{7,5},{8,10},{9,11},{10,... | collective-permute-start | bytes 3538952 | tf_op jit(solution)/shard_map/ppermute | solution.py:757
  309.4 27.5 %collective-permute-start.38 = (bf16[2,384,768]{2,1,0:T(8,128)(2,1)}, bf16[2,384,768]{2,1,0:T(8,128)(2,1)S(1)}, u32[]{:S(2)}, u32[]{:S(2)}) collective-permute-start(bf16[2,384,768]{2,1,0:T(8,128)(2,1)} %get-tuple-element.379), channel_id=1, source_target_pairs={{0,4},{4,0},{8,12},{12,8},{16,20},{20,16},{24,28},{28,24},{1,5},{5... | collective-permute-start | bytes 3538952 | tf_op jit(solution)/shard_map/ppermute | solution.py:762
  344.3 35.5 %collective-permute-start.42 = (bf16[2,192,768]{2,1,0:T(8,128)(2,1)}, bf16[2,192,768]{2,1,0:T(8,128)(2,1)S(1)}, u32[]{:S(2)}, u32[]{:S(2)}) collective-permute-start(bf16[2,192,768]{2,1,0:T(8,128)(2,1)} %get-tuple-element.403), channel_id=1, source_target_pairs={{0,8},{4,12},{8,0},{12,4},{16,24},{20,28},{24,16},{28,20},{1,9},{5... | collective-permute-start | bytes 1769480 | tf_op jit(solution)/shard_map/ppermute | solution.py:762
  345.8 34.1 %collective-permute-start.44 = (bf16[384,768]{1,0:T(8,128)(2,1)}, bf16[384,768]{1,0:T(8,128)(2,1)S(1)}, u32[]{:S(2)}, u32[]{:S(2)}) collective-permute-start(bf16[384,768]{1,0:T(8,128)(2,1)} %get-tuple-element.406), channel_id=1, source_target_pairs={{0,4},{4,0},{8,12},{12,8},{16,20},{20,16},{24,28},{28,24},{1,5},{5... | collective-permute-start | bytes 1769480 | tf_op jit(solution)/shard_map/ppermute | solution.py:762
  347.2 32.6 %collective-permute-start.45 = (bf16[384,768]{1,0:T(8,128)(2,1)S(1)}, bf16[384,768]{1,0:T(8,128)(2,1)S(1)}, u32[]{:S(2)}, u32[]{:S(2)}) collective-permute-start(bf16[384,768]{1,0:T(8,128)(2,1)S(1)} %add_convert_fusion.8), channel_id=1, source_target_pairs={{0,16},{4,20},{8,24},{12,28},{16,0},{20,4},{24,8},{28,12},{1,17},{... | collective-permute-start | bytes 1769480 | tf_op jit(solution)/shard_map/ppermute | solution.py:762
  348.3 31.6 %collective-permute-start.46 = (bf16[384,768]{1,0:T(8,128)(2,1)S(1)}, bf16[384,768]{1,0:T(8,128)(2,1)S(1)}, u32[]{:S(2)}, u32[]{:S(2)}) collective-permute-start(bf16[384,768]{1,0:T(8,128)(2,1)S(1)} %add_convert_fusion.7.mine_ref), channel_id=1, source_target_pairs={{0,4},{4,0},{8,12},{12,8},{16,20},{20,16},{24,28},{28,24},{1,5},{5... | collective-permute-start | bytes 1769480 | tf_op jit(solution)/shard_map/ppermute | solution.py:762
  348.9 31.0 %collective-permute-start.43 = (bf16[768,768]{1,0:T(8,128)(2,1)S(1)}, bf16[768,768]{1,0:T(8,128)(2,1)S(1)}, u32[]{:S(2)}, u32[]{:S(2)}) collective-permute-start(bf16[768,768]{1,0:T(8,128)(2,1)S(1)} %fusion.3), channel_id=1, source_target_pairs={{0,2},{1,3},{2,0},{3,1},{4,6},{5,7},{6,4},{7,5},{8,10},{9,11},{10,... | collective-permute-start | bytes 3538952 | tf_op jit(solution)/shard_map/ppermute | solution.py:757
  392.6 29.3 %collective-permute-start.52 = (bf16[768,768]{1,0:T(8,128)(2,1)S(1)}, bf16[768,768]{1,0:T(8,128)(2,1)S(1)}, u32[]{:S(2)}, u32[]{:S(2)}) collective-permute-start(bf16[768,768]{1,0:T(8,128)(2,1)S(1)} %fusion.4), channel_id=1, source_target_pairs={{0,2},{1,3},{2,0},{3,1},{4,6},{5,7},{6,4},{7,5},{8,10},{9,11},{10,... | collective-permute-start | bytes 3538952 | tf_op jit(solution)/shard_map/ppermute | solution.py:757
  393.2 28.6 %collective-permute-start.51 = (bf16[384,768]{1,0:T(8,128)(2,1)S(1)}, bf16[384,768]{1,0:T(8,128)(2,1)S(1)}, u32[]{:S(2)}, u32[]{:S(2)}) collective-permute-start(bf16[384,768]{1,0:T(8,128)(2,1)S(1)} %get-tuple-element.430), channel_id=1, source_target_pairs={{0,4},{4,0},{8,12},{12,8},{16,20},{20,16},{24,28},{28,24},{1,5},{5... | collective-permute-start | bytes 1769480 | tf_op jit(solution)/shard_map/ppermute | solution.py:762
  394.7 27.2 %collective-permute-start.54 = (bf16[384,768]{1,0:T(8,128)(2,1)S(1)}, bf16[384,768]{1,0:T(8,128)(2,1)S(1)}, u32[]{:S(2)}, u32[]{:S(2)}) collective-permute-start(bf16[384,768]{1,0:T(8,128)(2,1)S(1)} %add_convert_fusion.5.mine_ref), channel_id=1, source_target_pairs={{0,4},{4,0},{8,12},{12,8},{16,20},{20,16},{24,28},{28,24},{1,5},{5... | collective-permute-start | bytes 1769480 | tf_op jit(solution)/shard_map/ppermute | solution.py:762
  395.3 21.4 %collective-permute-start.50 = (bf16[192,768]{1,0:T(8,128)(2,1)S(1)}, bf16[192,768]{1,0:T(8,128)(2,1)S(1)}, u32[]{:S(2)}, u32[]{:S(2)}) collective-permute-start(bf16[192,768]{1,0:T(8,128)(2,1)S(1)} %add_convert_fusion.18), channel_id=1, source_target_pairs={{0,16},{4,20},{8,24},{12,28},{16,0},{20,4},{24,8},{28,12},{1,17},{... | collective-permute-start | bytes 884744 | tf_op jit(solution)/shard_map/ppermute | solution.py:762
  397.1 24.7 %collective-permute-start.53 = (bf16[192,768]{1,0:T(8,128)(2,1)S(1)}, bf16[192,768]{1,0:T(8,128)(2,1)S(1)}, u32[]{:S(2)}, u32[]{:S(2)}) collective-permute-start(bf16[192,768]{1,0:T(8,128)(2,1)S(1)} %add_convert_fusion.19), channel_id=1, source_target_pairs={{0,16},{4,20},{8,24},{12,28},{16,0},{20,4},{24,8},{28,12},{1,17},{... | collective-permute-start | bytes 884744 | tf_op jit(solution)/shard_map/ppermute | solution.py:762
  422.8 17.4 %collective-permute-start.58 = (bf16[384,768]{1,0:T(8,128)(2,1)S(1)}, bf16[384,768]{1,0:T(8,128)(2,1)S(1)}, u32[]{:S(2)}, u32[]{:S(2)}) collective-permute-start(bf16[384,768]{1,0:T(8,128)(2,1)S(1)} %get-tuple-element.444), channel_id=1, source_target_pairs={{0,4},{4,0},{8,12},{12,8},{16,20},{20,16},{24,28},{28,24},{1,5},{5... | collective-permute-start | bytes 1769480 | tf_op jit(solution)/shard_map/ppermute | solution.py:762
  424.5 15.7 %collective-permute-start.57 = (bf16[192,768]{1,0:T(8,128)(2,1)S(1)}, bf16[192,768]{1,0:T(8,128)(2,1)S(1)}, u32[]{:S(2)}, u32[]{:S(2)}) collective-permute-start(bf16[192,768]{1,0:T(8,128)(2,1)S(1)} %get-tuple-element.443), channel_id=1, source_target_pairs={{0,8},{4,12},{8,0},{12,4},{16,24},{20,28},{24,16},{28,20},{1,9},{5... | collective-permute-start | bytes 884744 | tf_op jit(solution)/shard_map/ppermute | solution.py:762
  440.6 22.8 %collective-permute-start.63 = (bf16[384,768]{1,0:T(8,128)(2,1)S(1)}, bf16[384,768]{1,0:T(8,128)(2,1)S(1)}, u32[]{:S(2)}, u32[]{:S(2)}) collective-permute-start(bf16[384,768]{1,0:T(8,128)(2,1)S(1)} %pad_maximum_fusion.6.mine_ref), channel_id=1, source_target_pairs={{0,4},{4,0},{8,12},{12,8},{16,20},{20,16},{24,28},{28,24},{1,5},{5... | collective-permute-start | bytes 1769480 | tf_op jit(solution)/shard_map/ppermute | solution.py:762
  442.7 15.6 %collective-permute-start.60 = (bf16[192,768]{1,0:T(8,128)(2,1)S(1)}, bf16[192,768]{1,0:T(8,128)(2,1)S(1)}, u32[]{:S(2)}, u32[]{:S(2)}) collective-permute-start(bf16[192,768]{1,0:T(8,128)(2,1)S(1)} %add_convert_fusion.15), channel_id=1, source_target_pairs={{0,8},{4,12},{8,0},{12,4},{16,24},{20,28},{24,16},{28,20},{1,9},{5... | collective-permute-start | bytes 884744 | tf_op jit(solution)/shard_map/ppermute | solution.py:762
  443.0 15.3 %collective-permute-start.61 = (bf16[192,768]{1,0:T(8,128)(2,1)S(1)}, bf16[192,768]{1,0:T(8,128)(2,1)S(1)}, u32[]{:S(2)}, u32[]{:S(2)}) collective-permute-start(bf16[192,768]{1,0:T(8,128)(2,1)S(1)} %add_convert_fusion.16), channel_id=1, source_target_pairs={{0,16},{4,20},{8,24},{12,28},{16,0},{20,4},{24,8},{28,12},{1,17},{... | collective-permute-start | bytes 884744 | tf_op jit(solution)/shard_map/ppermute | solution.py:762
  445.1 18.2 %collective-permute-start.62 = (bf16[192,768]{1,0:T(8,128)(2,1)S(1)}, bf16[192,768]{1,0:T(8,128)(2,1)S(1)}, u32[]{:S(2)}, u32[]{:S(2)}) collective-permute-start(bf16[192,768]{1,0:T(8,128)(2,1)S(1)} %get-tuple-element.458), channel_id=1, source_target_pairs={{0,8},{4,12},{8,0},{12,4},{16,24},{20,28},{24,16},{28,20},{1,9},{5... | collective-permute-start | bytes 884744 | tf_op jit(solution)/shard_map/ppermute | solution.py:762
  463.6 16.8 %collective-permute-start.67 = (bf16[384,768]{1,0:T(8,128)(2,1)S(1)}, bf16[384,768]{1,0:T(8,128)(2,1)S(1)}, u32[]{:S(2)}, u32[]{:S(2)}) collective-permute-start(bf16[384,768]{1,0:T(8,128)(2,1)S(1)} %pad_maximum_fusion.7.mine_ref), channel_id=1, source_target_pairs={{0,4},{4,0},{8,12},{12,8},{16,20},{20,16},{24,28},{28,24},{1,5},{5... | collective-permute-start | bytes 1769480 | tf_op jit(solution)/shard_map/ppermute | solution.py:762
  465.2 15.3 %collective-permute-start.64 = (f32[40,768]{1,0:T(8,128)S(1)}, f32[40,768]{1,0:T(8,128)S(1)}, u32[]{:S(2)}, u32[]{:S(2)}) collective-permute-start(f32[40,768]{1,0:T(8,128)S(1)} %add.202), channel_id=1, source_target_pairs={{0,4},{4,0},{8,12},{12,8},{16,20},{20,16},{24,28},{28,24},{1,5},{5... | collective-permute-start | bytes 368648 | tf_op jit(solution)/shard_map/ppermute | solution.py:762
  465.8 14.6 %collective-permute-start.65 = (bf16[192,768]{1,0:T(8,128)(2,1)S(1)}, bf16[192,768]{1,0:T(8,128)(2,1)S(1)}, u32[]{:S(2)}, u32[]{:S(2)}) collective-permute-start(bf16[192,768]{1,0:T(8,128)(2,1)S(1)} %add_convert_fusion.13), channel_id=1, source_target_pairs={{0,8},{4,12},{8,0},{12,4},{16,24},{20,28},{24,16},{28,20},{1,9},{5... | collective-permute-start | bytes 884744 | tf_op jit(solution)/shard_map/ppermute | solution.py:762
  (79 other events, 776.4 us)
Sparse Core Ops, SparseCore 0:
  85.2 50.4 all-gather.1

commit v8 on v7

--- a/solution.py
+++ b/solution.py
@@ -145,8 +145,9 @@
     return (source == plain).astype(f32).astype(bf16)
 
 
-def small_rows(ref, start, count=1):
-    terms = [ref[SMALLS * n + start : SMALLS * n + start + count, :].astype(f32) for n in range(3)]
+def small_rows(ref, start):
+    rows = ref[...].astype(f32)
+    terms = [rows[SMALLS * n + start : SMALLS * n + start + 1, :] for n in range(3)]
     return terms[0] + terms[1] + terms[2]
 
 
@@ -231,9 +232,10 @@
     if layer == 0:
         given = marks_ref[pl.ds(pl.program_id(0), 1), :]
         high = given >> 4
-        both = jnp.concatenate([high, given - 16 * high], axis=0).astype(f32).astype(bf16)
+        both = [jnp.broadcast_to(v, (8, WINDOW)) for v in (high, given - 16 * high)]
+        both = jnp.concatenate(both, axis=0).astype(f32).astype(bf16)
         both = dot(both, shuffle_of(place_ref, 1))
-        marks = 16.0 * both[0:1] + both[1:2]
+        marks = 16.0 * both[0:1] + both[8:9]
         for k in range(4):
             mark_refs[k][pl.ds(pl.program_id(0), 1), :] = marks[:, k * BAND : (k + 1) * BAND]
     x_ref[...] = stream.astype(bf16)
@@ -1077,7 +1079,7 @@
     up_0 = Pack(order, *parts)
     order.close()
     move(up_0)
-    for one in (down_0, attn_1, up_1, down_1):
+    for one in (attn_1, up_1, down_1, down_0):
         one.prepare()
     order.close()
     move(up_0, down_0, attn_1, up_1, down_1)

time: 525 us -> 523 us (level)
    unnamed x112 -> x104, local copies, waits for them, and re-layouts: 13.4 us -> 12.2 us
  transfers between devices with their start and end apart: 74 -> 74, of which waited for: 30 -> 31; matrix products, arithmetic and copies ran while one was open for 6% -> 6% of each run, Pallas kernels for 40% -> 40%
where the time goes in v8:
time: 523 us; the launch traced here: 515 us
  Pallas kernels  229 us (44%)
  waiting for transfers between devices  147 us (28%)
  starting transfers between devices  66.4 us (13%)
  other arithmetic  28.2 us (5%)
  local copies, waits for them, and re-layouts  26.7 us (5%)
  between operations  17.6 us (3%)
    pallas_call x17, Pallas kernels, call(): pl.pallas_call(kernel, grid_spec=pltpu.PrefetchScalarGridSpec(num_scalar_...  229 us
    ppermute x35, waiting for transfers between devices, clip_swap(): lax.ppermute(values, 'clip', [(i, i ^ distance) for i in range(count)])  86.7 us
    ppermute x38, waiting for transfers between devices, head_swap(): lax.ppermute(values, 'head', [(i, i ^ distance) for i in range(count)])  43.2 us
    ppermute x35, starting transfers between devices, clip_swap(): lax.ppermute(values, 'clip', [(i, i ^ distance) for i in range(count)])  41.8 us
    ppermute x38, starting transfers between devices, head_swap(): lax.ppermute(values, 'head', [(i, i ^ distance) for i in range(count)])  24.6 us
    all_gather x1, waiting for transfers between devices, over_clips(): return lax.all_gather(chunk_across, 'clip', axis=0, tiled=True)  16.9 us
    unnamed x104, local copies, waits for them, and re-layouts  12.2 us
  transfers between devices with their start and end apart: 74, of which 31 were waited for; matrix products, arithmetic and copies ran while one was open for 6% of the time, Pallas kernels for 40%

profile of v8, /device:TPU:0, one launch (start us, length us, event | category | flops | bytes accessed | tf_op | source)
XLA Modules:
  0.0 515.0 jit_solution(10497485745705096376)
XLA Ops:
  7.2 2.8 fusion.8
  10.1 3.0 collective-permute-start
  13.1 2.8 fusion.9
  16.9 2.5 fusion.10
  20.9 5.6 %collective-permute-done.1 = bf16[192,768]{1,0:T(8,128)(2,1)} collective-permute-done((bf16[192,768]{1,0:T(8,128)(2,1)S(1)}, bf16[192,768]{1,0:T(8,128)(2,1)}, u32[]{:S(2)}, u32[]{:S(2)}) %collective-permute-start.1) | collective-permute-done | bytes 294944 | tf_op jit(solution)/shard_map/ppermute | solution.py:759
  30.5 4.3 collective-permute-done.3
  39.9 4.4 collective-permute-done.5
  45.3 3.2 collective-permute-done.4
  48.7 6.7 %collective-permute-done.2.refs_6_.refs_10_.refs_4_.refs_11_.refs_8_ = bf16[784,768]{1,0:T(8,128)(2,1)} collective-permute-done((bf16[784,768]{1,0:T(8,128)(2,1)S(1)}, bf16[784,768]{1,0:T(8,128)(2,1)}, u32[]{:S(2)}, u32[]{:S(2)}) %collective-permute-start.2) | collective-permute-done | bytes 1204256 | tf_op jit(solution)/shard_map/ppermute | solution.py:759
  55.5 3.1 collective-permute-done.7.refs_7_.refs_11_.refs_5_.refs_12_.refs_9_
  62.2 15.7 %attend.2 = (bf16[1024,768]{1,0:T(8,128)(2,1)S(1)}, bf16[1024,768]{1,0:T(8,128)(2,1)S(1)}, bf16[1024,2304]{1,0:T(8,128)(2,1)}, bf16[1024,768]{1,0:T(8,128)(2,1)S...) custom-call(s32[3]{0:T(128)S(1)} %pad_add_fusion.place_ref, ...), custom_call_target="tpu_custom_call" | custom-call | flops 19549999104 | bytes 61200000 | tf_op jit(solution)/shard_map/attend/pallas_call | solution.py:281
  85.3 2.4 pad_maximum_fusion.3.refs_10_.refs_2_.refs_6_
  88.6 23.2 %feed.2 = (f32[1024,768]{1,0:T(8,128)}, bf16[1024,768]{1,0:T(8,128)(2,1)}, bf16[1024,3072]{1,0:T(8,128)(2,1)}, bf16[1024,3072]{1,0:T(8,128)(2,1)}, bf16[4,64,768...) custom-call(s32[3]{0:T(128)S(1)} %pad_add_fusion.place_ref, ...), custom_call_target="tpu_custom_call" | custom-call | flops 26449999872 | bytes 82800000 | tf_op jit(solution)/shard_map/feed/pallas_call | solution.py:281
  112.5 4.1 collective-permute-done.14.refs_12_.refs_4_.refs_8_
  119.0 16.9 %all-gather.2.cloned.1.call-done = bf16[1536,768]{1,0:T(8,128)(2,1)} async-done(((bf16[192,768]{1,0:T(8,128)(2,1)}), bf16[1536,768]{1,0:T(8,128)(2,1)}) %all-gather.2.cloned.1.call-update) | async-done | bytes 2359312 | tf_op jit(solution)/shard_map/all_gather | solution.py:925
  140.2 17.2 %attend.3 = (bf16[1024,768]{1,0:T(8,128)(2,1)}, bf16[1024,768]{1,0:T(8,128)(2,1)}, bf16[1024,2304]{1,0:T(8,128)(2,1)}, bf16[1024,768]{1,0:T(8,128)(2,1)}, f32[64...) custom-call(s32[3]{0:T(128)S(1)} %pad_add_fusion.place_ref, bf16[4,4,16,768]{3,2,1,0:T(8,128)(2,1)S(1)} %bitcast.91, ...), custom_call_target="tpu_custom_call" | custom-call | flops 19549999104 | bytes 61200000 | tf_op jit(solution)/shard_map/attend/pallas_call | solution.py:281
  157.5 22.8 %feed.3 = (f32[1024,768]{1,0:T(8,128)}, bf16[1024,768]{1,0:T(8,128)(2,1)}, bf16[1024,3072]{1,0:T(8,128)(2,1)}, bf16[1024,3072]{1,0:T(8,128)(2,1)}, bf16[1024,768]{1,0:T(8,128)(2,1)}) custom-call(s32[3]{0:T(128)S(1)} %pad_add_fusion.place_ref, bf16[1024,768]{1,0:T(8,128)(2,1)} %get-tuple-element.295.refs_0_.refs_2_, ...), custom_call_target="tpu_custom_call" | custom-call | flops 26449999872 | bytes 82800000 | tf_op jit(solution)/shard_map/feed/pallas_call | solution.py:281
  181.7 19.0 %code_loss.1 = (f32[1024,768]{1,0:T(8,128)}, f32[8,768]{1,0:T(8,128)S(1)}, bf16[2,768,768]{2,1,0:T(8,128)(2,1)S(1)}, bf16[2,768,768]{2,1,0:T(8,128)(2,1)S(1)}) custom-call(s32[3]{0:T(128)S(1)} %pad_add_fusion.place_ref, bf16[1024,768]{1,0:T(8,128)(2,1)S(1)} %copy-done.31, bf16[768,1024]{1,0:T(8,128)(2,1)S(1)} %copy-done.4, ...), custom_call_target="tpu_custom_call" | custom-call | flops 20700000256 | bytes 64800000 | tf_op jit(solution)/shard_map/code_loss/pallas_call | solution.py:281
  201.2 4.2 collective-permute-done.25
  207.8 25.0 %feed_back.2 = (f32[1024,768]{1,0:T(8,128)}, bf16[1024,768]{1,0:T(8,128)(2,1)S(1)}, f32[8,768]{1,0:T(8,128)S(1)}, bf16[2,768,768]{2,1,0:T(8,128)(2,1)}, bf16[2,768,768]{2,1,0:T(8,128)(2,1)}) custom-call(s32[3]{0:T(128)S(1)} %pad_add_fusion.place_ref, f32[1024,768]{1,0:T(8,128)} %get-tuple-element.311.refs_0_, bf16[1024,3072]{1,0:T(8,128)(2,1)} %get-tuple-element.312.refs_1_, ...), custom_call_target="tpu_custom_call" | custom-call | flops 29899999232 | bytes 93600000 | tf_op jit(solution)/shard_map/feed_back/pallas_call | solution.py:281
  236.5 2.4 collective-permute-done.27
  242.8 23.6 %attend_back.2 = (bf16[4,1024,576]{2,1,0:T(8,128)(2,1)}, bf16[4,4,16,768]{3,2,1,0:T(8,128)(2,1)S(1)}, bf16[4,4,16,768]{3,2,1,0:T(8,128)(2,1)S(1)}, bf16[4,4,16,7...) custom-call(s32[3]{0:T(128)S(1)} %pad_add_fusion.place_ref, ...), custom_call_target="tpu_custom_call" | custom-call | flops 28750000128 | bytes 90000000 | tf_op jit(solution)/shard_map/attend_back/pallas_call | solution.py:281
  266.4 2.8 collective-permute-done.28
  276.2 2.5 copy-done.20
  278.7 6.8 %grads_attn.1 = (bf16[2,768,768]{2,1,0:T(8,128)(2,1)S(1)}, bf16[2,768,768]{2,1,0:T(8,128)(2,1)S(1)}) custom-call(s32[3]{0:T(128)S(1)} %pad_add_fusion.place_ref, bf16[4,1024,576]{2,1,0:T(8,128)(2,1)S(1)} %copy-done.20, bf16[1024,768]{1,0:T(8,128)(2,1)S(1)} %copy-done.22, bf16[4,1024,192]{2,1,0:T(8,128)(2,1)S(1)} %copy-done.21, bf16[1024,768]{1,0:T(8,128)(2,1)S(1)} %copy-done.24), custom_call_target="tpu_custom_call" | custom-call | flops 12650000384 | bytes 39600000 | tf_op jit(solution)/shard_map/grads_attn/pallas_call | solution.py:281
  285.5 5.4 %collective-permute-done.32 = bf16[4,4,16,768]{3,2,1,0:T(8,128)(2,1)S(1)} collective-permute-done((bf16[4,4,16,768]{3,2,1,0:T(8,128)(2,1)S(1)}, bf16[4,4,16,768]{3,2,1,0:T(8,128)(2,1)S(1)}, u32[]{:S(2)}, u32[]{:S(2)}) %collective-permute-start.32) | collective-permute-done | bytes 393248 | tf_op jit(solution)/shard_map/ppermute | solution.py:759
  291.4 7.3 %grads_down.1 = (bf16[2,768,768]{2,1,0:T(8,128)(2,1)S(1)}, bf16[2,768,768]{2,1,0:T(8,128)(2,1)S(1)}) custom-call(s32[3]{0:T(128)S(1)} %pad_add_fusion.place_ref, bf16[1024,3072]{1,0:T(8,128)(2,1)S(1)} %bitcast.93, bf16[1024,768]{1,0:T(8,128)(2,1)S(1)} %bitcast.80), custom_call_target="tpu_custom_call" | custom-call | flops 11500000256 | bytes 36000000 | tf_op jit(solution)/shard_map/grads_down/pallas_call | solution.py:281
  301.1 2.2 collective-permute-done.36
  309.0 25.0 %feed_back.3 = (f32[1024,768]{1,0:T(8,128)}, bf16[1024,768]{1,0:T(8,128)(2,1)S(1)}, f32[8,768]{1,0:T(8,128)S(1)}, bf16[2,768,768]{2,1,0:T(8,128)(2,1)}, bf16[2,768,768]{2,1,0:T(8,128)(2,1)}) custom-call(s32[3]{0:T(128)S(1)} %pad_add_fusion.place_ref, bf16[1024,768]{1,0:T(8,128)(2,1)S(1)} %bitcast.81, bf16[1024,3072]{1,0:T(8,128)(2,1)} %get-tuple-element.370.refs_1_, ...), custom_call_target="tpu_custom_call" | custom-call | flops 29899999232 | bytes 93600000 | tf_op jit(solution)/shard_map/feed_back/pallas_call | solution.py:281
  347.3 30.4 %attend_back.3 = (f32[1024,768]{1,0:T(8,128)}, f32[8,768]{1,0:T(8,128)S(1)}, bf16[2,768,768]{2,1,0:T(8,128)(2,1)}, bf16[2,768,768]{2,1,0:T(8,128)(2,1)}) custom-call(s32[3]{0:T(128)S(1)} %pad_add_fusion.place_ref, f32[1024,768]{1,0:T(8,128)} %get-tuple-element.394.refs_0_, bf16[1024,768]{1,0:T(8,128)(2,1)S(1)} %get-tuple-element.395.refs_1_, ...), custom_call_target="tpu_custom_call" | custom-call | flops 28750000128 | bytes 90000000 | tf_op jit(solution)/shard_map/attend_back/pallas_call | solution.py:281
  383.7 5.2 %collective-permute-done.47 = bf16[192,768]{1,0:T(8,128)(2,1)S(1)} collective-permute-done((bf16[192,768]{1,0:T(8,128)(2,1)S(1)}, bf16[192,768]{1,0:T(8,128)(2,1)S(1)}, u32[]{:S(2)}, u32[]{:S(2)}) %collective-permute-start.47) | collective-permute-done | bytes 294944 | tf_op jit(solution)/shard_map/ppermute | solution.py:759
  396.1 18.7 %collective-permute-done.50 = bf16[192,768]{1,0:T(8,128)(2,1)S(1)} collective-permute-done((bf16[192,768]{1,0:T(8,128)(2,1)S(1)}, bf16[192,768]{1,0:T(8,128)(2,1)S(1)}, u32[]{:S(2)}, u32[]{:S(2)}) %collective-permute-start.50) | collective-permute-done | bytes 294944 | tf_op jit(solution)/shard_map/ppermute | solution.py:764
  414.8 5.2 %collective-permute-done.53 = bf16[192,768]{1,0:T(8,128)(2,1)S(1)} collective-permute-done((bf16[192,768]{1,0:T(8,128)(2,1)S(1)}, bf16[192,768]{1,0:T(8,128)(2,1)S(1)}, u32[]{:S(2)}, u32[]{:S(2)}) %collective-permute-start.53) | collective-permute-done | bytes 294944 | tf_op jit(solution)/shard_map/ppermute | solution.py:764
  424.7 2.3 emit.6.refs_0_
  427.0 5.5 %collective-permute-done.56 = bf16[192,768]{1,0:T(8,128)(2,1)S(1)} collective-permute-done((bf16[192,768]{1,0:T(8,128)(2,1)S(1)}, bf16[192,768]{1,0:T(8,128)(2,1)S(1)}, u32[]{:S(2)}, u32[]{:S(2)}) %collective-permute-start.56) | collective-permute-done | bytes 294944 | tf_op jit(solution)/shard_map/ppermute | solution.py:764
  432.4 5.9 %collective-permute-done.57 = bf16[192,768]{1,0:T(8,128)(2,1)S(1)} collective-permute-done((bf16[192,768]{1,0:T(8,128)(2,1)S(1)}, bf16[192,768]{1,0:T(8,128)(2,1)S(1)}, u32[]{:S(2)}, u32[]{:S(2)}) %collective-permute-start.57) | collective-permute-done | bytes 294944 | tf_op jit(solution)/shard_map/ppermute | solution.py:764
  441.2 2.2 collective-permute-start.61
  443.6 2.2 emit.7.refs_0_
  445.8 10.6 %collective-permute-done.60 = bf16[192,768]{1,0:T(8,128)(2,1)S(1)} collective-permute-done((bf16[192,768]{1,0:T(8,128)(2,1)S(1)}, bf16[192,768]{1,0:T(8,128)(2,1)S(1)}, u32[]{:S(2)}, u32[]{:S(2)}) %collective-permute-start.60) | collective-permute-done | bytes 294944 | tf_op jit(solution)/shard_map/ppermute | solution.py:764
  456.5 5.1 collective-permute-done.62
  466.4 2.2 emit.8
  468.7 10.0 %collective-permute-done.64 = f32[40,768]{1,0:T(8,128)S(1)} collective-permute-done((f32[40,768]{1,0:T(8,128)S(1)}, f32[40,768]{1,0:T(8,128)S(1)}, u32[]{:S(2)}, u32[]{:S(2)}) %collective-permute-start.64) | collective-permute-done | bytes 122912 | tf_op jit(solution)/shard_map/ppermute | solution.py:764
  482.5 2.2 emit.9
  486.5 3.1 collective-permute-done.69
  489.7 2.4 collective-permute-done.70.other_ref
  493.9 2.2 emit.10
  496.1 2.2 collective-permute-done.71
  504.7 2.2 emit.11
  (312 shorter events, 111.0 us)
Async XLA Ops:
  7.2 128.7 %all-gather.2.cloned.1.call-start = ((), (), s32[]{:S(2)}) async-start(), calls=%async_computation | async-start | bytes 2654208 | tf_op jit(solution)/shard_map/all_gather | solution.py:925
  28.3 27.2 %collective-permute-start.2 = (bf16[784,768]{1,0:T(8,128)(2,1)S(1)}, bf16[784,768]{1,0:T(8,128)(2,1)}, u32[]{:S(2)}, u32[]{:S(2)}) collective-permute-start(bf16[784,768]{1,0:T(8,128)(2,1)S(1)} %concatenate.40.refs_4_.refs_8_.refs_2_.refs_9_.refs_6_), channel_id=1, source_target_pairs={{0,2},{1,3},{2,0},{3,1},{4,6},{5,7},{6,4},{7,5},{8,10},{9,11},{10,... | collective-permute-start | bytes 3612680 | tf_op jit(solution)/shard_map/ppermute | solution.py:759
  39.9 15.6 %collective-permute-start.6 = (bf16[784,768]{1,0:T(8,128)(2,1)S(1)}, bf16[784,768]{1,0:T(8,128)(2,1)S(1)}, u32[]{:S(2)}, u32[]{:S(2)}) collective-permute-start(bf16[784,768]{1,0:T(8,128)(2,1)S(1)} %concatenate.40.refs_4_.refs_8_.refs_2_.refs_9_.refs_6_), channel_id=1, source_target_pairs={{0,1},{1,0},{2,3},{3,2},{4,5},{5,4},{6,7},{7,6},{8,9},{9,8},{10,11... | collective-permute-start | bytes 3612680 | tf_op jit(solution)/shard_map/ppermute | solution.py:759
  58.6 22.8 %collective-permute-start.10 = (bf16[2,768,768]{2,1,0:T(8,128)(2,1)}, bf16[2,768,768]{2,1,0:T(8,128)(2,1)}, u32[]{:S(2)}, u32[]{:S(2)}) collective-permute-start(bf16[2,768,768]{2,1,0:T(8,128)(2,1)} %refs_5_.8), channel_id=1, source_target_pairs={{0,1},{1,0},{2,3},{3,2},{4,5},{5,4},{6,7},{7,6},{8,9},{9,8},{10,11... | collective-permute-start | bytes 7077896 | tf_op jit(solution)/shard_map/ppermute | solution.py:759
  58.7 22.7 %collective-permute-start.11 = (bf16[2,768,768]{2,1,0:T(8,128)(2,1)}, bf16[2,768,768]{2,1,0:T(8,128)(2,1)}, u32[]{:S(2)}, u32[]{:S(2)}) collective-permute-start(bf16[2,768,768]{2,1,0:T(8,128)(2,1)} %refs_9_.3), channel_id=1, source_target_pairs={{0,1},{1,0},{2,3},{3,2},{4,5},{5,4},{6,7},{7,6},{8,9},{9,8},{10,11... | collective-permute-start | bytes 7077896 | tf_op jit(solution)/shard_map/ppermute | solution.py:759
  59.1 22.3 %collective-permute-start.9 = (bf16[192,768]{1,0:T(8,128)(2,1)S(1)}, bf16[192,768]{1,0:T(8,128)(2,1)}, u32[]{:S(2)}, u32[]{:S(2)}) collective-permute-start(bf16[192,768]{1,0:T(8,128)(2,1)S(1)} %pad_maximum_fusion.10), channel_id=1, source_target_pairs={{0,2},{1,3},{2,0},{3,1},{4,6},{5,7},{6,4},{7,5},{8,10},{9,11},{10,... | collective-permute-start | bytes 884744 | tf_op jit(solution)/shard_map/ppermute | solution.py:759
  60.6 20.8 %collective-permute-start.8 = (bf16[384,768]{1,0:T(8,128)(2,1)S(1)}, bf16[384,768]{1,0:T(8,128)(2,1)}, u32[]{:S(2)}, u32[]{:S(2)}) collective-permute-start(bf16[384,768]{1,0:T(8,128)(2,1)S(1)} %pad_maximum_fusion.5), channel_id=1, source_target_pairs={{0,8},{4,12},{8,0},{12,4},{16,24},{20,28},{24,16},{28,20},{1,9},{5... | collective-permute-start | bytes 1769480 | tf_op jit(solution)/shard_map/ppermute | solution.py:764
  62.1 19.2 %collective-permute-start.12 = (bf16[768,768]{1,0:T(8,128)(2,1)S(1)}, bf16[768,768]{1,0:T(8,128)(2,1)}, u32[]{:S(2)}, u32[]{:S(2)}) collective-permute-start(bf16[768,768]{1,0:T(8,128)(2,1)S(1)} %pad_maximum_fusion.1.refs_15_.refs_7_), channel_id=1, source_target_pairs={{0,1},{1,0},{2,3},{3,2},{4,5},{5,4},{6,7},{7,6},{8,9},{9,8},{10,11... | collective-permute-start | bytes 3538952 | tf_op jit(solution)/shard_map/ppermute | solution.py:759
  88.0 28.6 %collective-permute-start.14 = (bf16[768,768]{1,0:T(8,128)(2,1)}, bf16[768,768]{1,0:T(8,128)(2,1)}, u32[]{:S(2)}, u32[]{:S(2)}) collective-permute-start(bf16[768,768]{1,0:T(8,128)(2,1)} %pad_maximum_fusion.3.refs_10_.refs_2_.refs_6_), channel_id=1, source_target_pairs={{0,2},{1,3},{2,0},{3,1},{4,6},{5,7},{6,4},{7,5},{8,10},{9,11},{10,... | collective-permute-start | bytes 3538952 | tf_op jit(solution)/shard_map/ppermute | solution.py:759
  116.6 23.1 %collective-permute-start.18 = (bf16[768,768]{1,0:T(8,128)(2,1)}, bf16[768,768]{1,0:T(8,128)(2,1)}, u32[]{:S(2)}, u32[]{:S(2)}) collective-permute-start(bf16[768,768]{1,0:T(8,128)(2,1)} %collective-permute-done.14.refs_12_.refs_4_.refs_8_), channel_id=1, source_target_pairs={{0,1},{1,0},{2,3},{3,2},{4,5},{5,4},{6,7},{7,6},{8,9},{9,8},{10,11... | collective-permute-start | bytes 3538952 | tf_op jit(solution)/shard_map/ppermute | solution.py:759
  116.6 23.5 %collective-permute-start.19 = (bf16[768,768]{1,0:T(8,128)(2,1)}, bf16[768,768]{1,0:T(8,128)(2,1)}, u32[]{:S(2)}, u32[]{:S(2)}) collective-permute-start(bf16[768,768]{1,0:T(8,128)(2,1)} %pad_maximum_fusion.3.refs_10_.refs_2_.refs_6_), channel_id=1, source_target_pairs={{0,1},{1,0},{2,3},{3,2},{4,5},{5,4},{6,7},{7,6},{8,9},{9,8},{10,11... | collective-permute-start | bytes 3538952 | tf_op jit(solution)/shard_map/ppermute | solution.py:759
  117.1 20.6 %collective-permute-start.17 = (bf16[4,64,768]{2,1,0:T(8,128)(2,1)}, bf16[4,64,768]{2,1,0:T(8,128)(2,1)S(1)}, u32[]{:S(2)}, u32[]{:S(2)}) collective-permute-start(bf16[4,64,768]{2,1,0:T(8,128)(2,1)} %get-tuple-element.284), channel_id=1, source_target_pairs={{0,3},{1,2},{2,1},{3,0},{4,7},{5,6},{6,5},{7,4},{8,11},{9,10},{10,... | collective-permute-start | bytes 1179656 | tf_op jit(solution)/shard_map/ppermute | solution.py:759
  117.3 20.6 %collective-permute-start.16 = (bf16[4,64,768]{2,1,0:T(8,128)(2,1)}, bf16[4,64,768]{2,1,0:T(8,128)(2,1)S(1)}, u32[]{:S(2)}, u32[]{:S(2)}) collective-permute-start(bf16[4,64,768]{2,1,0:T(8,128)(2,1)} %get-tuple-element.282), channel_id=1, source_target_pairs={{0,2},{1,3},{2,0},{3,1},{4,6},{5,7},{6,4},{7,5},{8,10},{9,11},{10,... | collective-permute-start | bytes 1179656 | tf_op jit(solution)/shard_map/ppermute | solution.py:759
  118.7 20.6 %collective-permute-start.15 = (bf16[4,64,768]{2,1,0:T(8,128)(2,1)}, bf16[4,64,768]{2,1,0:T(8,128)(2,1)}, u32[]{:S(2)}, u32[]{:S(2)}) collective-permute-start(bf16[4,64,768]{2,1,0:T(8,128)(2,1)} %get-tuple-element.280), channel_id=1, source_target_pairs={{0,1},{1,0},{2,3},{3,2},{4,5},{5,4},{6,7},{7,6},{8,9},{9,8},{10,11... | collective-permute-start | bytes 1179656 | tf_op jit(solution)/shard_map/ppermute | solution.py:759
  137.8 42.5 %collective-permute-start.22 = (f32[4,64]{1,0:T(4,128)S(1)}, f32[4,64]{1,0:T(4,128)S(1)}, u32[]{:S(2)}, u32[]{:S(2)}) collective-permute-start(f32[4,64]{1,0:T(4,128)S(1)} %get-tuple-element.301), channel_id=1, source_target_pairs={{0,1},{1,0},{2,3},{3,2},{4,5},{5,4},{6,7},{7,6},{8,9},{9,8},{10,11... | collective-permute-start | bytes 3080 | tf_op jit(solution)/shard_map/ppermute | solution.py:759
  137.8 42.5 %collective-permute-start.23 = (f32[4,64]{1,0:T(4,128)S(1)}, f32[4,64]{1,0:T(4,128)S(1)}, u32[]{:S(2)}, u32[]{:S(2)}) collective-permute-start(f32[4,64]{1,0:T(4,128)S(1)} %get-tuple-element.302), channel_id=1, source_target_pairs={{0,2},{1,3},{2,0},{3,1},{4,6},{5,7},{6,4},{7,5},{8,10},{9,11},{10,... | collective-permute-start | bytes 3080 | tf_op jit(solution)/shard_map/ppermute | solution.py:759
  139.4 40.9 %collective-permute-start.24 = (f32[4,64]{1,0:T(4,128)S(1)}, f32[4,64]{1,0:T(4,128)S(1)}, u32[]{:S(2)}, u32[]{:S(2)}) collective-permute-start(f32[4,64]{1,0:T(4,128)S(1)} %get-tuple-element.303), channel_id=1, source_target_pairs={{0,3},{1,2},{2,1},{3,0},{4,7},{5,6},{6,5},{7,4},{8,11},{9,10},{10,... | collective-permute-start | bytes 3080 | tf_op jit(solution)/shard_map/ppermute | solution.py:759
  139.7 17.8 %collective-permute-start.20 = (bf16[768,768]{1,0:T(8,128)(2,1)S(1)}, bf16[768,768]{1,0:T(8,128)(2,1)S(1)}, u32[]{:S(2)}, u32[]{:S(2)}) collective-permute-start(bf16[768,768]{1,0:T(8,128)(2,1)S(1)} %bitcast.85), channel_id=1, source_target_pairs={{0,1},{1,0},{2,3},{3,2},{4,5},{5,4},{6,7},{7,6},{8,9},{9,8},{10,11... | collective-permute-start | bytes 3538952 | tf_op jit(solution)/shard_map/ppermute | solution.py:759
  140.1 17.4 %collective-permute-start.21 = (bf16[768,768]{1,0:T(8,128)(2,1)S(1)}, bf16[768,768]{1,0:T(8,128)(2,1)S(1)}, u32[]{:S(2)}, u32[]{:S(2)}) collective-permute-start(bf16[768,768]{1,0:T(8,128)(2,1)S(1)} %bitcast.82), channel_id=1, source_target_pairs={{0,1},{1,0},{2,3},{3,2},{4,5},{5,4},{6,7},{7,6},{8,9},{9,8},{10,11... | collective-permute-start | bytes 3538952 | tf_op jit(solution)/shard_map/ppermute | solution.py:759
  205.7 28.4 %collective-permute-start.26 = (bf16[768,768]{1,0:T(8,128)(2,1)S(1)}, bf16[768,768]{1,0:T(8,128)(2,1)}, u32[]{:S(2)}, u32[]{:S(2)}) collective-permute-start(bf16[768,768]{1,0:T(8,128)(2,1)S(1)} %fusion), channel_id=1, source_target_pairs={{0,2},{1,3},{2,0},{3,1},{4,6},{5,7},{6,4},{7,5},{8,10},{9,11},{10,... | collective-permute-start | bytes 3538952 | tf_op jit(solution)/shard_map/ppermute | solution.py:759
  240.7 25.7 %collective-permute-start.29 = (bf16[384,768]{1,0:T(8,128)(2,1)S(1)}, bf16[384,768]{1,0:T(8,128)(2,1)S(1)}, u32[]{:S(2)}, u32[]{:S(2)}) collective-permute-start(bf16[384,768]{1,0:T(8,128)(2,1)S(1)} %get-tuple-element.333), channel_id=1, source_target_pairs={{0,4},{4,0},{8,12},{12,8},{16,20},{20,16},{24,28},{28,24},{1,5},{5... | collective-permute-start | bytes 1769480 | tf_op jit(solution)/shard_map/ppermute | solution.py:764
  241.3 27.9 %collective-permute-start.28 = (bf16[768,768]{1,0:T(8,128)(2,1)S(1)}, bf16[768,768]{1,0:T(8,128)(2,1)S(1)}, u32[]{:S(2)}, u32[]{:S(2)}) collective-permute-start(bf16[768,768]{1,0:T(8,128)(2,1)S(1)} %fusion.1), channel_id=1, source_target_pairs={{0,2},{1,3},{2,0},{3,1},{4,6},{5,7},{6,4},{7,5},{8,10},{9,11},{10,... | collective-permute-start | bytes 3538952 | tf_op jit(solution)/shard_map/ppermute | solution.py:759
  272.9 18.0 %collective-permute-start.32 = (bf16[4,4,16,768]{3,2,1,0:T(8,128)(2,1)S(1)}, bf16[4,4,16,768]{3,2,1,0:T(8,128)(2,1)S(1)}, u32[]{:S(2)}, u32[]{:S(2)}) collective-permute-start(bf16[4,4,16,768]{3,2,1,0:T(8,128)(2,1)S(1)} %get-tuple-element.338), channel_id=1, source_target_pairs={{0,3},{1,2},{2,1},{3,0},{4,7},{5,6},{6,5},{7,4},{8,11},{9,10},{10,... | collective-permute-start | bytes 1179656 | tf_op jit(solution)/shard_map/ppermute | solution.py:759
  273.2 17.6 %collective-permute-start.33 = (bf16[384,768]{1,0:T(8,128)(2,1)S(1)}, bf16[384,768]{1,0:T(8,128)(2,1)S(1)}, u32[]{:S(2)}, u32[]{:S(2)}) collective-permute-start(bf16[384,768]{1,0:T(8,128)(2,1)S(1)} %get-tuple-element.352), channel_id=1, source_target_pairs={{0,4},{4,0},{8,12},{12,8},{16,20},{20,16},{24,28},{28,24},{1,5},{5... | collective-permute-start | bytes 1769480 | tf_op jit(solution)/shard_map/ppermute | solution.py:764
  274.7 16.2 %collective-permute-start.34 = (bf16[384,768]{1,0:T(8,128)(2,1)S(1)}, bf16[384,768]{1,0:T(8,128)(2,1)S(1)}, u32[]{:S(2)}, u32[]{:S(2)}) collective-permute-start(bf16[384,768]{1,0:T(8,128)(2,1)S(1)} %add_convert_fusion.11), channel_id=1, source_target_pairs={{0,8},{4,12},{8,0},{12,4},{16,24},{20,28},{24,16},{28,20},{1,9},{5... | collective-permute-start | bytes 1769480 | tf_op jit(solution)/shard_map/ppermute | solution.py:764
  303.6 30.4 %collective-permute-start.39 = (bf16[384,768]{1,0:T(8,128)(2,1)S(1)}, bf16[384,768]{1,0:T(8,128)(2,1)S(1)}, u32[]{:S(2)}, u32[]{:S(2)}) collective-permute-start(bf16[384,768]{1,0:T(8,128)(2,1)S(1)} %add_convert_fusion.10), channel_id=1, source_target_pairs={{0,16},{4,20},{8,24},{12,28},{16,0},{20,4},{24,8},{28,12},{1,17},{... | collective-permute-start | bytes 1769480 | tf_op jit(solution)/shard_map/ppermute | solution.py:764
  305.5 28.5 %collective-permute-start.40 = (bf16[384,768]{1,0:T(8,128)(2,1)S(1)}, bf16[384,768]{1,0:T(8,128)(2,1)S(1)}, u32[]{:S(2)}, u32[]{:S(2)}) collective-permute-start(bf16[384,768]{1,0:T(8,128)(2,1)S(1)} %add_convert_fusion.9), channel_id=1, source_target_pairs={{0,8},{4,12},{8,0},{12,4},{16,24},{20,28},{24,16},{28,20},{1,9},{5... | collective-permute-start | bytes 1769480 | tf_op jit(solution)/shard_map/ppermute | solution.py:764
  306.1 28.0 %collective-permute-start.37 = (bf16[768,768]{1,0:T(8,128)(2,1)S(1)}, bf16[768,768]{1,0:T(8,128)(2,1)}, u32[]{:S(2)}, u32[]{:S(2)}) collective-permute-start(bf16[768,768]{1,0:T(8,128)(2,1)S(1)} %fusion.2), channel_id=1, source_target_pairs={{0,2},{1,3},{2,0},{3,1},{4,6},{5,7},{6,4},{7,5},{8,10},{9,11},{10,... | collective-permute-start | bytes 3538952 | tf_op jit(solution)/shard_map/ppermute | solution.py:759
  307.6 27.6 %collective-permute-start.38 = (bf16[2,384,768]{2,1,0:T(8,128)(2,1)}, bf16[2,384,768]{2,1,0:T(8,128)(2,1)}, u32[]{:S(2)}, u32[]{:S(2)}) collective-permute-start(bf16[2,384,768]{2,1,0:T(8,128)(2,1)} %get-tuple-element.379), channel_id=1, source_target_pairs={{0,4},{4,0},{8,12},{12,8},{16,20},{20,16},{24,28},{28,24},{1,5},{5... | collective-permute-start | bytes 3538952 | tf_op jit(solution)/shard_map/ppermute | solution.py:764
  342.1 35.5 %collective-permute-start.42 = (bf16[2,192,768]{2,1,0:T(8,128)(2,1)}, bf16[2,192,768]{2,1,0:T(8,128)(2,1)S(1)}, u32[]{:S(2)}, u32[]{:S(2)}) collective-permute-start(bf16[2,192,768]{2,1,0:T(8,128)(2,1)} %get-tuple-element.403), channel_id=1, source_target_pairs={{0,8},{4,12},{8,0},{12,4},{16,24},{20,28},{24,16},{28,20},{1,9},{5... | collective-permute-start | bytes 1769480 | tf_op jit(solution)/shard_map/ppermute | solution.py:764
  343.6 34.1 %collective-permute-start.44 = (bf16[384,768]{1,0:T(8,128)(2,1)}, bf16[384,768]{1,0:T(8,128)(2,1)S(1)}, u32[]{:S(2)}, u32[]{:S(2)}) collective-permute-start(bf16[384,768]{1,0:T(8,128)(2,1)} %get-tuple-element.406), channel_id=1, source_target_pairs={{0,4},{4,0},{8,12},{12,8},{16,20},{20,16},{24,28},{28,24},{1,5},{5... | collective-permute-start | bytes 1769480 | tf_op jit(solution)/shard_map/ppermute | solution.py:764
  345.1 32.6 %collective-permute-start.45 = (bf16[384,768]{1,0:T(8,128)(2,1)S(1)}, bf16[384,768]{1,0:T(8,128)(2,1)S(1)}, u32[]{:S(2)}, u32[]{:S(2)}) collective-permute-start(bf16[384,768]{1,0:T(8,128)(2,1)S(1)} %add_convert_fusion.8), channel_id=1, source_target_pairs={{0,16},{4,20},{8,24},{12,28},{16,0},{20,4},{24,8},{28,12},{1,17},{... | collective-permute-start | bytes 1769480 | tf_op jit(solution)/shard_map/ppermute | solution.py:764
  346.1 31.6 %collective-permute-start.46 = (bf16[384,768]{1,0:T(8,128)(2,1)S(1)}, bf16[384,768]{1,0:T(8,128)(2,1)S(1)}, u32[]{:S(2)}, u32[]{:S(2)}) collective-permute-start(bf16[384,768]{1,0:T(8,128)(2,1)S(1)} %add_convert_fusion.7.mine_ref), channel_id=1, source_target_pairs={{0,4},{4,0},{8,12},{12,8},{16,20},{20,16},{24,28},{28,24},{1,5},{5... | collective-permute-start | bytes 1769480 | tf_op jit(solution)/shard_map/ppermute | solution.py:764
  346.7 31.0 %collective-permute-start.43 = (bf16[768,768]{1,0:T(8,128)(2,1)S(1)}, bf16[768,768]{1,0:T(8,128)(2,1)S(1)}, u32[]{:S(2)}, u32[]{:S(2)}) collective-permute-start(bf16[768,768]{1,0:T(8,128)(2,1)S(1)} %fusion.3), channel_id=1, source_target_pairs={{0,2},{1,3},{2,0},{3,1},{4,6},{5,7},{6,4},{7,5},{8,10},{9,11},{10,... | collective-permute-start | bytes 3538952 | tf_op jit(solution)/shard_map/ppermute | solution.py:759
  390.6 29.5 %collective-permute-start.52 = (bf16[768,768]{1,0:T(8,128)(2,1)S(1)}, bf16[768,768]{1,0:T(8,128)(2,1)S(1)}, u32[]{:S(2)}, u32[]{:S(2)}) collective-permute-start(bf16[768,768]{1,0:T(8,128)(2,1)S(1)} %fusion.4), channel_id=1, source_target_pairs={{0,2},{1,3},{2,0},{3,1},{4,6},{5,7},{6,4},{7,5},{8,10},{9,11},{10,... | collective-permute-start | bytes 3538952 | tf_op jit(solution)/shard_map/ppermute | solution.py:759
  391.2 28.9 %collective-permute-start.51 = (bf16[384,768]{1,0:T(8,128)(2,1)S(1)}, bf16[384,768]{1,0:T(8,128)(2,1)S(1)}, u32[]{:S(2)}, u32[]{:S(2)}) collective-permute-start(bf16[384,768]{1,0:T(8,128)(2,1)S(1)} %get-tuple-element.430), channel_id=1, source_target_pairs={{0,4},{4,0},{8,12},{12,8},{16,20},{20,16},{24,28},{28,24},{1,5},{5... | collective-permute-start | bytes 1769480 | tf_op jit(solution)/shard_map/ppermute | solution.py:764
  392.7 27.4 %collective-permute-start.54 = (bf16[384,768]{1,0:T(8,128)(2,1)S(1)}, bf16[384,768]{1,0:T(8,128)(2,1)S(1)}, u32[]{:S(2)}, u32[]{:S(2)}) collective-permute-start(bf16[384,768]{1,0:T(8,128)(2,1)S(1)} %add_convert_fusion.5.mine_ref), channel_id=1, source_target_pairs={{0,4},{4,0},{8,12},{12,8},{16,20},{20,16},{24,28},{28,24},{1,5},{5... | collective-permute-start | bytes 1769480 | tf_op jit(solution)/shard_map/ppermute | solution.py:764
  393.2 21.6 %collective-permute-start.50 = (bf16[192,768]{1,0:T(8,128)(2,1)S(1)}, bf16[192,768]{1,0:T(8,128)(2,1)S(1)}, u32[]{:S(2)}, u32[]{:S(2)}) collective-permute-start(bf16[192,768]{1,0:T(8,128)(2,1)S(1)} %add_convert_fusion.18), channel_id=1, source_target_pairs={{0,16},{4,20},{8,24},{12,28},{16,0},{20,4},{24,8},{28,12},{1,17},{... | collective-permute-start | bytes 884744 | tf_op jit(solution)/shard_map/ppermute | solution.py:764
  395.1 25.0 %collective-permute-start.53 = (bf16[192,768]{1,0:T(8,128)(2,1)S(1)}, bf16[192,768]{1,0:T(8,128)(2,1)S(1)}, u32[]{:S(2)}, u32[]{:S(2)}) collective-permute-start(bf16[192,768]{1,0:T(8,128)(2,1)S(1)} %add_convert_fusion.19), channel_id=1, source_target_pairs={{0,16},{4,20},{8,24},{12,28},{16,0},{20,4},{24,8},{28,12},{1,17},{... | collective-permute-start | bytes 884744 | tf_op jit(solution)/shard_map/ppermute | solution.py:764
  420.9 17.4 %collective-permute-start.58 = (bf16[384,768]{1,0:T(8,128)(2,1)S(1)}, bf16[384,768]{1,0:T(8,128)(2,1)S(1)}, u32[]{:S(2)}, u32[]{:S(2)}) collective-permute-start(bf16[384,768]{1,0:T(8,128)(2,1)S(1)} %get-tuple-element.444), channel_id=1, source_target_pairs={{0,4},{4,0},{8,12},{12,8},{16,20},{20,16},{24,28},{28,24},{1,5},{5... | collective-permute-start | bytes 1769480 | tf_op jit(solution)/shard_map/ppermute | solution.py:764
  422.6 15.7 %collective-permute-start.57 = (bf16[192,768]{1,0:T(8,128)(2,1)S(1)}, bf16[192,768]{1,0:T(8,128)(2,1)S(1)}, u32[]{:S(2)}, u32[]{:S(2)}) collective-permute-start(bf16[192,768]{1,0:T(8,128)(2,1)S(1)} %get-tuple-element.443), channel_id=1, source_target_pairs={{0,8},{4,12},{8,0},{12,4},{16,24},{20,28},{24,16},{28,20},{1,9},{5... | collective-permute-start | bytes 884744 | tf_op jit(solution)/shard_map/ppermute | solution.py:764
  438.8 22.8 %collective-permute-start.63 = (bf16[384,768]{1,0:T(8,128)(2,1)S(1)}, bf16[384,768]{1,0:T(8,128)(2,1)S(1)}, u32[]{:S(2)}, u32[]{:S(2)}) collective-permute-start(bf16[384,768]{1,0:T(8,128)(2,1)S(1)} %pad_maximum_fusion.6.mine_ref), channel_id=1, source_target_pairs={{0,4},{4,0},{8,12},{12,8},{16,20},{20,16},{24,28},{28,24},{1,5},{5... | collective-permute-start | bytes 1769480 | tf_op jit(solution)/shard_map/ppermute | solution.py:764
  440.9 15.6 %collective-permute-start.60 = (bf16[192,768]{1,0:T(8,128)(2,1)S(1)}, bf16[192,768]{1,0:T(8,128)(2,1)S(1)}, u32[]{:S(2)}, u32[]{:S(2)}) collective-permute-start(bf16[192,768]{1,0:T(8,128)(2,1)S(1)} %add_convert_fusion.15), channel_id=1, source_target_pairs={{0,8},{4,12},{8,0},{12,4},{16,24},{20,28},{24,16},{28,20},{1,9},{5... | collective-permute-start | bytes 884744 | tf_op jit(solution)/shard_map/ppermute | solution.py:764
  441.2 15.3 %collective-permute-start.61 = (bf16[192,768]{1,0:T(8,128)(2,1)S(1)}, bf16[192,768]{1,0:T(8,128)(2,1)S(1)}, u32[]{:S(2)}, u32[]{:S(2)}) collective-permute-start(bf16[192,768]{1,0:T(8,128)(2,1)S(1)} %add_convert_fusion.16), channel_id=1, source_target_pairs={{0,16},{4,20},{8,24},{12,28},{16,0},{20,4},{24,8},{28,12},{1,17},{... | collective-permute-start | bytes 884744 | tf_op jit(solution)/shard_map/ppermute | solution.py:764
  443.3 18.2 %collective-permute-start.62 = (bf16[192,768]{1,0:T(8,128)(2,1)S(1)}, bf16[192,768]{1,0:T(8,128)(2,1)S(1)}, u32[]{:S(2)}, u32[]{:S(2)}) collective-permute-start(bf16[192,768]{1,0:T(8,128)(2,1)S(1)} %get-tuple-element.458), channel_id=1, source_target_pairs={{0,8},{4,12},{8,0},{12,4},{16,24},{20,28},{24,16},{28,20},{1,9},{5... | collective-permute-start | bytes 884744 | tf_op jit(solution)/shard_map/ppermute | solution.py:764
  461.8 16.8 %collective-permute-start.67 = (bf16[384,768]{1,0:T(8,128)(2,1)S(1)}, bf16[384,768]{1,0:T(8,128)(2,1)S(1)}, u32[]{:S(2)}, u32[]{:S(2)}) collective-permute-start(bf16[384,768]{1,0:T(8,128)(2,1)S(1)} %pad_maximum_fusion.7.mine_ref), channel_id=1, source_target_pairs={{0,4},{4,0},{8,12},{12,8},{16,20},{20,16},{24,28},{28,24},{1,5},{5... | collective-permute-start | bytes 1769480 | tf_op jit(solution)/shard_map/ppermute | solution.py:764
  463.4 15.2 %collective-permute-start.64 = (f32[40,768]{1,0:T(8,128)S(1)}, f32[40,768]{1,0:T(8,128)S(1)}, u32[]{:S(2)}, u32[]{:S(2)}) collective-permute-start(f32[40,768]{1,0:T(8,128)S(1)} %add.202), channel_id=1, source_target_pairs={{0,4},{4,0},{8,12},{12,8},{16,20},{20,16},{24,28},{28,24},{1,5},{5... | collective-permute-start | bytes 368648 | tf_op jit(solution)/shard_map/ppermute | solution.py:764
  464.0 14.6 %collective-permute-start.65 = (bf16[192,768]{1,0:T(8,128)(2,1)S(1)}, bf16[192,768]{1,0:T(8,128)(2,1)S(1)}, u32[]{:S(2)}, u32[]{:S(2)}) collective-permute-start(bf16[192,768]{1,0:T(8,128)(2,1)S(1)} %add_convert_fusion.13), channel_id=1, source_target_pairs={{0,8},{4,12},{8,0},{12,4},{16,24},{20,28},{24,16},{28,20},{1,9},{5... | collective-permute-start | bytes 884744 | tf_op jit(solution)/shard_map/ppermute | solution.py:764
  (75 other events, 768.3 us)
Sparse Core Ops, SparseCore 0:
  85.4 50.4 all-gather.1

commit v9 on v8

--- a/solution.py
+++ b/solution.py
@@ -1087,7 +1087,8 @@
     attn_0 = Pack(order, *parts)
     order.close()
     move(attn_0)
-    move(attn_1, down_0)
+    move(attn_1)
+    move(down_0)
     for one in (up_0, up_1):
         one.prepare()
     order.close()

time: 523 us -> 523 us (level)
  no operation moved by 1% of the time
where the time goes in v9:
time: 523 us; the launch traced here: 515 us
  Pallas kernels  229 us (44%)
  waiting for transfers between devices  147 us (28%)
  starting transfers between devices  66.4 us (13%)
  other arithmetic  28.2 us (5%)
  local copies, waits for them, and re-layouts  26.7 us (5%)
  between operations  17.6 us (3%)
    pallas_call x17, Pallas kernels, call(): pl.pallas_call(kernel, grid_spec=pltpu.PrefetchScalarGridSpec(num_scalar_...  229 us
    ppermute x35, waiting for transfers between devices, clip_swap(): lax.ppermute(values, 'clip', [(i, i ^ distance) for i in range(count)])  86.7 us
    ppermute x38, waiting for transfers between devices, head_swap(): lax.ppermute(values, 'head', [(i, i ^ distance) for i in range(count)])  43.2 us
    ppermute x35, starting transfers between devices, clip_swap(): lax.ppermute(values, 'clip', [(i, i ^ distance) for i in range(count)])  41.8 us
    ppermute x38, starting transfers between devices, head_swap(): lax.ppermute(values, 'head', [(i, i ^ distance) for i in range(count)])  24.6 us
    all_gather x1, waiting for transfers between devices, over_clips(): return lax.all_gather(chunk_across, 'clip', axis=0, tiled=True)  16.9 us
    unnamed x104, local copies, waits for them, and re-layouts  12.2 us
  transfers between devices with their start and end apart: 74, of which 31 were waited for; matrix products, arithmetic and copies ran while one was open for 6% of the time, Pallas kernels for 40%

profile of v9, /device:TPU:0, one launch (start us, length us, event | category | flops | bytes accessed | tf_op | source)
XLA Modules:
  0.0 515.0 jit_solution(15487280800613881685)
XLA Ops:
  7.2 2.8 fusion.8
  10.1 3.0 collective-permute-start
  13.1 2.8 fusion.9
  16.9 2.5 fusion.10
  20.9 5.6 %collective-permute-done.1 = bf16[192,768]{1,0:T(8,128)(2,1)} collective-permute-done((bf16[192,768]{1,0:T(8,128)(2,1)S(1)}, bf16[192,768]{1,0:T(8,128)(2,1)}, u32[]{:S(2)}, u32[]{:S(2)}) %collective-permute-start.1) | collective-permute-done | bytes 294944 | tf_op jit(solution)/shard_map/ppermute | solution.py:759
  30.5 4.3 collective-permute-done.3
  39.9 4.4 collective-permute-done.5
  45.3 3.2 collective-permute-done.4
  48.7 6.7 %collective-permute-done.2.refs_6_.refs_10_.refs_4_.refs_11_.refs_8_ = bf16[784,768]{1,0:T(8,128)(2,1)} collective-permute-done((bf16[784,768]{1,0:T(8,128)(2,1)S(1)}, bf16[784,768]{1,0:T(8,128)(2,1)}, u32[]{:S(2)}, u32[]{:S(2)}) %collective-permute-start.2) | collective-permute-done | bytes 1204256 | tf_op jit(solution)/shard_map/ppermute | solution.py:759
  55.5 3.1 collective-permute-done.7.refs_7_.refs_11_.refs_5_.refs_12_.refs_9_
  62.2 15.7 %attend.2 = (bf16[1024,768]{1,0:T(8,128)(2,1)S(1)}, bf16[1024,768]{1,0:T(8,128)(2,1)S(1)}, bf16[1024,2304]{1,0:T(8,128)(2,1)}, bf16[1024,768]{1,0:T(8,128)(2,1)S...) custom-call(s32[3]{0:T(128)S(1)} %pad_add_fusion.place_ref, ...), custom_call_target="tpu_custom_call" | custom-call | flops 19549999104 | bytes 61200000 | tf_op jit(solution)/shard_map/attend/pallas_call | solution.py:281
  85.3 2.4 pad_maximum_fusion.3.refs_10_.refs_2_.refs_6_
  88.6 23.2 %feed.2 = (f32[1024,768]{1,0:T(8,128)}, bf16[1024,768]{1,0:T(8,128)(2,1)}, bf16[1024,3072]{1,0:T(8,128)(2,1)}, bf16[1024,3072]{1,0:T(8,128)(2,1)}, bf16[4,64,768...) custom-call(s32[3]{0:T(128)S(1)} %pad_add_fusion.place_ref, ...), custom_call_target="tpu_custom_call" | custom-call | flops 26449999872 | bytes 82800000 | tf_op jit(solution)/shard_map/feed/pallas_call | solution.py:281
  112.5 4.1 collective-permute-done.14.refs_12_.refs_4_.refs_8_
  119.0 16.9 %all-gather.2.cloned.1.call-done = bf16[1536,768]{1,0:T(8,128)(2,1)} async-done(((bf16[192,768]{1,0:T(8,128)(2,1)}), bf16[1536,768]{1,0:T(8,128)(2,1)}) %all-gather.2.cloned.1.call-update) | async-done | bytes 2359312 | tf_op jit(solution)/shard_map/all_gather | solution.py:925
  140.2 17.2 %attend.3 = (bf16[1024,768]{1,0:T(8,128)(2,1)}, bf16[1024,768]{1,0:T(8,128)(2,1)}, bf16[1024,2304]{1,0:T(8,128)(2,1)}, bf16[1024,768]{1,0:T(8,128)(2,1)}, f32[64...) custom-call(s32[3]{0:T(128)S(1)} %pad_add_fusion.place_ref, bf16[4,4,16,768]{3,2,1,0:T(8,128)(2,1)S(1)} %bitcast.91, ...), custom_call_target="tpu_custom_call" | custom-call | flops 19549999104 | bytes 61200000 | tf_op jit(solution)/shard_map/attend/pallas_call | solution.py:281
  157.5 22.8 %feed.3 = (f32[1024,768]{1,0:T(8,128)}, bf16[1024,768]{1,0:T(8,128)(2,1)}, bf16[1024,3072]{1,0:T(8,128)(2,1)}, bf16[1024,3072]{1,0:T(8,128)(2,1)}, bf16[1024,768]{1,0:T(8,128)(2,1)}) custom-call(s32[3]{0:T(128)S(1)} %pad_add_fusion.place_ref, bf16[1024,768]{1,0:T(8,128)(2,1)} %get-tuple-element.295.refs_0_.refs_2_, ...), custom_call_target="tpu_custom_call" | custom-call | flops 26449999872 | bytes 82800000 | tf_op jit(solution)/shard_map/feed/pallas_call | solution.py:281
  181.7 19.0 %code_loss.1 = (f32[1024,768]{1,0:T(8,128)}, f32[8,768]{1,0:T(8,128)S(1)}, bf16[2,768,768]{2,1,0:T(8,128)(2,1)S(1)}, bf16[2,768,768]{2,1,0:T(8,128)(2,1)S(1)}) custom-call(s32[3]{0:T(128)S(1)} %pad_add_fusion.place_ref, bf16[1024,768]{1,0:T(8,128)(2,1)S(1)} %copy-done.31, bf16[768,1024]{1,0:T(8,128)(2,1)S(1)} %copy-done.4, ...), custom_call_target="tpu_custom_call" | custom-call | flops 20700000256 | bytes 64800000 | tf_op jit(solution)/shard_map/code_loss/pallas_call | solution.py:281
  201.2 4.2 collective-permute-done.25
  207.8 25.0 %feed_back.2 = (f32[1024,768]{1,0:T(8,128)}, bf16[1024,768]{1,0:T(8,128)(2,1)S(1)}, f32[8,768]{1,0:T(8,128)S(1)}, bf16[2,768,768]{2,1,0:T(8,128)(2,1)}, bf16[2,768,768]{2,1,0:T(8,128)(2,1)}) custom-call(s32[3]{0:T(128)S(1)} %pad_add_fusion.place_ref, f32[1024,768]{1,0:T(8,128)} %get-tuple-element.311.refs_0_, bf16[1024,3072]{1,0:T(8,128)(2,1)} %get-tuple-element.312.refs_1_, ...), custom_call_target="tpu_custom_call" | custom-call | flops 29899999232 | bytes 93600000 | tf_op jit(solution)/shard_map/feed_back/pallas_call | solution.py:281
  236.5 2.4 collective-permute-done.27
  242.8 23.6 %attend_back.2 = (bf16[4,1024,576]{2,1,0:T(8,128)(2,1)}, bf16[4,4,16,768]{3,2,1,0:T(8,128)(2,1)S(1)}, bf16[4,4,16,768]{3,2,1,0:T(8,128)(2,1)S(1)}, bf16[4,4,16,7...) custom-call(s32[3]{0:T(128)S(1)} %pad_add_fusion.place_ref, ...), custom_call_target="tpu_custom_call" | custom-call | flops 28750000128 | bytes 90000000 | tf_op jit(solution)/shard_map/attend_back/pallas_call | solution.py:281
  266.4 2.8 collective-permute-done.28
  276.2 2.5 copy-done.20
  278.7 6.8 %grads_attn.1 = (bf16[2,768,768]{2,1,0:T(8,128)(2,1)S(1)}, bf16[2,768,768]{2,1,0:T(8,128)(2,1)S(1)}) custom-call(s32[3]{0:T(128)S(1)} %pad_add_fusion.place_ref, bf16[4,1024,576]{2,1,0:T(8,128)(2,1)S(1)} %copy-done.20, bf16[1024,768]{1,0:T(8,128)(2,1)S(1)} %copy-done.22, bf16[4,1024,192]{2,1,0:T(8,128)(2,1)S(1)} %copy-done.21, bf16[1024,768]{1,0:T(8,128)(2,1)S(1)} %copy-done.24), custom_call_target="tpu_custom_call" | custom-call | flops 12650000384 | bytes 39600000 | tf_op jit(solution)/shard_map/grads_attn/pallas_call | solution.py:281
  285.5 5.4 %collective-permute-done.32 = bf16[4,4,16,768]{3,2,1,0:T(8,128)(2,1)S(1)} collective-permute-done((bf16[4,4,16,768]{3,2,1,0:T(8,128)(2,1)S(1)}, bf16[4,4,16,768]{3,2,1,0:T(8,128)(2,1)S(1)}, u32[]{:S(2)}, u32[]{:S(2)}) %collective-permute-start.32) | collective-permute-done | bytes 393248 | tf_op jit(solution)/shard_map/ppermute | solution.py:759
  291.4 7.3 %grads_down.1 = (bf16[2,768,768]{2,1,0:T(8,128)(2,1)S(1)}, bf16[2,768,768]{2,1,0:T(8,128)(2,1)S(1)}) custom-call(s32[3]{0:T(128)S(1)} %pad_add_fusion.place_ref, bf16[1024,3072]{1,0:T(8,128)(2,1)S(1)} %bitcast.93, bf16[1024,768]{1,0:T(8,128)(2,1)S(1)} %bitcast.80), custom_call_target="tpu_custom_call" | custom-call | flops 11500000256 | bytes 36000000 | tf_op jit(solution)/shard_map/grads_down/pallas_call | solution.py:281
  301.1 2.2 collective-permute-done.36
  309.0 25.0 %feed_back.3 = (f32[1024,768]{1,0:T(8,128)}, bf16[1024,768]{1,0:T(8,128)(2,1)S(1)}, f32[8,768]{1,0:T(8,128)S(1)}, bf16[2,768,768]{2,1,0:T(8,128)(2,1)}, bf16[2,768,768]{2,1,0:T(8,128)(2,1)}) custom-call(s32[3]{0:T(128)S(1)} %pad_add_fusion.place_ref, bf16[1024,768]{1,0:T(8,128)(2,1)S(1)} %bitcast.81, bf16[1024,3072]{1,0:T(8,128)(2,1)} %get-tuple-element.370.refs_1_, ...), custom_call_target="tpu_custom_call" | custom-call | flops 29899999232 | bytes 93600000 | tf_op jit(solution)/shard_map/feed_back/pallas_call | solution.py:281
  347.3 30.4 %attend_back.3 = (f32[1024,768]{1,0:T(8,128)}, f32[8,768]{1,0:T(8,128)S(1)}, bf16[2,768,768]{2,1,0:T(8,128)(2,1)}, bf16[2,768,768]{2,1,0:T(8,128)(2,1)}) custom-call(s32[3]{0:T(128)S(1)} %pad_add_fusion.place_ref, f32[1024,768]{1,0:T(8,128)} %get-tuple-element.394.refs_0_, bf16[1024,768]{1,0:T(8,128)(2,1)S(1)} %get-tuple-element.395.refs_1_, ...), custom_call_target="tpu_custom_call" | custom-call | flops 28750000128 | bytes 90000000 | tf_op jit(solution)/shard_map/attend_back/pallas_call | solution.py:281
  383.7 5.2 %collective-permute-done.47 = bf16[192,768]{1,0:T(8,128)(2,1)S(1)} collective-permute-done((bf16[192,768]{1,0:T(8,128)(2,1)S(1)}, bf16[192,768]{1,0:T(8,128)(2,1)S(1)}, u32[]{:S(2)}, u32[]{:S(2)}) %collective-permute-start.47) | collective-permute-done | bytes 294944 | tf_op jit(solution)/shard_map/ppermute | solution.py:759
  396.1 18.7 %collective-permute-done.50 = bf16[192,768]{1,0:T(8,128)(2,1)S(1)} collective-permute-done((bf16[192,768]{1,0:T(8,128)(2,1)S(1)}, bf16[192,768]{1,0:T(8,128)(2,1)S(1)}, u32[]{:S(2)}, u32[]{:S(2)}) %collective-permute-start.50) | collective-permute-done | bytes 294944 | tf_op jit(solution)/shard_map/ppermute | solution.py:764
  414.8 5.2 %collective-permute-done.53 = bf16[192,768]{1,0:T(8,128)(2,1)S(1)} collective-permute-done((bf16[192,768]{1,0:T(8,128)(2,1)S(1)}, bf16[192,768]{1,0:T(8,128)(2,1)S(1)}, u32[]{:S(2)}, u32[]{:S(2)}) %collective-permute-start.53) | collective-permute-done | bytes 294944 | tf_op jit(solution)/shard_map/ppermute | solution.py:764
  424.7 2.3 emit.6.refs_0_
  427.0 5.5 %collective-permute-done.56 = bf16[192,768]{1,0:T(8,128)(2,1)S(1)} collective-permute-done((bf16[192,768]{1,0:T(8,128)(2,1)S(1)}, bf16[192,768]{1,0:T(8,128)(2,1)S(1)}, u32[]{:S(2)}, u32[]{:S(2)}) %collective-permute-start.56) | collective-permute-done | bytes 294944 | tf_op jit(solution)/shard_map/ppermute | solution.py:764
  432.4 5.9 %collective-permute-done.57 = bf16[192,768]{1,0:T(8,128)(2,1)S(1)} collective-permute-done((bf16[192,768]{1,0:T(8,128)(2,1)S(1)}, bf16[192,768]{1,0:T(8,128)(2,1)S(1)}, u32[]{:S(2)}, u32[]{:S(2)}) %collective-permute-start.57) | collective-permute-done | bytes 294944 | tf_op jit(solution)/shard_map/ppermute | solution.py:764
  441.2 2.2 collective-permute-start.61
  443.6 2.2 emit.7.refs_0_
  445.8 10.6 %collective-permute-done.60 = bf16[192,768]{1,0:T(8,128)(2,1)S(1)} collective-permute-done((bf16[192,768]{1,0:T(8,128)(2,1)S(1)}, bf16[192,768]{1,0:T(8,128)(2,1)S(1)}, u32[]{:S(2)}, u32[]{:S(2)}) %collective-permute-start.60) | collective-permute-done | bytes 294944 | tf_op jit(solution)/shard_map/ppermute | solution.py:764
  456.5 5.1 collective-permute-done.62
  466.4 2.2 emit.8
  468.7 10.0 %collective-permute-done.64 = f32[40,768]{1,0:T(8,128)S(1)} collective-permute-done((f32[40,768]{1,0:T(8,128)S(1)}, f32[40,768]{1,0:T(8,128)S(1)}, u32[]{:S(2)}, u32[]{:S(2)}) %collective-permute-start.64) | collective-permute-done | bytes 122912 | tf_op jit(solution)/shard_map/ppermute | solution.py:764
  482.5 2.2 emit.9
  486.5 3.1 collective-permute-done.69
  489.7 2.4 collective-permute-done.70.other_ref
  493.9 2.2 emit.10
  496.1 2.2 collective-permute-done.71
  504.7 2.2 emit.11
  (312 shorter events, 111.0 us)
Async XLA Ops:
  7.2 128.7 %all-gather.2.cloned.1.call-start = ((), (), s32[]{:S(2)}) async-start(), calls=%async_computation | async-start | bytes 2654208 | tf_op jit(solution)/shard_map/all_gather | solution.py:925
  28.3 27.2 %collective-permute-start.2 = (bf16[784,768]{1,0:T(8,128)(2,1)S(1)}, bf16[784,768]{1,0:T(8,128)(2,1)}, u32[]{:S(2)}, u32[]{:S(2)}) collective-permute-start(bf16[784,768]{1,0:T(8,128)(2,1)S(1)} %concatenate.40.refs_4_.refs_8_.refs_2_.refs_9_.refs_6_), channel_id=1, source_target_pairs={{0,2},{1,3},{2,0},{3,1},{4,6},{5,7},{6,4},{7,5},{8,10},{9,11},{10,... | collective-permute-start | bytes 3612680 | tf_op jit(solution)/shard_map/ppermute | solution.py:759
  39.9 15.6 %collective-permute-start.6 = (bf16[784,768]{1,0:T(8,128)(2,1)S(1)}, bf16[784,768]{1,0:T(8,128)(2,1)S(1)}, u32[]{:S(2)}, u32[]{:S(2)}) collective-permute-start(bf16[784,768]{1,0:T(8,128)(2,1)S(1)} %concatenate.40.refs_4_.refs_8_.refs_2_.refs_9_.refs_6_), channel_id=1, source_target_pairs={{0,1},{1,0},{2,3},{3,2},{4,5},{5,4},{6,7},{7,6},{8,9},{9,8},{10,11... | collective-permute-start | bytes 3612680 | tf_op jit(solution)/shard_map/ppermute | solution.py:759
  58.6 22.8 %collective-permute-start.10 = (bf16[2,768,768]{2,1,0:T(8,128)(2,1)}, bf16[2,768,768]{2,1,0:T(8,128)(2,1)}, u32[]{:S(2)}, u32[]{:S(2)}) collective-permute-start(bf16[2,768,768]{2,1,0:T(8,128)(2,1)} %refs_5_.8), channel_id=1, source_target_pairs={{0,1},{1,0},{2,3},{3,2},{4,5},{5,4},{6,7},{7,6},{8,9},{9,8},{10,11... | collective-permute-start | bytes 7077896 | tf_op jit(solution)/shard_map/ppermute | solution.py:759
  58.7 22.7 %collective-permute-start.11 = (bf16[2,768,768]{2,1,0:T(8,128)(2,1)}, bf16[2,768,768]{2,1,0:T(8,128)(2,1)}, u32[]{:S(2)}, u32[]{:S(2)}) collective-permute-start(bf16[2,768,768]{2,1,0:T(8,128)(2,1)} %refs_9_.3), channel_id=1, source_target_pairs={{0,1},{1,0},{2,3},{3,2},{4,5},{5,4},{6,7},{7,6},{8,9},{9,8},{10,11... | collective-permute-start | bytes 7077896 | tf_op jit(solution)/shard_map/ppermute | solution.py:759
  59.1 22.3 %collective-permute-start.9 = (bf16[192,768]{1,0:T(8,128)(2,1)S(1)}, bf16[192,768]{1,0:T(8,128)(2,1)}, u32[]{:S(2)}, u32[]{:S(2)}) collective-permute-start(bf16[192,768]{1,0:T(8,128)(2,1)S(1)} %pad_maximum_fusion.10), channel_id=1, source_target_pairs={{0,2},{1,3},{2,0},{3,1},{4,6},{5,7},{6,4},{7,5},{8,10},{9,11},{10,... | collective-permute-start | bytes 884744 | tf_op jit(solution)/shard_map/ppermute | solution.py:759
  60.6 20.8 %collective-permute-start.8 = (bf16[384,768]{1,0:T(8,128)(2,1)S(1)}, bf16[384,768]{1,0:T(8,128)(2,1)}, u32[]{:S(2)}, u32[]{:S(2)}) collective-permute-start(bf16[384,768]{1,0:T(8,128)(2,1)S(1)} %pad_maximum_fusion.5), channel_id=1, source_target_pairs={{0,8},{4,12},{8,0},{12,4},{16,24},{20,28},{24,16},{28,20},{1,9},{5... | collective-permute-start | bytes 1769480 | tf_op jit(solution)/shard_map/ppermute | solution.py:764
  62.1 19.2 %collective-permute-start.12 = (bf16[768,768]{1,0:T(8,128)(2,1)S(1)}, bf16[768,768]{1,0:T(8,128)(2,1)}, u32[]{:S(2)}, u32[]{:S(2)}) collective-permute-start(bf16[768,768]{1,0:T(8,128)(2,1)S(1)} %pad_maximum_fusion.1.refs_15_.refs_7_), channel_id=1, source_target_pairs={{0,1},{1,0},{2,3},{3,2},{4,5},{5,4},{6,7},{7,6},{8,9},{9,8},{10,11... | collective-permute-start | bytes 3538952 | tf_op jit(solution)/shard_map/ppermute | solution.py:759
  88.0 28.6 %collective-permute-start.14 = (bf16[768,768]{1,0:T(8,128)(2,1)}, bf16[768,768]{1,0:T(8,128)(2,1)}, u32[]{:S(2)}, u32[]{:S(2)}) collective-permute-start(bf16[768,768]{1,0:T(8,128)(2,1)} %pad_maximum_fusion.3.refs_10_.refs_2_.refs_6_), channel_id=1, source_target_pairs={{0,2},{1,3},{2,0},{3,1},{4,6},{5,7},{6,4},{7,5},{8,10},{9,11},{10,... | collective-permute-start | bytes 3538952 | tf_op jit(solution)/shard_map/ppermute | solution.py:759
  116.6 23.1 %collective-permute-start.18 = (bf16[768,768]{1,0:T(8,128)(2,1)}, bf16[768,768]{1,0:T(8,128)(2,1)}, u32[]{:S(2)}, u32[]{:S(2)}) collective-permute-start(bf16[768,768]{1,0:T(8,128)(2,1)} %collective-permute-done.14.refs_12_.refs_4_.refs_8_), channel_id=1, source_target_pairs={{0,1},{1,0},{2,3},{3,2},{4,5},{5,4},{6,7},{7,6},{8,9},{9,8},{10,11... | collective-permute-start | bytes 3538952 | tf_op jit(solution)/shard_map/ppermute | solution.py:759
  116.6 23.5 %collective-permute-start.19 = (bf16[768,768]{1,0:T(8,128)(2,1)}, bf16[768,768]{1,0:T(8,128)(2,1)}, u32[]{:S(2)}, u32[]{:S(2)}) collective-permute-start(bf16[768,768]{1,0:T(8,128)(2,1)} %pad_maximum_fusion.3.refs_10_.refs_2_.refs_6_), channel_id=1, source_target_pairs={{0,1},{1,0},{2,3},{3,2},{4,5},{5,4},{6,7},{7,6},{8,9},{9,8},{10,11... | collective-permute-start | bytes 3538952 | tf_op jit(solution)/shard_map/ppermute | solution.py:759
  117.1 20.6 %collective-permute-start.17 = (bf16[4,64,768]{2,1,0:T(8,128)(2,1)}, bf16[4,64,768]{2,1,0:T(8,128)(2,1)S(1)}, u32[]{:S(2)}, u32[]{:S(2)}) collective-permute-start(bf16[4,64,768]{2,1,0:T(8,128)(2,1)} %get-tuple-element.284), channel_id=1, source_target_pairs={{0,3},{1,2},{2,1},{3,0},{4,7},{5,6},{6,5},{7,4},{8,11},{9,10},{10,... | collective-permute-start | bytes 1179656 | tf_op jit(solution)/shard_map/ppermute | solution.py:759
  117.3 20.6 %collective-permute-start.16 = (bf16[4,64,768]{2,1,0:T(8,128)(2,1)}, bf16[4,64,768]{2,1,0:T(8,128)(2,1)S(1)}, u32[]{:S(2)}, u32[]{:S(2)}) collective-permute-start(bf16[4,64,768]{2,1,0:T(8,128)(2,1)} %get-tuple-element.282), channel_id=1, source_target_pairs={{0,2},{1,3},{2,0},{3,1},{4,6},{5,7},{6,4},{7,5},{8,10},{9,11},{10,... | collective-permute-start | bytes 1179656 | tf_op jit(solution)/shard_map/ppermute | solution.py:759
  118.7 20.6 %collective-permute-start.15 = (bf16[4,64,768]{2,1,0:T(8,128)(2,1)}, bf16[4,64,768]{2,1,0:T(8,128)(2,1)}, u32[]{:S(2)}, u32[]{:S(2)}) collective-permute-start(bf16[4,64,768]{2,1,0:T(8,128)(2,1)} %get-tuple-element.280), channel_id=1, source_target_pairs={{0,1},{1,0},{2,3},{3,2},{4,5},{5,4},{6,7},{7,6},{8,9},{9,8},{10,11... | collective-permute-start | bytes 1179656 | tf_op jit(solution)/shard_map/ppermute | solution.py:759
  137.8 42.5 %collective-permute-start.22 = (f32[4,64]{1,0:T(4,128)S(1)}, f32[4,64]{1,0:T(4,128)S(1)}, u32[]{:S(2)}, u32[]{:S(2)}) collective-permute-start(f32[4,64]{1,0:T(4,128)S(1)} %get-tuple-element.301), channel_id=1, source_target_pairs={{0,1},{1,0},{2,3},{3,2},{4,5},{5,4},{6,7},{7,6},{8,9},{9,8},{10,11... | collective-permute-start | bytes 3080 | tf_op jit(solution)/shard_map/ppermute | solution.py:759
  137.8 42.5 %collective-permute-start.23 = (f32[4,64]{1,0:T(4,128)S(1)}, f32[4,64]{1,0:T(4,128)S(1)}, u32[]{:S(2)}, u32[]{:S(2)}) collective-permute-start(f32[4,64]{1,0:T(4,128)S(1)} %get-tuple-element.302), channel_id=1, source_target_pairs={{0,2},{1,3},{2,0},{3,1},{4,6},{5,7},{6,4},{7,5},{8,10},{9,11},{10,... | collective-permute-start | bytes 3080 | tf_op jit(solution)/shard_map/ppermute | solution.py:759
  139.4 40.9 %collective-permute-start.24 = (f32[4,64]{1,0:T(4,128)S(1)}, f32[4,64]{1,0:T(4,128)S(1)}, u32[]{:S(2)}, u32[]{:S(2)}) collective-permute-start(f32[4,64]{1,0:T(4,128)S(1)} %get-tuple-element.303), channel_id=1, source_target_pairs={{0,3},{1,2},{2,1},{3,0},{4,7},{5,6},{6,5},{7,4},{8,11},{9,10},{10,... | collective-permute-start | bytes 3080 | tf_op jit(solution)/shard_map/ppermute | solution.py:759
  139.7 17.8 %collective-permute-start.20 = (bf16[768,768]{1,0:T(8,128)(2,1)S(1)}, bf16[768,768]{1,0:T(8,128)(2,1)S(1)}, u32[]{:S(2)}, u32[]{:S(2)}) collective-permute-start(bf16[768,768]{1,0:T(8,128)(2,1)S(1)} %bitcast.85), channel_id=1, source_target_pairs={{0,1},{1,0},{2,3},{3,2},{4,5},{5,4},{6,7},{7,6},{8,9},{9,8},{10,11... | collective-permute-start | bytes 3538952 | tf_op jit(solution)/shard_map/ppermute | solution.py:759
  140.1 17.4 %collective-permute-start.21 = (bf16[768,768]{1,0:T(8,128)(2,1)S(1)}, bf16[768,768]{1,0:T(8,128)(2,1)S(1)}, u32[]{:S(2)}, u32[]{:S(2)}) collective-permute-start(bf16[768,768]{1,0:T(8,128)(2,1)S(1)} %bitcast.82), channel_id=1, source_target_pairs={{0,1},{1,0},{2,3},{3,2},{4,5},{5,4},{6,7},{7,6},{8,9},{9,8},{10,11... | collective-permute-start | bytes 3538952 | tf_op jit(solution)/shard_map/ppermute | solution.py:759
  205.7 28.4 %collective-permute-start.26 = (bf16[768,768]{1,0:T(8,128)(2,1)S(1)}, bf16[768,768]{1,0:T(8,128)(2,1)}, u32[]{:S(2)}, u32[]{:S(2)}) collective-permute-start(bf16[768,768]{1,0:T(8,128)(2,1)S(1)} %fusion), channel_id=1, source_target_pairs={{0,2},{1,3},{2,0},{3,1},{4,6},{5,7},{6,4},{7,5},{8,10},{9,11},{10,... | collective-permute-start | bytes 3538952 | tf_op jit(solution)/shard_map/ppermute | solution.py:759
  240.7 25.7 %collective-permute-start.29 = (bf16[384,768]{1,0:T(8,128)(2,1)S(1)}, bf16[384,768]{1,0:T(8,128)(2,1)S(1)}, u32[]{:S(2)}, u32[]{:S(2)}) collective-permute-start(bf16[384,768]{1,0:T(8,128)(2,1)S(1)} %get-tuple-element.333), channel_id=1, source_target_pairs={{0,4},{4,0},{8,12},{12,8},{16,20},{20,16},{24,28},{28,24},{1,5},{5... | collective-permute-start | bytes 1769480 | tf_op jit(solution)/shard_map/ppermute | solution.py:764
  241.3 27.9 %collective-permute-start.28 = (bf16[768,768]{1,0:T(8,128)(2,1)S(1)}, bf16[768,768]{1,0:T(8,128)(2,1)S(1)}, u32[]{:S(2)}, u32[]{:S(2)}) collective-permute-start(bf16[768,768]{1,0:T(8,128)(2,1)S(1)} %fusion.1), channel_id=1, source_target_pairs={{0,2},{1,3},{2,0},{3,1},{4,6},{5,7},{6,4},{7,5},{8,10},{9,11},{10,... | collective-permute-start | bytes 3538952 | tf_op jit(solution)/shard_map/ppermute | solution.py:759
  272.9 18.0 %collective-permute-start.32 = (bf16[4,4,16,768]{3,2,1,0:T(8,128)(2,1)S(1)}, bf16[4,4,16,768]{3,2,1,0:T(8,128)(2,1)S(1)}, u32[]{:S(2)}, u32[]{:S(2)}) collective-permute-start(bf16[4,4,16,768]{3,2,1,0:T(8,128)(2,1)S(1)} %get-tuple-element.338), channel_id=1, source_target_pairs={{0,3},{1,2},{2,1},{3,0},{4,7},{5,6},{6,5},{7,4},{8,11},{9,10},{10,... | collective-permute-start | bytes 1179656 | tf_op jit(solution)/shard_map/ppermute | solution.py:759
  273.2 17.6 %collective-permute-start.33 = (bf16[384,768]{1,0:T(8,128)(2,1)S(1)}, bf16[384,768]{1,0:T(8,128)(2,1)S(1)}, u32[]{:S(2)}, u32[]{:S(2)}) collective-permute-start(bf16[384,768]{1,0:T(8,128)(2,1)S(1)} %get-tuple-element.352), channel_id=1, source_target_pairs={{0,4},{4,0},{8,12},{12,8},{16,20},{20,16},{24,28},{28,24},{1,5},{5... | collective-permute-start | bytes 1769480 | tf_op jit(solution)/shard_map/ppermute | solution.py:764
  274.7 16.2 %collective-permute-start.34 = (bf16[384,768]{1,0:T(8,128)(2,1)S(1)}, bf16[384,768]{1,0:T(8,128)(2,1)S(1)}, u32[]{:S(2)}, u32[]{:S(2)}) collective-permute-start(bf16[384,768]{1,0:T(8,128)(2,1)S(1)} %add_convert_fusion.11), channel_id=1, source_target_pairs={{0,8},{4,12},{8,0},{12,4},{16,24},{20,28},{24,16},{28,20},{1,9},{5... | collective-permute-start | bytes 1769480 | tf_op jit(solution)/shard_map/ppermute | solution.py:764
  303.6 30.4 %collective-permute-start.39 = (bf16[384,768]{1,0:T(8,128)(2,1)S(1)}, bf16[384,768]{1,0:T(8,128)(2,1)S(1)}, u32[]{:S(2)}, u32[]{:S(2)}) collective-permute-start(bf16[384,768]{1,0:T(8,128)(2,1)S(1)} %add_convert_fusion.10), channel_id=1, source_target_pairs={{0,16},{4,20},{8,24},{12,28},{16,0},{20,4},{24,8},{28,12},{1,17},{... | collective-permute-start | bytes 1769480 | tf_op jit(solution)/shard_map/ppermute | solution.py:764
  305.5 28.5 %collective-permute-start.40 = (bf16[384,768]{1,0:T(8,128)(2,1)S(1)}, bf16[384,768]{1,0:T(8,128)(2,1)S(1)}, u32[]{:S(2)}, u32[]{:S(2)}) collective-permute-start(bf16[384,768]{1,0:T(8,128)(2,1)S(1)} %add_convert_fusion.9), channel_id=1, source_target_pairs={{0,8},{4,12},{8,0},{12,4},{16,24},{20,28},{24,16},{28,20},{1,9},{5... | collective-permute-start | bytes 1769480 | tf_op jit(solution)/shard_map/ppermute | solution.py:764
  306.1 28.0 %collective-permute-start.37 = (bf16[768,768]{1,0:T(8,128)(2,1)S(1)}, bf16[768,768]{1,0:T(8,128)(2,1)}, u32[]{:S(2)}, u32[]{:S(2)}) collective-permute-start(bf16[768,768]{1,0:T(8,128)(2,1)S(1)} %fusion.2), channel_id=1, source_target_pairs={{0,2},{1,3},{2,0},{3,1},{4,6},{5,7},{6,4},{7,5},{8,10},{9,11},{10,... | collective-permute-start | bytes 3538952 | tf_op jit(solution)/shard_map/ppermute | solution.py:759
  307.6 27.6 %collective-permute-start.38 = (bf16[2,384,768]{2,1,0:T(8,128)(2,1)}, bf16[2,384,768]{2,1,0:T(8,128)(2,1)}, u32[]{:S(2)}, u32[]{:S(2)}) collective-permute-start(bf16[2,384,768]{2,1,0:T(8,128)(2,1)} %get-tuple-element.379), channel_id=1, source_target_pairs={{0,4},{4,0},{8,12},{12,8},{16,20},{20,16},{24,28},{28,24},{1,5},{5... | collective-permute-start | bytes 3538952 | tf_op jit(solution)/shard_map/ppermute | solution.py:764
  342.1 35.5 %collective-permute-start.42 = (bf16[2,192,768]{2,1,0:T(8,128)(2,1)}, bf16[2,192,768]{2,1,0:T(8,128)(2,1)S(1)}, u32[]{:S(2)}, u32[]{:S(2)}) collective-permute-start(bf16[2,192,768]{2,1,0:T(8,128)(2,1)} %get-tuple-element.403), channel_id=1, source_target_pairs={{0,8},{4,12},{8,0},{12,4},{16,24},{20,28},{24,16},{28,20},{1,9},{5... | collective-permute-start | bytes 1769480 | tf_op jit(solution)/shard_map/ppermute | solution.py:764
  343.6 34.1 %collective-permute-start.44 = (bf16[384,768]{1,0:T(8,128)(2,1)}, bf16[384,768]{1,0:T(8,128)(2,1)S(1)}, u32[]{:S(2)}, u32[]{:S(2)}) collective-permute-start(bf16[384,768]{1,0:T(8,128)(2,1)} %get-tuple-element.406), channel_id=1, source_target_pairs={{0,4},{4,0},{8,12},{12,8},{16,20},{20,16},{24,28},{28,24},{1,5},{5... | collective-permute-start | bytes 1769480 | tf_op jit(solution)/shard_map/ppermute | solution.py:764
  345.1 32.6 %collective-permute-start.45 = (bf16[384,768]{1,0:T(8,128)(2,1)S(1)}, bf16[384,768]{1,0:T(8,128)(2,1)S(1)}, u32[]{:S(2)}, u32[]{:S(2)}) collective-permute-start(bf16[384,768]{1,0:T(8,128)(2,1)S(1)} %add_convert_fusion.8), channel_id=1, source_target_pairs={{0,16},{4,20},{8,24},{12,28},{16,0},{20,4},{24,8},{28,12},{1,17},{... | collective-permute-start | bytes 1769480 | tf_op jit(solution)/shard_map/ppermute | solution.py:764
  346.1 31.6 %collective-permute-start.46 = (bf16[384,768]{1,0:T(8,128)(2,1)S(1)}, bf16[384,768]{1,0:T(8,128)(2,1)S(1)}, u32[]{:S(2)}, u32[]{:S(2)}) collective-permute-start(bf16[384,768]{1,0:T(8,128)(2,1)S(1)} %add_convert_fusion.7.mine_ref), channel_id=1, source_target_pairs={{0,4},{4,0},{8,12},{12,8},{16,20},{20,16},{24,28},{28,24},{1,5},{5... | collective-permute-start | bytes 1769480 | tf_op jit(solution)/shard_map/ppermute | solution.py:764
  346.7 31.0 %collective-permute-start.43 = (bf16[768,768]{1,0:T(8,128)(2,1)S(1)}, bf16[768,768]{1,0:T(8,128)(2,1)S(1)}, u32[]{:S(2)}, u32[]{:S(2)}) collective-permute-start(bf16[768,768]{1,0:T(8,128)(2,1)S(1)} %fusion.3), channel_id=1, source_target_pairs={{0,2},{1,3},{2,0},{3,1},{4,6},{5,7},{6,4},{7,5},{8,10},{9,11},{10,... | collective-permute-start | bytes 3538952 | tf_op jit(solution)/shard_map/ppermute | solution.py:759
  390.6 29.5 %collective-permute-start.52 = (bf16[768,768]{1,0:T(8,128)(2,1)S(1)}, bf16[768,768]{1,0:T(8,128)(2,1)S(1)}, u32[]{:S(2)}, u32[]{:S(2)}) collective-permute-start(bf16[768,768]{1,0:T(8,128)(2,1)S(1)} %fusion.4), channel_id=1, source_target_pairs={{0,2},{1,3},{2,0},{3,1},{4,6},{5,7},{6,4},{7,5},{8,10},{9,11},{10,... | collective-permute-start | bytes 3538952 | tf_op jit(solution)/shard_map/ppermute | solution.py:759
  391.2 28.9 %collective-permute-start.51 = (bf16[384,768]{1,0:T(8,128)(2,1)S(1)}, bf16[384,768]{1,0:T(8,128)(2,1)S(1)}, u32[]{:S(2)}, u32[]{:S(2)}) collective-permute-start(bf16[384,768]{1,0:T(8,128)(2,1)S(1)} %get-tuple-element.430), channel_id=1, source_target_pairs={{0,4},{4,0},{8,12},{12,8},{16,20},{20,16},{24,28},{28,24},{1,5},{5... | collective-permute-start | bytes 1769480 | tf_op jit(solution)/shard_map/ppermute | solution.py:764
  392.7 27.4 %collective-permute-start.54 = (bf16[384,768]{1,0:T(8,128)(2,1)S(1)}, bf16[384,768]{1,0:T(8,128)(2,1)S(1)}, u32[]{:S(2)}, u32[]{:S(2)}) collective-permute-start(bf16[384,768]{1,0:T(8,128)(2,1)S(1)} %add_convert_fusion.5.mine_ref), channel_id=1, source_target_pairs={{0,4},{4,0},{8,12},{12,8},{16,20},{20,16},{24,28},{28,24},{1,5},{5... | collective-permute-start | bytes 1769480 | tf_op jit(solution)/shard_map/ppermute | solution.py:764
  393.2 21.6 %collective-permute-start.50 = (bf16[192,768]{1,0:T(8,128)(2,1)S(1)}, bf16[192,768]{1,0:T(8,128)(2,1)S(1)}, u32[]{:S(2)}, u32[]{:S(2)}) collective-permute-start(bf16[192,768]{1,0:T(8,128)(2,1)S(1)} %add_convert_fusion.18), channel_id=1, source_target_pairs={{0,16},{4,20},{8,24},{12,28},{16,0},{20,4},{24,8},{28,12},{1,17},{... | collective-permute-start | bytes 884744 | tf_op jit(solution)/shard_map/ppermute | solution.py:764
  395.1 25.0 %collective-permute-start.53 = (bf16[192,768]{1,0:T(8,128)(2,1)S(1)}, bf16[192,768]{1,0:T(8,128)(2,1)S(1)}, u32[]{:S(2)}, u32[]{:S(2)}) collective-permute-start(bf16[192,768]{1,0:T(8,128)(2,1)S(1)} %add_convert_fusion.19), channel_id=1, source_target_pairs={{0,16},{4,20},{8,24},{12,28},{16,0},{20,4},{24,8},{28,12},{1,17},{... | collective-permute-start | bytes 884744 | tf_op jit(solution)/shard_map/ppermute | solution.py:764
  420.9 17.4 %collective-permute-start.58 = (bf16[384,768]{1,0:T(8,128)(2,1)S(1)}, bf16[384,768]{1,0:T(8,128)(2,1)S(1)}, u32[]{:S(2)}, u32[]{:S(2)}) collective-permute-start(bf16[384,768]{1,0:T(8,128)(2,1)S(1)} %get-tuple-element.444), channel_id=1, source_target_pairs={{0,4},{4,0},{8,12},{12,8},{16,20},{20,16},{24,28},{28,24},{1,5},{5... | collective-permute-start | bytes 1769480 | tf_op jit(solution)/shard_map/ppermute | solution.py:764
  422.6 15.7 %collective-permute-start.57 = (bf16[192,768]{1,0:T(8,128)(2,1)S(1)}, bf16[192,768]{1,0:T(8,128)(2,1)S(1)}, u32[]{:S(2)}, u32[]{:S(2)}) collective-permute-start(bf16[192,768]{1,0:T(8,128)(2,1)S(1)} %get-tuple-element.443), channel_id=1, source_target_pairs={{0,8},{4,12},{8,0},{12,4},{16,24},{20,28},{24,16},{28,20},{1,9},{5... | collective-permute-start | bytes 884744 | tf_op jit(solution)/shard_map/ppermute | solution.py:764
  438.8 22.8 %collective-permute-start.63 = (bf16[384,768]{1,0:T(8,128)(2,1)S(1)}, bf16[384,768]{1,0:T(8,128)(2,1)S(1)}, u32[]{:S(2)}, u32[]{:S(2)}) collective-permute-start(bf16[384,768]{1,0:T(8,128)(2,1)S(1)} %pad_maximum_fusion.6.mine_ref), channel_id=1, source_target_pairs={{0,4},{4,0},{8,12},{12,8},{16,20},{20,16},{24,28},{28,24},{1,5},{5... | collective-permute-start | bytes 1769480 | tf_op jit(solution)/shard_map/ppermute | solution.py:764
  440.9 15.6 %collective-permute-start.60 = (bf16[192,768]{1,0:T(8,128)(2,1)S(1)}, bf16[192,768]{1,0:T(8,128)(2,1)S(1)}, u32[]{:S(2)}, u32[]{:S(2)}) collective-permute-start(bf16[192,768]{1,0:T(8,128)(2,1)S(1)} %add_convert_fusion.15), channel_id=1, source_target_pairs={{0,8},{4,12},{8,0},{12,4},{16,24},{20,28},{24,16},{28,20},{1,9},{5... | collective-permute-start | bytes 884744 | tf_op jit(solution)/shard_map/ppermute | solution.py:764
  441.2 15.3 %collective-permute-start.61 = (bf16[192,768]{1,0:T(8,128)(2,1)S(1)}, bf16[192,768]{1,0:T(8,128)(2,1)S(1)}, u32[]{:S(2)}, u32[]{:S(2)}) collective-permute-start(bf16[192,768]{1,0:T(8,128)(2,1)S(1)} %add_convert_fusion.16), channel_id=1, source_target_pairs={{0,16},{4,20},{8,24},{12,28},{16,0},{20,4},{24,8},{28,12},{1,17},{... | collective-permute-start | bytes 884744 | tf_op jit(solution)/shard_map/ppermute | solution.py:764
  443.3 18.2 %collective-permute-start.62 = (bf16[192,768]{1,0:T(8,128)(2,1)S(1)}, bf16[192,768]{1,0:T(8,128)(2,1)S(1)}, u32[]{:S(2)}, u32[]{:S(2)}) collective-permute-start(bf16[192,768]{1,0:T(8,128)(2,1)S(1)} %get-tuple-element.458), channel_id=1, source_target_pairs={{0,8},{4,12},{8,0},{12,4},{16,24},{20,28},{24,16},{28,20},{1,9},{5... | collective-permute-start | bytes 884744 | tf_op jit(solution)/shard_map/ppermute | solution.py:764
  461.8 16.8 %collective-permute-start.67 = (bf16[384,768]{1,0:T(8,128)(2,1)S(1)}, bf16[384,768]{1,0:T(8,128)(2,1)S(1)}, u32[]{:S(2)}, u32[]{:S(2)}) collective-permute-start(bf16[384,768]{1,0:T(8,128)(2,1)S(1)} %pad_maximum_fusion.7.mine_ref), channel_id=1, source_target_pairs={{0,4},{4,0},{8,12},{12,8},{16,20},{20,16},{24,28},{28,24},{1,5},{5... | collective-permute-start | bytes 1769480 | tf_op jit(solution)/shard_map/ppermute | solution.py:764
  463.4 15.2 %collective-permute-start.64 = (f32[40,768]{1,0:T(8,128)S(1)}, f32[40,768]{1,0:T(8,128)S(1)}, u32[]{:S(2)}, u32[]{:S(2)}) collective-permute-start(f32[40,768]{1,0:T(8,128)S(1)} %add.202), channel_id=1, source_target_pairs={{0,4},{4,0},{8,12},{12,8},{16,20},{20,16},{24,28},{28,24},{1,5},{5... | collective-permute-start | bytes 368648 | tf_op jit(solution)/shard_map/ppermute | solution.py:764
  464.0 14.6 %collective-permute-start.65 = (bf16[192,768]{1,0:T(8,128)(2,1)S(1)}, bf16[192,768]{1,0:T(8,128)(2,1)S(1)}, u32[]{:S(2)}, u32[]{:S(2)}) collective-permute-start(bf16[192,768]{1,0:T(8,128)(2,1)S(1)} %add_convert_fusion.13), channel_id=1, source_target_pairs={{0,8},{4,12},{8,0},{12,4},{16,24},{20,28},{24,16},{28,20},{1,9},{5... | collective-permute-start | bytes 884744 | tf_op jit(solution)/shard_map/ppermute | solution.py:764
  (75 other events, 768.3 us)
Sparse Core Ops, SparseCore 0:
  85.4 50.4 all-gather.1
